TPU v7x, 32 devices: a whole 2x2x4 slice. The times are simulated.
32 devices in a mesh: seq: 8 (over z, y), tp: 4 (over x, core).
Axes of the slice: x: 2, y: 2, z: 4, core: 2. Of those that a mesh axis runs over, the one named last changes fastest.
Arguments:
- head_input: bfloat16 [4096, 5120], P('seq', 'tp'), may hold values from -5 to 5
- gate_input: bfloat16 [4096, 5120], P('seq', 'tp'), may hold values from -1000 to 1000
- write_vecs: bfloat16 [4096, 128], P('seq'), may hold values from -2.09375 to 2.09375
- read_vecs: bfloat16 [4096, 128], P('seq'), may hold values from -2.09375 to 2.09375
- step_raw: bfloat16 [80, 4096], P('tp', 'seq'), may hold values from -4 to 12
- segment_ids: int32 [4096], P('seq'), may hold values from 0 to 3, never falling along the last dimension, each value on 1 to 2048 neighbouring positions
- decay_log: float32 [80], P('tp'), may hold values from -8 to 0
- step_bias: float32 [80], P('tp'), may hold values from -8 to -1
- skip_gain: float32 [80], P('tp'), may hold values from 0.5 to 1.5
- norm_gain: float32 [5120], P('tp'), may hold values from 0.1 to 1.9
- out_weight: bfloat16 [5120, 2560], P('tp'), may hold values from -0.078125 to 0.078125
Outputs:
- mixed_out: bfloat16 [2560, 4096], P('tp', 'seq')
Inputs may be any that keep to these rules, and one draw needn't show every extreme that they name: `segment_ids`: never falls along the tokens; each id covers 1 to 2048 consecutive tokens, and one covers exactly 2048.
All inputs are finite; a program needn't handle non-finite values.
Results may differ from a plain program's by a relative error of at most 0.0054.
Values may be sent and summed in bfloat16 or wider, within the bound.
No kernel may reach another device: no remote copies, remote signals or barrier semaphores. Data moves between devices by JAX's collectives and lax.ppermute only.
A program may use at most 128 MiB of HBM per device.

v0:
```python
import jax
import jax.numpy as jnp
from jax import lax
from jax.sharding import PartitionSpec as P

HEADS = 80
HEAD_DIM = 64
GROUP = 256


def prefix(part, axis, combine, identity):
    place = lax.axis_index(axis)
    gathered = jax.tree.map(lambda a: lax.all_gather(a, axis), part)
    state = jax.tree.map(lambda a, e: jnp.zeros_like(a) + jnp.asarray(e, a.dtype), part, identity)

    def one(hop, state):
        return combine(
            state, jax.tree.map(lambda a: lax.dynamic_index_in_dim(a, hop, 0, False), gathered)
        )

    return lax.fori_loop(0, place, one, state)


def chain_combine(earlier, later):
    early_decay, early_state, early_first, early_last, early_valid = earlier
    late_decay, late_state, late_first, late_last, late_valid = later
    joined = jnp.where(
        (early_valid > 0) & (late_valid > 0), (late_first == early_last).astype(jnp.float32), 1.0
    )
    carry_decay = late_decay * joined
    return (
        carry_decay * early_decay,
        carry_decay[:, None, None] * early_state + late_state,
        jnp.where(early_valid > 0, early_first, late_first),
        jnp.where(late_valid > 0, late_last, early_last),
        jnp.maximum(early_valid, late_valid),
    )


def on_device(
    head_input,
    gate_input,
    write_vecs,
    read_vecs,
    step_raw,
    segment_ids,
    decay_log,
    step_bias,
    skip_gain,
    norm_gain,
    out_weight,
):
    local_heads = decay_log.shape[0]
    tok_rows = head_input.shape[0]
    head_width = head_input.shape[1] // local_heads
    state_width = write_vecs.shape[1]
    num_blocks = tok_rows // GROUP
    step_size = jax.nn.softplus(step_raw.astype(jnp.float32) + step_bias[:, None])
    decay_rate = -jnp.exp(decay_log)[:, None] * step_size
    row_iota = lax.broadcasted_iota(jnp.int32, (GROUP, GROUP), 0)
    col_iota = lax.broadcasted_iota(jnp.int32, (GROUP, GROUP), 1)
    tri_upper = (row_iota <= col_iota).astype(jnp.float32)
    causal = row_iota >= col_iota
    cumul = jnp.einsum(
        "hku,ut->hkt",
        decay_rate.reshape(local_heads, num_blocks, GROUP),
        tri_upper,
        precision=lax.Precision.HIGHEST,
    )
    inputs3 = head_input.reshape(tok_rows, local_heads, head_width)
    first_id = segment_ids[0]
    entry_id = first_id
    running = jnp.zeros((local_heads, head_width, state_width), jnp.float32)
    through = jnp.ones((local_heads,), jnp.float32)
    saved = []
    for block_idx in range(num_blocks):
        low_row = block_idx * GROUP
        x_block = inputs3[low_row : low_row + GROUP]
        write_block = write_vecs[low_row : low_row + GROUP]
        read_block = read_vecs[low_row : low_row + GROUP]
        seg_block = segment_ids[low_row : low_row + GROUP]
        step_block = step_size[:, low_row : low_row + GROUP]
        cum_block = cumul[:, block_idx, :]
        same_seg = (seg_block[:, None] == seg_block[None, :]) & causal
        scores = jnp.dot(read_block, write_block.T, preferred_element_type=jnp.float32)
        gap_rate = jnp.where(same_seg[None], cum_block[:, :, None] - cum_block[:, None, :], 0.0)
        mix_weights = jnp.where(
            same_seg[None], scores[None] * jnp.exp(gap_rate) * step_block[:, None, :], 0.0
        ).astype(jnp.bfloat16)
        inner_out = jnp.einsum(
            "htu,uhp->thp", mix_weights, x_block, preferred_element_type=jnp.float32
        )
        last_id = seg_block[-1]
        tail_scale = jnp.where(
            (seg_block == last_id)[None, :],
            jnp.exp(cum_block[:, -1:] - cum_block) * step_block,
            0.0,
        )
        written = (write_block[None].astype(jnp.float32) * tail_scale[:, :, None]).astype(
            jnp.bfloat16
        )
        block_state = jnp.einsum(
            "uhp,hun->hpn", x_block, written, preferred_element_type=jnp.float32
        )
        keep_rate = jnp.exp(cum_block[:, -1]) * (last_id == entry_id).astype(jnp.float32)
        entry_mask = (seg_block == entry_id).astype(jnp.float32)
        saved.append((inner_out, running, through, entry_mask, cum_block, read_block, x_block))
        running = keep_rate[:, None, None] * running + block_state
        through = through * keep_rate
        entry_id = last_id
    first_val = first_id.astype(jnp.float32)[None]
    last_val = segment_ids[-1].astype(jnp.float32)[None]
    identity = (
        jnp.ones((local_heads,), jnp.float32),
        jnp.zeros_like(running),
        jnp.zeros((1,), jnp.float32),
        jnp.zeros((1,), jnp.float32),
        jnp.zeros((1,), jnp.float32),
    )
    prefix_all = prefix(
        (through, running, first_val, last_val, jnp.ones((1,), jnp.float32)),
        "seq",
        chain_combine,
        identity,
    )
    prior_state = prefix_all[1]
    link_flag = ((prefix_all[4] > 0) & (prefix_all[3] == first_val)).astype(jnp.float32)
    incoming = prior_state * link_flag[0]
    pieces = []
    for inner_out, zero_entry, entry_gain, entry_mask, cum_block, read_block, x_block in saved:
        entry_state = zero_entry + entry_gain[:, None, None] * incoming
        carried = jnp.einsum(
            "tn,hpn->thp",
            read_block.astype(jnp.float32),
            entry_state,
            precision=lax.Precision.HIGHEST,
        )
        carried = carried * jnp.exp(cum_block).T[:, :, None] * entry_mask[:, None, None]
        ssm_out = inner_out + carried + skip_gain[None, :, None] * x_block.astype(jnp.float32)
        pieces.append(ssm_out.reshape(GROUP, local_heads * head_width))
    ssm_all = jnp.concatenate(pieces, axis=0)
    gated = ssm_all * jax.nn.silu(gate_input.astype(jnp.float32))
    totals = lax.psum(jnp.sum(gated * gated, axis=1), "tp")
    inv_rms = lax.rsqrt(totals / (HEADS * HEAD_DIM) + 1e-05)
    normed = (gated * inv_rms[:, None] * norm_gain[None, :]).astype(jnp.bfloat16)
    mixed = lax.psum_scatter(
        lax.dot_general(
            out_weight, normed, (((0,), (1,)), ((), ())), preferred_element_type=jnp.float32
        ),
        "tp",
        scatter_dimension=0,
        tiled=True,
    )
    return mixed.astype(jnp.bfloat16)


def solution(mesh):
    in_specs = (
        P("seq", "tp"),
        P("seq", "tp"),
        P("seq", None),
        P("seq", None),
        P("tp", "seq"),
        P("seq"),
        P("tp"),
        P("tp"),
        P("tp"),
        P("tp"),
        P("tp", None),
    )
    out_specs = P("tp", "seq")
    return jax.shard_map(
        on_device, mesh=mesh, in_specs=in_specs, out_specs=out_specs, check_vma=False
    )
```

profile of v0, /device:TPU:0, one launch (start us, length us, event | category | flops | bytes accessed | tf_op | source)
XLA Modules:
  0.0 232.4 jit_solution(6189492734801400546)
XLA Ops:
  6.5 0.0 all-gather.4.cloned.1.call-start
  6.5 1.4 fusion.70
  10.5 2.7 %compare_convert_fusion.1 = (f32[256]{0:T(256)S(1)}, pred[256]{0:T(512)(128)(4,1)S(1)}, pred[256]{0:T(512)(128)(4,1)S(1)}, f32[256]{0:T(256)S(1)}) fusion(s32[]{:T(128)} %bitcast.11, s32[512]{0:T(512)} %param.18, s32[]{:T(128)} %bitcast.10, s32[]{:T(128)} %bitcast.13), kind=kLoop, calls=%fused_computation.97 | loop fusion | flops 1536 | bytes 4620 | tf_op jit(solution)/shard_map/convert_element_type | solution.py:106
  13.1 0.7 exponential_negate_fusion
  13.8 0.9 broadcast_multiply_fusion
  14.7 0.2 fusion.52
  14.9 0.2 slice_reduce_fusion
  15.2 1.4 fusion.68
  16.6 0.2 copy.25
  16.8 0.0 copy-done.1
  16.8 0.2 copy.26
  17.1 0.0 copy-start.5
  17.1 0.0 copy-start.2
  17.1 0.0 copy-start
  17.1 0.1 multiply_select_fusion
  17.2 1.0 fusion.39
  18.2 1.9 fusion.41
  20.1 0.0 all-gather.4.cloned.1.call-update
  20.1 0.0 reduce-scatter.2.cloned.1.call-start
  21.5 0.0 copy-done.5
  21.5 0.6 dynamic-slice
  22.7 0.7 dynamic-update-slice.2
  23.3 0.7 dynamic-update-slice.3
  24.0 0.7 dynamic-update-slice.1
  24.7 0.2 dynamic-update-slice
  24.9 23.7 %all-reduce.4 = (f32[160]{0:T(256)S(1)}, f32[8]{0:T(128)S(1)}, f32[8]{0:T(128)S(1)}, f32[8]{0:T(128)S(1)}) all-reduce(f32[160]{0:T(256)S(1)} %dynamic-update-slice, f32[8]{0:T(128)S(1)} %dynamic-update-slice.1, f32[8]{0:T(128)S(1)} %dynamic-update-slice.2, f32[8]{0:T(128)S(1)} %dynamic-update-slice.3), channel_id=2, replica_groups=mesh['seq'=8,'tp'=4] {'seq'}, use_global_device_ids=true, to_apply=%add | all-reduce | flops 184 | bytes 1472
  48.6 0.1 reshape.162
  48.7 0.1 fusion.49
  48.8 0.2 fusion.60
  49.0 0.2 fusion.57
  49.2 2.8 %fusion.21 = f32[256,20,64]{0,2,1:T(8,128)} fusion(bf16[256,20,64]{0,2,1:T(8,128)(2,1)S(1)} %bitcast.104, f32[20,256]{1,0:T(8,128)S(1)} %get-tuple-element.131, f32[20,256]{1,0:T(8,128)S(1)} %get-tuple-element.134, f32[256,256]{1,0:T(8,128)S(1)} %fusion.60, pred[256,256]{1,0:T(8,128)(4,1)S(1)} %get-tuple-element.148), kind=kOutput, calls=%fused_computation.35 | convolution fusion | flops 175636480 | bytes 2334720 | tf_op jit(solution)/shard_map/htu,uhp->thp/dot_general | solution.py:90
  52.0 2.8 %fusion.20 = f32[256,20,64]{0,2,1:T(8,128)} fusion(bf16[256,20,64]{0,2,1:T(8,128)(2,1)S(1)} %bitcast.99, f32[20,256]{1,0:T(8,128)S(1)} %get-tuple-element.132, f32[20,256]{1,0:T(8,128)S(1)} %get-tuple-element.135, f32[256,256]{1,0:T(8,128)S(1)} %fusion.57, pred[256,256]{1,0:T(8,128)(4,1)S(1)} %get-tuple-element.147), kind=kOutput, calls=%fused_computation.34 | convolution fusion | flops 175636480 | bytes 2334720 | tf_op jit(solution)/shard_map/htu,uhp->thp/dot_general | solution.py:90
  54.8 54.7 %all-gather.4.cloned.1.call-done = f32[160,64,128]{2,1,0:T(8,128)} async-done(((f32[20,64,128]{2,1,0:T(8,128)}), f32[160,64,128]{2,1,0:T(8,128)}) %all-gather.4.cloned.1.call-update) | async-done | bytes 5242896 | tf_op jit(solution)/shard_map/all_gather | solution.py:13
  109.5 0.1 broadcast.101
  109.6 0.0 copy-start.3
  109.6 0.6 copy-done.3
  110.3 3.1 %fusion.29 = f32[256,20,64]{0,2,1:T(8,128)} fusion(f32[256,20,64]{0,2,1:T(8,128)} %fusion.21, bf16[256,20,64]{0,2,1:T(8,128)(2,1)S(1)} %bitcast.105, f32[20]{0:T(128)S(1)} %copy-done.3, f32[256]{0:T(256)S(1)} %get-tuple-element.138, f32[256,20]{0,1:T(8,128)S(1)} %get-tuple-element.130, f32[20,64,128]{2,1,0:T(8,128)S(1)} %get-tuple-element.90, f32[]{:T(128)} %bitcast.25, ...), kind=kOutput, calls=%fused_computation.45 | convolution fusion | flops 505446400 | bytes 4023812 | tf_op jit(solution)/shard_map/tn,hpn->thp/dot_general | solution.py:132
  113.4 1.7 copy.27
  115.1 3.2 %fusion.25 = f32[256,20,64]{0,2,1:T(8,128)} fusion(f32[256,20,64]{0,2,1:T(8,128)} %fusion.20, bf16[256,20,64]{0,2,1:T(8,128)(2,1)S(1)} %bitcast.100, f32[256]{0:T(256)S(1)} %get-tuple-element.141, f32[256,20]{0,1:T(8,128)S(1)} %get-tuple-element.133, f32[20,64,128]{2,1,0:T(8,128)S(1)} %fusion.39, f32[20]{0:T(128)S(1)} %copy-done.3, ...), kind=kOutput, calls=%fused_computation.40 | convolution fusion | flops 505774080 | bytes 4679684 | tf_op jit(solution)/shard_map/tn,hpn->thp/dot_general | solution.py:132
  118.3 1.7 copy.28
  120.0 0.0 copy-start.4
  120.0 2.2 multiply_reduce_fusion
  122.2 5.7 %psum.7 = f32[512]{0:T(512)S(1)} all-reduce(f32[512]{0:T(512)S(1)} %multiply_reduce_fusion), channel_id=1, replica_groups=mesh['seq'=8,'tp'=4] {'tp'}, use_global_device_ids=true, to_apply=%region_3.4 | all-reduce | flops 512 | bytes 4096 | tf_op jit(solution)/shard_map/psum | solution.py:143
  127.9 9.7 %convolution_bitcast_fusion = f32[2560,512]{0,1:T(8,128)} fusion(bf16[1280,2560]{1,0:T(8,128)(2,1)} %param.23, f32[1280]{0:T(1024)S(1)} %copy-done.4, f32[512]{0:T(512)S(1)} %add_rsqrt_fusion, bf16[512,1280]{1,0:T(8,128)(2,1)} %param.14, f32[256,1280]{1,0:T(8,128)S(1)} %copy.28, f32[256,1280]{1,0:T(8,128)S(1)} %copy.27), kind=kOutput, calls=%fused_computation.9 | convolution fusion | flops 3361996800 | bytes 15735808 | tf_op jit(solution)/shard_map/dot_general | solution.py:147
  137.6 0.0 reduce-scatter.2.cloned.1.call-update
  137.7 85.4 %reduce-scatter.2.cloned.1.call-done = f32[640,512]{0,1:T(8,128)} async-done(((f32[2560,512]{0,1:T(8,128)}), f32[640,512]{0,1:T(8,128)}) %reduce-scatter.2.cloned.1.call-update) | async-done | bytes 1310736 | tf_op jit(solution)/shard_map/reduce_scatter | solution.py:146
  223.0 1.4 convert_element_type.81
  224.4 1.1 copy.29
  (16 shorter events, 0.1 us)
Async XLA Ops:
  6.5 10.3 %copy-start.1 = (bf16[512,128]{1,0:T(8,128)(2,1)S(1)}, bf16[512,128]{1,0:T(8,128)(2,1)}, u32[]{:S(2)}) copy-start(bf16[512,128]{1,0:T(8,128)(2,1)} %param.15) | copy-start | bytes 393220
  6.5 103.0 %all-gather.4.cloned.1.call-start = ((), (), s32[]{:S(2)}) async-start(), calls=%async_computation.2 | async-start | bytes 5898240 | tf_op jit(solution)/shard_map/all_gather | solution.py:13
  17.1 4.4 %copy-start.5 = (u32[32]{0:T(128)S(1)}, u32[32]{0:T(128)}, u32[]{:S(2)}) copy-start(u32[32]{0:T(128)} %constant.58) | copy-start | bytes 388
  17.1 31.6 %copy-start.2 = (s32[512]{0:T(512)S(1)}, s32[512]{0:T(512)}, u32[]{:S(2)}) copy-start(s32[512]{0:T(512)} %param.18) | copy-start | bytes 6148
  17.1 31.7 %copy-start = (bf16[512,128]{1,0:T(8,128)(2,1)S(1)}, bf16[512,128]{1,0:T(8,128)(2,1)}, u32[]{:S(2)}) copy-start(bf16[512,128]{1,0:T(8,128)(2,1)} %param.16) | copy-start | bytes 393220
  20.1 202.9 %reduce-scatter.2.cloned.1.call-start = ((), (), s32[]{:S(2)}) async-start(), calls=%async_computation.1 | async-start | bytes 6553600 | tf_op jit(solution)/shard_map/reduce_scatter | solution.py:146
  109.6 0.7 copy-start.3
  120.0 7.9 %copy-start.4 = (f32[1280]{0:T(1024)S(1)}, f32[1280]{0:T(1024)}, u32[]{:S(2)}) copy-start(f32[1280]{0:T(1024)} %param.22) | copy-start | bytes 15364
Sparse Core Ops, SparseCore 0:
  20.3 89.2 all-gather.3
  137.8 85.2 reduce-scatter.1
where the time goes:
time: 233 us; the launch traced here: 232 us
  waiting for transfers between devices  140 us (60%)
  blocking collectives  29.4 us (13%)
  matrix products  25.1 us (11%)
  between operations  18 us (8%)
  local copies, waits for them, and re-layouts  11.4 us (5%)
  other arithmetic  8.26 us (4%)
    reduce_scatter x1, waiting for transfers between devices, on_device(): lax.psum_scatter(lax.dot_general(out_weight, normed, (((0,), (1,)), ((),...  85.4 us
    all_gather x1, waiting for transfers between devices, prefix(): gathered = jax.tree.map(lambda a: lax.all_gather(a, axis), part)  54.7 us
    unnamed x1, blocking collectives  23.7 us
    dot_general x1, matrix products, on_device(): lax.dot_general(out_weight, normed, (((0,), (1,)), ((), ())), preferred_e...  9.7 us
    dot_general x2, matrix products, on_device(): jnp.einsum('tn,hpn->thp', read_block.astype(jnp.float32), entry_state, pr...  6.31 us
    psum x1, blocking collectives, on_device(): totals = lax.psum(jnp.sum(gated * gated, axis=1), 'tp')  5.7 us
    dot_general x2, matrix products, on_device(): jnp.einsum('htu,uhp->thp', mix_weights, x_block, preferred_element_type=j...  5.57 us
  transfers between devices with their start and end apart: 2, of which 2 were waited for; matrix products, arithmetic and copies ran while one was open for 4% of the time, Pallas kernels for 0%

commit v1 on v0

v1 whole, which is shorter than its diff:
```python
import functools

import jax
import jax.numpy as jnp
from jax import lax
from jax.experimental import pallas as pl
from jax.experimental.pallas import tpu as pltpu
from jax.sharding import PartitionSpec as P

GROUP = 256
LANES = 128
EPS = 1e-05
LOG2E = 1.4426950408889634
SEG_LANE = 32
VMEM = 48 * 1024 * 1024
F32 = jnp.float32
BF16 = jnp.bfloat16


def dot(a, b, dims=((1,), (0,))):
    return lax.dot_general(a, b, (dims, ((), ())), preferred_element_type=F32)


def lane_iota(rows):
    return lax.broadcasted_iota(jnp.int32, (rows, LANES), 1)


def spread(cols, first, width):
    rows = cols.shape[0]
    per = LANES // width
    lane = lane_iota(rows)
    out = jnp.broadcast_to(cols[:, first : first + 1], (rows, LANES))
    for k in range(1, per):
        nxt = jnp.broadcast_to(cols[:, first + k : first + k + 1], (rows, LANES))
        out = jnp.where(lane < k * width, out, nxt)
    return out


def call(body, n_in, grid, in_specs, out_specs, out_shape, scratch=(), flops=0, nbytes=0):
    del n_in
    return pl.pallas_call(
        body,
        grid_spec=pltpu.PrefetchScalarGridSpec(
            num_scalar_prefetch=1,
            grid=grid,
            in_specs=in_specs,
            out_specs=out_specs,
            scratch_shapes=list(scratch),
        ),
        out_shape=out_shape,
        compiler_params=pltpu.CompilerParams(vmem_limit_bytes=VMEM),
        cost_estimate=pl.CostEstimate(flops=flops, bytes_accessed=nbytes, transcendentals=0),
    )


def whole(shape):
    return pl.BlockSpec(shape, lambda i, sc: (0,) * len(shape))


def prepare(heads, width, sc, raw, seg, decay_log, bias, skip, x, write):
    toks = raw.shape[1]
    half_w = x.shape[1] // 2
    half_h = heads // 2
    blocks = toks // GROUP

    def body(
        sc_ref, raw_ref, seg_ref, dl_ref, sb_ref, sk_ref, x_ref, wr_ref,
        send_ref, ccol_ref, arow_ref, tail_ref, meta_ref, pad, rows,
    ):
        pad[...] = jnp.zeros_like(pad)
        pad[0:heads] = raw_ref[...].astype(F32)
        pad[SEG_LANE : SEG_LANE + 1] = seg_ref[...].astype(F32)
        rows[...] = jnp.zeros_like(rows)
        rows[0:1, 0:heads] = dl_ref[...]
        rows[1:2, 0:heads] = sb_ref[...]
        rows[2:3, 0:heads] = sk_ref[...]
        cols = jnp.transpose(pad[...])
        lane = lane_iota(toks)
        z = cols + rows[1:2]
        step = jnp.maximum(z, 0.0) + jnp.log1p(jnp.exp(-jnp.abs(z)))
        rate = -jnp.exp(rows[0:1]) * step
        tri = (
            lax.broadcasted_iota(jnp.int32, (GROUP, GROUP), 0)
            >= lax.broadcasted_iota(jnp.int32, (GROUP, GROUP), 1)
        ).astype(BF16)
        cum, full = [], []
        base = jnp.zeros((1, LANES), F32)
        for b in range(blocks):
            r = rate[b * GROUP : (b + 1) * GROUP]
            r1 = r.astype(BF16)
            d1 = r - r1.astype(F32)
            r2 = d1.astype(BF16)
            r3 = (d1 - r2.astype(F32)).astype(BF16)
            c = dot(tri, r1) + (dot(tri, r2) + dot(tri, r3))
            cum.append(c)
            full.append(c + base)
            base = base + c[GROUP - 1 : GROUP]
        total = base
        seg_col = cols[:, SEG_LANE : SEG_LANE + 1]
        last = cols[toks - 1 : toks, SEG_LANE : SEG_LANE + 1]
        cum_all = jnp.concatenate(cum, axis=0)
        tail = jnp.exp(total - jnp.concatenate(full, axis=0)) * step
        tail = jnp.where(seg_col == last, tail, 0.0)
        last0 = cols[GROUP - 1 : GROUP, SEG_LANE : SEG_LANE + 1]
        tail0 = jnp.exp(cum[0][GROUP - 1 : GROUP] - cum[0]) * step[0:GROUP]
        tail0 = jnp.where(seg_col[0:GROUP] == last0, tail0, 0.0)
        cc = cum_all * LOG2E
        a = jnp.where(lane == SEG_LANE, cols, cc - jnp.log(step) * LOG2E)
        arow_ref[...] = jnp.transpose(a)[0:64]
        seg_b = jnp.broadcast_to(seg_col, (toks, LANES))
        ccol_ref[0] = jnp.where(lane == SEG_LANE, seg_b, cc)
        ccol_ref[1] = jnp.where(lane == SEG_LANE, seg_b, pltpu.roll(cc, LANES - half_h, 1))
        tail_r = pltpu.roll(tail, LANES - half_h, 1)
        tail_ref[0, 0:toks] = tail
        tail_ref[1, 0:toks] = tail_r
        tail_ref[0, toks : toks + GROUP] = tail0
        tail_ref[1, toks : toks + GROUP] = pltpu.roll(tail0, LANES - half_h, 1)
        keep = jnp.exp(total)
        per = LANES // width
        for j in range(2):
            for i in range(half_w // LANES):
                at = j * half_h + i * per
                tile = slice(i * LANES, (i + 1) * LANES)
                meta_ref[j, 0:1, tile] = spread(keep, at, width)
                meta_ref[j, 1:2, tile] = jnp.broadcast_to(last, (1, LANES))
                meta_ref[j, 2:3, tile] = spread(rows[2:3], at, width)
                meta_ref[j, 3:8, tile] = jnp.zeros((5, LANES), F32)
        mine = jnp.where(sc_ref[1] == 0, tail, tail_r)
        parts = []
        for i in range(half_w // LANES):
            xt = x_ref[:, i * LANES : (i + 1) * LANES].astype(F32)
            parts.append((xt * spread(mine, i * per, width)).astype(BF16))
        xs = jnp.concatenate(parts, axis=1)
        send_ref[...] = dot(wr_ref[...], xs, ((0,), (0,))).astype(BF16)

    state = write.shape[1]
    return call(
        body, 7, (1,),
        [
            whole(raw.shape), whole(seg.shape), whole(decay_log.shape), whole(bias.shape), whole(skip.shape),
            pl.BlockSpec((toks, half_w), lambda i, sc: (0, sc[1])),
            whole(write.shape),
        ],
        [
            whole((state, half_w)), whole((2, toks, LANES)), whole((64, toks)),
            whole((2, toks + GROUP, LANES)), whole((2, 8, half_w)),
        ],
        [
            jax.ShapeDtypeStruct((state, half_w), BF16),
            jax.ShapeDtypeStruct((2, toks, LANES), F32),
            jax.ShapeDtypeStruct((64, toks), F32),
            jax.ShapeDtypeStruct((2, toks + GROUP, LANES), F32),
            jax.ShapeDtypeStruct((2, 8, half_w), F32),
        ],
        [pltpu.VMEM((LANES, toks), F32), pltpu.VMEM((8, LANES), F32)],
        flops=2 * toks * state * half_w, nbytes=4_000_000,
    )(sc, raw, seg, decay_log, bias, skip, x, write)


def kept_state(width, sc, tail, x, write):
    toks, state = write.shape
    half_w = x.shape[1] // 2
    per = LANES // width

    def body(sc_ref, tail_ref, x_ref, wr_ref, out_ref):
        mine = tail_ref[0]
        parts = []
        for i in range(half_w // LANES):
            xt = x_ref[:, i * LANES : (i + 1) * LANES].astype(F32)
            parts.append((xt * spread(mine, i * per, width)).astype(BF16))
        out_ref[...] = dot(wr_ref[...], jnp.concatenate(parts, axis=1), ((0,), (0,)))

    return call(
        body, 3, (1,),
        [
            pl.BlockSpec((1, toks, LANES), lambda i, sc: (sc[0], 0, 0)),
            pl.BlockSpec((toks, half_w), lambda i, sc: (0, sc[0])),
            whole(write.shape),
        ],
        whole((state, half_w)),
        jax.ShapeDtypeStruct((state, half_w), F32),
        flops=2 * toks * state * half_w, nbytes=2_000_000,
    )(sc, tail, x, write)


def local_part(which, heads, width, sc, x, gate, read, write, ccol, arow, tail, meta):
    toks, state = write.shape
    half_w = x.shape[1] // 2
    half_h = heads // 2
    per = LANES // width
    tiles = half_w // LANES
    blocks = toks // GROUP
    sub = GROUP // 2

    def body(
        sc_ref, x_ref, gate_ref, rd_ref, wr_ref, ccol_ref, arow_ref, tail0_ref, meta_ref,
        a_ref, b_ref, scores,
    ):
        i = pl.program_id(0)
        seg_col = ccol_ref[0, :, SEG_LANE : SEG_LANE + 1]

        @pl.when(i == 0)
        def _():
            for b in range(blocks):
                rows = slice(b * GROUP, (b + 1) * GROUP)
                s = dot(rd_ref[rows], wr_ref[rows], ((1,), (1,)))
                causal = lax.broadcasted_iota(jnp.int32, (GROUP, GROUP), 0) >= lax.broadcasted_iota(
                    jnp.int32, (GROUP, GROUP), 1
                )
                same = seg_col[rows] == arow_ref[SEG_LANE : SEG_LANE + 1, rows]
                scores[b] = jnp.where(causal & same, s, 0.0)

        turn = lax.rem(LANES - per * i, LANES)
        cr = pltpu.roll(ccol_ref[0], turn, 1)
        tr = pltpu.roll(tail0_ref[0], turn, 1)
        skip = meta_ref[0, 2:3, :]
        lane = lane_iota(GROUP)
        head0 = sc_ref[which] * half_h + per * i
        carry = None
        start = jnp.ones((1, LANES), F32)
        for b in range(blocks):
            rows = slice(b * GROUP, (b + 1) * GROUP)
            xb = x_ref[rows]
            inner = None
            dec_log = None
            for k in range(per):
                cb = jnp.broadcast_to(cr[rows, k : k + 1], (GROUP, LANES))
                ar = arow_ref[pl.ds(head0 + k, 1), rows]
                sb = scores[b]
                lo = jnp.exp2(jnp.minimum(cb - ar[:, 0:sub], 60.0)) * sb[:, 0:sub]
                hi = jnp.exp2(jnp.minimum(cb[sub:] - ar[:, sub:], 60.0)) * sb[sub:, sub:]
                lo = lo.astype(BF16)
                top = dot(lo[0:sub], xb[0:sub])
                bottom = dot(jnp.concatenate([lo[sub:], hi.astype(BF16)], axis=1), xb)
                o = jnp.concatenate([top, bottom], axis=0)
                inner = o if inner is None else jnp.where(lane < k * width, inner, o)
                dec_log = cb if dec_log is None else jnp.where(lane < k * width, dec_log, cb)
            dec = jnp.exp2(dec_log)
            xf = xb.astype(F32)
            y = inner + skip * xf
            if b == 1:
                linked = seg_col[rows] == seg_col[GROUP - 1 : GROUP]
                rm = jnp.where(linked, rd_ref[rows].astype(F32), 0.0).astype(BF16)
                y = y + (dot(rm, carry[0]) + dot(rm, carry[1])) * dec
            else:
                xs = (xf * spread(tr, 0, width)).astype(BF16)
                s0 = dot(wr_ref[rows], xs, ((0,), (0,)))
                s0h = s0.astype(BF16)
                carry = (s0h, (s0 - s0h.astype(F32)).astype(BF16))
            v = gate_ref[rows].astype(F32)
            sg = v / (1.0 + jnp.exp(-v))
            a_ref[rows] = sg * y
            b_ref[rows] = sg * (dec * start)
            start = start * dec[GROUP - 1 : GROUP]

    tile = pl.BlockSpec((toks, LANES), lambda i, sc: (0, sc[which] * tiles + i))
    out = pl.BlockSpec((toks, LANES), lambda i, sc: (0, i))
    return call(
        body, 8, (tiles,),
        [
            tile, tile, whole(read.shape), whole(write.shape),
            pl.BlockSpec((1, toks, LANES), lambda i, sc: (sc[which], 0, 0)),
            whole(arow.shape),
            pl.BlockSpec((1, GROUP, LANES), lambda i, sc: (sc[which], toks // GROUP, 0)),
            pl.BlockSpec((1, 8, LANES), lambda i, sc: (sc[which], 0, i)),
        ],
        [out, out],
        [jax.ShapeDtypeStruct((toks, half_w), F32), jax.ShapeDtypeStruct((toks, half_w), F32)],
        [pltpu.VMEM((blocks, GROUP, GROUP), F32)],
        flops=4_000_000_000, nbytes=8_000_000,
    )(sc, x, gate, read, write, ccol, arow, tail, meta)


def gated_tile(prev_ref, rd_ref, seg_ref, a_ref, b_ref, e_ref, gain_ref):
    linked = seg_ref[0, :, SEG_LANE : SEG_LANE + 1] == prev_ref[0:1, 0:1]
    rm = jnp.where(linked, rd_ref[...].astype(F32), 0.0).astype(BF16)
    gated = a_ref[...] + b_ref[...] * dot(rm, e_ref[...])
    sq = gated * gated
    part = sq[:, 0:LANES]
    for i in range(1, sq.shape[1] // LANES):
        part = part + sq[:, i * LANES : (i + 1) * LANES]
    squares = jnp.sum(jnp.transpose(part), axis=0, keepdims=True)
    return (gated * gain_ref[...]).astype(BF16), squares


def gate_specs(which, toks, half_w, state):
    return [
        whole((8, LANES)), whole((toks, state)),
        pl.BlockSpec((1, toks, LANES), lambda i, sc: (0, 0, 0)),
        whole((toks, half_w)), whole((toks, half_w)), whole((state, half_w)),
        pl.BlockSpec((1, half_w), lambda i, sc: (0, sc[which])),
    ]


def gated_half(which, sc, prev, read, ccol, a, b, e, gain):
    toks, half_w = a.shape

    def body(sc_ref, prev_ref, rd_ref, seg_ref, a_ref, b_ref, e_ref, gain_ref, g_ref, s_ref):
        g_ref[...], s_ref[...] = gated_tile(prev_ref, rd_ref, seg_ref, a_ref, b_ref, e_ref, gain_ref)

    return call(
        body, 7, (1,),
        gate_specs(which, toks, half_w, read.shape[1]),
        [whole((toks, half_w)), whole((1, toks))],
        [jax.ShapeDtypeStruct((toks, half_w), BF16), jax.ShapeDtypeStruct((1, toks), F32)],
        flops=2 * toks * half_w * read.shape[1], nbytes=4_000_000,
    )(sc, prev, read, ccol, a, b, e, gain)


def gate_and_project(which, quarter, sc, prev, read, ccol, a, b, e, gain, g_keep, weight):
    toks, half_w = a.shape
    cols = weight.shape[1] // 4

    def body(
        sc_ref, prev_ref, rd_ref, seg_ref, a_ref, b_ref, e_ref, gain_ref, gk_ref, w_ref,
        g_ref, s_ref, y_ref,
    ):
        g, s_ref[...] = gated_tile(prev_ref, rd_ref, seg_ref, a_ref, b_ref, e_ref, gain_ref)
        g_ref[...] = g
        y = dot(gk_ref[...], w_ref[pl.ds(sc_ref[0] * half_w, half_w)])
        y = y + dot(g, w_ref[pl.ds(sc_ref[1] * half_w, half_w)])
        y_ref[...] = y.astype(BF16)

    return call(
        body, 9, (1,),
        gate_specs(which, toks, half_w, read.shape[1])
        + [whole((toks, half_w)), pl.BlockSpec((2 * half_w, cols), lambda i, sc: (0, sc[quarter]))],
        [whole((toks, half_w)), whole((1, toks)), whole((toks, cols))],
        [
            jax.ShapeDtypeStruct((toks, half_w), BF16),
            jax.ShapeDtypeStruct((1, toks), F32),
            jax.ShapeDtypeStruct((toks, cols), BF16),
        ],
        flops=4 * toks * half_w * cols, nbytes=6_000_000,
    )(sc, prev, read, ccol, a, b, e, gain, g_keep, weight)


def project(quarter, dtype, sc, g_keep, g_other, weight):
    toks, half_w = g_keep.shape
    cols = weight.shape[1] // 4

    def body(sc_ref, gk_ref, go_ref, w_ref, y_ref):
        y = dot(gk_ref[...], w_ref[pl.ds(sc_ref[0] * half_w, half_w)])
        y = y + dot(go_ref[...], w_ref[pl.ds(sc_ref[1] * half_w, half_w)])
        y_ref[...] = y.astype(dtype)

    return call(
        body, 3, (1,),
        [
            whole((toks, half_w)), whole((toks, half_w)),
            pl.BlockSpec((2 * half_w, cols), lambda i, sc: (0, sc[quarter])),
        ],
        whole((toks, cols)),
        jax.ShapeDtypeStruct((toks, cols), dtype),
        flops=4 * toks * half_w * cols, nbytes=4_000_000,
    )(sc, g_keep, g_other, weight)


def finish(features, sc, own, from_core, from_far, squares):
    toks, cols = own.shape

    def body(sc_ref, own_ref, core_ref, far_ref, sq_ref, out_ref):
        y = (own_ref[...] + core_ref[...].astype(F32)) + far_ref[...].astype(F32)
        inv = lax.rsqrt(sq_ref[...] / features + EPS)
        out_ref[...] = (jnp.transpose(y) * inv).astype(BF16)

    return call(
        body, 4, (1,),
        [whole((toks, cols))] * 3 + [whole((1, toks))],
        whole((cols, toks)),
        jax.ShapeDtypeStruct((cols, toks), BF16),
        flops=4 * toks * cols, nbytes=3_000_000,
    )(sc, own, from_core, from_far, squares)


def on_device(
    n_seq, n_tp, head_input, gate_input, write_vecs, read_vecs, step_raw, segment_ids,
    decay_log, step_bias, skip_gain, norm_gain, out_weight,
):
    heads = decay_log.shape[0]
    toks, feats = head_input.shape
    width = feats // heads
    half_w = feats // 2
    place = lax.axis_index("seq")
    rank = lax.axis_index("tp")
    odd = lax.rem(place, 2)
    even = odd == 0
    near, far = rank ^ 1, rank ^ 2
    sc = jnp.stack([odd, 1 - odd, far ^ 1, far, near, rank]).astype(jnp.int32)

    def pair(a):
        return lax.ppermute(a, "seq", [(i, i ^ 1) for i in range(n_seq)])

    def shift(a, by):
        return lax.ppermute(a, "seq", [(i, i + by) for i in range(n_seq - by)])

    def across(a, bit):
        return lax.ppermute(a, "tp", [(i, i ^ bit) for i in range(n_tp)])

    send, ccol, arow, tail, meta = prepare(
        heads, width, sc, step_raw, segment_ids.reshape(1, toks), decay_log.reshape(1, heads),
        step_bias.reshape(1, heads), skip_gain.reshape(1, heads), head_input, write_vecs,
    )
    got_state = pair(send)
    got_meta = pair(lax.dynamic_index_in_dim(meta, 1 - odd, 0, False))
    own_meta = lax.dynamic_index_in_dim(meta, odd, 0, False)
    own_state = kept_state(width, sc, tail, head_input, write_vecs)
    a_keep, b_keep = local_part(
        0, heads, width, sc, head_input, gate_input, read_vecs, write_vecs, ccol, arow, tail, meta
    )
    keep_first = jnp.where(even, own_meta[0:1], got_meta[0:1])
    keep_second = jnp.where(even, got_meta[0:1], own_meta[0:1])
    last_first = jnp.where(even, own_meta[1:2, 0:1], got_meta[1:2, 0:1])
    last_second = jnp.where(even, got_meta[1:2, 0:1], own_meta[1:2, 0:1])
    got_f = got_state.astype(F32)
    first = jnp.where(even, own_state, got_f)
    second = jnp.where(even, got_f, own_state)
    joined = second + keep_second * (last_first == last_second).astype(F32) * first
    through = keep_first * keep_second
    last_tile = jnp.broadcast_to(last_second, (8, LANES))
    prev_last = shift(last_tile, 2)
    reach = 1
    pairs = n_seq // 2
    while reach < pairs // 2:
        before = shift(joined.astype(BF16), 2 * reach)
        last_before = prev_last if reach == 1 else shift(last_tile, 2 * reach)
        link = through * (last_before[0:1, 0:1] == last_second).astype(F32)
        joined = joined + link * before.astype(F32)
        if 2 * reach < pairs // 2:
            through = link * shift(through, 2 * reach)
        reach *= 2
    entry = shift(joined.astype(BF16), 2)
    a_other, b_other = local_part(
        1, heads, width, sc, head_input, gate_input, read_vecs, write_vecs, ccol, arow, tail, meta
    )
    prev_id = prev_last[0:1, 0:1]
    after_first = (
        first + keep_first * (last_first == prev_id).astype(F32) * entry.astype(F32)
    ).astype(BF16)
    e_other = pair(jnp.where(even, after_first, entry))
    e_keep = jnp.where(even, entry, after_first)
    prev = jnp.where(even, prev_last, jnp.broadcast_to(last_first, (8, LANES)))
    gain = norm_gain.reshape(1, feats)
    g_keep, s_keep = gated_half(0, sc, prev, read_vecs, ccol, a_keep, b_keep, e_keep, gain)
    g_other, s_other, y_far_near = gate_and_project(
        1, 2, sc, prev, read_vecs, ccol, a_other, b_other, e_other, gain, g_keep, out_weight
    )
    got_far = across(y_far_near, 1)
    y_far = project(3, F32, sc, g_keep, g_other, out_weight)
    got_x = across((y_far + got_far.astype(F32)).astype(BF16), 2)
    squares = s_keep + s_other
    squares = squares + across(squares, 1)
    squares = squares + across(squares, 2)
    got_near = across(project(4, BF16, sc, g_keep, g_other, out_weight), 1)
    y_own = project(5, F32, sc, g_keep, g_other, out_weight)
    return finish(feats * n_tp, sc, y_own, got_near, got_x, squares)


def solution(mesh):
    in_specs = (
        P("seq", "tp"),
        P("seq", "tp"),
        P("seq", None),
        P("seq", None),
        P("tp", "seq"),
        P("seq"),
        P("tp"),
        P("tp"),
        P("tp"),
        P("tp"),
        P("tp", None),
    )
    out_specs = P("tp", "seq")
    return jax.shard_map(
        functools.partial(on_device, mesh.shape["seq"], mesh.shape["tp"]),
        mesh=mesh, in_specs=in_specs, out_specs=out_specs, check_vma=False,
    )
```

time: 233 us -> 81 us (0.35)
  waiting for transfers between devices: 140 us -> 18 us
  Pallas kernels: 0 us -> 32.4 us
  blocking collectives: 29.4 us -> 0 us
  matrix products: 25.1 us -> 0 us
  starting transfers between devices: 0.04 us -> 18.1 us
  between operations: 18 us -> 4.07 us
  other arithmetic: 8.26 us -> 0.49 us
  local copies, waits for them, and re-layouts: 11.4 us -> 7.3 us
    reduce_scatter x1 -> x0, waiting for transfers between devices: 85.4 us -> none  [on_device(): lax.psum_scatter(lax.dot_general(out_weight, normed, (((0,), (1,)), ((),...]
    all_gather x1 -> x0, waiting for transfers between devices: 54.7 us -> none  [prefix(): gathered = jax.tree.map(lambda a: lax.all_gather(a, axis), part)]
    pallas_call x0 -> x10, Pallas kernels: none -> 32.4 us  [the longest x2 11.8 us: local_part(): call(body, 8, (tiles,), [tile, tile, whole(read.shape), whole(write.shape...]
    dot_general x10 -> x0, matrix products: 25.1 us -> none  [the longest x1 9.7 us: on_device(): lax.dot_general(out_weight, normed, (((0,), (1,)), ((), ())), preferred_e...]
    unnamed x1 -> x0, blocking collectives: 23.7 us -> none
    ppermute x0 -> x11, starting transfers between devices: none -> 18.1 us  [the longest x3 10.7 us: shift(): return lax.ppermute(a, 'seq', [(i, i + by) for i in range(n_seq - by)])]
    ppermute x0 -> x11, waiting for transfers between devices: none -> 18 us  [the longest x5 11.4 us: across(): return lax.ppermute(a, 'tp', [(i, i ^ bit) for i in range(n_tp)])]
    psum x1 -> x0, blocking collectives: 5.7 us -> none  [on_device(): totals = lax.psum(jnp.sum(gated * gated, axis=1), 'tp')]
  transfers between devices with their start and end apart: 2 -> 11, of which waited for: 2 -> 4; matrix products, arithmetic and copies ran while one was open for 4% -> 2% of each run, Pallas kernels for 0% -> 30%
where the time goes in v1:
time: 81 us; the launch traced here: 80.3 us
  Pallas kernels  32.4 us (40%)
  starting transfers between devices  18.1 us (22%)
  waiting for transfers between devices  18 us (22%)
  local copies, waits for them, and re-layouts  7.3 us (9%)
  between operations  4.07 us (5%)
    pallas_call x2, Pallas kernels, local_part(): call(body, 8, (tiles,), [tile, tile, whole(read.shape), whole(write.shape...  11.8 us
    ppermute x5, waiting for transfers between devices, across(): return lax.ppermute(a, 'tp', [(i, i ^ bit) for i in range(n_tp)])  11.4 us
    ppermute x3, starting transfers between devices, shift(): return lax.ppermute(a, 'seq', [(i, i + by) for i in range(n_seq - by)])  10.7 us
    pallas_call x3, Pallas kernels, project(): call(body, 3, (1,), [whole((toks, half_w)), whole((toks, half_w)), pl.Blo...  9.89 us
    ppermute x3, waiting for transfers between devices, pair(): return lax.ppermute(a, 'seq', [(i, i ^ 1) for i in range(n_seq)])  6.58 us
    unnamed x22, local copies, waits for them, and re-layouts  5.62 us
    ppermute x3, starting transfers between devices, pair(): return lax.ppermute(a, 'seq', [(i, i ^ 1) for i in range(n_seq)])  4.74 us
    pallas_call x1, Pallas kernels, gate_and_project(): call(body, 9, (1,), gate_specs(which, toks, half_w, read.shape[1]) + [who...  3.7 us
  transfers between devices with their start and end apart: 11, of which 4 were waited for; matrix products, arithmetic and copies ran while one was open for 2% of the time, Pallas kernels for 30%

profile of v1, /device:TPU:0, one launch (start us, length us, event | category | flops | bytes accessed | tf_op | source)
XLA Modules:
  0.0 80.3 jit_solution(17103414759607109836)
XLA Ops:
  0.0 0.1 stack.27.sc_ref
  0.1 1.3 %copy-done = bf16[512,1280]{1,0:T(8,128)(2,1)S(1)} copy-done((bf16[512,1280]{1,0:T(8,128)(2,1)S(1)}, bf16[512,1280]{1,0:T(8,128)(2,1)}, u32[]{:S(2)}) %copy-start) | copy-done | bytes 1310744
  1.4 0.9 %copy-done.3 = bf16[512,128]{1,0:T(8,128)(2,1)S(1)} copy-done((bf16[512,128]{1,0:T(8,128)(2,1)S(1)}, bf16[512,128]{1,0:T(8,128)(2,1)}, u32[]{:S(2)}) %copy-start.3) | copy-done | bytes 131096
  2.3 0.7 copy-done.5
  3.0 0.7 copy-done.6
  3.7 0.7 copy-done.7
  4.4 0.7 copy-done.8
  5.0 0.7 copy-done.9
  5.7 2.4 %shard_map.109 = (bf16[128,640]{1,0:T(8,128)(2,1)S(1)}, f32[2,512,128]{2,1,0:T(8,128)S(1)}, f32[64,512]{1,0:T(8,128)S(1)}, f32[2,768,128]{2,1,0:T(8,128)S(1)}, f32[2,8,640]{2,1,0:T(8,128)S(1)}) custom-call(s32[6]{0:T(128)S(1)} %stack.27.sc_ref, bf16[20,512]{1,0:T(8,128)(2,1)S(1)} %copy-done.5, s32[1,512]{1,0:T(1,128)S(1)} %bitcast.34, f32[1,20]{1,0:T(1,128)S(1)} %bitcast.35, ...), custom_call_target="tpu_custom_call" | custom-call | flops 83886080 | bytes 4000000 | tf_op jit(solution)/shard_map/pallas_call | solution.py:137
  8.1 3.0 %collective-permute-start.2 = (bf16[128,640]{1,0:T(8,128)(2,1)S(1)}, bf16[128,640]{1,0:T(8,128)(2,1)S(1)}, u32[]{:S(2)}, u32[]{:S(2)}) collective-permute-start(bf16[128,640]{1,0:T(8,128)(2,1)S(1)} %get-tuple-element.25), channel_id=1, source_target_pairs={{0,4},{4,0},{8,12},{12,8},{16,20},{20,16},{24,28},{28,24},{1,5},{5... | collective-permute-start | bytes 491528 | tf_op jit(solution)/shard_map/ppermute | solution.py:392
  11.2 0.1 collective-permute-start
  11.3 0.5 slice.30
  11.8 4.0 %collective-permute-done = f32[8,640]{1,0:T(8,128)S(1)} collective-permute-done((f32[8,640]{1,0:T(8,128)S(1)}, f32[8,640]{1,0:T(8,128)S(1)}, u32[]{:S(2)}, u32[]{:S(2)}) %collective-permute-start) | collective-permute-done | bytes 20512 | tf_op jit(solution)/shard_map/ppermute | solution.py:392
  15.8 0.5 slice.29
  17.6 3.7 %collective-permute-start.1 = (f32[8,128]{1,0:T(8,128)S(1)}, f32[8,128]{1,0:T(8,128)S(1)}, u32[]{:S(2)}, u32[]{:S(2)}) collective-permute-start(f32[8,128]{1,0:T(8,128)S(1)} %broadcast_in_dim.15), channel_id=1, source_target_pairs={{0,8},{4,12},{8,16},{12,20},{16,24},{20,28},{1,9},{5,13},{9,17},{1... | collective-permute-start | bytes 12296 | tf_op jit(solution)/shard_map/ppermute | solution.py:395
  21.3 0.0 copy-start.2
  21.4 1.5 %shard_map.111 = f32[128,640]{1,0:T(8,128)S(1)} custom-call(s32[6]{0:T(128)S(1)} %stack.27.sc_ref, f32[2,768,128]{2,1,0:T(8,128)S(1)} %get-tuple-element.22.tail0_ref.tail_ref, bf16[512,1280]{1,0:T(8,128)(2,1)S(1)} %copy-done.1, bf16[512,128]{1,0:T(8,128)(2,1)S(1)} %copy-done.4), custom_call_target="tpu_custom_call" | custom-call | flops 83886080 | bytes 2000000 | tf_op jit(solution)/shard_map/pallas_call | solution.py:173
  24.2 0.0 collective-permute-done.1
  24.2 0.5 slice.28
  26.0 0.0 collective-permute-done.2
  26.0 0.1 fusion.1
  26.1 3.5 %collective-permute-start.3 = (bf16[128,640]{1,0:T(8,128)(2,1)S(1)}, bf16[128,640]{1,0:T(8,128)(2,1)S(1)}, u32[]{:S(2)}, u32[]{:S(2)}) collective-permute-start(bf16[128,640]{1,0:T(8,128)(2,1)S(1)} %fusion.1), channel_id=1, source_target_pairs={{0,8},{4,12},{8,16},{12,20},{16,24},{20,28},{1,9},{5,13},{9,17},{1... | collective-permute-start | bytes 491528 | tf_op jit(solution)/shard_map/ppermute | solution.py:395
  29.6 5.9 %shard_map.110 = (f32[512,640]{1,0:T(8,128)S(1)}, f32[512,640]{1,0:T(8,128)S(1)}) custom-call(s32[6]{0:T(128)S(1)} %stack.27.sc_ref, bf16[512,1280]{1,0:T(8,128)(2,1)S(1)} %copy-done.1, bf16[512,1280]{1,0:T(8,128)(2,1)} %gate_ref.3, bf16[512,128]{1,0:T(8,128)(2,1)S(1)} %copy-done.2, bf16[512,128]{1,0:T(8,128)(2,1)S(1)} %copy-done.4, ...), custom_call_target="tpu_custom_call" | custom-call | flops 4000000000 | bytes 8000000 | tf_op jit(solution)/shard_map/pallas_call | solution.py:258
  35.5 0.0 collective-permute-done.3
  35.5 0.1 add_convert_fusion.2
  35.6 0.0 copy-start.10
  35.7 3.5 %collective-permute-start.4 = (bf16[128,640]{1,0:T(8,128)(2,1)S(1)}, bf16[128,640]{1,0:T(8,128)(2,1)S(1)}, u32[]{:S(2)}, u32[]{:S(2)}) collective-permute-start(bf16[128,640]{1,0:T(8,128)(2,1)S(1)} %add_convert_fusion.2), channel_id=1, source_target_pairs={{0,8},{4,12},{8,16},{12,20},{16,24},{20,28},{1,9},{5,13},{9,17},{1... | collective-permute-start | bytes 491528 | tf_op jit(solution)/shard_map/ppermute | solution.py:395
  39.2 5.9 %shard_map.113 = (f32[512,640]{1,0:T(8,128)S(1)}, f32[512,640]{1,0:T(8,128)S(1)}) custom-call(s32[6]{0:T(128)S(1)} %stack.27.sc_ref, bf16[512,1280]{1,0:T(8,128)(2,1)S(1)} %copy-done.1, bf16[512,1280]{1,0:T(8,128)(2,1)} %gate_ref.3, bf16[512,128]{1,0:T(8,128)(2,1)S(1)} %copy-done.2, bf16[512,128]{1,0:T(8,128)(2,1)S(1)} %copy-done.4, ...), custom_call_target="tpu_custom_call" | custom-call | flops 4000000000 | bytes 8000000 | tf_op jit(solution)/shard_map/pallas_call | solution.py:258
  45.1 0.0 collective-permute-done.4
  45.1 0.1 broadcast_select_fusion
  45.2 1.6 %collective-permute-start.5 = (bf16[128,640]{1,0:T(8,128)(2,1)S(1)}, bf16[128,640]{1,0:T(8,128)(2,1)S(1)}, u32[]{:S(2)}, u32[]{:S(2)}) collective-permute-start(bf16[128,640]{1,0:T(8,128)(2,1)S(1)} %get-tuple-element.36), channel_id=1, source_target_pairs={{0,4},{4,0},{8,12},{12,8},{16,20},{20,16},{24,28},{28,24},{1,5},{5... | collective-permute-start | bytes 491528 | tf_op jit(solution)/shard_map/ppermute | solution.py:392
  46.8 1.2 %shard_map.112 = (bf16[512,640]{1,0:T(8,128)(2,1)S(1)}, f32[1,512]{1,0:T(1,128)S(1)}) custom-call(s32[6]{0:T(128)S(1)} %stack.27.sc_ref, f32[8,128]{1,0:T(8,128)S(1)} %broadcast_select_fusion.4.prev_ref, bf16[512,128]{1,0:T(8,128)(2,1)S(1)} %copy-done.2, f32[2,512,128]{2,1,0:T(8,128)S(1)} %get-tuple-element.20.ccol_ref.seg_ref, ...), custom_call_target="tpu_custom_call" | custom-call | flops 83886080 | bytes 4000000 | tf_op jit(solution)/shard_map/pallas_call | solution.py:301
  48.0 2.6 %collective-permute-done.5.e_ref = bf16[128,640]{1,0:T(8,128)(2,1)S(1)} collective-permute-done((bf16[128,640]{1,0:T(8,128)(2,1)S(1)}, bf16[128,640]{1,0:T(8,128)(2,1)S(1)}, u32[]{:S(2)}, u32[]{:S(2)}) %collective-permute-start.5) | collective-permute-done | bytes 163872 | tf_op jit(solution)/shard_map/ppermute | solution.py:392
  50.6 3.7 %shard_map.114 = (bf16[512,640]{1,0:T(8,128)(2,1)S(1)}, f32[1,512]{1,0:T(1,128)S(1)}, bf16[512,640]{1,0:T(8,128)(2,1)S(1)}) custom-call(s32[6]{0:T(128)S(1)} %stack.27.sc_ref, f32[8,128]{1,0:T(8,128)S(1)} %broadcast_select_fusion.4.prev_ref, bf16[512,128]{1,0:T(8,128)(2,1)S(1)} %copy-done.2, f32[2,512,128]{2,1,0:T(8,128)S(1)} %get-tuple-element.20.ccol_ref.seg_ref, ...), custom_call_target="tpu_custom_call" | custom-call | flops 838860800 | bytes 6000000 | tf_op jit(solution)/shard_map/pallas_call | solution.py:324
  54.3 0.1 collective-permute-start.7
  54.4 3.3 %shard_map.116 = bf16[512,640]{1,0:T(8,128)(2,1)S(1)} custom-call(s32[6]{0:T(128)S(1)} %stack.27.sc_ref, bf16[512,640]{1,0:T(8,128)(2,1)S(1)} %get-tuple-element.26.gk_ref, bf16[512,640]{1,0:T(8,128)(2,1)S(1)} %get-tuple-element.29.go_ref, bf16[1280,2560]{1,0:T(8,128)(2,1)} %w_ref.7), custom_call_target="tpu_custom_call" | custom-call | flops 838860800 | bytes 4000000 | tf_op jit(solution)/shard_map/pallas_call | solution.py:347
  57.7 0.6 collective-permute-start.6
  58.3 3.3 %shard_map.117 = f32[512,640]{1,0:T(8,128)S(1)} custom-call(s32[6]{0:T(128)S(1)} %stack.27.sc_ref, bf16[512,640]{1,0:T(8,128)(2,1)S(1)} %get-tuple-element.26.gk_ref, bf16[512,640]{1,0:T(8,128)(2,1)S(1)} %get-tuple-element.29.go_ref, bf16[1280,2560]{1,0:T(8,128)(2,1)} %w_ref.7), custom_call_target="tpu_custom_call" | custom-call | flops 838860800 | bytes 4000000 | tf_op jit(solution)/shard_map/pallas_call | solution.py:347
  61.6 0.0 collective-permute-done.7
  61.6 0.2 add_convert_fusion
  61.7 1.6 %collective-permute-start.8 = (bf16[512,640]{1,0:T(8,128)(2,1)S(1)}, bf16[512,640]{1,0:T(8,128)(2,1)S(1)}, u32[]{:S(2)}, u32[]{:S(2)}) collective-permute-start(bf16[512,640]{1,0:T(8,128)(2,1)S(1)} %add_convert_fusion), channel_id=1, source_target_pairs={{0,2},{1,3},{2,0},{3,1},{4,6},{5,7},{6,4},{7,5},{8,10},{9,11},{10,... | collective-permute-start | bytes 1966088 | tf_op jit(solution)/shard_map/ppermute | solution.py:398
  63.3 0.0 collective-permute-start.9
  63.3 1.2 %collective-permute-done.9 = f32[1,512]{1,0:T(1,128)S(1)} collective-permute-done((f32[1,512]{1,0:T(1,128)S(1)}, f32[1,512]{1,0:T(1,128)S(1)}, u32[]{:S(2)}, u32[]{:S(2)}) %collective-permute-start.9) | collective-permute-done | bytes 2080 | tf_op jit(solution)/shard_map/ppermute | solution.py:398
  64.5 0.5 collective-permute-start.10
  65.0 3.3 %shard_map.115.own_ref = f32[512,640]{1,0:T(8,128)S(1)} custom-call(s32[6]{0:T(128)S(1)} %stack.27.sc_ref, bf16[512,640]{1,0:T(8,128)(2,1)S(1)} %get-tuple-element.26.gk_ref, bf16[512,640]{1,0:T(8,128)(2,1)S(1)} %get-tuple-element.29.go_ref, bf16[1280,2560]{1,0:T(8,128)(2,1)} %w_ref.7), custom_call_target="tpu_custom_call" | custom-call | flops 838860800 | bytes 4000000 | tf_op jit(solution)/shard_map/pallas_call | solution.py:347
  68.3 10.2 %collective-permute-done.10 = f32[1,512]{1,0:T(1,128)S(1)} collective-permute-done((f32[1,512]{1,0:T(1,128)S(1)}, f32[1,512]{1,0:T(1,128)S(1)}, u32[]{:S(2)}, u32[]{:S(2)}) %collective-permute-start.10) | collective-permute-done | bytes 2080 | tf_op jit(solution)/shard_map/ppermute | solution.py:398
  78.5 0.0 collective-permute-done.6.core_ref
  78.5 1.8 %shard_map.118 = bf16[640,512]{1,0:T(8,128)(2,1)} custom-call(s32[6]{0:T(128)S(1)} %stack.27.sc_ref, f32[512,640]{1,0:T(8,128)S(1)} %shard_map.115.own_ref, bf16[512,640]{1,0:T(8,128)(2,1)S(1)} %collective-permute-done.6.core_ref, bf16[512,640]{1,0:T(8,128)(2,1)S(1)} %collective-permute-done.8.far_ref, f32[1,512]{1,0:T(1,128)S(1)} %add.37.sq_ref), custom_call_target="tpu_custom_call" | custom-call | flops 1310720 | bytes 3000000 | tf_op jit(solution)/shard_map/pallas_call | solution.py:367
  (22 shorter events, 0.1 us)
Async XLA Ops:
  0.1 1.3 %copy-start = (bf16[512,1280]{1,0:T(8,128)(2,1)S(1)}, bf16[512,1280]{1,0:T(8,128)(2,1)}, u32[]{:S(2)}) copy-start(bf16[512,1280]{1,0:T(8,128)(2,1)} %x_ref.7) | copy-start | bytes 3932164
  1.4 0.9 %copy-start.3 = (bf16[512,128]{1,0:T(8,128)(2,1)S(1)}, bf16[512,128]{1,0:T(8,128)(2,1)}, u32[]{:S(2)}) copy-start(bf16[512,128]{1,0:T(8,128)(2,1)} %wr_ref.7) | copy-start | bytes 393220
  2.3 0.7 copy-start.5
  3.0 0.7 copy-start.6
  3.7 0.7 copy-start.7
  4.4 0.7 copy-start.8
  5.0 0.7 copy-start.9
  5.7 15.6 %copy-start.1 = (bf16[512,1280]{1,0:T(8,128)(2,1)S(1)}, bf16[512,1280]{1,0:T(8,128)(2,1)}, u32[]{:S(2)}) copy-start(bf16[512,1280]{1,0:T(8,128)(2,1)} %x_ref.7) | copy-start | bytes 3932164
  5.7 15.6 %copy-start.4 = (bf16[512,128]{1,0:T(8,128)(2,1)S(1)}, bf16[512,128]{1,0:T(8,128)(2,1)}, u32[]{:S(2)}) copy-start(bf16[512,128]{1,0:T(8,128)(2,1)} %wr_ref.7) | copy-start | bytes 393220
  8.1 17.9 %collective-permute-start.2 = (bf16[128,640]{1,0:T(8,128)(2,1)S(1)}, bf16[128,640]{1,0:T(8,128)(2,1)S(1)}, u32[]{:S(2)}, u32[]{:S(2)}) collective-permute-start(bf16[128,640]{1,0:T(8,128)(2,1)S(1)} %get-tuple-element.25), channel_id=1, source_target_pairs={{0,4},{4,0},{8,12},{12,8},{16,20},{20,16},{24,28},{28,24},{1,5},{5... | collective-permute-start | bytes 491528 | tf_op jit(solution)/shard_map/ppermute | solution.py:392
  11.2 4.6 %collective-permute-start = (f32[8,640]{1,0:T(8,128)S(1)}, f32[8,640]{1,0:T(8,128)S(1)}, u32[]{:S(2)}, u32[]{:S(2)}) collective-permute-start(f32[8,640]{1,0:T(8,128)S(1)} %get-tuple-element.39), channel_id=1, source_target_pairs={{0,4},{4,0},{8,12},{12,8},{16,20},{20,16},{24,28},{28,24},{1,5},{5... | collective-permute-start | bytes 61448 | tf_op jit(solution)/shard_map/ppermute | solution.py:392
  17.6 6.6 %collective-permute-start.1 = (f32[8,128]{1,0:T(8,128)S(1)}, f32[8,128]{1,0:T(8,128)S(1)}, u32[]{:S(2)}, u32[]{:S(2)}) collective-permute-start(f32[8,128]{1,0:T(8,128)S(1)} %broadcast_in_dim.15), channel_id=1, source_target_pairs={{0,8},{4,12},{8,16},{12,20},{16,24},{20,28},{1,9},{5,13},{9,17},{1... | collective-permute-start | bytes 12296 | tf_op jit(solution)/shard_map/ppermute | solution.py:395
  21.3 8.2 %copy-start.2 = (bf16[512,128]{1,0:T(8,128)(2,1)S(1)}, bf16[512,128]{1,0:T(8,128)(2,1)}, u32[]{:S(2)}) copy-start(bf16[512,128]{1,0:T(8,128)(2,1)} %rd_ref.7) | copy-start | bytes 393220
  26.1 9.4 %collective-permute-start.3 = (bf16[128,640]{1,0:T(8,128)(2,1)S(1)}, bf16[128,640]{1,0:T(8,128)(2,1)S(1)}, u32[]{:S(2)}, u32[]{:S(2)}) collective-permute-start(bf16[128,640]{1,0:T(8,128)(2,1)S(1)} %fusion.1), channel_id=1, source_target_pairs={{0,8},{4,12},{8,16},{12,20},{16,24},{20,28},{1,9},{5,13},{9,17},{1... | collective-permute-start | bytes 491528 | tf_op jit(solution)/shard_map/ppermute | solution.py:395
  35.6 9.4 %copy-start.10 = (f32[1280]{0:T(1024)S(1)}, f32[1280]{0:T(1024)}, u32[]{:S(2)}) copy-start(f32[1280]{0:T(1024)} %param.20) | copy-start | bytes 15364
  35.7 9.4 %collective-permute-start.4 = (bf16[128,640]{1,0:T(8,128)(2,1)S(1)}, bf16[128,640]{1,0:T(8,128)(2,1)S(1)}, u32[]{:S(2)}, u32[]{:S(2)}) collective-permute-start(bf16[128,640]{1,0:T(8,128)(2,1)S(1)} %add_convert_fusion.2), channel_id=1, source_target_pairs={{0,8},{4,12},{8,16},{12,20},{16,24},{20,28},{1,9},{5,13},{9,17},{1... | collective-permute-start | bytes 491528 | tf_op jit(solution)/shard_map/ppermute | solution.py:395
  45.2 5.4 %collective-permute-start.5 = (bf16[128,640]{1,0:T(8,128)(2,1)S(1)}, bf16[128,640]{1,0:T(8,128)(2,1)S(1)}, u32[]{:S(2)}, u32[]{:S(2)}) collective-permute-start(bf16[128,640]{1,0:T(8,128)(2,1)S(1)} %get-tuple-element.36), channel_id=1, source_target_pairs={{0,4},{4,0},{8,12},{12,8},{16,20},{20,16},{24,28},{28,24},{1,5},{5... | collective-permute-start | bytes 491528 | tf_op jit(solution)/shard_map/ppermute | solution.py:392
  54.3 7.2 %collective-permute-start.7 = (bf16[512,640]{1,0:T(8,128)(2,1)S(1)}, bf16[512,640]{1,0:T(8,128)(2,1)S(1)}, u32[]{:S(2)}, u32[]{:S(2)}) collective-permute-start(bf16[512,640]{1,0:T(8,128)(2,1)S(1)} %get-tuple-element.30), channel_id=1, source_target_pairs={{0,1},{1,0},{2,3},{3,2},{4,5},{5,4},{6,7},{7,6},{8,9},{9,8},{10,11... | collective-permute-start | bytes 1966088 | tf_op jit(solution)/shard_map/ppermute | solution.py:398
  57.7 20.8 %collective-permute-start.6 = (bf16[512,640]{1,0:T(8,128)(2,1)S(1)}, bf16[512,640]{1,0:T(8,128)(2,1)S(1)}, u32[]{:S(2)}, u32[]{:S(2)}) collective-permute-start(bf16[512,640]{1,0:T(8,128)(2,1)S(1)} %shard_map.116), channel_id=1, source_target_pairs={{0,1},{1,0},{2,3},{3,2},{4,5},{5,4},{6,7},{7,6},{8,9},{9,8},{10,11... | collective-permute-start | bytes 1966088 | tf_op jit(solution)/shard_map/ppermute | solution.py:398
  61.7 16.8 %collective-permute-start.8 = (bf16[512,640]{1,0:T(8,128)(2,1)S(1)}, bf16[512,640]{1,0:T(8,128)(2,1)S(1)}, u32[]{:S(2)}, u32[]{:S(2)}) collective-permute-start(bf16[512,640]{1,0:T(8,128)(2,1)S(1)} %add_convert_fusion), channel_id=1, source_target_pairs={{0,2},{1,3},{2,0},{3,1},{4,6},{5,7},{6,4},{7,5},{8,10},{9,11},{10,... | collective-permute-start | bytes 1966088 | tf_op jit(solution)/shard_map/ppermute | solution.py:398
  63.3 1.2 %collective-permute-start.9 = (f32[1,512]{1,0:T(1,128)S(1)}, f32[1,512]{1,0:T(1,128)S(1)}, u32[]{:S(2)}, u32[]{:S(2)}) collective-permute-start(f32[1,512]{1,0:T(1,128)S(1)} %add.35), channel_id=1, source_target_pairs={{0,1},{1,0},{2,3},{3,2},{4,5},{5,4},{6,7},{7,6},{8,9},{9,8},{10,11... | collective-permute-start | bytes 6152 | tf_op jit(solution)/shard_map/ppermute | solution.py:398
  64.5 14.0 %collective-permute-start.10 = (f32[1,512]{1,0:T(1,128)S(1)}, f32[1,512]{1,0:T(1,128)S(1)}, u32[]{:S(2)}, u32[]{:S(2)}) collective-permute-start(f32[1,512]{1,0:T(1,128)S(1)} %add.36), channel_id=1, source_target_pairs={{0,2},{1,3},{2,0},{3,1},{4,6},{5,7},{6,4},{7,5},{8,10},{9,11},{10,... | collective-permute-start | bytes 6152 | tf_op jit(solution)/shard_map/ppermute | solution.py:398

commit v2 on v1

--- a/solution.py
+++ b/solution.py
@@ -12,7 +12,9 @@
 EPS = 1e-05
 LOG2E = 1.4426950408889634
 SEG_LANE = 32
-VMEM = 48 * 1024 * 1024
+EXTRA = 16
+VMEM = 20 * 1024 * 1024
+VMEM_ALL = 63 * 1024 * 1024
 F32 = jnp.float32
 BF16 = jnp.bfloat16
 
@@ -36,7 +38,7 @@
     return out
 
 
-def call(body, n_in, grid, in_specs, out_specs, out_shape, scratch=(), flops=0, nbytes=0):
+def call(body, n_in, grid, in_specs, out_specs, out_shape, scratch=(), flops=0, nbytes=0, limit=VMEM):
     del n_in
     return pl.pallas_call(
         body,
@@ -48,7 +50,7 @@
             scratch_shapes=list(scratch),
         ),
         out_shape=out_shape,
-        compiler_params=pltpu.CompilerParams(vmem_limit_bytes=VMEM),
+        compiler_params=pltpu.CompilerParams(vmem_limit_bytes=limit),
         cost_estimate=pl.CostEstimate(flops=flops, bytes_accessed=nbytes, transcendentals=0),
     )
 
@@ -57,8 +59,18 @@
     return pl.BlockSpec(shape, lambda i, sc: (0,) * len(shape))
 
 
+def pack_rows(out_ref, state, meta):
+    keep = meta[0:1]
+    high = keep.astype(BF16)
+    low = (keep - high.astype(F32)).astype(BF16)
+    row = lax.broadcasted_iota(jnp.int32, (EXTRA, meta.shape[1]), 0)
+    rows = jnp.where(row == 0, high.astype(F32), jnp.where(row == 1, low.astype(F32), meta[1:2]))
+    out_ref[state : state + EXTRA] = rows.astype(BF16)
+
+
 def prepare(heads, width, sc, raw, seg, decay_log, bias, skip, x, write):
     toks = raw.shape[1]
+    state = write.shape[1]
     half_w = x.shape[1] // 2
     half_h = heads // 2
     blocks = toks // GROUP
@@ -131,9 +143,9 @@
             xt = x_ref[:, i * LANES : (i + 1) * LANES].astype(F32)
             parts.append((xt * spread(mine, i * per, width)).astype(BF16))
         xs = jnp.concatenate(parts, axis=1)
-        send_ref[...] = dot(wr_ref[...], xs, ((0,), (0,))).astype(BF16)
-
-    state = write.shape[1]
+        send_ref[0:state] = dot(wr_ref[...], xs, ((0,), (0,))).astype(BF16)
+        pack_rows(send_ref, state, meta_ref[sc_ref[1]])
+
     return call(
         body, 7, (1,),
         [
@@ -142,48 +154,55 @@
             whole(write.shape),
         ],
         [
-            whole((state, half_w)), whole((2, toks, LANES)), whole((64, toks)),
+            whole((state + EXTRA, half_w)), whole((2, toks, LANES)), whole((64, toks)),
             whole((2, toks + GROUP, LANES)), whole((2, 8, half_w)),
         ],
         [
-            jax.ShapeDtypeStruct((state, half_w), BF16),
+            jax.ShapeDtypeStruct((state + EXTRA, half_w), BF16),
             jax.ShapeDtypeStruct((2, toks, LANES), F32),
             jax.ShapeDtypeStruct((64, toks), F32),
             jax.ShapeDtypeStruct((2, toks + GROUP, LANES), F32),
             jax.ShapeDtypeStruct((2, 8, half_w), F32),
         ],
         [pltpu.VMEM((LANES, toks), F32), pltpu.VMEM((8, LANES), F32)],
-        flops=2 * toks * state * half_w, nbytes=4_000_000,
+        flops=2 * toks * state * half_w, nbytes=4_000_000, limit=VMEM_ALL,
     )(sc, raw, seg, decay_log, bias, skip, x, write)
 
 
-def kept_state(width, sc, tail, x, write):
+def kept_state(width, sc, tail, meta, x, write):
     toks, state = write.shape
     half_w = x.shape[1] // 2
     per = LANES // width
 
-    def body(sc_ref, tail_ref, x_ref, wr_ref, out_ref):
+    def body(sc_ref, tail_ref, meta_ref, x_ref, wr_ref, out_ref, send_ref):
         mine = tail_ref[0]
         parts = []
         for i in range(half_w // LANES):
             xt = x_ref[:, i * LANES : (i + 1) * LANES].astype(F32)
             parts.append((xt * spread(mine, i * per, width)).astype(BF16))
-        out_ref[...] = dot(wr_ref[...], jnp.concatenate(parts, axis=1), ((0,), (0,)))
+        own = dot(wr_ref[...], jnp.concatenate(parts, axis=1), ((0,), (0,)))
+        out_ref[...] = own
+        send_ref[0:state] = own.astype(BF16)
+        pack_rows(send_ref, state, meta_ref[0])
 
     return call(
         body, 3, (1,),
         [
             pl.BlockSpec((1, toks, LANES), lambda i, sc: (sc[0], 0, 0)),
+            pl.BlockSpec((1, 8, half_w), lambda i, sc: (sc[0], 0, 0)),
             pl.BlockSpec((toks, half_w), lambda i, sc: (0, sc[0])),
             whole(write.shape),
         ],
-        whole((state, half_w)),
-        jax.ShapeDtypeStruct((state, half_w), F32),
+        [whole((state, half_w)), whole((state + EXTRA, half_w))],
+        [
+            jax.ShapeDtypeStruct((state, half_w), F32),
+            jax.ShapeDtypeStruct((state + EXTRA, half_w), BF16),
+        ],
         flops=2 * toks * state * half_w, nbytes=2_000_000,
-    )(sc, tail, x, write)
-
-
-def local_part(which, heads, width, sc, x, gate, read, write, ccol, arow, tail, meta):
+    )(sc, tail, meta, x, write)
+
+
+def local_part(which, heads, width, sc, x, gate, read, write, ccol, arow, tail, meta, after):
     toks, state = write.shape
     half_w = x.shape[1] // 2
     half_h = heads // 2
@@ -193,7 +212,7 @@
     sub = GROUP // 2
 
     def body(
-        sc_ref, x_ref, gate_ref, rd_ref, wr_ref, ccol_ref, arow_ref, tail0_ref, meta_ref,
+        sc_ref, x_ref, gate_ref, rd_ref, wr_ref, ccol_ref, arow_ref, tail0_ref, meta_ref, after_ref,
         a_ref, b_ref, scores,
     ):
         i = pl.program_id(0)
@@ -263,12 +282,13 @@
             whole(arow.shape),
             pl.BlockSpec((1, GROUP, LANES), lambda i, sc: (sc[which], toks // GROUP, 0)),
             pl.BlockSpec((1, 8, LANES), lambda i, sc: (sc[which], 0, i)),
+            pl.BlockSpec(memory_space=pl.ANY),
         ],
         [out, out],
         [jax.ShapeDtypeStruct((toks, half_w), F32), jax.ShapeDtypeStruct((toks, half_w), F32)],
         [pltpu.VMEM((blocks, GROUP, GROUP), F32)],
         flops=4_000_000_000, nbytes=8_000_000,
-    )(sc, x, gate, read, write, ccol, arow, tail, meta)
+    )(sc, x, gate, read, write, ccol, arow, tail, meta, after)
 
 
 def gated_tile(prev_ref, rd_ref, seg_ref, a_ref, b_ref, e_ref, gain_ref):
@@ -319,58 +339,42 @@
         g_ref[...] = g
         y = dot(gk_ref[...], w_ref[pl.ds(sc_ref[0] * half_w, half_w)])
         y = y + dot(g, w_ref[pl.ds(sc_ref[1] * half_w, half_w)])
-        y_ref[...] = y.astype(BF16)
+        y_ref[...] = jnp.transpose(y).astype(BF16)
 
     return call(
         body, 9, (1,),
         gate_specs(which, toks, half_w, read.shape[1])
         + [whole((toks, half_w)), pl.BlockSpec((2 * half_w, cols), lambda i, sc: (0, sc[quarter]))],
-        [whole((toks, half_w)), whole((1, toks)), whole((toks, cols))],
+        [whole((toks, half_w)), whole((1, toks)), whole((cols, toks))],
         [
             jax.ShapeDtypeStruct((toks, half_w), BF16),
             jax.ShapeDtypeStruct((1, toks), F32),
-            jax.ShapeDtypeStruct((toks, cols), BF16),
+            jax.ShapeDtypeStruct((cols, toks), BF16),
         ],
         flops=4 * toks * half_w * cols, nbytes=6_000_000,
     )(sc, prev, read, ccol, a, b, e, gain, g_keep, weight)
 
 
-def project(quarter, dtype, sc, g_keep, g_other, weight):
+def project(quarter, dtype, sc, g_keep, g_other, weight, after):
     toks, half_w = g_keep.shape
     cols = weight.shape[1] // 4
 
-    def body(sc_ref, gk_ref, go_ref, w_ref, y_ref):
+    def body(sc_ref, gk_ref, go_ref, w_ref, after_ref, y_ref):
         y = dot(gk_ref[...], w_ref[pl.ds(sc_ref[0] * half_w, half_w)])
         y = y + dot(go_ref[...], w_ref[pl.ds(sc_ref[1] * half_w, half_w)])
-        y_ref[...] = y.astype(dtype)
-
-    return call(
-        body, 3, (1,),
+        y_ref[...] = jnp.transpose(y).astype(dtype)
+
+    return call(
+        body, 4, (1,),
         [
             whole((toks, half_w)), whole((toks, half_w)),
             pl.BlockSpec((2 * half_w, cols), lambda i, sc: (0, sc[quarter])),
-        ],
-        whole((toks, cols)),
-        jax.ShapeDtypeStruct((toks, cols), dtype),
+            pl.BlockSpec(memory_space=pl.ANY),
+        ],
+        whole((cols, toks)),
+        jax.ShapeDtypeStruct((cols, toks), dtype),
         flops=4 * toks * half_w * cols, nbytes=4_000_000,
-    )(sc, g_keep, g_other, weight)
-
-
-def finish(features, sc, own, from_core, from_far, squares):
-    toks, cols = own.shape
-
-    def body(sc_ref, own_ref, core_ref, far_ref, sq_ref, out_ref):
-        y = (own_ref[...] + core_ref[...].astype(F32)) + far_ref[...].astype(F32)
-        inv = lax.rsqrt(sq_ref[...] / features + EPS)
-        out_ref[...] = (jnp.transpose(y) * inv).astype(BF16)
-
-    return call(
-        body, 4, (1,),
-        [whole((toks, cols))] * 3 + [whole((1, toks))],
-        whole((cols, toks)),
-        jax.ShapeDtypeStruct((cols, toks), BF16),
-        flops=4 * toks * cols, nbytes=3_000_000,
-    )(sc, own, from_core, from_far, squares)
+    )(sc, g_keep, g_other, weight, after)
 
 
 def on_device(
@@ -380,7 +384,7 @@
     heads = decay_log.shape[0]
     toks, feats = head_input.shape
     width = feats // heads
-    half_w = feats // 2
+    state = write_vecs.shape[1]
     place = lax.axis_index("seq")
     rank = lax.axis_index("tp")
     odd = lax.rem(place, 2)
@@ -388,72 +392,87 @@
     near, far = rank ^ 1, rank ^ 2
     sc = jnp.stack([odd, 1 - odd, far ^ 1, far, near, rank]).astype(jnp.int32)
 
-    def pair(a):
-        return lax.ppermute(a, "seq", [(i, i ^ 1) for i in range(n_seq)])
-
-    def shift(a, by):
-        return lax.ppermute(a, "seq", [(i, i + by) for i in range(n_seq - by)])
+    def swap(a, bit):
+        return lax.ppermute(a, "seq", [(i, i ^ bit) for i in range(n_seq)])
 
     def across(a, bit):
         return lax.ppermute(a, "tp", [(i, i ^ bit) for i in range(n_tp)])
 
-    send, ccol, arow, tail, meta = prepare(
+    def member(payload):
+        f = payload.astype(F32)
+        return f[0:state], f[state : state + 1] + f[state + 1 : state + 2], f[state + 2 : state + 3, 0:1]
+
+    def joined(first, second):
+        link = second[1] * (first[2] == second[2]).astype(F32)
+        return second[0] + link * first[0], second[1] * first[1], second[2]
+
+    def ordered(swapped, one, two):
+        firsts = tuple(jnp.where(swapped, t, o) for o, t in zip(one, two))
+        seconds = tuple(jnp.where(swapped, o, t) for o, t in zip(one, two))
+        return firsts, seconds
+
+    send_other, ccol, arow, tail, meta = prepare(
         heads, width, sc, step_raw, segment_ids.reshape(1, toks), decay_log.reshape(1, heads),
         step_bias.reshape(1, heads), skip_gain.reshape(1, heads), head_input, write_vecs,
     )
-    got_state = pair(send)
-    got_meta = pair(lax.dynamic_index_in_dim(meta, 1 - odd, 0, False))
-    own_meta = lax.dynamic_index_in_dim(meta, odd, 0, False)
-    own_state = kept_state(width, sc, tail, head_input, write_vecs)
+    mate_raw = swap(send_other, 1)
+    cross_raw = swap(send_other, 3) if n_seq > 2 else None
+    own_state, send_keep = kept_state(width, sc, tail, meta, head_input, write_vecs)
+    side_raw = swap(send_keep, 2) if n_seq > 2 else None
     a_keep, b_keep = local_part(
-        0, heads, width, sc, head_input, gate_input, read_vecs, write_vecs, ccol, arow, tail, meta
-    )
-    keep_first = jnp.where(even, own_meta[0:1], got_meta[0:1])
-    keep_second = jnp.where(even, got_meta[0:1], own_meta[0:1])
-    last_first = jnp.where(even, own_meta[1:2, 0:1], got_meta[1:2, 0:1])
-    last_second = jnp.where(even, got_meta[1:2, 0:1], own_meta[1:2, 0:1])
-    got_f = got_state.astype(F32)
-    first = jnp.where(even, own_state, got_f)
-    second = jnp.where(even, got_f, own_state)
-    joined = second + keep_second * (last_first == last_second).astype(F32) * first
-    through = keep_first * keep_second
-    last_tile = jnp.broadcast_to(last_second, (8, LANES))
-    prev_last = shift(last_tile, 2)
-    reach = 1
-    pairs = n_seq // 2
-    while reach < pairs // 2:
-        before = shift(joined.astype(BF16), 2 * reach)
-        last_before = prev_last if reach == 1 else shift(last_tile, 2 * reach)
-        link = through * (last_before[0:1, 0:1] == last_second).astype(F32)
-        joined = joined + link * before.astype(F32)
-        if 2 * reach < pairs // 2:
-            through = link * shift(through, 2 * reach)
-        reach *= 2
-    entry = shift(joined.astype(BF16), 2)
+        0, heads, width, sc, head_input, gate_input, read_vecs, write_vecs, ccol, arow, tail, meta, send_keep
+    )
+    own = (own_state,) + member(send_keep)[1:]
+    first, second = ordered(odd == 1, own, member(mate_raw))
+    total = joined(first, second)
+    entry = jnp.zeros_like(own_state)
+    entry_through = jnp.ones_like(total[1])
+    entry_id = jnp.full((1, 1), -1.0, F32)
+    after = send_keep
+    bit = 2
+    while bit < n_seq:
+        upper = (place & bit) != 0
+        if bit == 2:
+            other = joined(*ordered(odd == 1, member(side_raw), member(cross_raw)))
+        else:
+            sent = total[0].astype(BF16)
+            after = sent
+            other_state = swap(sent, bit).astype(F32)
+            rows = swap(jnp.concatenate([total[1], jnp.broadcast_to(total[2], total[1].shape)], axis=0), bit)
+            other = (other_state, rows[0:1], rows[1:2, 0:1])
+        link = entry_through * ((entry_id < 0) | (other[2] == entry_id)).astype(F32)
+        link = jnp.where(upper, link, 0.0)
+        entry = entry + link * other[0]
+        entry_id = jnp.where(upper & (entry_id < 0), other[2], entry_id)
+        entry_through = entry_through * jnp.where(upper, other[1], 1.0)
+        if 2 * bit < n_seq:
+            total = joined(*ordered(upper, total, other))
+        bit *= 2
     a_other, b_other = local_part(
-        1, heads, width, sc, head_input, gate_input, read_vecs, write_vecs, ccol, arow, tail, meta
-    )
-    prev_id = prev_last[0:1, 0:1]
-    after_first = (
-        first + keep_first * (last_first == prev_id).astype(F32) * entry.astype(F32)
-    ).astype(BF16)
-    e_other = pair(jnp.where(even, after_first, entry))
-    e_keep = jnp.where(even, entry, after_first)
-    prev = jnp.where(even, prev_last, jnp.broadcast_to(last_first, (8, LANES)))
+        1, heads, width, sc, head_input, gate_input, read_vecs, write_vecs, ccol, arow, tail, meta, after
+    )
+    reached = first[0] + first[1] * (first[2] == entry_id).astype(F32) * entry
+    entry, reached = entry.astype(BF16), reached.astype(BF16)
+    e_other = swap(jnp.where(even, reached, entry), 1)
+    e_keep = jnp.where(even, entry, reached)
+    prev = jnp.broadcast_to(jnp.where(even, entry_id, first[2]), (8, LANES))
     gain = norm_gain.reshape(1, feats)
     g_keep, s_keep = gated_half(0, sc, prev, read_vecs, ccol, a_keep, b_keep, e_keep, gain)
     g_other, s_other, y_far_near = gate_and_project(
         1, 2, sc, prev, read_vecs, ccol, a_other, b_other, e_other, gain, g_keep, out_weight
     )
     got_far = across(y_far_near, 1)
-    y_far = project(3, F32, sc, g_keep, g_other, out_weight)
-    got_x = across((y_far + got_far.astype(F32)).astype(BF16), 2)
     squares = s_keep + s_other
     squares = squares + across(squares, 1)
+    y_far = project(3, F32, sc, g_keep, g_other, out_weight, y_far_near)
+    to_far = (y_far + got_far.astype(F32)).astype(BF16)
+    got_x = across(to_far, 2)
     squares = squares + across(squares, 2)
-    got_near = across(project(4, BF16, sc, g_keep, g_other, out_weight), 1)
-    y_own = project(5, F32, sc, g_keep, g_other, out_weight)
-    return finish(feats * n_tp, sc, y_own, got_near, got_x, squares)
+    got_near = across(project(4, BF16, sc, g_keep, g_other, out_weight, to_far), 1)
+    y_own = project(5, F32, sc, g_keep, g_other, out_weight, to_far)
+    inv = lax.rsqrt(squares / (feats * n_tp) + EPS)
+    out = (y_own + got_near.astype(F32)) + got_x.astype(F32)
+    return (out * inv).astype(BF16)
 
 
 def solution(mesh):

time: 81 us -> 91.8 us (1.13)
  local copies, waits for them, and re-layouts: 7.3 us -> 18.1 us
  starting transfers between devices: 18.1 us -> 10.9 us
  Pallas kernels: 32.4 us -> 26.2 us
  other arithmetic: 0.49 us -> 6.67 us
  waiting for transfers between devices: 18 us -> 22.9 us
  between operations: 4.07 us -> 6.28 us
    unnamed x22 -> x58, local copies, waits for them, and re-layouts: 5.62 us -> 12.9 us
    ppermute x6, starting transfers between devices: 15.4 us -> 8.22 us  [swap(): return lax.ppermute(a, 'seq', [(i, i ^ bit) for i in range(n_seq)])]
    pallas_call x4 -> x3, Pallas kernels: 11.7 us -> 6.34 us  [project(): call(body, 4, (1,), [whole((toks, half_w)), whole((toks, half_w)), pl.Blo...]
    convert_element_type x3 -> x7, other arithmetic: 0.34 us -> 5.63 us  [the longest x4 2.74 us: member(): f = payload.astype(F32)]
    ppermute x5, waiting for transfers between devices: 11.4 us -> 14.7 us  [across(): return lax.ppermute(a, 'tp', [(i, i ^ bit) for i in range(n_tp)])]
    slice x3 -> x5, local copies, waits for them, and re-layouts: 1.58 us -> 3.96 us  [the longest x4 2.81 us: member(): f[state + 2:state + 3, 0:1]]
    pallas_call x1, Pallas kernels: 2.44 us -> 4.54 us  [prepare(): call(body, 7, (1,), [whole(raw.shape), whole(seg.shape), whole(decay_log....]
    pallas_call x2, Pallas kernels: 11.8 us -> 10.1 us  [local_part(): call(body, 8, (tiles,), [tile, tile, whole(read.shape), whole(write.shape...]
  transfers between devices with their start and end apart: 11 -> 11, of which waited for: 4 -> 5; matrix products, arithmetic and copies ran while one was open for 2% -> 3% of each run, Pallas kernels for 30% -> 19%
where the time goes in v2:
time: 91.8 us; the launch traced here: 91.1 us
  Pallas kernels  26.2 us (29%)
  waiting for transfers between devices  22.9 us (25%)
  local copies, waits for them, and re-layouts  18.1 us (20%)
  starting transfers between devices  10.9 us (12%)
  other arithmetic  6.67 us (7%)
  between operations  6.28 us (7%)
    ppermute x5, waiting for transfers between devices, across(): return lax.ppermute(a, 'tp', [(i, i ^ bit) for i in range(n_tp)])  14.7 us
    unnamed x58, local copies, waits for them, and re-layouts  12.9 us
    pallas_call x2, Pallas kernels, local_part(): call(body, 8, (tiles,), [tile, tile, whole(read.shape), whole(write.shape...  10.1 us
    ppermute x6, waiting for transfers between devices, swap(): return lax.ppermute(a, 'seq', [(i, i ^ bit) for i in range(n_seq)])  8.25 us
    ppermute x6, starting transfers between devices, swap(): return lax.ppermute(a, 'seq', [(i, i ^ bit) for i in range(n_seq)])  8.22 us
    pallas_call x3, Pallas kernels, project(): call(body, 4, (1,), [whole((toks, half_w)), whole((toks, half_w)), pl.Blo...  6.34 us
    pallas_call x1, Pallas kernels, prepare(): call(body, 7, (1,), [whole(raw.shape), whole(seg.shape), whole(decay_log....  4.54 us
    slice x4, local copies, waits for them, and re-layouts, member(): f[state + 2:state + 3, 0:1]  2.81 us
  transfers between devices with their start and end apart: 11, of which 5 were waited for; matrix products, arithmetic and copies ran while one was open for 3% of the time, Pallas kernels for 19%

profile of v2, /device:TPU:0, one launch (start us, length us, event | category | flops | bytes accessed | tf_op | source)
XLA Modules:
  0.0 91.1 jit_solution(3578092398843559909)
XLA Ops:
  0.0 0.6 stack.27.sc_ref
  0.6 4.5 %shard_map.109 = (bf16[144,640]{1,0:T(8,128)(2,1)}, f32[2,512,128]{2,1,0:T(8,128)}, f32[64,512]{1,0:T(8,128)}, f32[2,768,128]{2,1,0:T(8,128)}, f32[2,8,640]{2,1,0:T(8,128)}) custom-call(s32[6]{0:T(128)} %stack.27.sc_ref, bf16[20,512]{1,0:T(8,128)(2,1)} %raw_ref.1, s32[1,512]{1,0:T(1,128)} %bitcast.25, f32[1,20]{1,0:T(1,128)} %bitcast.26, f32[1,20]{1,0:T(1,128)} %bitcast.27, ...), custom_call_target="tpu_custom_call" | custom-call | flops 83886080 | bytes 4000000 | tf_op jit(solution)/shard_map/pallas_call | solution.py:149
  5.2 4.0 %collective-permute-start.1 = (bf16[144,640]{1,0:T(8,128)(2,1)}, bf16[144,640]{1,0:T(8,128)(2,1)S(1)}, u32[]{:S(2)}, u32[]{:S(2)}) collective-permute-start(bf16[144,640]{1,0:T(8,128)(2,1)} %get-tuple-element.24), channel_id=1, source_target_pairs={{0,12},{4,8},{8,4},{12,0},{16,28},{20,24},{24,20},{28,16},{1,13},{... | collective-permute-start | bytes 552968 | tf_op jit(solution)/shard_map/ppermute | solution.py:396
  9.2 1.3 %copy-done = bf16[512,1280]{1,0:T(8,128)(2,1)S(1)} copy-done((bf16[512,1280]{1,0:T(8,128)(2,1)S(1)}, bf16[512,1280]{1,0:T(8,128)(2,1)}, u32[]{:S(2)}) %copy-start) | copy-done | bytes 1310744
  10.5 1.1 %copy-done.5 = f32[2,768,128]{2,1,0:T(8,128)S(1)} copy-done((f32[2,768,128]{2,1,0:T(8,128)S(1)}, f32[2,768,128]{2,1,0:T(8,128)}, u32[]{:S(2)}) %copy-start.5) | copy-done | bytes 786456
  11.6 0.8 copy-done.15
  12.4 1.6 %shard_map.110 = (f32[128,640]{1,0:T(8,128)S(1)}, bf16[144,640]{1,0:T(8,128)(2,1)S(1)}) custom-call(s32[6]{0:T(128)S(1)} %copy-done.17, f32[2,768,128]{2,1,0:T(8,128)S(1)} %copy-done.5, f32[2,8,640]{2,1,0:T(8,128)S(1)} %copy-done.15, bf16[512,1280]{1,0:T(8,128)(2,1)S(1)} %copy-done, bf16[512,128]{1,0:T(8,128)(2,1)S(1)} %copy-done.10), custom_call_target="tpu_custom_call" | custom-call | flops 83886080 | bytes 2000000 | tf_op jit(solution)/shard_map/pallas_call | solution.py:188
  14.0 0.5 collective-permute-start
  14.5 0.2 collective-permute-start.2
  14.7 0.6 slice.74
  15.2 0.8 convert_element_type.46
  16.0 0.5 slice.65
  16.5 3.7 %collective-permute-done = bf16[144,640]{1,0:T(8,128)(2,1)} collective-permute-done((bf16[144,640]{1,0:T(8,128)(2,1)S(1)}, bf16[144,640]{1,0:T(8,128)(2,1)}, u32[]{:S(2)}, u32[]{:S(2)}) %collective-permute-start) | collective-permute-done | bytes 184352 | tf_op jit(solution)/shard_map/ppermute | solution.py:396
  20.3 1.2 %slice.64 = f32[1,1]{1,0:T(1,128)} slice(bf16[144,640]{1,0:T(8,128)(2,1)} %collective-permute-done), slice={[130:131], [0:1]} | slice | bytes 8 | tf_op jit(solution)/shard_map/slice | solution.py:403
  23.9 0.5 slice.75
  25.6 1.9 %convert_element_type.44 = f32[144,640]{1,0:T(8,128)} convert(bf16[144,640]{1,0:T(8,128)(2,1)} %collective-permute-done) | non-fusion elementwise | flops 92160 | bytes 552960 | tf_op jit(solution)/shard_map/convert_element_type | solution.py:402
  27.5 0.8 fusion.1
  28.4 0.6 concatenate.3
  29.0 2.6 %collective-permute-start.3 = (f32[2,640]{1,0:T(2,128)}, f32[2,640]{1,0:T(2,128)}, u32[]{:S(2)}, u32[]{:S(2)}) collective-permute-start(f32[2,640]{1,0:T(2,128)} %concatenate.3), channel_id=1, source_target_pairs={{0,16},{4,20},{8,24},{12,28},{16,0},{20,4},{24,8},{28,12},{1,17},{... | collective-permute-start | bytes 15368 | tf_op jit(solution)/shard_map/ppermute | solution.py:396
  31.6 1.1 %copy-done.6 = f32[2,768,128]{2,1,0:T(8,128)S(1)} copy-done((f32[2,768,128]{2,1,0:T(8,128)S(1)}, f32[2,768,128]{2,1,0:T(8,128)}, u32[]{:S(2)}) %copy-start.6) | copy-done | bytes 786456
  32.7 0.9 copy-done.8
  33.6 0.9 copy-done.11
  34.5 0.9 %copy-done.14 = bf16[144,640]{1,0:T(8,128)(2,1)S(1)} copy-done((bf16[144,640]{1,0:T(8,128)(2,1)S(1)}, bf16[144,640]{1,0:T(8,128)(2,1)}, u32[]{:S(2)}) %copy-start.14) | copy-done | bytes 184344
  35.5 1.3 %copy-done.18 = bf16[512,1280]{1,0:T(8,128)(2,1)S(1)} copy-done((bf16[512,1280]{1,0:T(8,128)(2,1)S(1)}, bf16[512,1280]{1,0:T(8,128)(2,1)}, u32[]{:S(2)}) %copy-start.18) | copy-done | bytes 1310744
  36.8 0.9 copy-done.20
  37.7 5.2 %shard_map.111 = (f32[512,640]{1,0:T(8,128)S(1)}, f32[512,640]{1,0:T(8,128)S(1)}) custom-call(s32[6]{0:T(128)S(1)} %copy-done.17, bf16[512,1280]{1,0:T(8,128)(2,1)S(1)} %copy-done.1, bf16[512,1280]{1,0:T(8,128)(2,1)S(1)} %copy-done.18, bf16[512,128]{1,0:T(8,128)(2,1)S(1)} %copy-done.8, bf16[512,128]{1,0:T(8,128)(2,1)S(1)} %copy-done.11, ...), custom_call_target="tpu_custom_call" | custom-call | flops 4000000000 | bytes 8000000 | tf_op jit(solution)/shard_map/pallas_call | solution.py:277
  42.9 1.1 %copy-done.3 = f32[512,640]{1,0:T(8,128)} copy-done((f32[512,640]{1,0:T(8,128)}, f32[512,640]{1,0:T(8,128)S(1)}, u32[]{:S(2)}) %copy-start.3) | copy-done | bytes 1310744
  45.3 1.1 %slice.76 = f32[1,1]{1,0:T(1,128)} slice(f32[2,640]{1,0:T(2,128)} %collective-permute-done.3), slice={[1:2], [0:1]} | slice | bytes 8 | tf_op jit(solution)/shard_map/slice | solution.py:442
  47.6 1.5 %add_convert_fusion.2 = (bf16[128,640]{1,0:T(8,128)(2,1)S(1)}, f32[128,640]{1,0:T(8,128)S(1)}) fusion(f32[128,640]{1,0:T(8,128)S(1)} %get-tuple-element.29, f32[144,640]{1,0:T(8,128)} %copy-done.22, f32[640]{0:T(1024)S(1)} %get-tuple-element.38, f32[640]{0:T(1024)S(1)} %get-tuple-element.40, pred[]{:T(512)} %ne.7, pred[]{:T(512)} %eq.23, ...), kind=kLoop, calls=%fused_computation.4 | loop fusion | flops 1064960 | bytes 1809922 | tf_op jit(solution)/shard_map/convert_element_type | solution.py:438
  49.1 0.4 collective-permute-start.4
  49.5 1.6 %copy-done.19 = bf16[512,1280]{1,0:T(8,128)(2,1)S(1)} copy-done((bf16[512,1280]{1,0:T(8,128)(2,1)S(1)}, bf16[512,1280]{1,0:T(8,128)(2,1)}, u32[]{:S(2)}) %copy-start.19) | copy-done | bytes 1310744
  51.1 0.9 copy-done.21
  52.0 5.0 %shard_map.113 = (f32[512,640]{1,0:T(8,128)S(1)}, f32[512,640]{1,0:T(8,128)S(1)}) custom-call(s32[6]{0:T(128)S(1)} %copy-done.17, bf16[512,1280]{1,0:T(8,128)(2,1)S(1)} %copy-done.1, bf16[512,1280]{1,0:T(8,128)(2,1)S(1)} %copy-done.19, bf16[512,128]{1,0:T(8,128)(2,1)S(1)} %copy-done.9, bf16[512,128]{1,0:T(8,128)(2,1)S(1)} %copy-done.12, ...), custom_call_target="tpu_custom_call" | custom-call | flops 4000000000 | bytes 8000000 | tf_op jit(solution)/shard_map/pallas_call | solution.py:277
  57.0 0.9 %collective-permute-done.4 = bf16[128,640]{1,0:T(8,128)(2,1)S(1)} collective-permute-done((bf16[128,640]{1,0:T(8,128)(2,1)S(1)}, bf16[128,640]{1,0:T(8,128)(2,1)S(1)}, u32[]{:S(2)}, u32[]{:S(2)}) %collective-permute-start.4) | collective-permute-done | bytes 163872 | tf_op jit(solution)/shard_map/ppermute | solution.py:396
  58.1 0.6 collective-permute-start.5
  58.7 1.2 %shard_map.112 = (bf16[512,640]{1,0:T(8,128)(2,1)S(1)}, f32[1,512]{1,0:T(1,128)S(1)}) custom-call(s32[6]{0:T(128)S(1)} %copy-done.17, f32[8,128]{1,0:T(8,128)S(1)} %broadcast_in_dim.23.prev_ref, bf16[512,128]{1,0:T(8,128)(2,1)S(1)} %copy-done.9, f32[2,512,128]{2,1,0:T(8,128)S(1)} %copy-done.2, f32[512,640]{1,0:T(8,128)S(1)} %get-tuple-element.27.a_ref, ...), custom_call_target="tpu_custom_call" | custom-call | flops 83886080 | bytes 4000000 | tf_op jit(solution)/shard_map/pallas_call | solution.py:321
  59.9 3.6 %collective-permute-done.5.e_ref = bf16[128,640]{1,0:T(8,128)(2,1)S(1)} collective-permute-done((bf16[128,640]{1,0:T(8,128)(2,1)S(1)}, bf16[128,640]{1,0:T(8,128)(2,1)S(1)}, u32[]{:S(2)}, u32[]{:S(2)}) %collective-permute-start.5) | collective-permute-done | bytes 163872 | tf_op jit(solution)/shard_map/ppermute | solution.py:396
  63.4 2.4 %shard_map.114 = (bf16[512,640]{1,0:T(8,128)(2,1)S(1)}, f32[1,512]{1,0:T(1,128)S(1)}, bf16[640,512]{1,0:T(8,128)(2,1)S(1)}) custom-call(s32[6]{0:T(128)S(1)} %copy-done.17, f32[8,128]{1,0:T(8,128)S(1)} %broadcast_in_dim.23.prev_ref, bf16[512,128]{1,0:T(8,128)(2,1)S(1)} %copy-done.9, f32[2,512,128]{2,1,0:T(8,128)S(1)} %copy-done.2, ...), custom_call_target="tpu_custom_call" | custom-call | flops 838860800 | bytes 6000000 | tf_op jit(solution)/shard_map/pallas_call | solution.py:344
  66.0 2.1 %shard_map.115 = f32[640,512]{1,0:T(8,128)S(1)} custom-call(s32[6]{0:T(128)S(1)} %copy-done.17, bf16[512,640]{1,0:T(8,128)(2,1)S(1)} %get-tuple-element.30.gk_ref, bf16[512,640]{1,0:T(8,128)(2,1)S(1)} %get-tuple-element.33.go_ref, bf16[1280,2560]{1,0:T(8,128)(2,1)S(1)} %bitcast.23, bf16[640,512]{1,0:T(8,128)(2,1)S(1)} %get-tuple-element.34.after_ref), custom_call_target="tpu_custom_call" | custom-call | flops 838860800 | bytes 4000000 | tf_op jit(solution)/shard_map/pallas_call | solution.py:367
  68.1 0.2 add_convert_fusion.after_ref
  68.3 2.1 %shard_map.117 = bf16[640,512]{1,0:T(8,128)(2,1)S(1)} custom-call(s32[6]{0:T(128)S(1)} %copy-done.17, bf16[512,640]{1,0:T(8,128)(2,1)S(1)} %get-tuple-element.30.gk_ref, bf16[512,640]{1,0:T(8,128)(2,1)S(1)} %get-tuple-element.33.go_ref, bf16[1280,2560]{1,0:T(8,128)(2,1)S(1)} %bitcast.23, bf16[640,512]{1,0:T(8,128)(2,1)S(1)} %add_convert_fusion.after_ref), custom_call_target="tpu_custom_call" | custom-call | flops 838860800 | bytes 4000000 | tf_op jit(solution)/shard_map/pallas_call | solution.py:367
  70.4 0.6 collective-permute-start.7
  71.0 1.5 %collective-permute-start.8 = (bf16[640,512]{1,0:T(8,128)(2,1)S(1)}, bf16[640,512]{1,0:T(8,128)(2,1)S(1)}, u32[]{:S(2)}, u32[]{:S(2)}) collective-permute-start(bf16[640,512]{1,0:T(8,128)(2,1)S(1)} %add_convert_fusion.after_ref), channel_id=1, source_target_pairs={{0,2},{1,3},{2,0},{3,1},{4,6},{5,7},{6,4},{7,5},{8,10},{9,11},{10,... | collective-permute-start | bytes 1966088 | tf_op jit(solution)/shard_map/ppermute | solution.py:399
  72.5 1.2 %collective-permute-done.9 = f32[1,512]{1,0:T(1,128)S(1)} collective-permute-done((f32[1,512]{1,0:T(1,128)S(1)}, f32[1,512]{1,0:T(1,128)S(1)}, u32[]{:S(2)}, u32[]{:S(2)}) %collective-permute-start.9) | collective-permute-done | bytes 2080 | tf_op jit(solution)/shard_map/ppermute | solution.py:399
  73.7 0.6 collective-permute-start.10
  74.2 13.5 %collective-permute-done.10 = f32[1,512]{1,0:T(1,128)S(1)} collective-permute-done((f32[1,512]{1,0:T(1,128)S(1)}, f32[1,512]{1,0:T(1,128)S(1)}, u32[]{:S(2)}, u32[]{:S(2)}) %collective-permute-start.10) | collective-permute-done | bytes 2080 | tf_op jit(solution)/shard_map/ppermute | solution.py:399
  87.8 2.1 %shard_map.116 = f32[640,512]{1,0:T(8,128)S(1)} custom-call(s32[6]{0:T(128)S(1)} %copy-done.17, bf16[512,640]{1,0:T(8,128)(2,1)S(1)} %get-tuple-element.30.gk_ref, bf16[512,640]{1,0:T(8,128)(2,1)S(1)} %get-tuple-element.33.go_ref, bf16[1280,2560]{1,0:T(8,128)(2,1)S(1)} %bitcast.23, bf16[640,512]{1,0:T(8,128)(2,1)S(1)} %add_convert_fusion.after_ref), custom_call_target="tpu_custom_call" | custom-call | flops 838860800 | bytes 4000000 | tf_op jit(solution)/shard_map/pallas_call | solution.py:367
  89.9 1.2 %multiply_convert_fusion = bf16[640,512]{1,0:T(8,128)(2,1)} fusion(bf16[640,512]{1,0:T(8,128)(2,1)S(1)} %collective-permute-done.8, f32[640,512]{1,0:T(8,128)S(1)} %shard_map.116, bf16[640,512]{1,0:T(8,128)(2,1)S(1)} %collective-permute-done.7, f32[512]{0:T(512)S(1)} %bitcast.24), kind=kLoop, calls=%fused_computation | loop fusion | flops 1966080 | bytes 3278848 | tf_op jit(solution)/shard_map/convert_element_type | solution.py:475
  (65 shorter events, 0.5 us)
Async XLA Ops:
  0.0 9.2 %copy-start.10 = (bf16[512,128]{1,0:T(8,128)(2,1)S(1)}, bf16[512,128]{1,0:T(8,128)(2,1)}, u32[]{:S(2)}) copy-start(bf16[512,128]{1,0:T(8,128)(2,1)} %wr_ref.7) | copy-start | bytes 393220
  0.6 8.5 %copy-start.17 = (s32[6]{0:T(128)S(1)}, s32[6]{0:T(128)}, u32[]{:S(2)}) copy-start(s32[6]{0:T(128)} %stack.27.sc_ref) | copy-start | bytes 76
  5.2 10.8 %collective-permute-start.1 = (bf16[144,640]{1,0:T(8,128)(2,1)}, bf16[144,640]{1,0:T(8,128)(2,1)S(1)}, u32[]{:S(2)}, u32[]{:S(2)}) collective-permute-start(bf16[144,640]{1,0:T(8,128)(2,1)} %get-tuple-element.24), channel_id=1, source_target_pairs={{0,12},{4,8},{8,4},{12,0},{16,28},{20,24},{24,20},{28,16},{1,13},{... | collective-permute-start | bytes 552968 | tf_op jit(solution)/shard_map/ppermute | solution.py:396
  9.2 1.3 %copy-start = (bf16[512,1280]{1,0:T(8,128)(2,1)S(1)}, bf16[512,1280]{1,0:T(8,128)(2,1)}, u32[]{:S(2)}) copy-start(bf16[512,1280]{1,0:T(8,128)(2,1)} %x_ref.7) | copy-start | bytes 3932164
  10.5 1.1 %copy-start.5 = (f32[2,768,128]{2,1,0:T(8,128)S(1)}, f32[2,768,128]{2,1,0:T(8,128)}, u32[]{:S(2)}) copy-start(f32[2,768,128]{2,1,0:T(8,128)} %get-tuple-element.21.tail_ref.tail0_ref) | copy-start | bytes 2359300
  11.6 0.8 copy-start.15
  12.4 2.1 %copy-start.26 = (bf16[144,640]{1,0:T(8,128)(2,1)S(1)}, bf16[144,640]{1,0:T(8,128)(2,1)}, u32[]{:S(2)}) copy-start(bf16[144,640]{1,0:T(8,128)(2,1)} %get-tuple-element.24) | copy-start | bytes 552964
  14.0 17.6 %copy-start.13 = (bf16[144,640]{1,0:T(8,128)(2,1)}, bf16[144,640]{1,0:T(8,128)(2,1)S(1)}, u32[]{:S(2)}) copy-start(bf16[144,640]{1,0:T(8,128)(2,1)S(1)} %get-tuple-element.23.after_ref) | copy-start | bytes 552964
  14.0 17.6 %copy-start.1 = (bf16[512,1280]{1,0:T(8,128)(2,1)S(1)}, bf16[512,1280]{1,0:T(8,128)(2,1)}, u32[]{:S(2)}) copy-start(bf16[512,1280]{1,0:T(8,128)(2,1)} %x_ref.7) | copy-start | bytes 3932164
  14.0 17.6 %copy-start.2 = (f32[2,512,128]{2,1,0:T(8,128)S(1)}, f32[2,512,128]{2,1,0:T(8,128)}, u32[]{:S(2)}) copy-start(f32[2,512,128]{2,1,0:T(8,128)} %get-tuple-element.25.ccol_ref.seg_ref) | copy-start | bytes 1572868
  14.0 17.6 %copy-start.16 = (f32[2,8,640]{2,1,0:T(8,128)S(1)}, f32[2,8,640]{2,1,0:T(8,128)}, u32[]{:S(2)}) copy-start(f32[2,8,640]{2,1,0:T(8,128)} %get-tuple-element.22.meta_ref) | copy-start | bytes 122884
  14.0 6.3 %collective-permute-start = (bf16[144,640]{1,0:T(8,128)(2,1)S(1)}, bf16[144,640]{1,0:T(8,128)(2,1)}, u32[]{:S(2)}, u32[]{:S(2)}) collective-permute-start(bf16[144,640]{1,0:T(8,128)(2,1)S(1)} %get-tuple-element.23.after_ref), channel_id=1, source_target_pairs={{0,8},{4,12},{8,0},{12,4},{16,24},{20,28},{24,16},{28,20},{1,9},{5... | collective-permute-start | bytes 552968 | tf_op jit(solution)/shard_map/ppermute | solution.py:396
  14.5 9.3 %collective-permute-start.2 = (bf16[144,640]{1,0:T(8,128)(2,1)S(1)}, bf16[144,640]{1,0:T(8,128)(2,1)S(1)}, u32[]{:S(2)}, u32[]{:S(2)}) collective-permute-start(bf16[144,640]{1,0:T(8,128)(2,1)S(1)} %copy-done.26), channel_id=1, source_target_pairs={{0,4},{4,0},{8,12},{12,8},{16,20},{20,16},{24,28},{28,24},{1,5},{5... | collective-permute-start | bytes 552968 | tf_op jit(solution)/shard_map/ppermute | solution.py:396
  25.6 6.0 %copy-start.22 = (f32[144,640]{1,0:T(8,128)}, f32[144,640]{1,0:T(8,128)S(1)}, u32[]{:S(2)}) copy-start(f32[144,640]{1,0:T(8,128)S(1)} %convert_element_type.47) | copy-start | bytes 1105924
  25.6 6.0 %copy-start.24 = (f32[144,640]{1,0:T(8,128)}, f32[144,640]{1,0:T(8,128)S(1)}, u32[]{:S(2)}) copy-start(f32[144,640]{1,0:T(8,128)S(1)} %convert_element_type.45) | copy-start | bytes 1105924
  29.0 16.3 %collective-permute-start.3 = (f32[2,640]{1,0:T(2,128)}, f32[2,640]{1,0:T(2,128)}, u32[]{:S(2)}, u32[]{:S(2)}) collective-permute-start(f32[2,640]{1,0:T(2,128)} %concatenate.3), channel_id=1, source_target_pairs={{0,16},{4,20},{8,24},{12,28},{16,0},{20,4},{24,8},{28,12},{1,17},{... | collective-permute-start | bytes 15368 | tf_op jit(solution)/shard_map/ppermute | solution.py:396
  31.6 1.1 %copy-start.6 = (f32[2,768,128]{2,1,0:T(8,128)S(1)}, f32[2,768,128]{2,1,0:T(8,128)}, u32[]{:S(2)}) copy-start(f32[2,768,128]{2,1,0:T(8,128)} %get-tuple-element.21.tail_ref.tail0_ref) | copy-start | bytes 2359300
  32.7 0.9 copy-start.8
  33.6 0.9 copy-start.11
  34.5 0.9 %copy-start.14 = (bf16[144,640]{1,0:T(8,128)(2,1)S(1)}, bf16[144,640]{1,0:T(8,128)(2,1)}, u32[]{:S(2)}) copy-start(bf16[144,640]{1,0:T(8,128)(2,1)} %copy-done.13) | copy-start | bytes 552964
  35.5 1.3 %copy-start.18 = (bf16[512,1280]{1,0:T(8,128)(2,1)S(1)}, bf16[512,1280]{1,0:T(8,128)(2,1)}, u32[]{:S(2)}) copy-start(bf16[512,1280]{1,0:T(8,128)(2,1)} %gate_ref.3) | copy-start | bytes 3932164
  36.8 0.9 copy-start.20
  37.7 6.2 %copy-start.25 = (f32[1280]{0:T(1024)S(1)}, f32[1280]{0:T(1024)}, u32[]{:S(2)}) copy-start(f32[1280]{0:T(1024)} %param.20) | copy-start | bytes 15364
  42.9 1.1 %copy-start.3 = (f32[512,640]{1,0:T(8,128)}, f32[512,640]{1,0:T(8,128)S(1)}, u32[]{:S(2)}) copy-start(f32[512,640]{1,0:T(8,128)S(1)} %get-tuple-element.28.b_ref) | copy-start | bytes 3932164
  43.9 5.6 %copy-start.7 = (f32[2,768,128]{2,1,0:T(8,128)S(1)}, f32[2,768,128]{2,1,0:T(8,128)}, u32[]{:S(2)}) copy-start(f32[2,768,128]{2,1,0:T(8,128)} %get-tuple-element.21.tail_ref.tail0_ref) | copy-start | bytes 2359300
  43.9 5.6 %copy-start.9 = (bf16[512,128]{1,0:T(8,128)(2,1)S(1)}, bf16[512,128]{1,0:T(8,128)(2,1)}, u32[]{:S(2)}) copy-start(bf16[512,128]{1,0:T(8,128)(2,1)} %rd_ref.7) | copy-start | bytes 393220
  44.0 5.6 %copy-start.12 = (bf16[512,128]{1,0:T(8,128)(2,1)S(1)}, bf16[512,128]{1,0:T(8,128)(2,1)}, u32[]{:S(2)}) copy-start(bf16[512,128]{1,0:T(8,128)(2,1)} %wr_ref.7) | copy-start | bytes 393220
  47.6 15.8 %slice-start = ((s8[6553600]{0:T(1024)(128)(4,1)}), s8[4194304]{0:T(1024)(128)(4,1)S(1)}, s32[]{:S(2)}) async-start(s8[6553600]{0:T(1024)(128)(4,1)} %bitcast.22), calls=%async_computation | async-start | bytes 8388608
  49.1 14.4 %slice-start.1 = ((s8[6553600]{0:T(1024)(128)(4,1)}), s8[2359296]{0:T(1024)(128)(4,1)S(1)}, s32[]{:S(2)}) async-start(s8[6553600]{0:T(1024)(128)(4,1)} %bitcast.22), calls=%async_computation.1 | async-start | bytes 4718592
  49.1 8.8 %collective-permute-start.4 = (bf16[128,640]{1,0:T(8,128)(2,1)S(1)}, bf16[128,640]{1,0:T(8,128)(2,1)S(1)}, u32[]{:S(2)}, u32[]{:S(2)}) collective-permute-start(bf16[128,640]{1,0:T(8,128)(2,1)S(1)} %get-tuple-element.44.after_ref), channel_id=1, source_target_pairs={{0,16},{4,20},{8,24},{12,28},{16,0},{20,4},{24,8},{28,12},{1,17},{... | collective-permute-start | bytes 491528 | tf_op jit(solution)/shard_map/ppermute | solution.py:396
  49.5 1.6 %copy-start.19 = (bf16[512,1280]{1,0:T(8,128)(2,1)S(1)}, bf16[512,1280]{1,0:T(8,128)(2,1)}, u32[]{:S(2)}) copy-start(bf16[512,1280]{1,0:T(8,128)(2,1)} %gate_ref.3) | copy-start | bytes 3932164
  51.1 0.9 copy-start.21
  52.0 5.9 %copy-start.23 = (f32[144,640]{1,0:T(8,128)S(1)}, f32[144,640]{1,0:T(8,128)}, u32[]{:S(2)}) copy-start(f32[144,640]{1,0:T(8,128)} %copy-done.22) | copy-start | bytes 1105924
  57.0 1.7 %copy-start.4 = (f32[512,640]{1,0:T(8,128)S(1)}, f32[512,640]{1,0:T(8,128)}, u32[]{:S(2)}) copy-start(f32[512,640]{1,0:T(8,128)} %copy-done.3) | copy-start | bytes 3932164
  58.1 5.4 %collective-permute-start.5 = (bf16[128,640]{1,0:T(8,128)(2,1)S(1)}, bf16[128,640]{1,0:T(8,128)(2,1)S(1)}, u32[]{:S(2)}, u32[]{:S(2)}) collective-permute-start(bf16[128,640]{1,0:T(8,128)(2,1)S(1)} %get-tuple-element.41), channel_id=1, source_target_pairs={{0,4},{4,0},{8,12},{12,8},{16,20},{20,16},{24,28},{28,24},{1,5},{5... | collective-permute-start | bytes 491528 | tf_op jit(solution)/shard_map/ppermute | solution.py:396
  65.9 2.2 %collective-permute-start.6 = (bf16[640,512]{1,0:T(8,128)(2,1)S(1)}, bf16[640,512]{1,0:T(8,128)(2,1)S(1)}, u32[]{:S(2)}, u32[]{:S(2)}) collective-permute-start(bf16[640,512]{1,0:T(8,128)(2,1)S(1)} %get-tuple-element.34.after_ref), channel_id=1, source_target_pairs={{0,1},{1,0},{2,3},{3,2},{4,5},{5,4},{6,7},{7,6},{8,9},{9,8},{10,11... | collective-permute-start | bytes 1966088 | tf_op jit(solution)/shard_map/ppermute | solution.py:399
  70.4 19.5 %collective-permute-start.7 = (bf16[640,512]{1,0:T(8,128)(2,1)S(1)}, bf16[640,512]{1,0:T(8,128)(2,1)S(1)}, u32[]{:S(2)}, u32[]{:S(2)}) collective-permute-start(bf16[640,512]{1,0:T(8,128)(2,1)S(1)} %shard_map.117), channel_id=1, source_target_pairs={{0,1},{1,0},{2,3},{3,2},{4,5},{5,4},{6,7},{7,6},{8,9},{9,8},{10,11... | collective-permute-start | bytes 1966088 | tf_op jit(solution)/shard_map/ppermute | solution.py:399
  71.0 18.9 %collective-permute-start.8 = (bf16[640,512]{1,0:T(8,128)(2,1)S(1)}, bf16[640,512]{1,0:T(8,128)(2,1)S(1)}, u32[]{:S(2)}, u32[]{:S(2)}) collective-permute-start(bf16[640,512]{1,0:T(8,128)(2,1)S(1)} %add_convert_fusion.after_ref), channel_id=1, source_target_pairs={{0,2},{1,3},{2,0},{3,1},{4,6},{5,7},{6,4},{7,5},{8,10},{9,11},{10,... | collective-permute-start | bytes 1966088 | tf_op jit(solution)/shard_map/ppermute | solution.py:399
  72.5 1.2 %collective-permute-start.9 = (f32[1,512]{1,0:T(1,128)S(1)}, f32[1,512]{1,0:T(1,128)S(1)}, u32[]{:S(2)}, u32[]{:S(2)}) collective-permute-start(f32[1,512]{1,0:T(1,128)S(1)} %add.65), channel_id=1, source_target_pairs={{0,1},{1,0},{2,3},{3,2},{4,5},{5,4},{6,7},{7,6},{8,9},{9,8},{10,11... | collective-permute-start | bytes 6152 | tf_op jit(solution)/shard_map/ppermute | solution.py:399
  73.7 14.1 %collective-permute-start.10 = (f32[1,512]{1,0:T(1,128)S(1)}, f32[1,512]{1,0:T(1,128)S(1)}, u32[]{:S(2)}, u32[]{:S(2)}) collective-permute-start(f32[1,512]{1,0:T(1,128)S(1)} %add.66), channel_id=1, source_target_pairs={{0,2},{1,3},{2,0},{3,1},{4,6},{5,7},{6,4},{7,5},{8,10},{9,11},{10,... | collective-permute-start | bytes 6152 | tf_op jit(solution)/shard_map/ppermute | solution.py:399

commit v3 on v2

v3 whole, which is shorter than its diff:
```python
import functools

import jax
import jax.numpy as jnp
from jax import lax
from jax.experimental import pallas as pl
from jax.experimental.pallas import tpu as pltpu
from jax.sharding import PartitionSpec as P

GROUP = 256
LANES = 128
EPS = 1e-05
LOG2E = 1.4426950408889634
SEG_LANE = 32
EXTRA = 16
VMEM = 48 * 1024 * 1024
VMEM_ALL = 63 * 1024 * 1024
F32 = jnp.float32
BF16 = jnp.bfloat16


def dot(a, b, dims=((1,), (0,))):
    return lax.dot_general(a, b, (dims, ((), ())), preferred_element_type=F32)


def lane_iota(rows):
    return lax.broadcasted_iota(jnp.int32, (rows, LANES), 1)


def spread(cols, first, width):
    rows = cols.shape[0]
    per = LANES // width
    lane = lane_iota(rows)
    out = jnp.broadcast_to(cols[:, first : first + 1], (rows, LANES))
    for k in range(1, per):
        nxt = jnp.broadcast_to(cols[:, first + k : first + k + 1], (rows, LANES))
        out = jnp.where(lane < k * width, out, nxt)
    return out


def call(body, grid, in_specs, out_specs, out_shape, scratch=(), cost=0, limit=VMEM):
    return pl.pallas_call(
        body,
        grid_spec=pltpu.PrefetchScalarGridSpec(
            num_scalar_prefetch=1,
            grid=grid,
            in_specs=in_specs,
            out_specs=out_specs,
            scratch_shapes=list(scratch),
        ),
        out_shape=out_shape,
        compiler_params=pltpu.CompilerParams(vmem_limit_bytes=limit),
        cost_estimate=pl.CostEstimate(flops=cost, bytes_accessed=1000, transcendentals=0),
    )


def anywhere():
    return pl.BlockSpec(memory_space=pl.ANY)


def whole(shape):
    return pl.BlockSpec(shape, lambda i, sc: (0,) * len(shape))


def pack(out_ref, total):
    state, through, last = total
    size, lanes = state.shape
    high = through.astype(BF16).astype(F32)
    row = lax.broadcasted_iota(jnp.int32, (EXTRA, lanes), 0)
    rows = jnp.where(row == 0, high, jnp.where(row == 1, through - high, last))
    out_ref[0:size] = state.astype(BF16)
    out_ref[size : size + EXTRA] = rows.astype(BF16)


def unpack(ref):
    size = ref.shape[0] - EXTRA
    rows = ref[size : size + EXTRA].astype(F32)
    return ref[0:size].astype(F32), rows[0:1] + rows[1:2], rows[2:3, 0:1]


def joined(first, second):
    link = second[1] * (first[2] == second[2]).astype(F32)
    return second[0] + link * first[0], second[1] * first[1], second[2]


def ordered(swapped, one, two):
    firsts = tuple(jnp.where(swapped, t, o) for o, t in zip(one, two))
    seconds = tuple(jnp.where(swapped, o, t) for o, t in zip(one, two))
    return firsts, seconds


def prepare(heads, width, raw, seg, decay_log, bias, skip, x, write):
    toks = raw.shape[1]
    state = write.shape[1]
    half_w = x.shape[1] // 2
    half_h = heads // 2
    blocks = toks // GROUP

    def body(
        raw_ref, seg_ref, dl_ref, sb_ref, sk_ref, x_hbm, wr_ref,
        other_ref, keep_ref, own_ref, ccol_ref, arow_ref, tail_ref, skip_ref,
        pad, rows, x_ref, sem,
    ):
        copy = pltpu.make_async_copy(x_hbm, x_ref, sem)
        copy.start()
        pad[...] = jnp.zeros_like(pad)
        pad[0:heads] = raw_ref[...].astype(F32)
        pad[SEG_LANE : SEG_LANE + 1] = seg_ref[...].astype(F32)
        rows[...] = jnp.zeros_like(rows)
        rows[0:1, 0:heads] = dl_ref[...]
        rows[1:2, 0:heads] = sb_ref[...]
        rows[2:3, 0:heads] = sk_ref[...]
        cols = jnp.transpose(pad[...])
        lane = lane_iota(toks)
        z = cols + rows[1:2]
        step = jnp.maximum(z, 0.0) + jnp.log1p(jnp.exp(-jnp.abs(z)))
        rate = -jnp.exp(rows[0:1]) * step
        tri = (
            lax.broadcasted_iota(jnp.int32, (GROUP, GROUP), 0)
            >= lax.broadcasted_iota(jnp.int32, (GROUP, GROUP), 1)
        ).astype(BF16)
        cum, full = [], []
        base = jnp.zeros((1, LANES), F32)
        for b in range(blocks):
            r = rate[b * GROUP : (b + 1) * GROUP]
            r1 = r.astype(BF16)
            d1 = r - r1.astype(F32)
            r2 = d1.astype(BF16)
            r3 = (d1 - r2.astype(F32)).astype(BF16)
            c = dot(tri, r1) + (dot(tri, r2) + dot(tri, r3))
            cum.append(c)
            full.append(c + base)
            base = base + c[GROUP - 1 : GROUP]
        total = base
        seg_col = cols[:, SEG_LANE : SEG_LANE + 1]
        last = cols[toks - 1 : toks, SEG_LANE : SEG_LANE + 1]
        tail = jnp.exp(total - jnp.concatenate(full, axis=0)) * step
        tail = jnp.where(seg_col == last, tail, 0.0)
        per = LANES // width
        keep = jnp.exp(total)
        copy.wait()
        halves = []
        for j in range(2):
            parts, through = [], []
            for i in range(half_w // LANES):
                at = j * half_h + i * per
                xt = x_ref[:, j * half_w + i * LANES : j * half_w + (i + 1) * LANES].astype(F32)
                parts.append((xt * spread(tail, at, width)).astype(BF16))
                through.append(spread(keep, at, width))
            own = dot(wr_ref[...], jnp.concatenate(parts, axis=1), ((0,), (0,)))
            halves.append((own, jnp.concatenate(through, axis=1), last))
        odd = lax.rem(lax.axis_index("seq"), 2) == 1
        mine, other = ordered(odd, *halves)
        own_ref[...] = mine[0]
        pack(keep_ref, mine)
        pack(other_ref, other)
        cum_all = jnp.concatenate(cum, axis=0)
        last0 = cols[GROUP - 1 : GROUP, SEG_LANE : SEG_LANE + 1]
        tail0 = jnp.exp(cum[0][GROUP - 1 : GROUP] - cum[0]) * step[0:GROUP]
        tail0 = jnp.where(seg_col[0:GROUP] == last0, tail0, 0.0)
        cc = cum_all * LOG2E
        a = jnp.where(lane == SEG_LANE, cols, cc - jnp.log(step) * LOG2E)
        arow_ref[...] = jnp.transpose(a)[0:64]
        seg_b = jnp.broadcast_to(seg_col, (toks, LANES))
        ccol_ref[0] = jnp.where(lane == SEG_LANE, seg_b, cc)
        ccol_ref[1] = jnp.where(lane == SEG_LANE, seg_b, pltpu.roll(cc, LANES - half_h, 1))
        tail_ref[0] = tail0
        tail_ref[1] = pltpu.roll(tail0, LANES - half_h, 1)
        for j in range(2):
            for i in range(half_w // LANES):
                tile = slice(i * LANES, (i + 1) * LANES)
                gains = spread(rows[2:3], j * half_h + i * per, width)
                skip_ref[j, :, tile] = jnp.broadcast_to(gains, (8, LANES))

    vm = pl.BlockSpec(memory_space=pltpu.VMEM)
    return pl.pallas_call(
        body,
        in_specs=[vm, vm, vm, vm, vm, anywhere(), vm],
        out_specs=[vm] * 7,
        out_shape=[
            jax.ShapeDtypeStruct((state + EXTRA, half_w), BF16),
            jax.ShapeDtypeStruct((state + EXTRA, half_w), BF16),
            jax.ShapeDtypeStruct((state, half_w), F32),
            jax.ShapeDtypeStruct((2, toks, LANES), F32),
            jax.ShapeDtypeStruct((64, toks), F32),
            jax.ShapeDtypeStruct((2, GROUP, LANES), F32),
            jax.ShapeDtypeStruct((2, 8, half_w), F32),
        ],
        scratch_shapes=[
            pltpu.VMEM((LANES, toks), F32), pltpu.VMEM((8, LANES), F32),
            pltpu.VMEM(x.shape, BF16), pltpu.SemaphoreType.DMA(()),
        ],
        compiler_params=pltpu.CompilerParams(vmem_limit_bytes=VMEM_ALL),
        cost_estimate=pl.CostEstimate(flops=4_000_000_000, bytes_accessed=1000, transcendentals=0),
    )(raw, seg, decay_log, bias, skip, x, write)


def gather_level(upper, entry, other):
    state, through, last_id = entry
    link = through * ((last_id < 0) | (other[2] == last_id)).astype(F32)
    state = state + jnp.where(upper, link, 0.0) * other[0]
    last_id = jnp.where(upper & (last_id < 0), other[2], last_id)
    return state, through * jnp.where(upper, other[1], 1.0), last_id


def put_rows(rows_ref, rows):
    lanes = rows_ref.shape[1]
    for at, row in enumerate(rows):
        rows_ref[at : at + 1] = jnp.broadcast_to(row, (1, lanes))


def pair_step(sc, own, keep, mate, side, cross, after):
    size, lanes = own.shape

    def body(
        sc_ref, own_ref, keep_ref, mate_ref, side_ref, cross_ref, after_ref,
        send_ref, entry_ref, first_ref, total_ref, rows_ref,
    ):
        odd = sc_ref[0] == 1
        upper = (sc_ref[6] & 2) != 0
        mine = (own_ref[...],) + unpack(keep_ref)[1:]
        first, second = ordered(odd, mine, unpack(mate_ref))
        total = joined(first, second)
        other = joined(*ordered(odd, unpack(side_ref), unpack(cross_ref)))
        nothing = (jnp.zeros_like(own_ref), jnp.ones_like(total[1]), jnp.full((1, 1), -1.0, F32))
        entry = gather_level(upper, nothing, other)
        total = joined(*ordered(upper, total, other))
        pack(send_ref, total)
        entry_ref[...], first_ref[...], total_ref[...] = entry[0], first[0], total[0]
        put_rows(rows_ref, entry[1:] + first[1:] + total[1:])

    return call(
        body, (1,),
        [whole((size, lanes))] + [whole(mate.shape)] * 4 + [anywhere()],
        [whole(mate.shape)] + [whole((size, lanes))] * 3 + [whole((8, lanes))],
        [jax.ShapeDtypeStruct(mate.shape, BF16)]
        + [jax.ShapeDtypeStruct((size, lanes), F32)] * 3
        + [jax.ShapeDtypeStruct((8, lanes), F32)],
    )(sc, own, keep, mate, side, cross, after)


def level_step(bit, final, sc, got, entry, first, total, rows, after):
    size, lanes = entry.shape

    def body(
        sc_ref, got_ref, entry_ref, first_ref, total_ref, rows_ref, after_ref,
        send_ref, one_ref, two_ref, three_ref,
    ):
        upper = (sc_ref[6] & bit) != 0
        other = unpack(got_ref)
        old = (entry_ref[...], rows_ref[0:1], rows_ref[1:2, 0:1])
        new = gather_level(upper, old, other)
        if final:
            even = sc_ref[0] == 0
            last_first = rows_ref[3:4, 0:1]
            link = rows_ref[2:3] * (last_first == new[2]).astype(F32)
            reached = first_ref[...] + link * new[0]
            send_ref[...] = jnp.where(even, reached, new[0]).astype(BF16)
            one_ref[...] = jnp.where(even, new[0], reached).astype(BF16)
            two_ref[...] = jnp.broadcast_to(jnp.where(even, new[2], last_first), (8, LANES))
            three_ref[...] = jnp.zeros_like(three_ref)
        else:
            held = (total_ref[...], rows_ref[4:5], rows_ref[5:6, 0:1])
            held = joined(*ordered(upper, held, other))
            pack(send_ref, held)
            one_ref[...] = new[0]
            two_ref[...] = held[0]
            put_rows(three_ref, new[1:] + (rows_ref[2:3], rows_ref[3:4]) + held[1:])

    state = [jax.ShapeDtypeStruct((size, lanes), F32)]
    if final:
        out = [jax.ShapeDtypeStruct((size, lanes), BF16)] * 2 + [jax.ShapeDtypeStruct((8, LANES), F32)] * 2
    else:
        out = [jax.ShapeDtypeStruct(got.shape, BF16)] + state * 2 + [jax.ShapeDtypeStruct((8, lanes), F32)]
    return call(
        body, (1,),
        [whole(got.shape)] + [whole((size, lanes))] * 3 + [whole((8, lanes)), anywhere()],
        [whole(o.shape) for o in out],
        out,
    )(sc, got, entry, first, total, rows, after)


def local_part(which, heads, width, sc, x, gate, read, write, ccol, arow, tail, skip, after):
    toks = write.shape[0]
    half_w = x.shape[1] // 2
    half_h = heads // 2
    per = LANES // width
    tiles = half_w // LANES
    blocks = toks // GROUP
    strip = 64

    def body(
        sc_ref, x_ref, gate_ref, rd_ref, wr_ref, ccol_ref, arow_ref, tail0_ref, skip_ref, after_ref,
        a_ref, b_ref, scores, mix,
    ):
        i = pl.program_id(0)
        seg_col = ccol_ref[0, :, SEG_LANE : SEG_LANE + 1]

        @pl.when(i == 0)
        def _():
            mix[...] = jnp.zeros_like(mix)
            for b in range(blocks):
                rows = slice(b * GROUP, (b + 1) * GROUP)
                s = dot(rd_ref[rows], wr_ref[rows], ((1,), (1,)))
                causal = lax.broadcasted_iota(jnp.int32, (GROUP, GROUP), 0) >= lax.broadcasted_iota(
                    jnp.int32, (GROUP, GROUP), 1
                )
                same = seg_col[rows] == arow_ref[SEG_LANE : SEG_LANE + 1, rows]
                scores[b] = jnp.where(causal & same, s, 0.0)

        turn = lax.rem(LANES - per * i, LANES)
        cr = pltpu.roll(ccol_ref[0], turn, 1)
        tr = pltpu.roll(tail0_ref[0], turn, 1)
        gains = skip_ref[0, 0:1, :]
        lane = lane_iota(GROUP)
        head0 = sc_ref[which] * half_h + per * i
        carry = None
        start = jnp.ones((1, LANES), F32)
        for b in range(blocks):
            rows = slice(b * GROUP, (b + 1) * GROUP)
            xb = x_ref[rows]
            logs = []
            for k in range(per):
                cb = jnp.broadcast_to(cr[rows, k : k + 1], (GROUP, LANES))
                logs.append(cb)
                ar = arow_ref[pl.ds(head0 + k, 1), rows]
                for low in range(0, GROUP, strip):
                    for left in range(0, min(low + strip, GROUP), LANES):
                        part = jnp.exp2(jnp.minimum(cb[low : low + strip] - ar[:, left : left + LANES], 60.0))
                        part = part * scores[b, low : low + strip, left : left + LANES]
                        mix[b, k * GROUP + low : k * GROUP + low + strip, left : left + LANES] = part.astype(BF16)
            both = dot(mix[b], xb)
            inner, dec_log = both[0:GROUP], logs[0]
            for k in range(1, per):
                inner = jnp.where(lane < k * width, inner, both[k * GROUP : (k + 1) * GROUP])
                dec_log = jnp.where(lane < k * width, dec_log, logs[k])
            dec = jnp.exp2(dec_log)
            xf = xb.astype(F32)
            y = inner + gains * xf
            if b == 1:
                linked = seg_col[rows] == seg_col[GROUP - 1 : GROUP]
                rm = jnp.where(linked, rd_ref[rows].astype(F32), 0.0).astype(BF16)
                y = y + (dot(rm, carry[0]) + dot(rm, carry[1])) * dec
            else:
                xs = (xf * spread(tr, 0, width)).astype(BF16)
                s0 = dot(wr_ref[rows], xs, ((0,), (0,)))
                s0h = s0.astype(BF16)
                carry = (s0h, (s0 - s0h.astype(F32)).astype(BF16))
            v = gate_ref[rows].astype(F32)
            sg = v / (1.0 + jnp.exp(-v))
            a_ref[rows] = sg * y
            b_ref[rows] = sg * (dec * start)
            start = start * dec[GROUP - 1 : GROUP]

    tile = pl.BlockSpec((toks, LANES), lambda i, sc: (0, sc[which] * tiles + i))
    out = pl.BlockSpec((toks, LANES), lambda i, sc: (0, i))
    return call(
        body, (tiles,),
        [
            tile, tile, whole(read.shape), whole(write.shape),
            pl.BlockSpec((1, toks, LANES), lambda i, sc: (sc[which], 0, 0)),
            whole(arow.shape),
            pl.BlockSpec((1, GROUP, LANES), lambda i, sc: (sc[which], 0, 0)),
            pl.BlockSpec((1, 8, LANES), lambda i, sc: (sc[which], 0, i)),
            anywhere(),
        ],
        [out, out],
        [jax.ShapeDtypeStruct((toks, half_w), F32), jax.ShapeDtypeStruct((toks, half_w), F32)],
        [pltpu.VMEM((blocks, GROUP, GROUP), F32), pltpu.VMEM((blocks, per * GROUP, GROUP), BF16)],
        cost=4_000_000_000,
    )(sc, x, gate, read, write, ccol, arow, tail, skip, after)


def gated_tile(prev_ref, rd_ref, seg_ref, a_ref, b_ref, e_ref, gain_ref):
    linked = seg_ref[0, :, SEG_LANE : SEG_LANE + 1] == prev_ref[0:1, 0:1]
    rm = jnp.where(linked, rd_ref[...].astype(F32), 0.0).astype(BF16)
    gated = a_ref[...] + b_ref[...] * dot(rm, e_ref[...])
    sq = gated * gated
    part = sq[:, 0:LANES]
    for i in range(1, sq.shape[1] // LANES):
        part = part + sq[:, i * LANES : (i + 1) * LANES]
    squares = jnp.sum(jnp.transpose(part), axis=0, keepdims=True)
    return (gated * gain_ref[...]).astype(BF16), squares


def gate_specs(which, toks, half_w, state):
    return [
        whole((8, LANES)), whole((toks, state)),
        pl.BlockSpec((1, toks, LANES), lambda i, sc: (0, 0, 0)),
        whole((toks, half_w)), whole((toks, half_w)), whole((state, half_w)),
        pl.BlockSpec((1, half_w), lambda i, sc: (0, sc[which])),
    ]


def gated_half(which, sc, prev, read, ccol, a, b, e, gain):
    toks, half_w = a.shape

    def body(sc_ref, prev_ref, rd_ref, seg_ref, a_ref, b_ref, e_ref, gain_ref, g_ref, s_ref):
        g_ref[...], s_ref[...] = gated_tile(prev_ref, rd_ref, seg_ref, a_ref, b_ref, e_ref, gain_ref)

    return call(
        body, (1,),
        gate_specs(which, toks, half_w, read.shape[1]),
        [whole((toks, half_w)), whole((1, toks))],
        [jax.ShapeDtypeStruct((toks, half_w), BF16), jax.ShapeDtypeStruct((1, toks), F32)],
        cost=1_000_000_000,
    )(sc, prev, read, ccol, a, b, e, gain)


def weight_block(sc_ref, quarter, w_hbm, w_ref, sems):
    half_w, cols = w_ref.shape[1:]
    copies = []
    for at in range(2):
        rows = pl.ds(pl.multiple_of(sc_ref[at] * half_w, LANES), half_w)
        columns = pl.ds(pl.multiple_of(sc_ref[quarter] * cols, LANES), cols)
        copies.append(pltpu.make_async_copy(w_hbm.at[rows, columns], w_ref.at[at], sems.at[at]))
        copies[-1].start()
    return copies


def gate_and_project(which, quarter, sc, prev, read, ccol, a, b, e, gain, g_keep, weight):
    toks, half_w = a.shape
    cols = weight.shape[1] // 4

    def body(
        sc_ref, prev_ref, rd_ref, seg_ref, a_ref, b_ref, e_ref, gain_ref, gk_ref, w_hbm,
        g_ref, s_ref, y_ref, w_ref, sems,
    ):
        copies = weight_block(sc_ref, quarter, w_hbm, w_ref, sems)
        g, s_ref[...] = gated_tile(prev_ref, rd_ref, seg_ref, a_ref, b_ref, e_ref, gain_ref)
        g_ref[...] = g
        copies[0].wait()
        y = dot(gk_ref[...], w_ref[0])
        copies[1].wait()
        y = y + dot(g, w_ref[1])
        y_ref[...] = jnp.transpose(y).astype(BF16)

    return call(
        body, (1,),
        gate_specs(which, toks, half_w, read.shape[1]) + [whole((toks, half_w)), anywhere()],
        [whole((toks, half_w)), whole((1, toks)), whole((cols, toks))],
        [
            jax.ShapeDtypeStruct((toks, half_w), BF16),
            jax.ShapeDtypeStruct((1, toks), F32),
            jax.ShapeDtypeStruct((cols, toks), BF16),
        ],
        [pltpu.VMEM((2, half_w, cols), BF16), pltpu.SemaphoreType.DMA((2,))],
        cost=1_000_000_000,
    )(sc, prev, read, ccol, a, b, e, gain, g_keep, weight)


def project(quarter, dtype, sc, g_keep, g_other, weight, after):
    toks, half_w = g_keep.shape
    cols = weight.shape[1] // 4

    def body(sc_ref, gk_ref, go_ref, w_hbm, after_ref, y_ref, w_ref, sems):
        copies = weight_block(sc_ref, quarter, w_hbm, w_ref, sems)
        copies[0].wait()
        y = dot(gk_ref[...], w_ref[0])
        copies[1].wait()
        y = y + dot(go_ref[...], w_ref[1])
        y_ref[...] = jnp.transpose(y).astype(dtype)

    return call(
        body, (1,),
        [whole((toks, half_w)), whole((toks, half_w)), anywhere(), anywhere()],
        whole((cols, toks)),
        jax.ShapeDtypeStruct((cols, toks), dtype),
        [pltpu.VMEM((2, half_w, cols), BF16), pltpu.SemaphoreType.DMA((2,))],
        cost=1_000_000,
    )(sc, g_keep, g_other, weight, after)


def on_device(
    n_seq, n_tp, head_input, gate_input, write_vecs, read_vecs, step_raw, segment_ids,
    decay_log, step_bias, skip_gain, norm_gain, out_weight,
):
    heads = decay_log.shape[0]
    toks, feats = head_input.shape
    width = feats // heads
    place = lax.axis_index("seq")
    rank = lax.axis_index("tp")
    odd = lax.rem(place, 2)
    near, far = rank ^ 1, rank ^ 2
    sc = jnp.stack([odd, 1 - odd, far ^ 1, far, near, rank, place]).astype(jnp.int32)

    def swap(a, bit):
        return lax.ppermute(a, "seq", [(i, i ^ bit) for i in range(n_seq)])

    def across(a, bit):
        return lax.ppermute(a, "tp", [(i, i ^ bit) for i in range(n_tp)])

    send_other, send_keep, own, ccol, arow, tail, skip = prepare(
        heads, width, step_raw, segment_ids.reshape(1, toks), decay_log.reshape(1, heads),
        step_bias.reshape(1, heads), skip_gain.reshape(1, heads), head_input, write_vecs,
    )
    mate = swap(send_other, 1)
    cross = swap(send_other, 3)
    side = swap(send_keep, 2)
    shared = (head_input, gate_input, read_vecs, write_vecs, ccol, arow, tail, skip)
    a_keep, b_keep = local_part(0, heads, width, sc, *shared, send_keep)
    sent, entry, first, total, rows = pair_step(sc, own, send_keep, mate, side, cross, a_keep)
    a_other, b_other = local_part(1, heads, width, sc, *shared, sent)
    bit = 4
    while 2 * bit < n_seq:
        sent, entry, total, rows = level_step(
            bit, False, sc, swap(sent, bit), entry, first, total, rows, a_other
        )
        bit *= 2
    sent, e_keep, prev, _ = level_step(bit, True, sc, swap(sent, bit), entry, first, total, rows, a_other)
    e_other = swap(sent, 1)
    gain = norm_gain.reshape(1, feats)
    g_keep, s_keep = gated_half(0, sc, prev, read_vecs, ccol, a_keep, b_keep, e_keep, gain)
    g_other, s_other, y_far_near = gate_and_project(
        1, 2, sc, prev, read_vecs, ccol, a_other, b_other, e_other, gain, g_keep, out_weight
    )
    got_far = across(y_far_near, 1)
    squares = s_keep + s_other
    squares = squares + across(squares, 1)
    y_far = project(3, F32, sc, g_keep, g_other, out_weight, y_far_near)
    to_far = (y_far + got_far.astype(F32)).astype(BF16)
    got_x = across(to_far, 2)
    squares = squares + across(squares, 2)
    got_near = across(project(4, BF16, sc, g_keep, g_other, out_weight, to_far), 1)
    y_own = project(5, F32, sc, g_keep, g_other, out_weight, to_far)
    inv = lax.rsqrt(squares / (feats * n_tp) + EPS)
    out = (y_own + got_near.astype(F32)) + got_x.astype(F32)
    return (out * inv).astype(BF16)


def solution(mesh):
    in_specs = (
        P("seq", "tp"),
        P("seq", "tp"),
        P("seq", None),
        P("seq", None),
        P("tp", "seq"),
        P("seq"),
        P("tp"),
        P("tp"),
        P("tp"),
        P("tp"),
        P("tp", None),
    )
    out_specs = P("tp", "seq")
    return jax.shard_map(
        functools.partial(on_device, mesh.shape["seq"], mesh.shape["tp"]),
        mesh=mesh, in_specs=in_specs, out_specs=out_specs, check_vma=False,
    )
```

time: 91.8 us -> 74 us (0.81)
  local copies, waits for them, and re-layouts: 18.1 us -> 6.03 us
  Pallas kernels: 26.2 us -> 34.7 us
  between operations: 6.28 us -> 0.2 us
  other arithmetic: 6.67 us -> 1.41 us
  waiting for transfers between devices: 22.9 us -> 19 us
  starting transfers between devices: 10.9 us -> 12 us
    pallas_call x9 -> x10, Pallas kernels: 26.2 us -> 34.7 us  [the longest x2 12 us: local_part(): call(body, (tiles,), [tile, tile, whole(read.shape), whole(write.shape),...]
    unnamed x58 -> x28, local copies, waits for them, and re-layouts: 12.9 us -> 5.94 us
    convert_element_type x5 -> x0, other arithmetic: 4.21 us -> none  [the longest x4 2.74 us: member(): f = payload.astype(F32)]
    slice x5 -> x0, local copies, waits for them, and re-layouts: 3.96 us -> none  [the longest x4 2.81 us: member(): f[state + 2:state + 3, 0:1]]
    ppermute x6 -> x5, waiting for transfers between devices: 8.25 us -> 4.36 us  [swap(): return lax.ppermute(a, 'seq', [(i, i ^ bit) for i in range(n_seq)])]
    ppermute x6 -> x5, starting transfers between devices: 8.22 us -> 9.22 us  [swap(): return lax.ppermute(a, 'seq', [(i, i ^ bit) for i in range(n_seq)])]
  transfers between devices with their start and end apart: 11 -> 10, of which waited for: 5 -> 4; matrix products, arithmetic and copies ran while one was open for 3% -> 0% of each run, Pallas kernels for 19% -> 27%
where the time goes in v3:
time: 74 us; the launch traced here: 73.3 us
  Pallas kernels  34.7 us (47%)
  waiting for transfers between devices  19 us (26%)
  starting transfers between devices  12 us (16%)
  local copies, waits for them, and re-layouts  6.03 us (8%)
  other arithmetic  1.41 us (2%)
    ppermute x5, waiting for transfers between devices, across(): return lax.ppermute(a, 'tp', [(i, i ^ bit) for i in range(n_tp)])  14.6 us
    pallas_call x2, Pallas kernels, local_part(): call(body, (tiles,), [tile, tile, whole(read.shape), whole(write.shape),...  12 us
    pallas_call x3, Pallas kernels, project(): call(body, (1,), [whole((toks, half_w)), whole((toks, half_w)), anywhere(...  10.2 us
    ppermute x5, starting transfers between devices, swap(): return lax.ppermute(a, 'seq', [(i, i ^ bit) for i in range(n_seq)])  9.22 us
    unnamed x28, local copies, waits for them, and re-layouts  5.94 us
    pallas_call x1, Pallas kernels, prepare(): pl.pallas_call(body, in_specs=[vm, vm, vm, vm, vm, anywhere(), vm], out_s...  5.31 us
    ppermute x5, waiting for transfers between devices, swap(): return lax.ppermute(a, 'seq', [(i, i ^ bit) for i in range(n_seq)])  4.36 us
    pallas_call x1, Pallas kernels, gate_and_project(): call(body, (1,), gate_specs(which, toks, half_w, read.shape[1]) + [whole(...  3.97 us
  transfers between devices with their start and end apart: 10, of which 4 were waited for; matrix products, arithmetic and copies ran while one was open for 0% of the time, Pallas kernels for 27%

profile of v3, /device:TPU:0, one launch (start us, length us, event | category | flops | bytes accessed | tf_op | source)
XLA Modules:
  0.0 73.3 jit_solution(16134723191346737828)
XLA Ops:
  0.0 5.3 %shard_map.109 = (bf16[144,640]{1,0:T(8,128)(2,1)}, bf16[144,640]{1,0:T(8,128)(2,1)}, f32[128,640]{1,0:T(8,128)}, f32[2,512,128]{2,1,0:T(8,128)}, f32[64,512]{1,...) custom-call(bf16[20,512]{1,0:T(8,128)(2,1)} %raw_ref.1, s32[1,512]{1,0:T(1,128)} %bitcast.13, f32[1,20]{1,0:T(1,128)} %bitcast.14, ...), custom_call_target="tpu_custom_call" | custom-call | flops 4000000000 | bytes 1000 | tf_op jit(solution)/shard_map/pallas_call | solution.py:176
  5.3 3.0 %collective-permute-start = (bf16[144,640]{1,0:T(8,128)(2,1)}, bf16[144,640]{1,0:T(8,128)(2,1)S(1)}, u32[]{:S(2)}, u32[]{:S(2)}) collective-permute-start(bf16[144,640]{1,0:T(8,128)(2,1)} %get-tuple-element.31), channel_id=1, source_target_pairs={{0,4},{4,0},{8,12},{12,8},{16,20},{20,16},{24,28},{28,24},{1,5},{5... | collective-permute-start | bytes 552968 | tf_op jit(solution)/shard_map/ppermute | solution.py:488
  8.4 1.5 %collective-permute-start.2 = (bf16[144,640]{1,0:T(8,128)(2,1)}, bf16[144,640]{1,0:T(8,128)(2,1)S(1)}, u32[]{:S(2)}, u32[]{:S(2)}) collective-permute-start(bf16[144,640]{1,0:T(8,128)(2,1)} %get-tuple-element.31), channel_id=1, source_target_pairs={{0,12},{4,8},{8,4},{12,0},{16,28},{20,24},{24,20},{28,16},{1,13},{... | collective-permute-start | bytes 552968 | tf_op jit(solution)/shard_map/ppermute | solution.py:488
  9.9 0.1 collective-permute-start.1
  9.9 0.1 stack.31.sc_ref
  10.0 0.0 copy-done.5
  10.0 0.0 copy-start
  10.0 1.0 %copy-done = f32[2,512,128]{2,1,0:T(8,128)S(1)} copy-done((f32[2,512,128]{2,1,0:T(8,128)S(1)}, f32[2,512,128]{2,1,0:T(8,128)}, u32[]{:S(2)}) %copy-start) | copy-done | bytes 524312
  11.1 0.9 %copy-done.3 = bf16[144,640]{1,0:T(8,128)(2,1)S(1)} copy-done((bf16[144,640]{1,0:T(8,128)(2,1)S(1)}, bf16[144,640]{1,0:T(8,128)(2,1)}, u32[]{:S(2)}) %copy-start.3) | copy-done | bytes 184344
  12.0 1.3 %copy-done.6 = bf16[512,1280]{1,0:T(8,128)(2,1)S(1)} copy-done((bf16[512,1280]{1,0:T(8,128)(2,1)S(1)}, bf16[512,1280]{1,0:T(8,128)(2,1)}, u32[]{:S(2)}) %copy-start.6) | copy-done | bytes 1310744
  13.3 0.9 %copy-done.8 = f32[2,256,128]{2,1,0:T(8,128)S(1)} copy-done((f32[2,256,128]{2,1,0:T(8,128)S(1)}, f32[2,256,128]{2,1,0:T(8,128)}, u32[]{:S(2)}) %copy-start.8) | copy-done | bytes 262168
  14.3 0.9 %copy-done.10 = f32[64,512]{1,0:T(8,128)S(1)} copy-done((f32[64,512]{1,0:T(8,128)S(1)}, f32[64,512]{1,0:T(8,128)}, u32[]{:S(2)}) %copy-start.10) | copy-done | bytes 131096
  15.2 0.8 %copy-done.11 = f32[2,8,640]{2,1,0:T(8,128)S(1)} copy-done((f32[2,8,640]{2,1,0:T(8,128)S(1)}, f32[2,8,640]{2,1,0:T(8,128)}, u32[]{:S(2)}) %copy-start.11) | copy-done | bytes 40984
  15.9 6.1 %shard_map.110 = (f32[512,640]{1,0:T(8,128)S(1)}, f32[512,640]{1,0:T(8,128)S(1)}) custom-call(s32[7]{0:T(128)S(1)} %stack.31.sc_ref, bf16[512,1280]{1,0:T(8,128)(2,1)S(1)} %copy-done.6, bf16[512,1280]{1,0:T(8,128)(2,1)} %gate_ref.3, bf16[512,128]{1,0:T(8,128)(2,1)S(1)} %copy-done.5, bf16[512,128]{1,0:T(8,128)(2,1)S(1)} %copy-done.7, ...), custom_call_target="tpu_custom_call" | custom-call | flops 4000000000 | bytes 1000 | tf_op jit(solution)/shard_map/pallas_call | solution.py:357
  22.0 0.0 copy-start.1
  22.1 0.0 copy-start.9
  22.1 0.0 copy-start.12
  22.1 0.0 collective-permute-done.1.side_ref
  22.1 0.0 collective-permute-done.mate_ref
  22.1 0.0 collective-permute-done.2.cross_ref
  22.1 0.0 copy-done.2
  22.1 0.0 copy-done.4
  22.1 1.0 %shard_map.111 = (bf16[144,640]{1,0:T(8,128)(2,1)S(1)}, f32[128,640]{1,0:T(8,128)S(1)}, f32[128,640]{1,0:T(8,128)S(1)}, f32[128,640]{1,0:T(8,128)S(1)}, f32[8,640]{1,0:T(8,128)S(1)}) custom-call(s32[7]{0:T(128)S(1)} %stack.31.sc_ref, f32[128,640]{1,0:T(8,128)S(1)} %copy-done.2, bf16[144,640]{1,0:T(8,128)(2,1)S(1)} %copy-done.4, ...), custom_call_target="tpu_custom_call" | custom-call | bytes 1000 | tf_op jit(solution)/shard_map/pallas_call | solution.py:232
  23.1 3.0 %collective-permute-start.3 = (bf16[144,640]{1,0:T(8,128)(2,1)S(1)}, bf16[144,640]{1,0:T(8,128)(2,1)S(1)}, u32[]{:S(2)}, u32[]{:S(2)}) collective-permute-start(bf16[144,640]{1,0:T(8,128)(2,1)S(1)} %get-tuple-element.37.after_ref), channel_id=1, source_target_pairs={{0,16},{4,20},{8,24},{12,28},{16,0},{20,4},{24,8},{28,12},{1,17},{... | collective-permute-start | bytes 552968 | tf_op jit(solution)/shard_map/ppermute | solution.py:488
  26.1 0.0 copy-done.9
  26.1 5.9 %shard_map.112 = (f32[512,640]{1,0:T(8,128)S(1)}, f32[512,640]{1,0:T(8,128)S(1)}) custom-call(s32[7]{0:T(128)S(1)} %stack.31.sc_ref, bf16[512,1280]{1,0:T(8,128)(2,1)S(1)} %copy-done.6, bf16[512,1280]{1,0:T(8,128)(2,1)} %gate_ref.3, bf16[512,128]{1,0:T(8,128)(2,1)S(1)} %copy-done.5, bf16[512,128]{1,0:T(8,128)(2,1)S(1)} %copy-done.7, ...), custom_call_target="tpu_custom_call" | custom-call | flops 4000000000 | bytes 1000 | tf_op jit(solution)/shard_map/pallas_call | solution.py:357
  32.1 0.0 copy-start.13
  32.1 1.8 %collective-permute-done.3.got_ref = bf16[144,640]{1,0:T(8,128)(2,1)S(1)} collective-permute-done((bf16[144,640]{1,0:T(8,128)(2,1)S(1)}, bf16[144,640]{1,0:T(8,128)(2,1)S(1)}, u32[]{:S(2)}, u32[]{:S(2)}) %collective-permute-start.3) | collective-permute-done | bytes 184352 | tf_op jit(solution)/shard_map/ppermute | solution.py:488
  33.9 1.1 %shard_map.113 = (bf16[128,640]{1,0:T(8,128)(2,1)S(1)}, bf16[128,640]{1,0:T(8,128)(2,1)S(1)}, f32[8,128]{1,0:T(8,128)S(1)}, f32[8,128]{1,0:T(8,128)}) custom-call(s32[7]{0:T(128)S(1)} %stack.31.sc_ref, bf16[144,640]{1,0:T(8,128)(2,1)S(1)} %collective-permute-done.3.got_ref, f32[128,640]{1,0:T(8,128)S(1)} %get-tuple-element.38.entry_ref, ...), custom_call_target="tpu_custom_call" | custom-call | bytes 1000 | tf_op jit(solution)/shard_map/pallas_call | solution.py:275
  35.0 1.6 %collective-permute-start.4 = (bf16[128,640]{1,0:T(8,128)(2,1)S(1)}, bf16[128,640]{1,0:T(8,128)(2,1)S(1)}, u32[]{:S(2)}, u32[]{:S(2)}) collective-permute-start(bf16[128,640]{1,0:T(8,128)(2,1)S(1)} %get-tuple-element.48), channel_id=1, source_target_pairs={{0,4},{4,0},{8,12},{12,8},{16,20},{20,16},{24,28},{28,24},{1,5},{5... | collective-permute-start | bytes 491528 | tf_op jit(solution)/shard_map/ppermute | solution.py:488
  36.6 1.2 %shard_map.114 = (bf16[512,640]{1,0:T(8,128)(2,1)S(1)}, f32[1,512]{1,0:T(1,128)S(1)}) custom-call(s32[7]{0:T(128)S(1)} %stack.31.sc_ref, f32[8,128]{1,0:T(8,128)S(1)} %get-tuple-element.43.prev_ref, bf16[512,128]{1,0:T(8,128)(2,1)S(1)} %copy-done.5, f32[2,512,128]{2,1,0:T(8,128)S(1)} %copy-done.1, f32[512,640]{1,0:T(8,128)S(1)} %get-tuple-element.36.after_ref.a_ref, ...), custom_call_target="tpu_custom_call" | custom-call | flops 1000000000 | bytes 1000 | tf_op jit(solution)/shard_map/pallas_call | solution.py:401
  37.8 2.5 %collective-permute-done.4.e_ref = bf16[128,640]{1,0:T(8,128)(2,1)S(1)} collective-permute-done((bf16[128,640]{1,0:T(8,128)(2,1)S(1)}, bf16[128,640]{1,0:T(8,128)(2,1)S(1)}, u32[]{:S(2)}, u32[]{:S(2)}) %collective-permute-start.4) | collective-permute-done | bytes 163872 | tf_op jit(solution)/shard_map/ppermute | solution.py:488
  40.3 4.0 %shard_map.115 = (bf16[512,640]{1,0:T(8,128)(2,1)S(1)}, f32[1,512]{1,0:T(1,128)S(1)}, bf16[640,512]{1,0:T(8,128)(2,1)S(1)}) custom-call(s32[7]{0:T(128)S(1)} %stack.31.sc_ref, f32[8,128]{1,0:T(8,128)S(1)} %get-tuple-element.43.prev_ref, bf16[512,128]{1,0:T(8,128)(2,1)S(1)} %copy-done.5, f32[2,512,128]{2,1,0:T(8,128)S(1)} %copy-done.1, ...), custom_call_target="tpu_custom_call" | custom-call | flops 1000000000 | bytes 1000 | tf_op jit(solution)/shard_map/pallas_call | solution.py:438
  44.3 0.1 collective-permute-start.5
  44.4 3.4 %shard_map.116 = f32[640,512]{1,0:T(8,128)S(1)} custom-call(s32[7]{0:T(128)S(1)} %stack.31.sc_ref, bf16[512,640]{1,0:T(8,128)(2,1)S(1)} %get-tuple-element.46.gk_ref, bf16[512,640]{1,0:T(8,128)(2,1)S(1)} %get-tuple-element.49.go_ref, bf16[1280,2560]{1,0:T(8,128)(2,1)} %w_hbm.7, bf16[640,512]{1,0:T(8,128)(2,1)S(1)} %get-tuple-element.50.after_ref), custom_call_target="tpu_custom_call" | custom-call | flops 1000000 | bytes 1000 | tf_op jit(solution)/shard_map/pallas_call | solution.py:464
  47.8 0.0 collective-permute-done.5
  47.8 0.3 add_convert_fusion.after_ref
  48.1 3.4 %shard_map.118 = bf16[640,512]{1,0:T(8,128)(2,1)S(1)} custom-call(s32[7]{0:T(128)S(1)} %stack.31.sc_ref, bf16[512,640]{1,0:T(8,128)(2,1)S(1)} %get-tuple-element.46.gk_ref, bf16[512,640]{1,0:T(8,128)(2,1)S(1)} %get-tuple-element.49.go_ref, bf16[1280,2560]{1,0:T(8,128)(2,1)} %w_hbm.7, bf16[640,512]{1,0:T(8,128)(2,1)S(1)} %add_convert_fusion.after_ref), custom_call_target="tpu_custom_call" | custom-call | flops 1000000 | bytes 1000 | tf_op jit(solution)/shard_map/pallas_call | solution.py:464
  51.5 0.6 collective-permute-start.6
  52.0 1.5 %collective-permute-start.7 = (bf16[640,512]{1,0:T(8,128)(2,1)S(1)}, bf16[640,512]{1,0:T(8,128)(2,1)S(1)}, u32[]{:S(2)}, u32[]{:S(2)}) collective-permute-start(bf16[640,512]{1,0:T(8,128)(2,1)S(1)} %add_convert_fusion.after_ref), channel_id=1, source_target_pairs={{0,2},{1,3},{2,0},{3,1},{4,6},{5,7},{6,4},{7,5},{8,10},{9,11},{10,... | collective-permute-start | bytes 1966088 | tf_op jit(solution)/shard_map/ppermute | solution.py:491
  53.6 0.0 collective-permute-start.8
  53.6 1.2 %collective-permute-done.8 = f32[1,512]{1,0:T(1,128)S(1)} collective-permute-done((f32[1,512]{1,0:T(1,128)S(1)}, f32[1,512]{1,0:T(1,128)S(1)}, u32[]{:S(2)}, u32[]{:S(2)}) %collective-permute-start.8) | collective-permute-done | bytes 2080 | tf_op jit(solution)/shard_map/ppermute | solution.py:491
  54.7 0.6 collective-permute-start.9
  55.3 13.5 %collective-permute-done.9 = f32[1,512]{1,0:T(1,128)S(1)} collective-permute-done((f32[1,512]{1,0:T(1,128)S(1)}, f32[1,512]{1,0:T(1,128)S(1)}, u32[]{:S(2)}, u32[]{:S(2)}) %collective-permute-start.9) | collective-permute-done | bytes 2080 | tf_op jit(solution)/shard_map/ppermute | solution.py:491
  68.8 3.4 %shard_map.117 = f32[640,512]{1,0:T(8,128)S(1)} custom-call(s32[7]{0:T(128)S(1)} %stack.31.sc_ref, bf16[512,640]{1,0:T(8,128)(2,1)S(1)} %get-tuple-element.46.gk_ref, bf16[512,640]{1,0:T(8,128)(2,1)S(1)} %get-tuple-element.49.go_ref, bf16[1280,2560]{1,0:T(8,128)(2,1)} %w_hbm.7, bf16[640,512]{1,0:T(8,128)(2,1)S(1)} %add_convert_fusion.after_ref), custom_call_target="tpu_custom_call" | custom-call | flops 1000000 | bytes 1000 | tf_op jit(solution)/shard_map/pallas_call | solution.py:464
  72.2 0.0 collective-permute-done.6
  72.2 0.0 collective-permute-done.7
  72.2 1.1 %multiply_convert_fusion = bf16[640,512]{1,0:T(8,128)(2,1)} fusion(bf16[640,512]{1,0:T(8,128)(2,1)S(1)} %collective-permute-done.7, f32[640,512]{1,0:T(8,128)S(1)} %shard_map.117, bf16[640,512]{1,0:T(8,128)(2,1)S(1)} %collective-permute-done.6, f32[512]{0:T(512)S(1)} %bitcast.12), kind=kLoop, calls=%fused_computation | loop fusion | flops 1966080 | bytes 3278848 | tf_op jit(solution)/shard_map/convert_element_type | solution.py:528
  (17 shorter events, 0.0 us)
Async XLA Ops:
  0.0 10.0 %copy-start.5 = (bf16[512,128]{1,0:T(8,128)(2,1)S(1)}, bf16[512,128]{1,0:T(8,128)(2,1)}, u32[]{:S(2)}) copy-start(bf16[512,128]{1,0:T(8,128)(2,1)} %rd_ref.7) | copy-start | bytes 393220
  0.0 10.0 %copy-start.7 = (bf16[512,128]{1,0:T(8,128)(2,1)S(1)}, bf16[512,128]{1,0:T(8,128)(2,1)}, u32[]{:S(2)}) copy-start(bf16[512,128]{1,0:T(8,128)(2,1)} %wr_ref.5) | copy-start | bytes 393220
  5.3 16.8 %collective-permute-start = (bf16[144,640]{1,0:T(8,128)(2,1)}, bf16[144,640]{1,0:T(8,128)(2,1)S(1)}, u32[]{:S(2)}, u32[]{:S(2)}) collective-permute-start(bf16[144,640]{1,0:T(8,128)(2,1)} %get-tuple-element.31), channel_id=1, source_target_pairs={{0,4},{4,0},{8,12},{12,8},{16,20},{20,16},{24,28},{28,24},{1,5},{5... | collective-permute-start | bytes 552968 | tf_op jit(solution)/shard_map/ppermute | solution.py:488
  8.4 13.7 %collective-permute-start.2 = (bf16[144,640]{1,0:T(8,128)(2,1)}, bf16[144,640]{1,0:T(8,128)(2,1)S(1)}, u32[]{:S(2)}, u32[]{:S(2)}) collective-permute-start(bf16[144,640]{1,0:T(8,128)(2,1)} %get-tuple-element.31), channel_id=1, source_target_pairs={{0,12},{4,8},{8,4},{12,0},{16,28},{20,24},{24,20},{28,16},{1,13},{... | collective-permute-start | bytes 552968 | tf_op jit(solution)/shard_map/ppermute | solution.py:488
  9.9 12.2 %collective-permute-start.1 = (bf16[144,640]{1,0:T(8,128)(2,1)}, bf16[144,640]{1,0:T(8,128)(2,1)S(1)}, u32[]{:S(2)}, u32[]{:S(2)}) collective-permute-start(bf16[144,640]{1,0:T(8,128)(2,1)} %get-tuple-element.30.after_ref.keep_ref), channel_id=1, source_target_pairs={{0,8},{4,12},{8,0},{12,4},{16,24},{20,28},{24,16},{28,20},{1,9},{5... | collective-permute-start | bytes 552968 | tf_op jit(solution)/shard_map/ppermute | solution.py:488
  10.0 1.0 %copy-start = (f32[2,512,128]{2,1,0:T(8,128)S(1)}, f32[2,512,128]{2,1,0:T(8,128)}, u32[]{:S(2)}) copy-start(f32[2,512,128]{2,1,0:T(8,128)} %get-tuple-element.32.ccol_ref.seg_ref) | copy-start | bytes 1572868
  11.1 0.9 %copy-start.3 = (bf16[144,640]{1,0:T(8,128)(2,1)S(1)}, bf16[144,640]{1,0:T(8,128)(2,1)}, u32[]{:S(2)}) copy-start(bf16[144,640]{1,0:T(8,128)(2,1)} %get-tuple-element.30.after_ref.keep_ref) | copy-start | bytes 552964
  12.0 1.3 %copy-start.6 = (bf16[512,1280]{1,0:T(8,128)(2,1)S(1)}, bf16[512,1280]{1,0:T(8,128)(2,1)}, u32[]{:S(2)}) copy-start(bf16[512,1280]{1,0:T(8,128)(2,1)} %x_ref.3) | copy-start | bytes 3932164
  13.3 0.9 %copy-start.8 = (f32[2,256,128]{2,1,0:T(8,128)S(1)}, f32[2,256,128]{2,1,0:T(8,128)}, u32[]{:S(2)}) copy-start(f32[2,256,128]{2,1,0:T(8,128)} %get-tuple-element.34.tail0_ref) | copy-start | bytes 786436
  14.3 0.9 %copy-start.10 = (f32[64,512]{1,0:T(8,128)S(1)}, f32[64,512]{1,0:T(8,128)}, u32[]{:S(2)}) copy-start(f32[64,512]{1,0:T(8,128)} %get-tuple-element.33.arow_ref) | copy-start | bytes 393220
  15.2 0.8 %copy-start.11 = (f32[2,8,640]{2,1,0:T(8,128)S(1)}, f32[2,8,640]{2,1,0:T(8,128)}, u32[]{:S(2)}) copy-start(f32[2,8,640]{2,1,0:T(8,128)} %get-tuple-element.35.skip_ref) | copy-start | bytes 122884
  15.9 6.2 %copy-start.2 = (f32[128,640]{1,0:T(8,128)S(1)}, f32[128,640]{1,0:T(8,128)}, u32[]{:S(2)}) copy-start(f32[128,640]{1,0:T(8,128)} %get-tuple-element.29.own_ref) | copy-start | bytes 983044
  15.9 6.2 %copy-start.4 = (bf16[144,640]{1,0:T(8,128)(2,1)S(1)}, bf16[144,640]{1,0:T(8,128)(2,1)}, u32[]{:S(2)}) copy-start(bf16[144,640]{1,0:T(8,128)(2,1)} %get-tuple-element.30.after_ref.keep_ref) | copy-start | bytes 552964
  22.0 4.1 %copy-start.1 = (f32[2,512,128]{2,1,0:T(8,128)S(1)}, f32[2,512,128]{2,1,0:T(8,128)}, u32[]{:S(2)}) copy-start(f32[2,512,128]{2,1,0:T(8,128)} %get-tuple-element.32.ccol_ref.seg_ref) | copy-start | bytes 1572868
  22.1 4.1 %copy-start.9 = (f32[2,256,128]{2,1,0:T(8,128)S(1)}, f32[2,256,128]{2,1,0:T(8,128)}, u32[]{:S(2)}) copy-start(f32[2,256,128]{2,1,0:T(8,128)} %get-tuple-element.34.tail0_ref) | copy-start | bytes 786436
  22.1 4.1 %copy-start.12 = (f32[2,8,640]{2,1,0:T(8,128)S(1)}, f32[2,8,640]{2,1,0:T(8,128)}, u32[]{:S(2)}) copy-start(f32[2,8,640]{2,1,0:T(8,128)} %get-tuple-element.35.skip_ref) | copy-start | bytes 122884
  23.1 10.8 %collective-permute-start.3 = (bf16[144,640]{1,0:T(8,128)(2,1)S(1)}, bf16[144,640]{1,0:T(8,128)(2,1)S(1)}, u32[]{:S(2)}, u32[]{:S(2)}) collective-permute-start(bf16[144,640]{1,0:T(8,128)(2,1)S(1)} %get-tuple-element.37.after_ref), channel_id=1, source_target_pairs={{0,16},{4,20},{8,24},{12,28},{16,0},{20,4},{24,8},{28,12},{1,17},{... | collective-permute-start | bytes 552968 | tf_op jit(solution)/shard_map/ppermute | solution.py:488
  32.1 4.5 %copy-start.13 = (f32[1280]{0:T(1024)S(1)}, f32[1280]{0:T(1024)}, u32[]{:S(2)}) copy-start(f32[1280]{0:T(1024)} %param.20) | copy-start | bytes 15364
  35.0 5.3 %collective-permute-start.4 = (bf16[128,640]{1,0:T(8,128)(2,1)S(1)}, bf16[128,640]{1,0:T(8,128)(2,1)S(1)}, u32[]{:S(2)}, u32[]{:S(2)}) collective-permute-start(bf16[128,640]{1,0:T(8,128)(2,1)S(1)} %get-tuple-element.48), channel_id=1, source_target_pairs={{0,4},{4,0},{8,12},{12,8},{16,20},{20,16},{24,28},{28,24},{1,5},{5... | collective-permute-start | bytes 491528 | tf_op jit(solution)/shard_map/ppermute | solution.py:488
  44.3 3.5 %collective-permute-start.5 = (bf16[640,512]{1,0:T(8,128)(2,1)S(1)}, bf16[640,512]{1,0:T(8,128)(2,1)S(1)}, u32[]{:S(2)}, u32[]{:S(2)}) collective-permute-start(bf16[640,512]{1,0:T(8,128)(2,1)S(1)} %get-tuple-element.50.after_ref), channel_id=1, source_target_pairs={{0,1},{1,0},{2,3},{3,2},{4,5},{5,4},{6,7},{7,6},{8,9},{9,8},{10,11... | collective-permute-start | bytes 1966088 | tf_op jit(solution)/shard_map/ppermute | solution.py:491
  51.5 20.7 %collective-permute-start.6 = (bf16[640,512]{1,0:T(8,128)(2,1)S(1)}, bf16[640,512]{1,0:T(8,128)(2,1)S(1)}, u32[]{:S(2)}, u32[]{:S(2)}) collective-permute-start(bf16[640,512]{1,0:T(8,128)(2,1)S(1)} %shard_map.118), channel_id=1, source_target_pairs={{0,1},{1,0},{2,3},{3,2},{4,5},{5,4},{6,7},{7,6},{8,9},{9,8},{10,11... | collective-permute-start | bytes 1966088 | tf_op jit(solution)/shard_map/ppermute | solution.py:491
  52.0 20.2 %collective-permute-start.7 = (bf16[640,512]{1,0:T(8,128)(2,1)S(1)}, bf16[640,512]{1,0:T(8,128)(2,1)S(1)}, u32[]{:S(2)}, u32[]{:S(2)}) collective-permute-start(bf16[640,512]{1,0:T(8,128)(2,1)S(1)} %add_convert_fusion.after_ref), channel_id=1, source_target_pairs={{0,2},{1,3},{2,0},{3,1},{4,6},{5,7},{6,4},{7,5},{8,10},{9,11},{10,... | collective-permute-start | bytes 1966088 | tf_op jit(solution)/shard_map/ppermute | solution.py:491
  53.6 1.2 %collective-permute-start.8 = (f32[1,512]{1,0:T(1,128)S(1)}, f32[1,512]{1,0:T(1,128)S(1)}, u32[]{:S(2)}, u32[]{:S(2)}) collective-permute-start(f32[1,512]{1,0:T(1,128)S(1)} %add.27), channel_id=1, source_target_pairs={{0,1},{1,0},{2,3},{3,2},{4,5},{5,4},{6,7},{7,6},{8,9},{9,8},{10,11... | collective-permute-start | bytes 6152 | tf_op jit(solution)/shard_map/ppermute | solution.py:491
  54.7 14.1 %collective-permute-start.9 = (f32[1,512]{1,0:T(1,128)S(1)}, f32[1,512]{1,0:T(1,128)S(1)}, u32[]{:S(2)}, u32[]{:S(2)}) collective-permute-start(f32[1,512]{1,0:T(1,128)S(1)} %add.28), channel_id=1, source_target_pairs={{0,2},{1,3},{2,0},{3,1},{4,6},{5,7},{6,4},{7,5},{8,10},{9,11},{10,... | collective-permute-start | bytes 6152 | tf_op jit(solution)/shard_map/ppermute | solution.py:491

commit v4 on v0

v4 whole, which is shorter than its diff:
```python
import functools

import jax
import jax.numpy as jnp
from jax import lax
from jax.experimental import pallas as pl
from jax.experimental.pallas import tpu as pltpu
from jax.sharding import PartitionSpec as P

GROUP = 256
LANES = 128
EPS = 1e-05
LOG2E = 1.4426950408889634
SEG_LANE = 24
EXTRA = 16
VMEM = 16 * 1024 * 1024
VMEM_ALL = 56 * 1024 * 1024
F32 = jnp.float32
BF16 = jnp.bfloat16


def dot(a, b, dims=((1,), (0,))):
    return lax.dot_general(a, b, (dims, ((), ())), preferred_element_type=F32)


def lane_iota(rows):
    return lax.broadcasted_iota(jnp.int32, (rows, LANES), 1)


def spread(cols, first, width):
    rows = cols.shape[0]
    per = LANES // width
    lane = lane_iota(rows)
    out = jnp.broadcast_to(cols[:, first : first + 1], (rows, LANES))
    for k in range(1, per):
        nxt = jnp.broadcast_to(cols[:, first + k : first + k + 1], (rows, LANES))
        out = jnp.where(lane < k * width, out, nxt)
    return out


def call(body, sc, args, out_shape, scratch=(), cost=0, after=None):
    vm = pl.BlockSpec(memory_space=pltpu.VMEM)
    specs = [pl.BlockSpec(memory_space=pltpu.SMEM)] + [vm] * len(args)
    operands = [sc, *args]
    kernel = body
    if after is not None:
        specs.append(pl.BlockSpec(memory_space=pl.ANY))
        operands.append(after)
        at = len(operands) - 1

        def kernel(*refs):
            body(*refs[:at], *refs[at + 1 :])

    return pl.pallas_call(
        kernel,
        in_specs=specs,
        out_specs=jax.tree.map(lambda _: vm, out_shape),
        out_shape=out_shape,
        scratch_shapes=list(scratch),
        compiler_params=pltpu.CompilerParams(vmem_limit_bytes=VMEM),
        cost_estimate=pl.CostEstimate(flops=cost, bytes_accessed=1000, transcendentals=0),
    )(*operands)


def shaped(*shapes):
    return [jax.ShapeDtypeStruct(shape, dtype) for shape, dtype in shapes]


def pack(out_ref, total):
    state, through, last = total
    size, lanes = state.shape
    high = through.astype(BF16).astype(F32)
    row = lax.broadcasted_iota(jnp.int32, (EXTRA, lanes), 0)
    rows = jnp.where(row == 0, high, jnp.where(row == 1, through - high, last))
    out_ref[0:size] = state.astype(BF16)
    out_ref[size : size + EXTRA] = rows.astype(BF16)


def unpack(ref):
    size = ref.shape[0] - EXTRA
    rows = ref[size : size + EXTRA].astype(F32)
    return ref[0:size].astype(F32), rows[0:1] + rows[1:2], rows[2:3, 0:1]


def merged(swapped, one, two):
    later = jnp.where(swapped, one[1], two[1])
    link = later * (one[2] == two[2]).astype(F32)
    state = jnp.where(swapped, 1.0, link) * one[0] + jnp.where(swapped, link, 1.0) * two[0]
    return state, one[1] * two[1], jnp.where(swapped, one[2], two[2])


def ordered(swapped, one, two):
    firsts = tuple(jnp.where(swapped, t, o) for o, t in zip(one, two))
    seconds = tuple(jnp.where(swapped, o, t) for o, t in zip(one, two))
    return firsts, seconds


def stash_rows(state):
    return slice(0, state), slice(state + 8, state + 40), slice(state + 40, state + 72)


def put_rows(rows_ref, rows):
    lanes = rows_ref.shape[1]
    for at, row in enumerate(rows):
        rows_ref[at : at + 1] = jnp.broadcast_to(row, (1, lanes))


def prepare(heads, width, raw, seg, decay_log, bias, x, write):
    toks, state = write.shape
    half_w = x.shape[1] // 2
    half_h = heads // 2
    blocks = toks // GROUP
    arrays = (raw, seg, decay_log, bias, write, x)

    def body(*refs):
        hbm, (other_ref, keep_ref, stash_ref) = refs[: len(arrays)], refs[len(arrays) : -10]
        raw_ref, seg_ref, dl_ref, sb_ref, wr_ref, x_ref, rows, pad, cols, sems = refs[-10:]
        copies = [
            pltpu.make_async_copy(src, dst, sems.at[k])
            for k, (src, dst) in enumerate(zip(hbm, (raw_ref, seg_ref, dl_ref, sb_ref, wr_ref, x_ref)))
        ]
        for copy in copies:
            copy.start()
        rows[...] = jnp.zeros_like(rows)
        pad[...] = jnp.zeros_like(pad)
        tri = (
            lax.broadcasted_iota(jnp.int32, (GROUP, GROUP), 0)
            <= lax.broadcasted_iota(jnp.int32, (GROUP, GROUP), 1)
        ).astype(BF16)
        for copy in copies[:4]:
            copy.wait()
        rows[0:1, 0:heads] = dl_ref[...]
        rows[1:2, 0:heads] = sb_ref[...]
        pad[0:heads] = raw_ref[...].astype(F32)
        params = jnp.transpose(rows[...])[0:32]
        z = pad[0:32] + params[:, 1:2]
        step = jnp.maximum(z, 0.0) + jnp.log1p(jnp.exp(-jnp.abs(z)))
        rate = -jnp.exp(params[:, 0:1]) * step
        cum, full = [], []
        base = jnp.zeros((32, 1), F32)
        for b in range(blocks):
            r = rate[:, b * GROUP : (b + 1) * GROUP]
            r1 = r.astype(BF16)
            d1 = r - r1.astype(F32)
            r2 = d1.astype(BF16)
            r3 = (d1 - r2.astype(F32)).astype(BF16)
            c = dot(r1, tri) + (dot(r2, tri) + dot(r3, tri))
            cum.append(c)
            full.append(c + base)
            base = base + c[:, GROUP - 1 : GROUP]
        seg_row = seg_ref[...].astype(F32)
        last = seg_row[:, toks - 1 : toks]
        tail = jnp.exp(base - jnp.concatenate(full, axis=1)) * step
        pad[0:32] = jnp.where(seg_row == last, tail, 0.0)
        own_rows, cum_rows, step_rows = stash_rows(state)
        stash_ref[cum_rows, 0:toks] = jnp.concatenate(cum, axis=1)
        stash_ref[cum_rows.start + SEG_LANE : cum_rows.start + SEG_LANE + 1, 0:toks] = seg_row
        stash_ref[step_rows, 0:toks] = step
        cols[...] = jnp.transpose(pad[...])
        rows[...] = jnp.zeros_like(rows)
        rows[0:32] = jnp.broadcast_to(jnp.exp(base), (32, LANES))
        keep = jnp.transpose(rows[...])[0:1]
        per = LANES // width
        odd = lax.rem(lax.axis_index("seq"), 2) == 1
        for copy in copies[4:]:
            copy.wait()
        halves = []
        for j in range(2):
            parts, through = [], []
            for i in range(half_w // LANES):
                at = j * half_h + i * per
                xt = x_ref[:, j * half_w + i * LANES : j * half_w + (i + 1) * LANES].astype(F32)
                parts.append((xt * spread(cols[...], at, width)).astype(BF16))
                through.append(spread(keep, at, width))
            own = dot(wr_ref[...], jnp.concatenate(parts, axis=1), ((0,), (0,)))
            halves.append((own, jnp.concatenate(through, axis=1), last))
        mine, other = ordered(odd, *halves)
        stash_ref[own_rows] = mine[0]
        put_rows(stash_ref.at[state : state + 8], mine[1:])
        pack(keep_ref, mine)
        pack(other_ref, other)

    vm = pl.BlockSpec(memory_space=pltpu.VMEM)
    out_shape = shaped(
        ((state + EXTRA, half_w), BF16), ((state + EXTRA, half_w), BF16),
        ((stash_rows(state)[2].stop, max(half_w, toks)), F32),
    )
    return pl.pallas_call(
        body,
        in_specs=[pl.BlockSpec(memory_space=pltpu.HBM)] * len(arrays),
        out_specs=[vm] * len(out_shape),
        out_shape=out_shape,
        scratch_shapes=[
            *[pltpu.VMEM(a.shape, a.dtype) for a in arrays],
            pltpu.VMEM((LANES, LANES), F32), pltpu.VMEM((LANES, toks), F32), pltpu.VMEM((toks, LANES), F32),
            pltpu.SemaphoreType.DMA((len(arrays),)),
        ],
        compiler_params=pltpu.CompilerParams(vmem_limit_bytes=VMEM_ALL),
        cost_estimate=pl.CostEstimate(flops=4_000_000_000, bytes_accessed=1000, transcendentals=0),
    )(*arrays)


def gather_level(upper, entry, other):
    state, through, last_id = entry
    link = through * ((last_id < 0) | (other[2] == last_id)).astype(F32)
    state = state + jnp.where(upper, link, 0.0) * other[0]
    last_id = jnp.where(upper & (last_id < 0), other[2], last_id)
    return state, through * jnp.where(upper, other[1], 1.0), last_id


def pair_step(sc, stash, mate, side, cross, after):
    size, lanes = mate.shape[0] - EXTRA, mate.shape[1]

    def body(
        sc_ref, stash_ref, mate_ref, side_ref, cross_ref, send_ref, entry_ref, first_ref, total_ref, rows_ref
    ):
        odd = sc_ref[0] == 1
        upper = (sc_ref[6] & 2) != 0
        mine = (
            stash_ref[0:size, 0:lanes], stash_ref[size : size + 1, 0:lanes], stash_ref[size + 1 : size + 2, 0:1]
        )
        mate = unpack(mate_ref)
        total = merged(odd, mine, mate)
        other = merged(odd, unpack(side_ref), unpack(cross_ref))
        nothing = (0.0, jnp.ones_like(total[1]), jnp.full((1, 1), -1.0, F32))
        entry = gather_level(upper, nothing, other)
        total = merged(upper, total, other)
        pack(send_ref, total)
        entry_ref[...], total_ref[...] = entry[0], total[0]
        first_ref[...] = jnp.where(odd, mate[0], mine[0])
        rows = tuple(jnp.where(odd, m, o) for o, m in zip(mine[1:], mate[1:]))
        put_rows(rows_ref, entry[1:] + rows + total[1:])

    state = ((size, lanes), F32)
    return call(
        body, sc, (stash, mate, side, cross),
        shaped((mate.shape, BF16), state, state, state, ((8, lanes), F32)), after=after,
    )


def level_step(bit, final, sc, got, entry, first, total, rows, after):
    size, lanes = entry.shape

    def body(
        sc_ref, got_ref, entry_ref, first_ref, total_ref, rows_ref,
        send_ref, one_ref, two_ref, three_ref,
    ):
        upper = (sc_ref[6] & bit) != 0
        other = unpack(got_ref)
        old = (entry_ref[...], rows_ref[0:1], rows_ref[1:2, 0:1])
        new = gather_level(upper, old, other)
        if final:
            even = sc_ref[0] == 0
            last_first = rows_ref[3:4, 0:1]
            link = rows_ref[2:3] * (last_first == new[2]).astype(F32)
            reached = first_ref[...] + link * new[0]
            send_ref[...] = jnp.where(even, reached, new[0]).astype(BF16)
            one_ref[...] = jnp.where(even, new[0], reached).astype(BF16)
            two_ref[...] = jnp.broadcast_to(jnp.where(even, new[2], last_first), (8, LANES))
            three_ref[...] = jnp.zeros_like(three_ref)
        else:
            held = (total_ref[...], rows_ref[4:5], rows_ref[5:6, 0:1])
            held = merged(upper, held, other)
            pack(send_ref, held)
            one_ref[...] = new[0]
            two_ref[...] = held[0]
            put_rows(three_ref, new[1:] + (rows_ref[2:3], rows_ref[3:4]) + held[1:])

    if final:
        out = shaped(((size, lanes), BF16), ((size, lanes), BF16), ((8, LANES), F32), ((8, LANES), F32))
    else:
        out = shaped((got.shape, BF16), ((size, lanes), F32), ((size, lanes), F32), ((8, lanes), F32))
    return call(body, sc, (got, entry, first, total, rows), out, after=after)


def local_part(heads, width, sc, x, gate, read, write, stash, skip, after):
    toks = write.shape[0]
    feats = x.shape[1]
    per = LANES // width
    blocks = toks // GROUP
    strip = 64

    def body(
        sc_ref, x_ref, gate_ref, rd_ref, wr_ref, stash_ref, skip_ref,
        a_ref, b_ref, log_cum, scores, mix, pad, tails, rows_ref,
    ):
        _, cum_rows, step_rows = stash_rows(write.shape[1])
        cum_ref = stash_ref.at[cum_rows, 0:toks]
        step_ref = stash_ref.at[step_rows, 0:toks]
        lane = lane_iota(GROUP)
        mix[...] = jnp.zeros_like(mix)
        pad[...] = jnp.zeros_like(pad)
        rows_ref[...] = jnp.zeros_like(rows_ref)
        rows_ref[0:1, 0:heads] = skip_ref[...]
        skips = rows_ref[0:1]
        seg_row = cum_ref[SEG_LANE : SEG_LANE + 1]
        log_row = cum_ref[...] * LOG2E - jnp.log(step_ref[...]) * LOG2E
        pad[0:32] = cum_ref[...] * LOG2E
        pad[SEG_LANE : SEG_LANE + 1] = seg_row
        log_cum[...] = jnp.transpose(pad[...])
        seg_col = log_cum[:, SEG_LANE : SEG_LANE + 1]
        tail0 = jnp.exp(cum_ref[:, GROUP - 1 : GROUP] - cum_ref[:, 0:GROUP]) * step_ref[:, 0:GROUP]
        same = seg_row[:, 0:GROUP] == seg_row[:, GROUP - 1 : GROUP]
        pad[0:32, 0:GROUP] = jnp.where(same, tail0, 0.0)
        tails[...] = jnp.transpose(pad[:, 0:GROUP])
        masked = []
        for b in range(blocks):
            rows = slice(b * GROUP, (b + 1) * GROUP)
            s = dot(rd_ref[rows], wr_ref[rows], ((1,), (1,)))
            causal = lax.broadcasted_iota(jnp.int32, (GROUP, GROUP), 0) >= lax.broadcasted_iota(
                jnp.int32, (GROUP, GROUP), 1
            )
            scores[b] = jnp.where(causal & (seg_col[rows] == seg_row[:, rows]), s, 0.0)
            linked = seg_col[rows] == seg_col[b * GROUP - 1 : b * GROUP] if b else None
            masked.append(jnp.where(linked, rd_ref[rows].astype(F32), 0.0).astype(BF16) if b else None)
        for i in range(feats // LANES):
            tile = slice(i * LANES, (i + 1) * LANES)
            gains = spread(skips, i * per, width)
            carry = None
            start = jnp.ones((1, LANES), F32)
            for b in range(blocks):
                rows = slice(b * GROUP, (b + 1) * GROUP)
                slot = (i * blocks + b) % mix.shape[0]
                xb = x_ref[rows, tile]
                logs = []
                for k in range(per):
                    head = i * per + k
                    cb = jnp.broadcast_to(log_cum[rows, head : head + 1], (GROUP, LANES))
                    logs.append(cb)
                    ar = log_row[head : head + 1, rows]
                    for low in range(0, GROUP, strip):
                        for left in range(0, min(low + strip, GROUP), LANES):
                            gap = cb[low : low + strip] - ar[:, left : left + LANES]
                            part = jnp.exp2(jnp.minimum(gap, 60.0))
                            part = part * scores[b, low : low + strip, left : left + LANES]
                            at = k * GROUP + low
                            mix[slot, at : at + strip, left : left + LANES] = part.astype(BF16)
                both = dot(mix[slot], xb)
                inner, dec_log = both[0:GROUP], logs[0]
                for k in range(1, per):
                    inner = jnp.where(lane < k * width, inner, both[k * GROUP : (k + 1) * GROUP])
                    dec_log = jnp.where(lane < k * width, dec_log, logs[k])
                dec = jnp.exp2(dec_log)
                xf = xb.astype(F32)
                y = inner + gains * xf
                if b == 1:
                    y = y + (dot(masked[b], carry[0]) + dot(masked[b], carry[1])) * dec
                else:
                    xs = (xf * spread(tails[...], i * per, width)).astype(BF16)
                    s0 = dot(wr_ref[rows], xs, ((0,), (0,)))
                    s0h = s0.astype(BF16)
                    carry = (s0h, (s0 - s0h.astype(F32)).astype(BF16))
                v = gate_ref[rows, tile].astype(F32)
                sg = v / (1.0 + jnp.exp(-v))
                a_ref[rows, tile] = sg * y
                b_ref[rows, tile] = sg * (dec * start)
                start = start * dec[GROUP - 1 : GROUP]

    return call(
        body, sc, (x, gate, read, write, stash, skip),
        shaped(((toks, feats), F32), ((toks, feats), F32), ((toks, LANES), F32)),
        [
            pltpu.VMEM((blocks, GROUP, GROUP), F32), pltpu.VMEM((4, per * GROUP, GROUP), BF16),
            pltpu.VMEM((LANES, toks), F32), pltpu.VMEM((GROUP, LANES), F32), pltpu.VMEM((8, LANES), F32),
        ],
        cost=8_000_000_000, after=after,
    )


def gated_tile(which, sc_ref, prev_ref, rd_ref, cum_ref, a_ref, b_ref, e_ref, gain_ref):
    half_w = e_ref.shape[1]
    here = pl.ds(pl.multiple_of(sc_ref[which] * half_w, LANES), half_w)
    linked = cum_ref[:, SEG_LANE : SEG_LANE + 1] == prev_ref[0:1, 0:1]
    rm = jnp.where(linked, rd_ref[...].astype(F32), 0.0).astype(BF16)
    gated = a_ref[:, here] + b_ref[:, here] * dot(rm, e_ref[...])
    sq = gated * gated
    part = sq[:, 0:LANES]
    for i in range(1, half_w // LANES):
        part = part + sq[:, i * LANES : (i + 1) * LANES]
    squares = jnp.sum(jnp.transpose(part), axis=0, keepdims=True)
    return (gated * gain_ref[:, here]).astype(BF16), squares


def projected(which, quarter, sc_ref, w_ref, g):
    half_w = g.shape[1]
    cols = w_ref.shape[1] // 4
    rows = pl.ds(pl.multiple_of(sc_ref[which] * half_w, LANES), half_w)
    columns = pl.ds(pl.multiple_of(sc_ref[quarter] * cols, LANES), cols)
    return dot(w_ref[rows, columns], g, ((0,), (1,)))


def put_squares(out_ref, size, squares):
    high = squares.astype(BF16).astype(F32)
    middle = (squares - high).astype(BF16).astype(F32)
    row = lax.broadcasted_iota(jnp.int32, (EXTRA, squares.shape[1]), 0)
    rows = jnp.where(row == 0, high, jnp.where(row == 1, middle, squares - high - middle))
    out_ref[size : size + EXTRA] = rows.astype(BF16)


def get_squares(ref):
    rows = ref[ref.shape[0] - EXTRA :].astype(F32)
    return rows[0:1] + (rows[1:2] + rows[2:3])


def gated_first(sc, prev, read, cum, a, b, e, gain, weight):
    toks = a.shape[0]
    half_w = e.shape[1]
    feats = weight.shape[1]

    def body(
        sc_ref, prev_ref, rd_ref, cum_ref, a_ref, b_ref, e_ref, gain_ref, w_ref, g_ref, s_ref, y_ref
    ):
        g, s_ref[...] = gated_tile(0, sc_ref, prev_ref, rd_ref, cum_ref, a_ref, b_ref, e_ref, gain_ref)
        g_ref[...] = g
        for quarter in range(4):
            y_ref[quarter] = projected(0, 2 + quarter, sc_ref, w_ref, g)

    return call(
        body, sc, (prev, read, cum, a, b, e, gain, weight),
        shaped(((toks, half_w), BF16), ((1, toks), F32), ((4, feats // 4, toks), F32)),
        cost=2_000_000_000,
    )


def gated_second(sc, prev, read, cum, a, b, e, gain, partial, s_first, weight):
    toks = a.shape[0]
    half_w = e.shape[1]
    cols = weight.shape[1] // 4

    def body(
        sc_ref, prev_ref, rd_ref, cum_ref, a_ref, b_ref, e_ref, gain_ref, p_ref, sf_ref, w_ref, g_ref, y_ref
    ):
        g, squares = gated_tile(1, sc_ref, prev_ref, rd_ref, cum_ref, a_ref, b_ref, e_ref, gain_ref)
        g_ref[...] = g
        y_ref[0:cols] = (p_ref[0] + projected(1, 2, sc_ref, w_ref, g)).astype(BF16)
        put_squares(y_ref, cols, sf_ref[...] + squares)

    return call(
        body, sc, (prev, read, cum, a, b, e, gain, partial, s_first, weight),
        shaped(((toks, half_w), BF16), ((cols + EXTRA, toks), BF16)), cost=1_000_000_000,
    )


def project_rest(quarter, dtype, cost, sc, g, partial, weight, after, add=None):
    toks = g.shape[0]
    block = (weight.shape[1] // 4, toks)

    def body(sc_ref, g_ref, p_ref, w_ref, *refs):
        y = p_ref[quarter] + projected(1, 2 + quarter, sc_ref, w_ref, g_ref[...])
        if add is not None:
            y = y + refs[0][...].astype(F32)
        refs[-1][...] = y.astype(dtype)

    more = () if add is None else (add,)
    return call(
        body, sc, (g, partial, weight, *more), jax.ShapeDtypeStruct(block, dtype), cost=cost, after=after
    )


def add_far(sc, y_far, to_near, got_near):
    size = y_far.shape[0]

    def body(sc_ref, y_ref, mine_ref, got_ref, out_ref):
        out_ref[0:size] = (y_ref[...] + got_ref[0:size].astype(F32)).astype(BF16)
        put_squares(out_ref, size, get_squares(mine_ref) + get_squares(got_ref))

    return call(body, sc, (y_far, to_near, got_near), jax.ShapeDtypeStruct(got_near.shape, BF16))


def finish(features, sc, y_own, to_far, got_far):
    size = y_own.shape[0]

    def body(sc_ref, own_ref, mine_ref, far_ref, out_ref):
        inv = lax.rsqrt((get_squares(mine_ref) + get_squares(far_ref)) / features + EPS)
        out_ref[...] = ((own_ref[...] + far_ref[0:size].astype(F32)) * inv).astype(BF16)

    return call(body, sc, (y_own, to_far, got_far), jax.ShapeDtypeStruct(y_own.shape, BF16))


def on_device(
    n_seq, n_tp, head_input, gate_input, write_vecs, read_vecs, step_raw, segment_ids,
    decay_log, step_bias, skip_gain, norm_gain, out_weight,
):
    heads = decay_log.shape[0]
    toks, feats = head_input.shape
    width = feats // heads
    place = lax.axis_index("seq")
    rank = lax.axis_index("tp")
    odd = lax.rem(place, 2)
    near, far = rank ^ 1, rank ^ 2
    sc = jnp.stack([odd, 1 - odd, far ^ 1, far, near, rank, place]).astype(jnp.int32)

    def swap(a, bit):
        return lax.ppermute(a, "seq", [(i, i ^ bit) for i in range(n_seq)])

    def across(a, bit):
        return lax.ppermute(a, "tp", [(i, i ^ bit) for i in range(n_tp)])

    send_other, send_keep, stash = prepare(
        heads, width, step_raw, segment_ids.reshape(1, toks), decay_log.reshape(1, heads),
        step_bias.reshape(1, heads), head_input, write_vecs,
    )
    side = swap(send_keep, 2)
    cross = swap(send_other, 3)
    mate = swap(send_other, 1)
    a, b, log_cum = local_part(
        heads, width, sc, head_input, gate_input, read_vecs, write_vecs, stash,
        skip_gain.reshape(1, heads), None,
    )
    sent, entry, first, total, rows = pair_step(sc, stash, mate, side, cross, a)
    bit = 4
    while 2 * bit < n_seq:
        sent, entry, total, rows = level_step(bit, False, sc, swap(sent, bit), entry, first, total, rows, None)
        bit *= 2
    sent, e_keep, prev, _ = level_step(bit, True, sc, swap(sent, bit), entry, first, total, rows, None)
    e_other = swap(sent, 1)
    gain = norm_gain.reshape(1, feats)
    shared = (prev, read_vecs, log_cum, a, b)
    g_keep, s_keep, partial = gated_first(sc, *shared, e_keep, gain, out_weight)
    g_other, to_near = gated_second(sc, *shared, e_other, gain, partial, s_keep, out_weight)
    got_near = across(to_near, 1)
    y_near = project_rest(2, BF16, 500_000_000, sc, g_other, partial, out_weight, to_near)
    got_own = across(y_near, 1)
    y_far = project_rest(1, F32, 500_000_000, sc, g_other, partial, out_weight, y_near)
    to_far = add_far(sc, y_far, to_near, got_near)
    got_far = across(to_far, 2)
    y_own = project_rest(3, F32, 10_000_000_000, sc, g_other, partial, out_weight, to_far, got_own)
    return finish(feats * n_tp, sc, y_own, to_far, got_far)


def solution(mesh):
    in_specs = (
        P("seq", "tp"),
        P("seq", "tp"),
        P("seq", None),
        P("seq", None),
        P("tp", "seq"),
        P("seq"),
        P("tp"),
        P("tp"),
        P("tp"),
        P("tp"),
        P("tp", None),
    )
    out_specs = P("tp", "seq")
    return jax.shard_map(
        functools.partial(on_device, mesh.shape["seq"], mesh.shape["tp"]),
        mesh=mesh, in_specs=in_specs, out_specs=out_specs, check_vma=False,
    )
```

time: 233 us -> 60.4 us (0.26)
  waiting for transfers between devices: 140 us -> 26.6 us
  blocking collectives: 29.4 us -> 0 us
  matrix products: 25.1 us -> 0 us
  Pallas kernels: 0 us -> 21.7 us
  between operations: 18 us -> 0.14 us
  starting transfers between devices: 0.04 us -> 10.5 us
  local copies, waits for them, and re-layouts: 11.4 us -> 1.3 us
  other arithmetic: 8.26 us -> 0.01 us
    reduce_scatter x1 -> x0, waiting for transfers between devices: 85.4 us -> none  [on_device(): lax.psum_scatter(lax.dot_general(out_weight, normed, (((0,), (1,)), ((),...]
    all_gather x1 -> x0, waiting for transfers between devices: 54.7 us -> none  [prefix(): gathered = jax.tree.map(lambda a: lax.all_gather(a, axis), part)]
    ppermute x0 -> x8, waiting for transfers between devices: none -> 26.6 us  [the longest x3 14.2 us: across(): return lax.ppermute(a, 'tp', [(i, i ^ bit) for i in range(n_tp)])]
    dot_general x10 -> x0, matrix products: 25.1 us -> none  [the longest x1 9.7 us: on_device(): lax.dot_general(out_weight, normed, (((0,), (1,)), ((), ())), preferred_e...]
    unnamed x1 -> x0, blocking collectives: 23.7 us -> none
    pallas_call x0 -> x11, Pallas kernels: none -> 21.7 us  [the longest x10 17.4 us: call(): pl.pallas_call(kernel, in_specs=specs, out_specs=jax.tree.map(lambda _: v...]
    ppermute x0 -> x8, starting transfers between devices: none -> 10.5 us  [the longest x5 8.28 us: swap(): return lax.ppermute(a, 'seq', [(i, i ^ bit) for i in range(n_seq)])]
    psum x1 -> x0, blocking collectives: 5.7 us -> none  [on_device(): totals = lax.psum(jnp.sum(gated * gated, axis=1), 'tp')]
  transfers between devices with their start and end apart: 2 -> 8, of which waited for: 2 -> 4; matrix products, arithmetic and copies ran while one was open for 4% -> 0% of each run, Pallas kernels for 0% -> 20%
where the time goes in v4:
time: 60.4 us; the launch traced here: 60.2 us
  waiting for transfers between devices  26.6 us (44%)
  Pallas kernels  21.7 us (36%)
  starting transfers between devices  10.5 us (17%)
  local copies, waits for them, and re-layouts  1.3 us (2%)
    pallas_call x10, Pallas kernels, call(): pl.pallas_call(kernel, in_specs=specs, out_specs=jax.tree.map(lambda _: v...  17.4 us
    ppermute x3, waiting for transfers between devices, across(): return lax.ppermute(a, 'tp', [(i, i ^ bit) for i in range(n_tp)])  14.2 us
    ppermute x5, waiting for transfers between devices, swap(): return lax.ppermute(a, 'seq', [(i, i ^ bit) for i in range(n_seq)])  12.4 us
    ppermute x5, starting transfers between devices, swap(): return lax.ppermute(a, 'seq', [(i, i ^ bit) for i in range(n_seq)])  8.28 us
    pallas_call x1, Pallas kernels, prepare(): pl.pallas_call(body, in_specs=[pl.BlockSpec(memory_space=pltpu.HBM)] * le...  4.27 us
    ppermute x3, starting transfers between devices, across(): return lax.ppermute(a, 'tp', [(i, i ^ bit) for i in range(n_tp)])  2.21 us
    unnamed x18, local copies, waits for them, and re-layouts  1.21 us
  transfers between devices with their start and end apart: 8, of which 4 were waited for; matrix products, arithmetic and copies ran while one was open for 0% of the time, Pallas kernels for 20%

profile of v4, /device:TPU:0, one launch (start us, length us, event | category | flops | bytes accessed | tf_op | source)
XLA Modules:
  0.0 60.2 jit_solution(17340022557386432831)
XLA Ops:
  0.0 0.0 copy-start
  0.0 0.0 copy-start.2
  0.0 0.0 copy-start.3
  0.0 0.0 copy-start.4
  0.0 0.0 copy-start.5
  0.0 4.3 %shard_map.109 = (bf16[144,640]{1,0:T(8,128)(2,1)}, bf16[144,640]{1,0:T(8,128)(2,1)}, f32[200,640]{1,0:T(8,128)}) custom-call(bf16[20,512]{1,0:T(8,128)(2,1)} %refs_0_.1, s32[1,512]{1,0:T(1,128)} %bitcast.14, f32[1,20]{1,0:T(1,128)} %bitcast.15, f32[1,20]{1,0:T(1,128)} %bitcast.16, bf16[512,128]{1,0:T(8,128)(2,1)} %wr_ref.1, bf16[512,1280]{1,0:T(8,128)(2,1)} %x_ref.1), custom_call_target="tpu_custom_call" | custom-call | flops 4000000000 | bytes 1000 | tf_op jit(solution)/shard_map/pallas_call | solution.py:188
  4.3 4.1 %collective-permute-start.2 = (bf16[144,640]{1,0:T(8,128)(2,1)}, bf16[144,640]{1,0:T(8,128)(2,1)S(1)}, u32[]{:S(2)}, u32[]{:S(2)}) collective-permute-start(bf16[144,640]{1,0:T(8,128)(2,1)} %get-tuple-element.24), channel_id=1, source_target_pairs={{0,12},{4,8},{8,4},{12,0},{16,28},{20,24},{24,20},{28,16},{1,13},{... | collective-permute-start | bytes 552968 | tf_op jit(solution)/shard_map/ppermute | solution.py:494
  8.4 0.5 collective-permute-start
  8.9 0.1 collective-permute-start.1
  9.0 0.1 stack.31.sc_ref.refs_0_
  9.1 0.0 slice-start
  9.1 0.0 copy-done
  9.1 0.0 copy-done.2
  9.1 0.0 copy-done.3
  9.1 0.0 copy-done.4
  9.1 0.0 copy-done.5
  9.1 0.0 copy-start.1
  9.1 1.2 %copy-done.1 = f32[200,640]{1,0:T(8,128)S(1)} copy-done((f32[200,640]{1,0:T(8,128)S(1)}, f32[200,640]{1,0:T(8,128)}, u32[]{:S(2)}) %copy-start.1) | copy-done | bytes 512024
  10.3 0.0 slice-start.1
  10.3 4.4 %shard_map.110 = (f32[512,1280]{1,0:T(8,128)S(1)}, f32[512,1280]{1,0:T(8,128)S(1)}, f32[512,128]{1,0:T(8,128)S(1)}) custom-call(s32[7]{0:T(128)S(1)} %stack.31.sc_ref.refs_0_, bf16[512,1280]{1,0:T(8,128)(2,1)S(1)} %copy-done.2, bf16[512,1280]{1,0:T(8,128)(2,1)S(1)} %copy-done.3, bf16[512,128]{1,0:T(8,128)(2,1)S(1)} %copy-done, ...), custom_call_target="tpu_custom_call" | custom-call | flops 8000000000 | bytes 1000 | tf_op jit(solution)/shard_map/pallas_call | solution.py:54
  14.8 0.0 copy-start.6
  14.8 2.6 %collective-permute-done.1.refs_3_ = bf16[144,640]{1,0:T(8,128)(2,1)S(1)} collective-permute-done((bf16[144,640]{1,0:T(8,128)(2,1)}, bf16[144,640]{1,0:T(8,128)(2,1)S(1)}, u32[]{:S(2)}, u32[]{:S(2)}) %collective-permute-start.1) | collective-permute-done | bytes 184352 | tf_op jit(solution)/shard_map/ppermute | solution.py:494
  17.4 0.0 collective-permute-done.2.refs_4_
  17.4 0.0 collective-permute-done.refs_2_
  17.4 0.9 %shard_map.111 = (bf16[144,640]{1,0:T(8,128)(2,1)S(1)}, f32[128,640]{1,0:T(8,128)S(1)}, f32[128,640]{1,0:T(8,128)S(1)}, f32[128,640]{1,0:T(8,128)S(1)}, f32[8,640]{1,0:T(8,128)S(1)}) custom-call(s32[7]{0:T(128)S(1)} %stack.31.sc_ref.refs_0_, f32[200,640]{1,0:T(8,128)S(1)} %copy-done.1, bf16[144,640]{1,0:T(8,128)(2,1)S(1)} %collective-permute-done.refs_2_, ...), custom_call_target="tpu_custom_call" | custom-call | bytes 1000 | tf_op jit(solution)/shard_map/pallas_call | solution.py:54
  18.3 2.7 %collective-permute-start.3 = (bf16[144,640]{1,0:T(8,128)(2,1)S(1)}, bf16[144,640]{1,0:T(8,128)(2,1)S(1)}, u32[]{:S(2)}, u32[]{:S(2)}) collective-permute-start(bf16[144,640]{1,0:T(8,128)(2,1)S(1)} %get-tuple-element.27), channel_id=1, source_target_pairs={{0,16},{4,20},{8,24},{12,28},{16,0},{20,4},{24,8},{28,12},{1,17},{... | collective-permute-start | bytes 552968 | tf_op jit(solution)/shard_map/ppermute | solution.py:494
  20.9 0.0 copy-done.6
  20.9 8.7 %collective-permute-done.3.got_ref = bf16[144,640]{1,0:T(8,128)(2,1)S(1)} collective-permute-done((bf16[144,640]{1,0:T(8,128)(2,1)S(1)}, bf16[144,640]{1,0:T(8,128)(2,1)S(1)}, u32[]{:S(2)}, u32[]{:S(2)}) %collective-permute-start.3) | collective-permute-done | bytes 184352 | tf_op jit(solution)/shard_map/ppermute | solution.py:494
  29.6 1.1 %shard_map.112 = (bf16[128,640]{1,0:T(8,128)(2,1)S(1)}, bf16[128,640]{1,0:T(8,128)(2,1)S(1)}, f32[8,128]{1,0:T(8,128)S(1)}, f32[8,128]{1,0:T(8,128)}) custom-call(s32[7]{0:T(128)S(1)} %stack.31.sc_ref.refs_0_, bf16[144,640]{1,0:T(8,128)(2,1)S(1)} %collective-permute-done.3.got_ref, f32[128,640]{1,0:T(8,128)S(1)} %get-tuple-element.28.entry_ref, ...), custom_call_target="tpu_custom_call" | custom-call | bytes 1000 | tf_op jit(solution)/shard_map/pallas_call | solution.py:54
  30.7 0.9 %collective-permute-start.4 = (bf16[128,640]{1,0:T(8,128)(2,1)S(1)}, bf16[128,640]{1,0:T(8,128)(2,1)S(1)}, u32[]{:S(2)}, u32[]{:S(2)}) collective-permute-start(bf16[128,640]{1,0:T(8,128)(2,1)S(1)} %get-tuple-element.35), channel_id=1, source_target_pairs={{0,4},{4,0},{8,12},{12,8},{16,20},{20,16},{24,28},{28,24},{1,5},{5... | collective-permute-start | bytes 491528 | tf_op jit(solution)/shard_map/ppermute | solution.py:494
  31.7 0.0 slice-done
  31.7 0.0 slice-done.1
  31.7 3.3 %shard_map.113 = (bf16[512,640]{1,0:T(8,128)(2,1)}, f32[1,512]{1,0:T(1,128)S(1)}, f32[4,640,512]{2,1,0:T(8,128)S(1)}) custom-call(s32[7]{0:T(128)S(1)} %stack.31.sc_ref.refs_0_, f32[8,128]{1,0:T(8,128)S(1)} %get-tuple-element.32.prev_ref, bf16[512,128]{1,0:T(8,128)(2,1)S(1)} %copy-done, f32[512,128]{1,0:T(8,128)S(1)} %get-tuple-element.33.cum_ref, ...), custom_call_target="tpu_custom_call" | custom-call | flops 2000000000 | bytes 1000 | tf_op jit(solution)/shard_map/pallas_call | solution.py:54
  34.9 1.1 %collective-permute-done.4.e_ref = bf16[128,640]{1,0:T(8,128)(2,1)S(1)} collective-permute-done((bf16[128,640]{1,0:T(8,128)(2,1)S(1)}, bf16[128,640]{1,0:T(8,128)(2,1)S(1)}, u32[]{:S(2)}, u32[]{:S(2)}) %collective-permute-start.4) | collective-permute-done | bytes 163872 | tf_op jit(solution)/shard_map/ppermute | solution.py:494
  36.1 1.7 %shard_map.114 = (bf16[512,640]{1,0:T(8,128)(2,1)S(1)}, bf16[656,512]{1,0:T(8,128)(2,1)S(1)}) custom-call(s32[7]{0:T(128)S(1)} %stack.31.sc_ref.refs_0_, f32[8,128]{1,0:T(8,128)S(1)} %get-tuple-element.32.prev_ref, bf16[512,128]{1,0:T(8,128)(2,1)S(1)} %copy-done, f32[512,128]{1,0:T(8,128)S(1)} %get-tuple-element.33.cum_ref, ...), custom_call_target="tpu_custom_call" | custom-call | flops 1000000000 | bytes 1000 | tf_op jit(solution)/shard_map/pallas_call | solution.py:54
  37.8 0.1 collective-permute-start.6
  37.8 1.3 %shard_map.115.refs_4_ = bf16[640,512]{1,0:T(8,128)(2,1)S(1)} custom-call(s32[7]{0:T(128)S(1)} %stack.31.sc_ref.refs_0_, bf16[512,640]{1,0:T(8,128)(2,1)S(1)} %get-tuple-element.39.refs_1_, f32[4,640,512]{2,1,0:T(8,128)S(1)} %get-tuple-element.37.p_ref.refs_2_, bf16[1280,2560]{1,0:T(8,128)(2,1)S(1)} %bitcast.12, ...), custom_call_target="tpu_custom_call" | custom-call | flops 500000000 | bytes 1000 | tf_op jit(solution)/shard_map/pallas_call | solution.py:54
  39.1 0.5 collective-permute-start.5
  39.7 1.3 %shard_map.116.y_ref = f32[640,512]{1,0:T(8,128)S(1)} custom-call(s32[7]{0:T(128)S(1)} %stack.31.sc_ref.refs_0_, bf16[512,640]{1,0:T(8,128)(2,1)S(1)} %get-tuple-element.39.refs_1_, f32[4,640,512]{2,1,0:T(8,128)S(1)} %get-tuple-element.37.p_ref.refs_2_, bf16[1280,2560]{1,0:T(8,128)(2,1)S(1)} %bitcast.12, bf16[640,512]{1,0:T(8,128)(2,1)S(1)} %shard_map.115.refs_4_), custom_call_target="tpu_custom_call" | custom-call | flops 500000000 | bytes 1000 | tf_op jit(solution)/shard_map/pallas_call | solution.py:54
  40.9 0.0 collective-permute-done.6.got_ref
  40.9 0.7 %shard_map.117.refs_5_.mine_ref = bf16[656,512]{1,0:T(8,128)(2,1)S(1)} custom-call(s32[7]{0:T(128)S(1)} %stack.31.sc_ref.refs_0_, f32[640,512]{1,0:T(8,128)S(1)} %shard_map.116.y_ref, bf16[656,512]{1,0:T(8,128)(2,1)S(1)} %get-tuple-element.40.refs_4_.mine_ref, bf16[656,512]{1,0:T(8,128)(2,1)S(1)} %collective-permute-done.6.got_ref), custom_call_target="tpu_custom_call" | custom-call | bytes 1000 | tf_op jit(solution)/shard_map/pallas_call | solution.py:54
  41.6 1.6 %collective-permute-start.7 = (bf16[656,512]{1,0:T(8,128)(2,1)S(1)}, bf16[656,512]{1,0:T(8,128)(2,1)S(1)}, u32[]{:S(2)}, u32[]{:S(2)}) collective-permute-start(bf16[656,512]{1,0:T(8,128)(2,1)S(1)} %shard_map.117.refs_5_.mine_ref), channel_id=1, source_target_pairs={{0,2},{1,3},{2,0},{3,1},{4,6},{5,7},{6,4},{7,5},{8,10},{9,11},{10,... | collective-permute-start | bytes 2015240 | tf_op jit(solution)/shard_map/ppermute | solution.py:497
  43.2 0.0 collective-permute-done.5.refs_4_
  43.2 1.3 %shard_map.118.own_ref = f32[640,512]{1,0:T(8,128)S(1)} custom-call(s32[7]{0:T(128)S(1)} %stack.31.sc_ref.refs_0_, bf16[512,640]{1,0:T(8,128)(2,1)S(1)} %get-tuple-element.39.refs_1_, f32[4,640,512]{2,1,0:T(8,128)S(1)} %get-tuple-element.37.p_ref.refs_2_, bf16[1280,2560]{1,0:T(8,128)(2,1)S(1)} %bitcast.12, ...), custom_call_target="tpu_custom_call" | custom-call | flops 10000000000 | bytes 1000 | tf_op jit(solution)/shard_map/pallas_call | solution.py:54
  44.5 14.2 %collective-permute-done.7.far_ref = bf16[656,512]{1,0:T(8,128)(2,1)S(1)} collective-permute-done((bf16[656,512]{1,0:T(8,128)(2,1)S(1)}, bf16[656,512]{1,0:T(8,128)(2,1)S(1)}, u32[]{:S(2)}, u32[]{:S(2)}) %collective-permute-start.7) | collective-permute-done | bytes 671776 | tf_op jit(solution)/shard_map/ppermute | solution.py:497
  58.7 1.5 %shard_map.119 = bf16[640,512]{1,0:T(8,128)(2,1)} custom-call(s32[7]{0:T(128)S(1)} %stack.31.sc_ref.refs_0_, f32[640,512]{1,0:T(8,128)S(1)} %shard_map.118.own_ref, bf16[656,512]{1,0:T(8,128)(2,1)S(1)} %shard_map.117.refs_5_.mine_ref, bf16[656,512]{1,0:T(8,128)(2,1)S(1)} %collective-permute-done.7.far_ref), custom_call_target="tpu_custom_call" | custom-call | bytes 1000 | tf_op jit(solution)/shard_map/pallas_call | solution.py:54
  (2 shorter events, 0.0 us)
Async XLA Ops:
  0.0 9.1 %copy-start = (bf16[512,128]{1,0:T(8,128)(2,1)S(1)}, bf16[512,128]{1,0:T(8,128)(2,1)}, u32[]{:S(2)}) copy-start(bf16[512,128]{1,0:T(8,128)(2,1)} %rd_ref.5) | copy-start | bytes 393220
  0.0 9.1 %copy-start.2 = (bf16[512,1280]{1,0:T(8,128)(2,1)S(1)}, bf16[512,1280]{1,0:T(8,128)(2,1)}, u32[]{:S(2)}) copy-start(bf16[512,1280]{1,0:T(8,128)(2,1)} %x_ref.1) | copy-start | bytes 3932164
  0.0 9.1 %copy-start.3 = (bf16[512,1280]{1,0:T(8,128)(2,1)S(1)}, bf16[512,1280]{1,0:T(8,128)(2,1)}, u32[]{:S(2)}) copy-start(bf16[512,1280]{1,0:T(8,128)(2,1)} %gate_ref.1) | copy-start | bytes 3932164
  0.0 9.1 %copy-start.4 = (bf16[512,128]{1,0:T(8,128)(2,1)S(1)}, bf16[512,128]{1,0:T(8,128)(2,1)}, u32[]{:S(2)}) copy-start(bf16[512,128]{1,0:T(8,128)(2,1)} %wr_ref.1) | copy-start | bytes 393220
  0.0 9.1 %copy-start.5 = (f32[20]{0:T(128)S(1)}, f32[20]{0:T(128)}, u32[]{:S(2)}) copy-start(f32[20]{0:T(128)} %param.19) | copy-start | bytes 244
  4.3 13.1 %collective-permute-start.2 = (bf16[144,640]{1,0:T(8,128)(2,1)}, bf16[144,640]{1,0:T(8,128)(2,1)S(1)}, u32[]{:S(2)}, u32[]{:S(2)}) collective-permute-start(bf16[144,640]{1,0:T(8,128)(2,1)} %get-tuple-element.24), channel_id=1, source_target_pairs={{0,12},{4,8},{8,4},{12,0},{16,28},{20,24},{24,20},{28,16},{1,13},{... | collective-permute-start | bytes 552968 | tf_op jit(solution)/shard_map/ppermute | solution.py:494
  8.4 9.0 %collective-permute-start = (bf16[144,640]{1,0:T(8,128)(2,1)}, bf16[144,640]{1,0:T(8,128)(2,1)S(1)}, u32[]{:S(2)}, u32[]{:S(2)}) collective-permute-start(bf16[144,640]{1,0:T(8,128)(2,1)} %get-tuple-element.24), channel_id=1, source_target_pairs={{0,4},{4,0},{8,12},{12,8},{16,20},{20,16},{24,28},{28,24},{1,5},{5... | collective-permute-start | bytes 552968 | tf_op jit(solution)/shard_map/ppermute | solution.py:494
  8.9 8.5 %collective-permute-start.1 = (bf16[144,640]{1,0:T(8,128)(2,1)}, bf16[144,640]{1,0:T(8,128)(2,1)S(1)}, u32[]{:S(2)}, u32[]{:S(2)}) collective-permute-start(bf16[144,640]{1,0:T(8,128)(2,1)} %get-tuple-element.25), channel_id=1, source_target_pairs={{0,8},{4,12},{8,0},{12,4},{16,24},{20,28},{24,16},{28,20},{1,9},{5... | collective-permute-start | bytes 552968 | tf_op jit(solution)/shard_map/ppermute | solution.py:494
  9.1 22.6 %slice-start = ((s8[6553600]{0:T(1024)(128)(4,1)}), s8[4194304]{0:T(1024)(128)(4,1)S(1)}, s32[]{:S(2)}) async-start(s8[6553600]{0:T(1024)(128)(4,1)} %bitcast.11), calls=%async_computation | async-start | bytes 8388608
  9.1 1.2 %copy-start.1 = (f32[200,640]{1,0:T(8,128)S(1)}, f32[200,640]{1,0:T(8,128)}, u32[]{:S(2)}) copy-start(f32[200,640]{1,0:T(8,128)} %get-tuple-element.23.stash_ref.refs_1_) | copy-start | bytes 1536004
  10.3 21.3 %slice-start.1 = ((s8[6553600]{0:T(1024)(128)(4,1)}), s8[2359296]{0:T(1024)(128)(4,1)S(1)}, s32[]{:S(2)}) async-start(s8[6553600]{0:T(1024)(128)(4,1)} %bitcast.11), calls=%async_computation.1 | async-start | bytes 4718592
  14.8 6.2 %copy-start.6 = (f32[1280]{0:T(1024)S(1)}, f32[1280]{0:T(1024)}, u32[]{:S(2)}) copy-start(f32[1280]{0:T(1024)} %param.20) | copy-start | bytes 15364
  18.3 11.3 %collective-permute-start.3 = (bf16[144,640]{1,0:T(8,128)(2,1)S(1)}, bf16[144,640]{1,0:T(8,128)(2,1)S(1)}, u32[]{:S(2)}, u32[]{:S(2)}) collective-permute-start(bf16[144,640]{1,0:T(8,128)(2,1)S(1)} %get-tuple-element.27), channel_id=1, source_target_pairs={{0,16},{4,20},{8,24},{12,28},{16,0},{20,4},{24,8},{28,12},{1,17},{... | collective-permute-start | bytes 552968 | tf_op jit(solution)/shard_map/ppermute | solution.py:494
  30.7 5.3 %collective-permute-start.4 = (bf16[128,640]{1,0:T(8,128)(2,1)S(1)}, bf16[128,640]{1,0:T(8,128)(2,1)S(1)}, u32[]{:S(2)}, u32[]{:S(2)}) collective-permute-start(bf16[128,640]{1,0:T(8,128)(2,1)S(1)} %get-tuple-element.35), channel_id=1, source_target_pairs={{0,4},{4,0},{8,12},{12,8},{16,20},{20,16},{24,28},{28,24},{1,5},{5... | collective-permute-start | bytes 491528 | tf_op jit(solution)/shard_map/ppermute | solution.py:494
  37.8 3.2 %collective-permute-start.6 = (bf16[656,512]{1,0:T(8,128)(2,1)S(1)}, bf16[656,512]{1,0:T(8,128)(2,1)S(1)}, u32[]{:S(2)}, u32[]{:S(2)}) collective-permute-start(bf16[656,512]{1,0:T(8,128)(2,1)S(1)} %get-tuple-element.40.refs_4_.mine_ref), channel_id=1, source_target_pairs={{0,1},{1,0},{2,3},{3,2},{4,5},{5,4},{6,7},{7,6},{8,9},{9,8},{10,11... | collective-permute-start | bytes 2015240 | tf_op jit(solution)/shard_map/ppermute | solution.py:497
  39.1 4.1 %collective-permute-start.5 = (bf16[640,512]{1,0:T(8,128)(2,1)S(1)}, bf16[640,512]{1,0:T(8,128)(2,1)S(1)}, u32[]{:S(2)}, u32[]{:S(2)}) collective-permute-start(bf16[640,512]{1,0:T(8,128)(2,1)S(1)} %shard_map.115.refs_4_), channel_id=1, source_target_pairs={{0,1},{1,0},{2,3},{3,2},{4,5},{5,4},{6,7},{7,6},{8,9},{9,8},{10,11... | collective-permute-start | bytes 1966088 | tf_op jit(solution)/shard_map/ppermute | solution.py:497
  41.6 17.1 %collective-permute-start.7 = (bf16[656,512]{1,0:T(8,128)(2,1)S(1)}, bf16[656,512]{1,0:T(8,128)(2,1)S(1)}, u32[]{:S(2)}, u32[]{:S(2)}) collective-permute-start(bf16[656,512]{1,0:T(8,128)(2,1)S(1)} %shard_map.117.refs_5_.mine_ref), channel_id=1, source_target_pairs={{0,2},{1,3},{2,0},{3,1},{4,6},{5,7},{6,4},{7,5},{8,10},{9,11},{10,... | collective-permute-start | bytes 2015240 | tf_op jit(solution)/shard_map/ppermute | solution.py:497

commit v5 on v4

--- a/solution.py
+++ b/solution.py
@@ -12,7 +12,7 @@
 EPS = 1e-05
 LOG2E = 1.4426950408889634
 SEG_LANE = 24
-EXTRA = 16
+EXTRA = 8
 VMEM = 16 * 1024 * 1024
 VMEM_ALL = 56 * 1024 * 1024
 F32 = jnp.float32
@@ -38,10 +38,17 @@
     return out
 
 
-def call(body, sc, args, out_shape, scratch=(), cost=0, after=None):
+def position():
+    place, rank = lax.axis_index("seq"), lax.axis_index("tp")
+    odd = place & 1
+    far = rank ^ 2
+    return odd, 1 - odd, far ^ 1, far, rank ^ 1, rank, place
+
+
+def call(body, args, out_shape, scratch=(), cost=0, after=None):
     vm = pl.BlockSpec(memory_space=pltpu.VMEM)
-    specs = [pl.BlockSpec(memory_space=pltpu.SMEM)] + [vm] * len(args)
-    operands = [sc, *args]
+    specs = [vm] * len(args)
+    operands = list(args)
     kernel = body
     if after is not None:
         specs.append(pl.BlockSpec(memory_space=pl.ANY))
@@ -68,18 +75,16 @@
 
 def pack(out_ref, total):
     state, through, last = total
-    size, lanes = state.shape
     high = through.astype(BF16).astype(F32)
-    row = lax.broadcasted_iota(jnp.int32, (EXTRA, lanes), 0)
+    row = lax.broadcasted_iota(jnp.int32, (EXTRA, state.shape[1]), 0)
     rows = jnp.where(row == 0, high, jnp.where(row == 1, through - high, last))
-    out_ref[0:size] = state.astype(BF16)
-    out_ref[size : size + EXTRA] = rows.astype(BF16)
+    out_ref[...] = jnp.concatenate([state, rows], axis=0).astype(BF16)
 
 
 def unpack(ref):
     size = ref.shape[0] - EXTRA
-    rows = ref[size : size + EXTRA].astype(F32)
-    return ref[0:size].astype(F32), rows[0:1] + rows[1:2], rows[2:3, 0:1]
+    whole = ref[...].astype(F32)
+    return whole[0:size], whole[size : size + 1] + whole[size + 1 : size + 2], whole[size + 2 : size + 3]
 
 
 def merged(swapped, one, two):
@@ -95,8 +100,8 @@
     return firsts, seconds
 
 
-def stash_rows(state):
-    return slice(0, state), slice(state + 8, state + 40), slice(state + 40, state + 72)
+def stash_rows():
+    return slice(0, 32), slice(32, 64)
 
 
 def put_rows(rows_ref, rows):
@@ -113,8 +118,8 @@
     arrays = (raw, seg, decay_log, bias, write, x)
 
     def body(*refs):
-        hbm, (other_ref, keep_ref, stash_ref) = refs[: len(arrays)], refs[len(arrays) : -10]
-        raw_ref, seg_ref, dl_ref, sb_ref, wr_ref, x_ref, rows, pad, cols, sems = refs[-10:]
+        hbm, (other_ref, keep_ref, stash_ref) = refs[: len(arrays)], refs[len(arrays) : -9]
+        raw_ref, seg_ref, dl_ref, sb_ref, wr_ref, x_ref, rows, pad, sems = refs[-9:]
         copies = [
             pltpu.make_async_copy(src, dst, sems.at[k])
             for k, (src, dst) in enumerate(zip(hbm, (raw_ref, seg_ref, dl_ref, sb_ref, wr_ref, x_ref)))
@@ -127,8 +132,9 @@
             lax.broadcasted_iota(jnp.int32, (GROUP, GROUP), 0)
             <= lax.broadcasted_iota(jnp.int32, (GROUP, GROUP), 1)
         ).astype(BF16)
-        for copy in copies[:4]:
+        for copy in copies[:5]:
             copy.wait()
+        vecs = jnp.transpose(wr_ref[...].astype(F32))
         rows[0:1, 0:heads] = dl_ref[...]
         rows[1:2, 0:heads] = sb_ref[...]
         pad[0:heads] = raw_ref[...].astype(F32)
@@ -151,39 +157,38 @@
         seg_row = seg_ref[...].astype(F32)
         last = seg_row[:, toks - 1 : toks]
         tail = jnp.exp(base - jnp.concatenate(full, axis=1)) * step
-        pad[0:32] = jnp.where(seg_row == last, tail, 0.0)
-        own_rows, cum_rows, step_rows = stash_rows(state)
-        stash_ref[cum_rows, 0:toks] = jnp.concatenate(cum, axis=1)
-        stash_ref[cum_rows.start + SEG_LANE : cum_rows.start + SEG_LANE + 1, 0:toks] = seg_row
-        stash_ref[step_rows, 0:toks] = step
-        cols[...] = jnp.transpose(pad[...])
+        cum_rows, step_rows = stash_rows()
+        stash_ref[cum_rows] = jnp.concatenate(cum, axis=1)
+        stash_ref[SEG_LANE : SEG_LANE + 1] = seg_row
+        stash_ref[step_rows] = step
+        tails = jnp.where(seg_row == last, tail, 0.0)
         rows[...] = jnp.zeros_like(rows)
         rows[0:32] = jnp.broadcast_to(jnp.exp(base), (32, LANES))
         keep = jnp.transpose(rows[...])[0:1]
         per = LANES // width
         odd = lax.rem(lax.axis_index("seq"), 2) == 1
-        for copy in copies[4:]:
-            copy.wait()
+        lane = lane_iota(state)
+        copies[5].wait()
         halves = []
         for j in range(2):
-            parts, through = [], []
+            own, through = [], []
             for i in range(half_w // LANES):
                 at = j * half_h + i * per
-                xt = x_ref[:, j * half_w + i * LANES : j * half_w + (i + 1) * LANES].astype(F32)
-                parts.append((xt * spread(cols[...], at, width)).astype(BF16))
+                written = [(vecs * tails[at + k : at + k + 1]).astype(BF16) for k in range(per)]
+                both = dot(jnp.concatenate(written, axis=0), x_ref[:, j * half_w + i * LANES : j * half_w + (i + 1) * LANES])
+                tile = both[0:state]
+                for k in range(1, per):
+                    tile = jnp.where(lane < k * width, tile, both[k * state : (k + 1) * state])
+                own.append(tile)
                 through.append(spread(keep, at, width))
-            own = dot(wr_ref[...], jnp.concatenate(parts, axis=1), ((0,), (0,)))
-            halves.append((own, jnp.concatenate(through, axis=1), last))
+            halves.append((jnp.concatenate(own, axis=1), jnp.concatenate(through, axis=1), last))
         mine, other = ordered(odd, *halves)
-        stash_ref[own_rows] = mine[0]
-        put_rows(stash_ref.at[state : state + 8], mine[1:])
         pack(keep_ref, mine)
         pack(other_ref, other)
 
     vm = pl.BlockSpec(memory_space=pltpu.VMEM)
     out_shape = shaped(
-        ((state + EXTRA, half_w), BF16), ((state + EXTRA, half_w), BF16),
-        ((stash_rows(state)[2].stop, max(half_w, toks)), F32),
+        ((state + EXTRA, half_w), BF16), ((state + EXTRA, half_w), BF16), ((stash_rows()[1].stop, toks), F32),
     )
     return pl.pallas_call(
         body,
@@ -192,7 +197,7 @@
         out_shape=out_shape,
         scratch_shapes=[
             *[pltpu.VMEM(a.shape, a.dtype) for a in arrays],
-            pltpu.VMEM((LANES, LANES), F32), pltpu.VMEM((LANES, toks), F32), pltpu.VMEM((toks, LANES), F32),
+            pltpu.VMEM((LANES, LANES), F32), pltpu.VMEM((32, toks), F32),
             pltpu.SemaphoreType.DMA((len(arrays),)),
         ],
         compiler_params=pltpu.CompilerParams(vmem_limit_bytes=VMEM_ALL),
@@ -208,21 +213,18 @@
     return state, through * jnp.where(upper, other[1], 1.0), last_id
 
 
-def pair_step(sc, stash, mate, side, cross, after):
+def pair_step(keep, mate, side, cross, after):
     size, lanes = mate.shape[0] - EXTRA, mate.shape[1]
 
     def body(
-        sc_ref, stash_ref, mate_ref, side_ref, cross_ref, send_ref, entry_ref, first_ref, total_ref, rows_ref
+        keep_ref, mate_ref, side_ref, cross_ref, send_ref, entry_ref, first_ref, total_ref, rows_ref
     ):
-        odd = sc_ref[0] == 1
-        upper = (sc_ref[6] & 2) != 0
-        mine = (
-            stash_ref[0:size, 0:lanes], stash_ref[size : size + 1, 0:lanes], stash_ref[size + 1 : size + 2, 0:1]
-        )
-        mate = unpack(mate_ref)
+        odd = position()[0] == 1
+        upper = (position()[6] & 2) != 0
+        mine, mate = unpack(keep_ref), unpack(mate_ref)
         total = merged(odd, mine, mate)
         other = merged(odd, unpack(side_ref), unpack(cross_ref))
-        nothing = (0.0, jnp.ones_like(total[1]), jnp.full((1, 1), -1.0, F32))
+        nothing = (0.0, jnp.ones_like(total[1]), jnp.full_like(total[2], -1.0))
         entry = gather_level(upper, nothing, other)
         total = merged(upper, total, other)
         pack(send_ref, total)
@@ -233,33 +235,34 @@
 
     state = ((size, lanes), F32)
     return call(
-        body, sc, (stash, mate, side, cross),
+        body, (keep, mate, side, cross),
         shaped((mate.shape, BF16), state, state, state, ((8, lanes), F32)), after=after,
     )
 
 
-def level_step(bit, final, sc, got, entry, first, total, rows, after):
+def level_step(bit, final, got, entry, first, total, rows, after):
     size, lanes = entry.shape
 
     def body(
-        sc_ref, got_ref, entry_ref, first_ref, total_ref, rows_ref,
+        got_ref, entry_ref, first_ref, total_ref, rows_ref,
         send_ref, one_ref, two_ref, three_ref,
     ):
-        upper = (sc_ref[6] & bit) != 0
+        upper = (position()[6] & bit) != 0
         other = unpack(got_ref)
-        old = (entry_ref[...], rows_ref[0:1], rows_ref[1:2, 0:1])
+        old = (entry_ref[...], rows_ref[0:1], rows_ref[1:2])
         new = gather_level(upper, old, other)
         if final:
-            even = sc_ref[0] == 0
-            last_first = rows_ref[3:4, 0:1]
+            even = position()[0] == 0
+            last_first = rows_ref[3:4]
             link = rows_ref[2:3] * (last_first == new[2]).astype(F32)
             reached = first_ref[...] + link * new[0]
             send_ref[...] = jnp.where(even, reached, new[0]).astype(BF16)
             one_ref[...] = jnp.where(even, new[0], reached).astype(BF16)
-            two_ref[...] = jnp.broadcast_to(jnp.where(even, new[2], last_first), (8, LANES))
+            prev = jnp.where(even, new[2], last_first)
+            two_ref[...] = jnp.broadcast_to(prev[:, 0:LANES], (8, LANES))
             three_ref[...] = jnp.zeros_like(three_ref)
         else:
-            held = (total_ref[...], rows_ref[4:5], rows_ref[5:6, 0:1])
+            held = (total_ref[...], rows_ref[4:5], rows_ref[5:6])
             held = merged(upper, held, other)
             pack(send_ref, held)
             one_ref[...] = new[0]
@@ -270,10 +273,10 @@
         out = shaped(((size, lanes), BF16), ((size, lanes), BF16), ((8, LANES), F32), ((8, LANES), F32))
     else:
         out = shaped((got.shape, BF16), ((size, lanes), F32), ((size, lanes), F32), ((8, lanes), F32))
-    return call(body, sc, (got, entry, first, total, rows), out, after=after)
-
-
-def local_part(heads, width, sc, x, gate, read, write, stash, skip, after):
+    return call(body, (got, entry, first, total, rows), out, after=after)
+
+
+def local_part(heads, width, x, gate, read, write, stash, skip, after):
     toks = write.shape[0]
     feats = x.shape[1]
     per = LANES // width
@@ -281,12 +284,10 @@
     strip = 64
 
     def body(
-        sc_ref, x_ref, gate_ref, rd_ref, wr_ref, stash_ref, skip_ref,
+        x_ref, gate_ref, rd_ref, wr_ref, stash_ref, skip_ref,
         a_ref, b_ref, log_cum, scores, mix, pad, tails, rows_ref,
     ):
-        _, cum_rows, step_rows = stash_rows(write.shape[1])
-        cum_ref = stash_ref.at[cum_rows, 0:toks]
-        step_ref = stash_ref.at[step_rows, 0:toks]
+        cum_ref, step_ref = (stash_ref.at[rows] for rows in stash_rows())
         lane = lane_iota(GROUP)
         mix[...] = jnp.zeros_like(mix)
         pad[...] = jnp.zeros_like(pad)
@@ -357,7 +358,7 @@
                 start = start * dec[GROUP - 1 : GROUP]
 
     return call(
-        body, sc, (x, gate, read, write, stash, skip),
+        body, (x, gate, read, write, stash, skip),
         shaped(((toks, feats), F32), ((toks, feats), F32), ((toks, LANES), F32)),
         [
             pltpu.VMEM((blocks, GROUP, GROUP), F32), pltpu.VMEM((4, per * GROUP, GROUP), BF16),
@@ -367,9 +368,9 @@
     )
 
 
-def gated_tile(which, sc_ref, prev_ref, rd_ref, cum_ref, a_ref, b_ref, e_ref, gain_ref):
+def gated_tile(which, prev_ref, rd_ref, cum_ref, a_ref, b_ref, e_ref, gain_ref):
     half_w = e_ref.shape[1]
-    here = pl.ds(pl.multiple_of(sc_ref[which] * half_w, LANES), half_w)
+    here = pl.ds(pl.multiple_of(position()[which] * half_w, LANES), half_w)
     linked = cum_ref[:, SEG_LANE : SEG_LANE + 1] == prev_ref[0:1, 0:1]
     rm = jnp.where(linked, rd_ref[...].astype(F32), 0.0).astype(BF16)
     gated = a_ref[:, here] + b_ref[:, here] * dot(rm, e_ref[...])
@@ -381,100 +382,116 @@
     return (gated * gain_ref[:, here]).astype(BF16), squares
 
 
-def projected(which, quarter, sc_ref, w_ref, g):
+def projected(which, quarter, w_ref, g):
     half_w = g.shape[1]
     cols = w_ref.shape[1] // 4
-    rows = pl.ds(pl.multiple_of(sc_ref[which] * half_w, LANES), half_w)
-    columns = pl.ds(pl.multiple_of(sc_ref[quarter] * cols, LANES), cols)
+    rows = pl.ds(pl.multiple_of(position()[which] * half_w, LANES), half_w)
+    columns = pl.ds(pl.multiple_of(position()[quarter] * cols, LANES), cols)
     return dot(w_ref[rows, columns], g, ((0,), (1,)))
 
 
-def put_squares(out_ref, size, squares):
+def with_squares(y, squares):
     high = squares.astype(BF16).astype(F32)
     middle = (squares - high).astype(BF16).astype(F32)
     row = lax.broadcasted_iota(jnp.int32, (EXTRA, squares.shape[1]), 0)
     rows = jnp.where(row == 0, high, jnp.where(row == 1, middle, squares - high - middle))
-    out_ref[size : size + EXTRA] = rows.astype(BF16)
-
-
-def get_squares(ref):
-    rows = ref[ref.shape[0] - EXTRA :].astype(F32)
-    return rows[0:1] + (rows[1:2] + rows[2:3])
-
-
-def gated_first(sc, prev, read, cum, a, b, e, gain, weight):
+    return jnp.concatenate([y, rows], axis=0).astype(BF16)
+
+
+def split_squares(ref):
+    size = ref.shape[0] - EXTRA
+    whole = ref[...].astype(F32)
+    return whole[0:size], whole[size : size + 1] + (whole[size + 1 : size + 2] + whole[size + 2 : size + 3])
+
+
+def gated_first(prev, read, cum, a, b, e, gain, weight):
     toks = a.shape[0]
     half_w = e.shape[1]
     feats = weight.shape[1]
 
     def body(
-        sc_ref, prev_ref, rd_ref, cum_ref, a_ref, b_ref, e_ref, gain_ref, w_ref, g_ref, s_ref, y_ref
+        prev_ref, rd_ref, cum_ref, a_ref, b_ref, e_ref, gain_ref, w_ref, g_ref, s_ref, y_ref
     ):
-        g, s_ref[...] = gated_tile(0, sc_ref, prev_ref, rd_ref, cum_ref, a_ref, b_ref, e_ref, gain_ref)
+        g, s_ref[...] = gated_tile(0, prev_ref, rd_ref, cum_ref, a_ref, b_ref, e_ref, gain_ref)
         g_ref[...] = g
         for quarter in range(4):
-            y_ref[quarter] = projected(0, 2 + quarter, sc_ref, w_ref, g)
+            y_ref[quarter] = projected(0, 2 + quarter, w_ref, g)
 
     return call(
-        body, sc, (prev, read, cum, a, b, e, gain, weight),
+        body, (prev, read, cum, a, b, e, gain, weight),
         shaped(((toks, half_w), BF16), ((1, toks), F32), ((4, feats // 4, toks), F32)),
         cost=2_000_000_000,
     )
 
 
-def gated_second(sc, prev, read, cum, a, b, e, gain, partial, s_first, weight):
+def gated_second(prev, read, cum, a, b, e, gain, partial, s_first, weight):
     toks = a.shape[0]
     half_w = e.shape[1]
     cols = weight.shape[1] // 4
 
     def body(
-        sc_ref, prev_ref, rd_ref, cum_ref, a_ref, b_ref, e_ref, gain_ref, p_ref, sf_ref, w_ref, g_ref, y_ref
+        prev_ref, rd_ref, cum_ref, a_ref, b_ref, e_ref, gain_ref, p_ref, sf_ref, w_ref, g_ref, y_ref
     ):
-        g, squares = gated_tile(1, sc_ref, prev_ref, rd_ref, cum_ref, a_ref, b_ref, e_ref, gain_ref)
+        g, squares = gated_tile(1, prev_ref, rd_ref, cum_ref, a_ref, b_ref, e_ref, gain_ref)
         g_ref[...] = g
-        y_ref[0:cols] = (p_ref[0] + projected(1, 2, sc_ref, w_ref, g)).astype(BF16)
-        put_squares(y_ref, cols, sf_ref[...] + squares)
+        y_ref[...] = with_squares(p_ref[0] + projected(1, 2, w_ref, g), sf_ref[...] + squares)
 
     return call(
-        body, sc, (prev, read, cum, a, b, e, gain, partial, s_first, weight),
+        body, (prev, read, cum, a, b, e, gain, partial, s_first, weight),
         shaped(((toks, half_w), BF16), ((cols + EXTRA, toks), BF16)), cost=1_000_000_000,
     )
 
 
-def project_rest(quarter, dtype, cost, sc, g, partial, weight, after, add=None):
+def project_rest(quarter, dtype, cost, g, partial, weight, after, add=None):
     toks = g.shape[0]
     block = (weight.shape[1] // 4, toks)
 
-    def body(sc_ref, g_ref, p_ref, w_ref, *refs):
-        y = p_ref[quarter] + projected(1, 2 + quarter, sc_ref, w_ref, g_ref[...])
+    def body(g_ref, p_ref, w_ref, *refs):
+        y = p_ref[quarter] + projected(1, 2 + quarter, w_ref, g_ref[...])
         if add is not None:
             y = y + refs[0][...].astype(F32)
         refs[-1][...] = y.astype(dtype)
 
     more = () if add is None else (add,)
     return call(
-        body, sc, (g, partial, weight, *more), jax.ShapeDtypeStruct(block, dtype), cost=cost, after=after
-    )
-
-
-def add_far(sc, y_far, to_near, got_near):
-    size = y_far.shape[0]
-
-    def body(sc_ref, y_ref, mine_ref, got_ref, out_ref):
-        out_ref[0:size] = (y_ref[...] + got_ref[0:size].astype(F32)).astype(BF16)
-        put_squares(out_ref, size, get_squares(mine_ref) + get_squares(got_ref))
-
-    return call(body, sc, (y_far, to_near, got_near), jax.ShapeDtypeStruct(got_near.shape, BF16))
-
-
-def finish(features, sc, y_own, to_far, got_far):
-    size = y_own.shape[0]
-
-    def body(sc_ref, own_ref, mine_ref, far_ref, out_ref):
-        inv = lax.rsqrt((get_squares(mine_ref) + get_squares(far_ref)) / features + EPS)
-        out_ref[...] = ((own_ref[...] + far_ref[0:size].astype(F32)) * inv).astype(BF16)
-
-    return call(body, sc, (y_own, to_far, got_far), jax.ShapeDtypeStruct(y_own.shape, BF16))
+        body, (g, partial, weight, *more), jax.ShapeDtypeStruct(block, dtype), cost=cost, after=after
+    )
+
+
+def add_far(y_far, to_near, got_near):
+    def body(y_ref, mine_ref, got_ref, out_ref):
+        got, squares = split_squares(got_ref)
+        out_ref[...] = with_squares(y_ref[...] + got, split_squares(mine_ref)[1] + squares)
+
+    return call(body, (y_far, to_near, got_near), jax.ShapeDtypeStruct(got_near.shape, BF16))
+
+
+def finish(features, y_own, to_far, got_far):
+    size, toks = y_own.shape
+    parts = 4
+    step = size // parts
+
+    def body(own_ref, mine_ref, far_ref, out_hbm, out_ref, sems):
+        squares = split_squares(mine_ref)[1] + split_squares(far_ref)[1]
+        inv = lax.rsqrt(squares / features + EPS)
+        copies = []
+        for k in range(parts):
+            rows = slice(k * step, (k + 1) * step)
+            out_ref[rows] = ((own_ref[rows] + far_ref[rows].astype(F32)) * inv).astype(BF16)
+            copies.append(pltpu.make_async_copy(out_ref.at[rows], out_hbm.at[rows], sems.at[k]))
+            copies[-1].start()
+        for copy in copies:
+            copy.wait()
+
+    vm = pl.BlockSpec(memory_space=pltpu.VMEM)
+    return pl.pallas_call(
+        body,
+        in_specs=[vm] * 3,
+        out_specs=pl.BlockSpec(memory_space=pl.ANY),
+        out_shape=jax.ShapeDtypeStruct((size, toks), BF16),
+        scratch_shapes=[pltpu.VMEM((size, toks), BF16), pltpu.SemaphoreType.DMA((parts,))],
+        compiler_params=pltpu.CompilerParams(vmem_limit_bytes=VMEM),
+    )(y_own, to_far, got_far)
 
 
 def on_device(
@@ -484,12 +501,6 @@
     heads = decay_log.shape[0]
     toks, feats = head_input.shape
     width = feats // heads
-    place = lax.axis_index("seq")
-    rank = lax.axis_index("tp")
-    odd = lax.rem(place, 2)
-    near, far = rank ^ 1, rank ^ 2
-    sc = jnp.stack([odd, 1 - odd, far ^ 1, far, near, rank, place]).astype(jnp.int32)
-
     def swap(a, bit):
         return lax.ppermute(a, "seq", [(i, i ^ bit) for i in range(n_seq)])
 
@@ -504,28 +515,28 @@
     cross = swap(send_other, 3)
     mate = swap(send_other, 1)
     a, b, log_cum = local_part(
-        heads, width, sc, head_input, gate_input, read_vecs, write_vecs, stash,
+        heads, width, head_input, gate_input, read_vecs, write_vecs, stash,
         skip_gain.reshape(1, heads), None,
     )
-    sent, entry, first, total, rows = pair_step(sc, stash, mate, side, cross, a)
+    sent, entry, first, total, rows = pair_step(send_keep, mate, side, cross, a)
     bit = 4
     while 2 * bit < n_seq:
-        sent, entry, total, rows = level_step(bit, False, sc, swap(sent, bit), entry, first, total, rows, None)
+        sent, entry, total, rows = level_step(bit, False, swap(sent, bit), entry, first, total, rows, None)
         bit *= 2
-    sent, e_keep, prev, _ = level_step(bit, True, sc, swap(sent, bit), entry, first, total, rows, None)
+    sent, e_keep, prev, _ = level_step(bit, True, swap(sent, bit), entry, first, total, rows, None)
     e_other = swap(sent, 1)
     gain = norm_gain.reshape(1, feats)
     shared = (prev, read_vecs, log_cum, a, b)
-    g_keep, s_keep, partial = gated_first(sc, *shared, e_keep, gain, out_weight)
-    g_other, to_near = gated_second(sc, *shared, e_other, gain, partial, s_keep, out_weight)
+    g_keep, s_keep, partial = gated_first(*shared, e_keep, gain, out_weight)
+    g_other, to_near = gated_second(*shared, e_other, gain, partial, s_keep, out_weight)
     got_near = across(to_near, 1)
-    y_near = project_rest(2, BF16, 500_000_000, sc, g_other, partial, out_weight, to_near)
+    y_near = project_rest(2, BF16, 500_000_000, g_other, partial, out_weight, to_near)
     got_own = across(y_near, 1)
-    y_far = project_rest(1, F32, 500_000_000, sc, g_other, partial, out_weight, y_near)
-    to_far = add_far(sc, y_far, to_near, got_near)
+    y_far = project_rest(1, F32, 500_000_000, g_other, partial, out_weight, y_near)
+    to_far = add_far(y_far, to_near, got_near)
     got_far = across(to_far, 2)
-    y_own = project_rest(3, F32, 10_000_000_000, sc, g_other, partial, out_weight, to_far, got_own)
-    return finish(feats * n_tp, sc, y_own, to_far, got_far)
+    y_own = project_rest(3, F32, 10_000_000_000, g_other, partial, out_weight, to_far, got_own)
+    return finish(feats * n_tp, y_own, to_far, got_far)
 
 
 def solution(mesh):

time: 60.4 us -> 54.6 us (0.904)
  Pallas kernels: 21.7 us -> 15.2 us
  waiting for transfers between devices: 26.6 us -> 27.5 us
    pallas_call x10 -> x9, Pallas kernels: 17.4 us -> 11.1 us  [call(): pl.pallas_call(kernel, in_specs=specs, out_specs=jax.tree.map(lambda _: v...]
    pallas_call x1, Pallas kernels: 4.27 us -> 3.27 us  [prepare(): pl.pallas_call(body, in_specs=[pl.BlockSpec(memory_space=pltpu.HBM)] * le...]
    pallas_call x0 -> x1, Pallas kernels: none -> 0.92 us  [finish(): pl.pallas_call(body, in_specs=[vm] * 3, out_specs=pl.BlockSpec(memory_spa...]
    unnamed x18 -> x20, local copies, waits for them, and re-layouts: 1.21 us -> 1.08 us
  transfers between devices with their start and end apart: 8 -> 8, of which waited for: 4 -> 5; matrix products, arithmetic and copies ran while one was open for 0% -> 0% of each run, Pallas kernels for 20% -> 16%
where the time goes in v5:
time: 54.6 us; the launch traced here: 54.5 us
  waiting for transfers between devices  27.5 us (50%)
  Pallas kernels  15.2 us (28%)
  starting transfers between devices  10.5 us (19%)
  local copies, waits for them, and re-layouts  1.09 us (2%)
    ppermute x3, waiting for transfers between devices, across(): return lax.ppermute(a, 'tp', [(i, i ^ bit) for i in range(n_tp)])  14.8 us
    ppermute x5, waiting for transfers between devices, swap(): return lax.ppermute(a, 'seq', [(i, i ^ bit) for i in range(n_seq)])  12.7 us
    pallas_call x9, Pallas kernels, call(): pl.pallas_call(kernel, in_specs=specs, out_specs=jax.tree.map(lambda _: v...  11.1 us
    ppermute x5, starting transfers between devices, swap(): return lax.ppermute(a, 'seq', [(i, i ^ bit) for i in range(n_seq)])  8.29 us
    pallas_call x1, Pallas kernels, prepare(): pl.pallas_call(body, in_specs=[pl.BlockSpec(memory_space=pltpu.HBM)] * le...  3.27 us
    ppermute x3, starting transfers between devices, across(): return lax.ppermute(a, 'tp', [(i, i ^ bit) for i in range(n_tp)])  2.24 us
  transfers between devices with their start and end apart: 8, of which 5 were waited for; matrix products, arithmetic and copies ran while one was open for 0% of the time, Pallas kernels for 16%

profile of v5, /device:TPU:0, one launch (start us, length us, event | category | flops | bytes accessed | tf_op | source)
XLA Modules:
  0.0 54.5 jit_solution(16993459670716836526)
XLA Ops:
  0.0 0.0 copy-start
  0.0 0.0 copy-start.2
  0.0 0.0 copy-start.3
  0.0 0.0 copy-start.4
  0.0 0.0 copy-start.5
  0.0 3.3 %shard_map.109 = (bf16[136,640]{1,0:T(8,128)(2,1)}, bf16[136,640]{1,0:T(8,128)(2,1)}, f32[64,512]{1,0:T(8,128)}) custom-call(bf16[20,512]{1,0:T(8,128)(2,1)} %refs_0_.1, s32[1,512]{1,0:T(1,128)} %bitcast.7, f32[1,20]{1,0:T(1,128)} %bitcast.8, f32[1,20]{1,0:T(1,128)} %bitcast.9, bf16[512,128]{1,0:T(8,128)(2,1)} %wr_ref.1, bf16[512,1280]{1,0:T(8,128)(2,1)} %x_ref.1), custom_call_target="tpu_custom_call" | custom-call | flops 4000000000 | bytes 1000 | tf_op jit(solution)/shard_map/pallas_call | solution.py:193
  3.3 4.1 %collective-permute-start.2 = (bf16[136,640]{1,0:T(8,128)(2,1)}, bf16[136,640]{1,0:T(8,128)(2,1)S(1)}, u32[]{:S(2)}, u32[]{:S(2)}) collective-permute-start(bf16[136,640]{1,0:T(8,128)(2,1)} %get-tuple-element.24), channel_id=1, source_target_pairs={{0,12},{4,8},{8,4},{12,0},{16,28},{20,24},{24,20},{28,16},{1,13},{... | collective-permute-start | bytes 522248 | tf_op jit(solution)/shard_map/ppermute | solution.py:505
  7.4 0.5 collective-permute-start
  7.9 0.1 collective-permute-start.1
  8.0 0.0 slice-start
  8.0 0.0 copy-done
  8.0 0.0 copy-done.2
  8.0 0.0 copy-done.3
  8.0 0.0 copy-done.4
  8.0 0.0 copy-done.5
  8.0 0.0 copy-start.6
  8.0 1.0 %copy-done.6 = f32[64,512]{1,0:T(8,128)S(1)} copy-done((f32[64,512]{1,0:T(8,128)S(1)}, f32[64,512]{1,0:T(8,128)}, u32[]{:S(2)}) %copy-start.6) | copy-done | bytes 131096
  9.1 0.0 copy-start.1
  9.1 0.0 slice-start.1
  9.1 3.9 %shard_map.110 = (f32[512,1280]{1,0:T(8,128)S(1)}, f32[512,1280]{1,0:T(8,128)S(1)}, f32[512,128]{1,0:T(8,128)S(1)}) custom-call(bf16[512,1280]{1,0:T(8,128)(2,1)S(1)} %copy-done.2, bf16[512,1280]{1,0:T(8,128)(2,1)S(1)} %copy-done.3, bf16[512,128]{1,0:T(8,128)(2,1)S(1)} %copy-done, bf16[512,128]{1,0:T(8,128)(2,1)S(1)} %copy-done.4, f32[64,512]{1,0:T(8,128)S(1)} %copy-done.6, ...), custom_call_target="tpu_custom_call" | custom-call | flops 8000000000 | bytes 1000 | tf_op jit(solution)/shard_map/pallas_call | solution.py:61
  13.0 0.0 copy-start.7
  13.0 2.9 %collective-permute-done.1.refs_2_ = bf16[136,640]{1,0:T(8,128)(2,1)S(1)} collective-permute-done((bf16[136,640]{1,0:T(8,128)(2,1)}, bf16[136,640]{1,0:T(8,128)(2,1)S(1)}, u32[]{:S(2)}, u32[]{:S(2)}) %collective-permute-start.1) | collective-permute-done | bytes 174112 | tf_op jit(solution)/shard_map/ppermute | solution.py:505
  15.9 0.0 collective-permute-done.2.refs_3_
  15.9 0.0 collective-permute-done.refs_1_
  15.9 0.0 copy-done.1
  15.9 0.3 shard_map.111
  16.2 2.7 %collective-permute-start.3 = (bf16[136,640]{1,0:T(8,128)(2,1)S(1)}, bf16[136,640]{1,0:T(8,128)(2,1)S(1)}, u32[]{:S(2)}, u32[]{:S(2)}) collective-permute-start(bf16[136,640]{1,0:T(8,128)(2,1)S(1)} %get-tuple-element.27), channel_id=1, source_target_pairs={{0,16},{4,20},{8,24},{12,28},{16,0},{20,4},{24,8},{28,12},{1,17},{... | collective-permute-start | bytes 522248 | tf_op jit(solution)/shard_map/ppermute | solution.py:505
  18.9 0.0 copy-done.7
  18.9 8.2 %collective-permute-done.3.got_ref = bf16[136,640]{1,0:T(8,128)(2,1)S(1)} collective-permute-done((bf16[136,640]{1,0:T(8,128)(2,1)S(1)}, bf16[136,640]{1,0:T(8,128)(2,1)S(1)}, u32[]{:S(2)}, u32[]{:S(2)}) %collective-permute-start.3) | collective-permute-done | bytes 174112 | tf_op jit(solution)/shard_map/ppermute | solution.py:505
  27.1 0.6 %shard_map.112 = (bf16[128,640]{1,0:T(8,128)(2,1)S(1)}, bf16[128,640]{1,0:T(8,128)(2,1)S(1)}, f32[8,128]{1,0:T(8,128)S(1)}, f32[8,128]{1,0:T(8,128)}) custom-call(bf16[136,640]{1,0:T(8,128)(2,1)S(1)} %collective-permute-done.3.got_ref, f32[128,640]{1,0:T(8,128)S(1)} %get-tuple-element.28.entry_ref, f32[128,640]{1,0:T(8,128)S(1)} %get-tuple-element.29.first_ref, ...), custom_call_target="tpu_custom_call" | custom-call | bytes 1000 | tf_op jit(solution)/shard_map/pallas_call | solution.py:61
  27.7 0.9 %collective-permute-start.4 = (bf16[128,640]{1,0:T(8,128)(2,1)S(1)}, bf16[128,640]{1,0:T(8,128)(2,1)S(1)}, u32[]{:S(2)}, u32[]{:S(2)}) collective-permute-start(bf16[128,640]{1,0:T(8,128)(2,1)S(1)} %get-tuple-element.35), channel_id=1, source_target_pairs={{0,4},{4,0},{8,12},{12,8},{16,20},{20,16},{24,28},{28,24},{1,5},{5... | collective-permute-start | bytes 491528 | tf_op jit(solution)/shard_map/ppermute | solution.py:505
  28.6 0.0 slice-done
  28.6 0.0 slice-done.1
  28.6 2.7 %shard_map.113 = (bf16[512,640]{1,0:T(8,128)(2,1)}, f32[1,512]{1,0:T(1,128)S(1)}, f32[4,640,512]{2,1,0:T(8,128)S(1)}) custom-call(f32[8,128]{1,0:T(8,128)S(1)} %get-tuple-element.32.prev_ref, bf16[512,128]{1,0:T(8,128)(2,1)S(1)} %copy-done, f32[512,128]{1,0:T(8,128)S(1)} %get-tuple-element.33.cum_ref, f32[512,1280]{1,0:T(8,128)S(1)} %get-tuple-element.26.refs_4_.a_ref, ...), custom_call_target="tpu_custom_call" | custom-call | flops 2000000000 | bytes 1000 | tf_op jit(solution)/shard_map/pallas_call | solution.py:61
  31.4 1.6 %collective-permute-done.4.e_ref = bf16[128,640]{1,0:T(8,128)(2,1)S(1)} collective-permute-done((bf16[128,640]{1,0:T(8,128)(2,1)S(1)}, bf16[128,640]{1,0:T(8,128)(2,1)S(1)}, u32[]{:S(2)}, u32[]{:S(2)}) %collective-permute-start.4) | collective-permute-done | bytes 163872 | tf_op jit(solution)/shard_map/ppermute | solution.py:505
  33.0 1.2 %shard_map.114 = (bf16[512,640]{1,0:T(8,128)(2,1)S(1)}, bf16[648,512]{1,0:T(8,128)(2,1)S(1)}) custom-call(f32[8,128]{1,0:T(8,128)S(1)} %get-tuple-element.32.prev_ref, bf16[512,128]{1,0:T(8,128)(2,1)S(1)} %copy-done, f32[512,128]{1,0:T(8,128)S(1)} %get-tuple-element.33.cum_ref, f32[512,1280]{1,0:T(8,128)S(1)} %get-tuple-element.26.refs_4_.a_ref, ...), custom_call_target="tpu_custom_call" | custom-call | flops 1000000000 | bytes 1000 | tf_op jit(solution)/shard_map/pallas_call | solution.py:61
  34.2 0.1 collective-permute-start.6
  34.3 0.7 %shard_map.115.refs_3_ = bf16[640,512]{1,0:T(8,128)(2,1)S(1)} custom-call(bf16[512,640]{1,0:T(8,128)(2,1)S(1)} %get-tuple-element.39.refs_0_, f32[4,640,512]{2,1,0:T(8,128)S(1)} %get-tuple-element.37.p_ref.refs_1_, bf16[1280,2560]{1,0:T(8,128)(2,1)S(1)} %bitcast.5, bf16[648,512]{1,0:T(8,128)(2,1)S(1)} %get-tuple-element.40.refs_3_.mine_ref), custom_call_target="tpu_custom_call" | custom-call | flops 500000000 | bytes 1000 | tf_op jit(solution)/shard_map/pallas_call | solution.py:61
  35.0 0.6 %collective-permute-start.5 = (bf16[640,512]{1,0:T(8,128)(2,1)S(1)}, bf16[640,512]{1,0:T(8,128)(2,1)S(1)}, u32[]{:S(2)}, u32[]{:S(2)}) collective-permute-start(bf16[640,512]{1,0:T(8,128)(2,1)S(1)} %shard_map.115.refs_3_), channel_id=1, source_target_pairs={{0,1},{1,0},{2,3},{3,2},{4,5},{5,4},{6,7},{7,6},{8,9},{9,8},{10,11... | collective-permute-start | bytes 1966088 | tf_op jit(solution)/shard_map/ppermute | solution.py:508
  35.6 0.7 %shard_map.116.y_ref = f32[640,512]{1,0:T(8,128)S(1)} custom-call(bf16[512,640]{1,0:T(8,128)(2,1)S(1)} %get-tuple-element.39.refs_0_, f32[4,640,512]{2,1,0:T(8,128)S(1)} %get-tuple-element.37.p_ref.refs_1_, bf16[1280,2560]{1,0:T(8,128)(2,1)S(1)} %bitcast.5, bf16[640,512]{1,0:T(8,128)(2,1)S(1)} %shard_map.115.refs_3_), custom_call_target="tpu_custom_call" | custom-call | flops 500000000 | bytes 1000 | tf_op jit(solution)/shard_map/pallas_call | solution.py:61
  36.3 0.1 collective-permute-done.6.got_ref
  36.4 0.2 shard_map.117.refs_4_.mine_ref
  36.6 1.6 %collective-permute-start.7 = (bf16[648,512]{1,0:T(8,128)(2,1)S(1)}, bf16[648,512]{1,0:T(8,128)(2,1)S(1)}, u32[]{:S(2)}, u32[]{:S(2)}) collective-permute-start(bf16[648,512]{1,0:T(8,128)(2,1)S(1)} %shard_map.117.refs_4_.mine_ref), channel_id=1, source_target_pairs={{0,2},{1,3},{2,0},{3,1},{4,6},{5,7},{6,4},{7,5},{8,10},{9,11},{10,... | collective-permute-start | bytes 1990664 | tf_op jit(solution)/shard_map/ppermute | solution.py:508
  38.2 0.0 collective-permute-done.5.refs_3_
  38.2 0.7 %shard_map.118.own_ref = f32[640,512]{1,0:T(8,128)S(1)} custom-call(bf16[512,640]{1,0:T(8,128)(2,1)S(1)} %get-tuple-element.39.refs_0_, f32[4,640,512]{2,1,0:T(8,128)S(1)} %get-tuple-element.37.p_ref.refs_1_, bf16[1280,2560]{1,0:T(8,128)(2,1)S(1)} %bitcast.5, bf16[640,512]{1,0:T(8,128)(2,1)S(1)} %collective-permute-done.5.refs_3_, ...), custom_call_target="tpu_custom_call" | custom-call | flops 10000000000 | bytes 1000 | tf_op jit(solution)/shard_map/pallas_call | solution.py:61
  38.9 14.7 %collective-permute-done.7.far_ref = bf16[648,512]{1,0:T(8,128)(2,1)S(1)} collective-permute-done((bf16[648,512]{1,0:T(8,128)(2,1)S(1)}, bf16[648,512]{1,0:T(8,128)(2,1)S(1)}, u32[]{:S(2)}, u32[]{:S(2)}) %collective-permute-start.7) | collective-permute-done | bytes 663584 | tf_op jit(solution)/shard_map/ppermute | solution.py:508
  53.6 0.9 %shard_map.119 = bf16[640,512]{1,0:T(8,128)(2,1)} custom-call(f32[640,512]{1,0:T(8,128)S(1)} %shard_map.118.own_ref, bf16[648,512]{1,0:T(8,128)(2,1)S(1)} %shard_map.117.refs_4_.mine_ref, bf16[648,512]{1,0:T(8,128)(2,1)S(1)} %collective-permute-done.7.far_ref), custom_call_target="tpu_custom_call" | custom-call | tf_op jit(solution)/shard_map/pallas_call | solution.py:487
  (2 shorter events, 0.0 us)
Async XLA Ops:
  0.0 8.0 %copy-start = (bf16[512,128]{1,0:T(8,128)(2,1)S(1)}, bf16[512,128]{1,0:T(8,128)(2,1)}, u32[]{:S(2)}) copy-start(bf16[512,128]{1,0:T(8,128)(2,1)} %rd_ref.5) | copy-start | bytes 393220
  0.0 8.0 %copy-start.2 = (bf16[512,1280]{1,0:T(8,128)(2,1)S(1)}, bf16[512,1280]{1,0:T(8,128)(2,1)}, u32[]{:S(2)}) copy-start(bf16[512,1280]{1,0:T(8,128)(2,1)} %x_ref.1) | copy-start | bytes 3932164
  0.0 8.0 %copy-start.3 = (bf16[512,1280]{1,0:T(8,128)(2,1)S(1)}, bf16[512,1280]{1,0:T(8,128)(2,1)}, u32[]{:S(2)}) copy-start(bf16[512,1280]{1,0:T(8,128)(2,1)} %gate_ref.1) | copy-start | bytes 3932164
  0.0 8.0 %copy-start.4 = (bf16[512,128]{1,0:T(8,128)(2,1)S(1)}, bf16[512,128]{1,0:T(8,128)(2,1)}, u32[]{:S(2)}) copy-start(bf16[512,128]{1,0:T(8,128)(2,1)} %wr_ref.1) | copy-start | bytes 393220
  0.0 8.0 %copy-start.5 = (f32[20]{0:T(128)S(1)}, f32[20]{0:T(128)}, u32[]{:S(2)}) copy-start(f32[20]{0:T(128)} %param.19) | copy-start | bytes 244
  3.3 12.6 %collective-permute-start.2 = (bf16[136,640]{1,0:T(8,128)(2,1)}, bf16[136,640]{1,0:T(8,128)(2,1)S(1)}, u32[]{:S(2)}, u32[]{:S(2)}) collective-permute-start(bf16[136,640]{1,0:T(8,128)(2,1)} %get-tuple-element.24), channel_id=1, source_target_pairs={{0,12},{4,8},{8,4},{12,0},{16,28},{20,24},{24,20},{28,16},{1,13},{... | collective-permute-start | bytes 522248 | tf_op jit(solution)/shard_map/ppermute | solution.py:505
  7.4 8.6 %collective-permute-start = (bf16[136,640]{1,0:T(8,128)(2,1)}, bf16[136,640]{1,0:T(8,128)(2,1)S(1)}, u32[]{:S(2)}, u32[]{:S(2)}) collective-permute-start(bf16[136,640]{1,0:T(8,128)(2,1)} %get-tuple-element.24), channel_id=1, source_target_pairs={{0,4},{4,0},{8,12},{12,8},{16,20},{20,16},{24,28},{28,24},{1,5},{5... | collective-permute-start | bytes 522248 | tf_op jit(solution)/shard_map/ppermute | solution.py:505
  7.9 8.1 %collective-permute-start.1 = (bf16[136,640]{1,0:T(8,128)(2,1)}, bf16[136,640]{1,0:T(8,128)(2,1)S(1)}, u32[]{:S(2)}, u32[]{:S(2)}) collective-permute-start(bf16[136,640]{1,0:T(8,128)(2,1)} %get-tuple-element.23.refs_0_), channel_id=1, source_target_pairs={{0,8},{4,12},{8,0},{12,4},{16,24},{20,28},{24,16},{28,20},{1,9},{5... | collective-permute-start | bytes 522248 | tf_op jit(solution)/shard_map/ppermute | solution.py:505
  8.0 20.6 %slice-start = ((s8[6553600]{0:T(1024)(128)(4,1)}), s8[4194304]{0:T(1024)(128)(4,1)S(1)}, s32[]{:S(2)}) async-start(s8[6553600]{0:T(1024)(128)(4,1)} %bitcast.4), calls=%async_computation | async-start | bytes 8388608
  8.0 1.1 %copy-start.6 = (f32[64,512]{1,0:T(8,128)S(1)}, f32[64,512]{1,0:T(8,128)}, u32[]{:S(2)}) copy-start(f32[64,512]{1,0:T(8,128)} %get-tuple-element.25.stash_ref) | copy-start | bytes 393220
  9.1 6.8 %copy-start.1 = (bf16[136,640]{1,0:T(8,128)(2,1)S(1)}, bf16[136,640]{1,0:T(8,128)(2,1)}, u32[]{:S(2)}) copy-start(bf16[136,640]{1,0:T(8,128)(2,1)} %get-tuple-element.23.refs_0_) | copy-start | bytes 522244
  9.1 19.6 %slice-start.1 = ((s8[6553600]{0:T(1024)(128)(4,1)}), s8[2359296]{0:T(1024)(128)(4,1)S(1)}, s32[]{:S(2)}) async-start(s8[6553600]{0:T(1024)(128)(4,1)} %bitcast.4), calls=%async_computation.1 | async-start | bytes 4718592
  13.0 5.8 %copy-start.7 = (f32[1280]{0:T(1024)S(1)}, f32[1280]{0:T(1024)}, u32[]{:S(2)}) copy-start(f32[1280]{0:T(1024)} %param.20) | copy-start | bytes 15364
  16.2 10.9 %collective-permute-start.3 = (bf16[136,640]{1,0:T(8,128)(2,1)S(1)}, bf16[136,640]{1,0:T(8,128)(2,1)S(1)}, u32[]{:S(2)}, u32[]{:S(2)}) collective-permute-start(bf16[136,640]{1,0:T(8,128)(2,1)S(1)} %get-tuple-element.27), channel_id=1, source_target_pairs={{0,16},{4,20},{8,24},{12,28},{16,0},{20,4},{24,8},{28,12},{1,17},{... | collective-permute-start | bytes 522248 | tf_op jit(solution)/shard_map/ppermute | solution.py:505
  27.7 5.3 %collective-permute-start.4 = (bf16[128,640]{1,0:T(8,128)(2,1)S(1)}, bf16[128,640]{1,0:T(8,128)(2,1)S(1)}, u32[]{:S(2)}, u32[]{:S(2)}) collective-permute-start(bf16[128,640]{1,0:T(8,128)(2,1)S(1)} %get-tuple-element.35), channel_id=1, source_target_pairs={{0,4},{4,0},{8,12},{12,8},{16,20},{20,16},{24,28},{28,24},{1,5},{5... | collective-permute-start | bytes 491528 | tf_op jit(solution)/shard_map/ppermute | solution.py:505
  34.2 2.2 %collective-permute-start.6 = (bf16[648,512]{1,0:T(8,128)(2,1)S(1)}, bf16[648,512]{1,0:T(8,128)(2,1)S(1)}, u32[]{:S(2)}, u32[]{:S(2)}) collective-permute-start(bf16[648,512]{1,0:T(8,128)(2,1)S(1)} %get-tuple-element.40.refs_3_.mine_ref), channel_id=1, source_target_pairs={{0,1},{1,0},{2,3},{3,2},{4,5},{5,4},{6,7},{7,6},{8,9},{9,8},{10,11... | collective-permute-start | bytes 1990664 | tf_op jit(solution)/shard_map/ppermute | solution.py:508
  35.0 3.2 %collective-permute-start.5 = (bf16[640,512]{1,0:T(8,128)(2,1)S(1)}, bf16[640,512]{1,0:T(8,128)(2,1)S(1)}, u32[]{:S(2)}, u32[]{:S(2)}) collective-permute-start(bf16[640,512]{1,0:T(8,128)(2,1)S(1)} %shard_map.115.refs_3_), channel_id=1, source_target_pairs={{0,1},{1,0},{2,3},{3,2},{4,5},{5,4},{6,7},{7,6},{8,9},{9,8},{10,11... | collective-permute-start | bytes 1966088 | tf_op jit(solution)/shard_map/ppermute | solution.py:508
  36.6 17.0 %collective-permute-start.7 = (bf16[648,512]{1,0:T(8,128)(2,1)S(1)}, bf16[648,512]{1,0:T(8,128)(2,1)S(1)}, u32[]{:S(2)}, u32[]{:S(2)}) collective-permute-start(bf16[648,512]{1,0:T(8,128)(2,1)S(1)} %shard_map.117.refs_4_.mine_ref), channel_id=1, source_target_pairs={{0,2},{1,3},{2,0},{3,1},{4,6},{5,7},{6,4},{7,5},{8,10},{9,11},{10,... | collective-permute-start | bytes 1990664 | tf_op jit(solution)/shard_map/ppermute | solution.py:508

commit v6 on v5

--- a/solution.py
+++ b/solution.py
@@ -13,8 +13,13 @@
 LOG2E = 1.4426950408889634
 SEG_LANE = 24
 EXTRA = 8
+EARLY_ROWS = 384
+NEAR_PIECES = 4
+EARLY_LANES = 384
 VMEM = 16 * 1024 * 1024
 VMEM_ALL = 56 * 1024 * 1024
+CHEAP = pl.CostEstimate(flops=1000, bytes_accessed=1000, transcendentals=0)
+LONG = pl.CostEstimate(flops=4_000_000_000, bytes_accessed=1000, transcendentals=0)
 F32 = jnp.float32
 BF16 = jnp.bfloat16
 
@@ -45,7 +50,7 @@
     return odd, 1 - odd, far ^ 1, far, rank ^ 1, rank, place
 
 
-def call(body, args, out_shape, scratch=(), cost=0, after=None):
+def call(body, args, out_shape, scratch=(), after=None, cost=CHEAP):
     vm = pl.BlockSpec(memory_space=pltpu.VMEM)
     specs = [vm] * len(args)
     operands = list(args)
@@ -65,7 +70,7 @@
         out_shape=out_shape,
         scratch_shapes=list(scratch),
         compiler_params=pltpu.CompilerParams(vmem_limit_bytes=VMEM),
-        cost_estimate=pl.CostEstimate(flops=cost, bytes_accessed=1000, transcendentals=0),
+        cost_estimate=cost,
     )(*operands)
 
 
@@ -201,7 +206,7 @@
             pltpu.SemaphoreType.DMA((len(arrays),)),
         ],
         compiler_params=pltpu.CompilerParams(vmem_limit_bytes=VMEM_ALL),
-        cost_estimate=pl.CostEstimate(flops=4_000_000_000, bytes_accessed=1000, transcendentals=0),
+        cost_estimate=LONG,
     )(*arrays)
 
 
@@ -217,7 +222,7 @@
     size, lanes = mate.shape[0] - EXTRA, mate.shape[1]
 
     def body(
-        keep_ref, mate_ref, side_ref, cross_ref, send_ref, entry_ref, first_ref, total_ref, rows_ref
+        keep_ref, mate_ref, side_ref, cross_ref, early_ref, late_ref, entry_ref, first_ref, total_ref, rows_ref
     ):
         odd = position()[0] == 1
         upper = (position()[6] & 2) != 0
@@ -227,7 +232,7 @@
         nothing = (0.0, jnp.ones_like(total[1]), jnp.full_like(total[2], -1.0))
         entry = gather_level(upper, nothing, other)
         total = merged(upper, total, other)
-        pack(send_ref, total)
+        pack_both(early_ref, late_ref, total)
         entry_ref[...], total_ref[...] = entry[0], total[0]
         first_ref[...] = jnp.where(odd, mate[0], mine[0])
         rows = tuple(jnp.where(odd, m, o) for o, m in zip(mine[1:], mate[1:]))
@@ -236,44 +241,62 @@
     state = ((size, lanes), F32)
     return call(
         body, (keep, mate, side, cross),
-        shaped((mate.shape, BF16), state, state, state, ((8, lanes), F32)), after=after,
-    )
-
-
-def level_step(bit, final, got, entry, first, total, rows, after):
+        lane_parts(mate.shape) + shaped(state, state, state, ((8, lanes), F32)), after=after, cost=LONG,
+    )
+
+
+def pack_both(early_ref, late_ref, total):
+    edge = early_ref.shape[1]
+    pack(early_ref, tuple(t[:, :edge] for t in total))
+    pack(late_ref, tuple(t[:, edge:] for t in total))
+
+
+def lane_parts(shape):
+    rows, lanes = shape
+    return shaped(((rows, EARLY_LANES), BF16), ((rows, lanes - EARLY_LANES), BF16))
+
+
+def level_step(bit, early, late, entry, first, total, rows):
     size, lanes = entry.shape
 
     def body(
-        got_ref, entry_ref, first_ref, total_ref, rows_ref,
-        send_ref, one_ref, two_ref, three_ref,
+        early_ref, late_ref, entry_ref, first_ref, total_ref, rows_ref,
+        early_out, late_out, entry_out, first_out, total_out, rows_out,
     ):
         upper = (position()[6] & bit) != 0
-        other = unpack(got_ref)
-        old = (entry_ref[...], rows_ref[0:1], rows_ref[1:2])
-        new = gather_level(upper, old, other)
-        if final:
-            even = position()[0] == 0
-            last_first = rows_ref[3:4]
-            link = rows_ref[2:3] * (last_first == new[2]).astype(F32)
-            reached = first_ref[...] + link * new[0]
-            send_ref[...] = jnp.where(even, reached, new[0]).astype(BF16)
-            one_ref[...] = jnp.where(even, new[0], reached).astype(BF16)
-            prev = jnp.where(even, new[2], last_first)
-            two_ref[...] = jnp.broadcast_to(prev[:, 0:LANES], (8, LANES))
-            three_ref[...] = jnp.zeros_like(three_ref)
-        else:
-            held = (total_ref[...], rows_ref[4:5], rows_ref[5:6])
-            held = merged(upper, held, other)
-            pack(send_ref, held)
-            one_ref[...] = new[0]
-            two_ref[...] = held[0]
-            put_rows(three_ref, new[1:] + (rows_ref[2:3], rows_ref[3:4]) + held[1:])
-
-    if final:
-        out = shaped(((size, lanes), BF16), ((size, lanes), BF16), ((8, LANES), F32), ((8, LANES), F32))
-    else:
-        out = shaped((got.shape, BF16), ((size, lanes), F32), ((size, lanes), F32), ((8, lanes), F32))
-    return call(body, (got, entry, first, total, rows), out, after=after)
+        other = tuple(jnp.concatenate(pair, axis=1) for pair in zip(unpack(early_ref), unpack(late_ref)))
+        new = gather_level(upper, (entry_ref[...], rows_ref[0:1], rows_ref[1:2]), other)
+        held = merged(upper, (total_ref[...], rows_ref[4:5], rows_ref[5:6]), other)
+        pack_both(early_out, late_out, held)
+        entry_out[...], first_out[...], total_out[...] = new[0], first_ref[...], held[0]
+        put_rows(rows_out, new[1:] + (rows_ref[2:3], rows_ref[3:4]) + held[1:])
+
+    state = ((size, lanes), F32)
+    return call(
+        body, (early, late, entry, first, total, rows),
+        lane_parts((early.shape[0], lanes)) + shaped(state, state, state, ((8, lanes), F32)),
+    )
+
+
+def entry_step(bit, lanes, got, entry, first, rows, after=None):
+    size = entry.shape[0]
+    width = lanes.stop - lanes.start
+
+    def body(got_ref, entry_ref, first_ref, rows_ref, other_ref, keep_ref, prev_ref):
+        upper = (position()[6] & bit) != 0
+        even = position()[0] == 0
+        old = (entry_ref[:, lanes], rows_ref[0:1, lanes], rows_ref[1:2, lanes])
+        new = gather_level(upper, old, unpack(got_ref))
+        last_first = rows_ref[3:4, lanes]
+        link = rows_ref[2:3, lanes] * (last_first == new[2]).astype(F32)
+        reached = first_ref[:, lanes] + link * new[0]
+        other_ref[...] = jnp.where(even, reached, new[0]).astype(BF16)
+        keep_ref[...] = jnp.where(even, new[0], reached).astype(BF16)
+        prev = jnp.where(even, new[2], last_first)
+        prev_ref[...] = jnp.broadcast_to(prev[:, 0:LANES], (8, LANES))
+
+    block = ((size, width), BF16)
+    return call(body, (got, entry, first, rows), shaped(block, block, ((8, LANES), F32)), after=after)
 
 
 def local_part(heads, width, x, gate, read, write, stash, skip, after):
@@ -364,30 +387,33 @@
             pltpu.VMEM((blocks, GROUP, GROUP), F32), pltpu.VMEM((4, per * GROUP, GROUP), BF16),
             pltpu.VMEM((LANES, toks), F32), pltpu.VMEM((GROUP, LANES), F32), pltpu.VMEM((8, LANES), F32),
         ],
-        cost=8_000_000_000, after=after,
-    )
-
-
-def gated_tile(which, prev_ref, rd_ref, cum_ref, a_ref, b_ref, e_ref, gain_ref):
-    half_w = e_ref.shape[1]
-    here = pl.ds(pl.multiple_of(position()[which] * half_w, LANES), half_w)
+        after=after, cost=LONG,
+    )
+
+
+def gated_part(which, lanes, prev_ref, rd_ref, cum_ref, a_ref, b_ref, states, gain_ref):
+    half_w = a_ref.shape[1] // 2
+    first = pl.multiple_of(position()[which] * half_w + lanes.start, LANES)
+    here = pl.ds(first, lanes.stop - lanes.start)
     linked = cum_ref[:, SEG_LANE : SEG_LANE + 1] == prev_ref[0:1, 0:1]
     rm = jnp.where(linked, rd_ref[...].astype(F32), 0.0).astype(BF16)
-    gated = a_ref[:, here] + b_ref[:, here] * dot(rm, e_ref[...])
+    carried = [dot(rm, state[...]) for state in states]
+    carried = carried[0] if len(carried) == 1 else jnp.concatenate(carried, axis=1)
+    gated = a_ref[:, here] + b_ref[:, here] * carried
     sq = gated * gated
     part = sq[:, 0:LANES]
-    for i in range(1, half_w // LANES):
+    for i in range(1, sq.shape[1] // LANES):
         part = part + sq[:, i * LANES : (i + 1) * LANES]
     squares = jnp.sum(jnp.transpose(part), axis=0, keepdims=True)
     return (gated * gain_ref[:, here]).astype(BF16), squares
 
 
-def projected(which, quarter, w_ref, g):
-    half_w = g.shape[1]
-    cols = w_ref.shape[1] // 4
-    rows = pl.ds(pl.multiple_of(position()[which] * half_w, LANES), half_w)
-    columns = pl.ds(pl.multiple_of(position()[quarter] * cols, LANES), cols)
-    return dot(w_ref[rows, columns], g, ((0,), (1,)))
+def projected(which, lanes, quarter, rows, w_ref, g):
+    half_w, cols = w_ref.shape[0] // 2, w_ref.shape[1] // 4
+    here = pl.multiple_of(position()[which] * half_w + lanes.start, LANES)
+    first = pl.multiple_of(position()[2 + quarter] * cols + rows.start, LANES)
+    block = w_ref[pl.ds(here, lanes.stop - lanes.start), pl.ds(first, rows.stop - rows.start)]
+    return dot(block, g, ((0,), (1,)))
 
 
 def with_squares(y, squares):
@@ -404,61 +430,76 @@
     return whole[0:size], whole[size : size + 1] + (whole[size + 1 : size + 2] + whole[size + 2 : size + 3])
 
 
-def gated_first(prev, read, cum, a, b, e, gain, weight):
+def gated_sums(which, lanes, prev, read, cum, a, b, states, gain, weight, partial=None, squares=None):
     toks = a.shape[0]
-    half_w = e.shape[1]
-    feats = weight.shape[1]
-
-    def body(
-        prev_ref, rd_ref, cum_ref, a_ref, b_ref, e_ref, gain_ref, w_ref, g_ref, s_ref, y_ref
-    ):
-        g, s_ref[...] = gated_tile(0, prev_ref, rd_ref, cum_ref, a_ref, b_ref, e_ref, gain_ref)
+    cols = weight.shape[1] // 4
+    earlier = () if partial is None else (partial, squares)
+
+    def body(prev_ref, rd_ref, cum_ref, a_ref, b_ref, gain_ref, w_ref, *refs):
+        states = refs[: len(states_in)]
+        old, (g_ref, s_ref, y_ref) = refs[len(states_in) : -3], refs[-3:]
+        g, s = gated_part(which, lanes, prev_ref, rd_ref, cum_ref, a_ref, b_ref, states, gain_ref)
         g_ref[...] = g
-        for quarter in range(4):
-            y_ref[quarter] = projected(0, 2 + quarter, w_ref, g)
-
+        s_ref[...] = s + old[1][...] if old else s
+        for quarter in range(2):
+            y = projected(which, lanes, quarter, slice(0, cols), w_ref, g)
+            y_ref[quarter] = y + old[0][quarter] if old else y
+
+    states_in = states
     return call(
-        body, (prev, read, cum, a, b, e, gain, weight),
-        shaped(((toks, half_w), BF16), ((1, toks), F32), ((4, feats // 4, toks), F32)),
-        cost=2_000_000_000,
-    )
-
-
-def gated_second(prev, read, cum, a, b, e, gain, partial, s_first, weight):
+        body, (prev, read, cum, a, b, gain, weight, *states, *earlier),
+        shaped(((toks, lanes.stop - lanes.start), BF16), ((1, toks), F32), ((2, cols, toks), F32)),
+    )
+
+
+def gated_last(lanes, rows, prev, read, cum, a, b, state, gain, weight, partial, squares):
     toks = a.shape[0]
-    half_w = e.shape[1]
+
+    def body(prev_ref, rd_ref, cum_ref, a_ref, b_ref, e_ref, gain_ref, w_ref, p_ref, s_ref, g_ref, y_ref):
+        g, s = gated_part(1, lanes, prev_ref, rd_ref, cum_ref, a_ref, b_ref, (e_ref,), gain_ref)
+        g_ref[...] = g
+        y = p_ref[0, rows] + projected(1, lanes, 0, rows, w_ref, g)
+        y_ref[...] = with_squares(y, s_ref[...] + s)
+
+    return call(
+        body, (prev, read, cum, a, b, state, gain, weight, partial, squares),
+        shaped(((toks, lanes.stop - lanes.start), BF16), ((rows.stop - rows.start + EXTRA, toks), BF16)),
+    )
+
+
+def project_last(lanes, pieces, g, partial, weight, after):
+    def body(g_ref, p_ref, w_ref, *outs):
+        for (quarter, rows, dtype), y_ref in zip(pieces, outs):
+            y = p_ref[quarter, rows] + projected(1, lanes, quarter, rows, w_ref, g_ref[...])
+            y_ref[...] = y.astype(dtype)
+
+    toks = g.shape[0]
+    out = shaped(*[((rows.stop - rows.start, toks), dtype) for _, rows, dtype in pieces])
+    return call(body, (g, partial, weight), out, after=after)
+
+
+def project_whole(quarter, groups, gs, weight, pieces, adds=(), after=None):
     cols = weight.shape[1] // 4
-
-    def body(
-        prev_ref, rd_ref, cum_ref, a_ref, b_ref, e_ref, gain_ref, p_ref, sf_ref, w_ref, g_ref, y_ref
-    ):
-        g, squares = gated_tile(1, prev_ref, rd_ref, cum_ref, a_ref, b_ref, e_ref, gain_ref)
-        g_ref[...] = g
-        y_ref[...] = with_squares(p_ref[0] + projected(1, 2, w_ref, g), sf_ref[...] + squares)
-
-    return call(
-        body, (prev, read, cum, a, b, e, gain, partial, s_first, weight),
-        shaped(((toks, half_w), BF16), ((cols + EXTRA, toks), BF16)), cost=1_000_000_000,
-    )
-
-
-def project_rest(quarter, dtype, cost, g, partial, weight, after, add=None):
-    toks = g.shape[0]
-    block = (weight.shape[1] // 4, toks)
-
-    def body(g_ref, p_ref, w_ref, *refs):
-        y = p_ref[quarter] + projected(1, 2 + quarter, w_ref, g_ref[...])
-        if add is not None:
-            y = y + refs[0][...].astype(F32)
-        refs[-1][...] = y.astype(dtype)
-
-    more = () if add is None else (add,)
-    return call(
-        body, (g, partial, weight, *more), jax.ShapeDtypeStruct(block, dtype), cost=cost, after=after
-    )
-
-
-def add_far(y_far, to_near, got_near):
+    toks = gs[0].shape[0]
+    step = cols // pieces
+
+    def body(w_ref, *refs):
+        g_refs, add_refs, outs = refs[: len(gs)], refs[len(gs) : len(gs) + len(adds)], refs[len(gs) + len(adds) :]
+        y = sum(
+            projected(which, lanes, quarter, slice(0, cols), w_ref, g_ref[...])
+            for (which, lanes), g_ref in zip(groups, g_refs)
+        )
+        if add_refs:
+            outs[0][...] = y + jnp.concatenate([r[...].astype(F32) for r in add_refs], axis=0)
+        else:
+            for k, y_ref in enumerate(outs):
+                y_ref[...] = y[k * step : (k + 1) * step].astype(BF16)
+
+    out = shaped(((cols, toks), F32)) if adds else shaped(*[((step, toks), BF16)] * pieces)
+    return call(body, (weight, *gs, *adds), out, after=after)
+
+
+def add_first(y_far, to_near, got_near):
     def body(y_ref, mine_ref, got_ref, out_ref):
         got, squares = split_squares(got_ref)
         out_ref[...] = with_squares(y_ref[...] + got, split_squares(mine_ref)[1] + squares)
@@ -466,32 +507,48 @@
     return call(body, (y_far, to_near, got_near), jax.ShapeDtypeStruct(got_near.shape, BF16))
 
 
-def finish(features, y_own, to_far, got_far):
+def add_second(y_far, got_near, after):
+    def body(y_ref, got_ref, out_ref):
+        out_ref[...] = (y_ref[...] + got_ref[...].astype(F32)).astype(BF16)
+
+    return call(body, (y_far, got_near), jax.ShapeDtypeStruct(got_near.shape, BF16), after=after)
+
+
+def finish(rows, y_own, inputs, out=None, features=None):
     size, toks = y_own.shape
-    parts = 4
-    step = size // parts
-
-    def body(own_ref, mine_ref, far_ref, out_hbm, out_ref, sems):
-        squares = split_squares(mine_ref)[1] + split_squares(far_ref)[1]
-        inv = lax.rsqrt(squares / features + EPS)
+    parts = 2
+    step = (rows.stop - rows.start) // parts
+    first = out is None
+
+    def body(own_ref, far_ref, factor_ref, *refs):
+        out_hbm, *more, out_ref, sems = refs if first else refs[1:]
+        if first:
+            inv = lax.rsqrt((split_squares(factor_ref)[1] + split_squares(far_ref)[1]) / features + EPS)
+            more[0][...] = inv
+        else:
+            inv = factor_ref[...]
         copies = []
         for k in range(parts):
-            rows = slice(k * step, (k + 1) * step)
-            out_ref[rows] = ((own_ref[rows] + far_ref[rows].astype(F32)) * inv).astype(BF16)
-            copies.append(pltpu.make_async_copy(out_ref.at[rows], out_hbm.at[rows], sems.at[k]))
+            here = slice(k * step, (k + 1) * step)
+            there = slice(rows.start + here.start, rows.start + here.stop)
+            out_ref[here] = ((own_ref[there] + far_ref[here].astype(F32)) * inv).astype(BF16)
+            copies.append(pltpu.make_async_copy(out_ref.at[here], out_hbm.at[there], sems.at[k]))
             copies[-1].start()
         for copy in copies:
             copy.wait()
 
-    vm = pl.BlockSpec(memory_space=pltpu.VMEM)
+    vm, where = pl.BlockSpec(memory_space=pltpu.VMEM), pl.BlockSpec(memory_space=pl.ANY)
+    result = jax.ShapeDtypeStruct((size, toks), BF16)
     return pl.pallas_call(
         body,
-        in_specs=[vm] * 3,
-        out_specs=pl.BlockSpec(memory_space=pl.ANY),
-        out_shape=jax.ShapeDtypeStruct((size, toks), BF16),
-        scratch_shapes=[pltpu.VMEM((size, toks), BF16), pltpu.SemaphoreType.DMA((parts,))],
+        in_specs=[vm] * 3 + ([] if first else [where]),
+        out_specs=[where, vm] if first else where,
+        out_shape=[result, jax.ShapeDtypeStruct((1, toks), F32)] if first else result,
+        scratch_shapes=[pltpu.VMEM((rows.stop - rows.start, toks), BF16), pltpu.SemaphoreType.DMA((parts,))],
+        input_output_aliases={} if first else {3: 0},
         compiler_params=pltpu.CompilerParams(vmem_limit_bytes=VMEM),
-    )(y_own, to_far, got_far)
+        cost_estimate=CHEAP,
+    )(y_own, *inputs, *(() if first else (out,)))
 
 
 def on_device(
@@ -518,25 +575,42 @@
         heads, width, head_input, gate_input, read_vecs, write_vecs, stash,
         skip_gain.reshape(1, heads), None,
     )
-    sent, entry, first, total, rows = pair_step(send_keep, mate, side, cross, a)
+    early, late, entry, first, total, rows = pair_step(send_keep, mate, side, cross, a)
     bit = 4
     while 2 * bit < n_seq:
-        sent, entry, total, rows = level_step(bit, False, swap(sent, bit), entry, first, total, rows, None)
+        early, late, entry, first, total, rows = level_step(
+            bit, swap(early, bit), swap(late, bit), entry, first, total, rows
+        )
         bit *= 2
-    sent, e_keep, prev, _ = level_step(bit, True, swap(sent, bit), entry, first, total, rows, None)
-    e_other = swap(sent, 1)
+    half_w = feats // 2
+    quarter = out_weight.shape[1] // 4
+    one, two, half = slice(0, EARLY_LANES), slice(EARLY_LANES, half_w), slice(0, half_w)
+    top, rest, every = slice(0, EARLY_ROWS), slice(EARLY_ROWS, quarter), slice(0, quarter)
+    got_early, got_late = swap(early, bit), swap(late, bit)
+    send_one, keep_one, prev = entry_step(bit, one, got_early, entry, first, rows)
+    other_one = swap(send_one, 1)
+    send_two, keep_two, _ = entry_step(bit, two, got_late, entry, first, rows, send_one)
+    other_two = swap(send_two, 1)
     gain = norm_gain.reshape(1, feats)
     shared = (prev, read_vecs, log_cum, a, b)
-    g_keep, s_keep, partial = gated_first(*shared, e_keep, gain, out_weight)
-    g_other, to_near = gated_second(*shared, e_other, gain, partial, s_keep, out_weight)
-    got_near = across(to_near, 1)
-    y_near = project_rest(2, BF16, 500_000_000, g_other, partial, out_weight, to_near)
-    got_own = across(y_near, 1)
-    y_far = project_rest(1, F32, 500_000_000, g_other, partial, out_weight, y_near)
-    to_far = add_far(y_far, to_near, got_near)
-    got_far = across(to_far, 2)
-    y_own = project_rest(3, F32, 10_000_000_000, g_other, partial, out_weight, to_far, got_own)
-    return finish(feats * n_tp, y_own, to_far, got_far)
+    g_keep, squares, partial = gated_sums(0, half, *shared, (keep_one, keep_two), gain, out_weight)
+    g_one, squares, partial = gated_sums(1, one, *shared, (other_one,), gain, out_weight, partial, squares)
+    g_two, near_top = gated_last(two, top, *shared, other_two, gain, out_weight, partial, squares)
+    got_top = across(near_top, 1)
+    near_rest, far_top, far_rest = project_last(
+        two, ((0, rest, BF16), (1, top, F32), (1, rest, F32)), g_two, partial, out_weight, near_top
+    )
+    got_rest = across(near_rest, 1)
+    to_far_top = add_first(far_top, near_top, got_top)
+    got_far_top = across(to_far_top, 2)
+    to_far_rest = add_second(far_rest, got_rest, to_far_top)
+    got_far_rest = across(to_far_rest, 2)
+    groups, gs = ((0, half), (1, one), (1, two)), (g_keep, g_one, g_two)
+    y_near = project_whole(2, groups, gs, out_weight, NEAR_PIECES, after=to_far_rest)
+    got_own = tuple(across(piece, 1) for piece in y_near)
+    (y_own,) = project_whole(3, groups, gs, out_weight, 1, got_own)
+    out, inv = finish(top, y_own, (got_far_top, to_far_top), features=feats * n_tp)
+    return finish(rest, y_own, (got_far_rest, inv), out)
 
 
 def solution(mesh):

time: 54.6 us -> 53.4 us (0.978)
  waiting for transfers between devices: 27.5 us -> 21.8 us
  starting transfers between devices: 10.5 us -> 13.4 us
  Pallas kernels: 15.2 us -> 16.9 us
    ppermute x3 -> x8, waiting for transfers between devices: 14.8 us -> 11.3 us  [across(): return lax.ppermute(a, 'tp', [(i, i ^ bit) for i in range(n_tp)])]
    ppermute x5 -> x7, waiting for transfers between devices: 12.7 us -> 10.4 us  [swap(): return lax.ppermute(a, 'seq', [(i, i ^ bit) for i in range(n_seq)])]
    ppermute x5 -> x7, starting transfers between devices: 8.29 us -> 9.72 us  [swap(): return lax.ppermute(a, 'seq', [(i, i ^ bit) for i in range(n_seq)])]
    ppermute x3 -> x8, starting transfers between devices: 2.24 us -> 3.66 us  [across(): return lax.ppermute(a, 'tp', [(i, i ^ bit) for i in range(n_tp)])]
    pallas_call x9 -> x12, Pallas kernels: 11.1 us -> 12.1 us  [call(): pl.pallas_call(kernel, in_specs=specs, out_specs=jax.tree.map(lambda _: v...]
    pallas_call x1 -> x2, Pallas kernels: 0.92 us -> 1.58 us  [finish(): pl.pallas_call(body, in_specs=[vm] * 3 + ([] if first else [where]), out_...]
  transfers between devices with their start and end apart: 8 -> 15, of which waited for: 5 -> 10; matrix products, arithmetic and copies ran while one was open for 0% -> 0% of each run, Pallas kernels for 16% -> 21%
where the time goes in v6:
time: 53.4 us; the launch traced here: 53.2 us
  waiting for transfers between devices  21.8 us (41%)
  Pallas kernels  16.9 us (32%)
  starting transfers between devices  13.4 us (25%)
  local copies, waits for them, and re-layouts  0.94 us (2%)
    pallas_call x12, Pallas kernels, call(): pl.pallas_call(kernel, in_specs=specs, out_specs=jax.tree.map(lambda _: v...  12.1 us
    ppermute x8, waiting for transfers between devices, across(): return lax.ppermute(a, 'tp', [(i, i ^ bit) for i in range(n_tp)])  11.3 us
    ppermute x7, waiting for transfers between devices, swap(): return lax.ppermute(a, 'seq', [(i, i ^ bit) for i in range(n_seq)])  10.4 us
    ppermute x7, starting transfers between devices, swap(): return lax.ppermute(a, 'seq', [(i, i ^ bit) for i in range(n_seq)])  9.72 us
    ppermute x8, starting transfers between devices, across(): return lax.ppermute(a, 'tp', [(i, i ^ bit) for i in range(n_tp)])  3.66 us
    pallas_call x1, Pallas kernels, prepare(): pl.pallas_call(body, in_specs=[pl.BlockSpec(memory_space=pltpu.HBM)] * le...  3.29 us
    pallas_call x2, Pallas kernels, finish(): pl.pallas_call(body, in_specs=[vm] * 3 + ([] if first else [where]), out_...  1.58 us
  transfers between devices with their start and end apart: 15, of which 10 were waited for; matrix products, arithmetic and copies ran while one was open for 0% of the time, Pallas kernels for 21%

profile of v6, /device:TPU:0, one launch (start us, length us, event | category | flops | bytes accessed | tf_op | source)
XLA Modules:
  0.0 53.2 jit_solution(11903568699990577874)
XLA Ops:
  0.0 3.3 %shard_map.109 = (bf16[136,640]{1,0:T(8,128)(2,1)}, bf16[136,640]{1,0:T(8,128)(2,1)}, f32[64,512]{1,0:T(8,128)}) custom-call(bf16[20,512]{1,0:T(8,128)(2,1)} %refs_0_.2, s32[1,512]{1,0:T(1,128)} %bitcast.7, f32[1,20]{1,0:T(1,128)} %bitcast.8, f32[1,20]{1,0:T(1,128)} %bitcast.9, bf16[512,128]{1,0:T(8,128)(2,1)} %wr_ref.1, bf16[512,1280]{1,0:T(8,128)(2,1)} %x_ref.1), custom_call_target="tpu_custom_call" | custom-call | flops 4000000000 | bytes 1000 | tf_op jit(solution)/shard_map/pallas_call | solution.py:198
  3.3 4.1 %collective-permute-start.2 = (bf16[136,640]{1,0:T(8,128)(2,1)}, bf16[136,640]{1,0:T(8,128)(2,1)S(1)}, u32[]{:S(2)}, u32[]{:S(2)}) collective-permute-start(bf16[136,640]{1,0:T(8,128)(2,1)} %get-tuple-element.39), channel_id=1, source_target_pairs={{0,12},{4,8},{8,4},{12,0},{16,28},{20,24},{24,20},{28,16},{1,13},{... | collective-permute-start | bytes 522248 | tf_op jit(solution)/shard_map/ppermute | solution.py:562
  7.4 0.5 collective-permute-start
  7.9 0.1 collective-permute-start.1
  8.0 0.9 %copy-done.6 = f32[64,512]{1,0:T(8,128)S(1)} copy-done((f32[64,512]{1,0:T(8,128)S(1)}, f32[64,512]{1,0:T(8,128)}, u32[]{:S(2)}) %copy-start.6) | copy-done | bytes 131096
  8.9 3.9 %shard_map.110 = (f32[512,1280]{1,0:T(8,128)S(1)}, f32[512,1280]{1,0:T(8,128)S(1)}, f32[512,128]{1,0:T(8,128)S(1)}) custom-call(bf16[512,1280]{1,0:T(8,128)(2,1)S(1)} %copy-done.1, bf16[512,1280]{1,0:T(8,128)(2,1)S(1)} %copy-done.2, bf16[512,128]{1,0:T(8,128)(2,1)S(1)} %copy-done, bf16[512,128]{1,0:T(8,128)(2,1)S(1)} %copy-done.4, f32[64,512]{1,0:T(8,128)S(1)} %copy-done.6, ...), custom_call_target="tpu_custom_call" | custom-call | flops 4000000000 | bytes 1000 | tf_op jit(solution)/shard_map/pallas_call | solution.py:66
  12.9 3.1 %collective-permute-done.1.refs_2_ = bf16[136,640]{1,0:T(8,128)(2,1)S(1)} collective-permute-done((bf16[136,640]{1,0:T(8,128)(2,1)}, bf16[136,640]{1,0:T(8,128)(2,1)S(1)}, u32[]{:S(2)}, u32[]{:S(2)}) %collective-permute-start.1) | collective-permute-done | bytes 174112 | tf_op jit(solution)/shard_map/ppermute | solution.py:562
  15.9 0.0 collective-permute-done.2.refs_3_
  15.9 0.0 collective-permute-done.refs_1_
  16.0 0.0 copy-start.7
  16.0 0.0 slice-start.1
  16.0 0.9 %shard_map.111 = (bf16[136,384]{1,0:T(8,128)(2,1)S(1)}, bf16[136,256]{1,0:T(8,128)(2,1)S(1)}, f32[128,640]{1,0:T(8,128)S(1)}, f32[128,640]{1,0:T(8,128)S(1)}, f32[128,640]{1,0:T(8,128)}, /*index=5*/f32[8,640]{1,0:T(8,128)S(1)}) custom-call(bf16[136,640]{1,0:T(8,128)(2,1)S(1)} %copy-done.3, bf16[136,640]{1,0:T(8,128)(2,1)S(1)} %collective-permute-done.refs_1_, ...), custom_call_target="tpu_custom_call" | custom-call | flops 4000000000 | bytes 1000 | tf_op jit(solution)/shard_map/pallas_call | solution.py:66
  16.9 2.6 %collective-permute-start.3 = (bf16[136,384]{1,0:T(8,128)(2,1)S(1)}, bf16[136,384]{1,0:T(8,128)(2,1)S(1)}, u32[]{:S(2)}, u32[]{:S(2)}) collective-permute-start(bf16[136,384]{1,0:T(8,128)(2,1)S(1)} %get-tuple-element.42), channel_id=1, source_target_pairs={{0,16},{4,20},{8,24},{12,28},{16,0},{20,4},{24,8},{28,12},{1,17},{... | collective-permute-start | bytes 313352 | tf_op jit(solution)/shard_map/ppermute | solution.py:562
  19.5 0.3 collective-permute-start.4
  19.8 7.1 %collective-permute-done.3.got_ref = bf16[136,384]{1,0:T(8,128)(2,1)S(1)} collective-permute-done((bf16[136,384]{1,0:T(8,128)(2,1)S(1)}, bf16[136,384]{1,0:T(8,128)(2,1)S(1)}, u32[]{:S(2)}, u32[]{:S(2)}) %collective-permute-start.3) | collective-permute-done | bytes 104480 | tf_op jit(solution)/shard_map/ppermute | solution.py:562
  26.9 0.1 shard_map.112
  27.0 0.7 %collective-permute-start.5 = (bf16[128,384]{1,0:T(8,128)(2,1)S(1)}, bf16[128,384]{1,0:T(8,128)(2,1)S(1)}, u32[]{:S(2)}, u32[]{:S(2)}) collective-permute-start(bf16[128,384]{1,0:T(8,128)(2,1)S(1)} %get-tuple-element.51.refs_4_), channel_id=1, source_target_pairs={{0,4},{4,0},{8,12},{12,8},{16,20},{20,16},{24,28},{28,24},{1,5},{5... | collective-permute-start | bytes 294920 | tf_op jit(solution)/shard_map/ppermute | solution.py:562
  27.7 0.0 collective-permute-done.4.refs_0_
  27.7 0.6 %shard_map.113 = (bf16[128,256]{1,0:T(8,128)(2,1)S(1)}, bf16[128,256]{1,0:T(8,128)(2,1)S(1)}, f32[8,128]{1,0:T(8,128)}) custom-call(bf16[136,256]{1,0:T(8,128)(2,1)S(1)} %collective-permute-done.4.refs_0_, f32[128,640]{1,0:T(8,128)S(1)} %get-tuple-element.43.entry_ref.refs_1_, f32[128,640]{1,0:T(8,128)S(1)} %get-tuple-element.44.first_ref.refs_2_, ...), custom_call_target="tpu_custom_call" | custom-call | flops 1000 | bytes 1000 | tf_op jit(solution)/shard_map/pallas_call | solution.py:66
  28.3 1.4 %collective-permute-start.6 = (bf16[128,256]{1,0:T(8,128)(2,1)S(1)}, bf16[128,256]{1,0:T(8,128)(2,1)S(1)}, u32[]{:S(2)}, u32[]{:S(2)}) collective-permute-start(bf16[128,256]{1,0:T(8,128)(2,1)S(1)} %get-tuple-element.57), channel_id=1, source_target_pairs={{0,4},{4,0},{8,12},{12,8},{16,20},{20,16},{24,28},{28,24},{1,5},{5... | collective-permute-start | bytes 196616 | tf_op jit(solution)/shard_map/ppermute | solution.py:562
  29.7 1.7 %shard_map.114 = (bf16[512,640]{1,0:T(8,128)(2,1)S(1)}, f32[1,512]{1,0:T(1,128)S(1)}, f32[2,640,512]{2,1,0:T(8,128)S(1)}) custom-call(f32[8,128]{1,0:T(8,128)S(1)} %get-tuple-element.46.prev_ref, bf16[512,128]{1,0:T(8,128)(2,1)S(1)} %copy-done, f32[512,128]{1,0:T(8,128)S(1)} %get-tuple-element.47.cum_ref, f32[512,1280]{1,0:T(8,128)S(1)} %get-tuple-element.41.refs_4_.a_ref, ...), custom_call_target="tpu_custom_call" | custom-call | flops 1000 | bytes 1000 | tf_op jit(solution)/shard_map/pallas_call | solution.py:66
  31.4 0.3 collective-permute-done.5.refs_0_
  31.7 1.2 %shard_map.115 = (bf16[512,384]{1,0:T(8,128)(2,1)S(1)}, f32[1,512]{1,0:T(1,128)S(1)}, f32[2,640,512]{2,1,0:T(8,128)S(1)}) custom-call(f32[8,128]{1,0:T(8,128)S(1)} %get-tuple-element.46.prev_ref, bf16[512,128]{1,0:T(8,128)(2,1)S(1)} %copy-done, f32[512,128]{1,0:T(8,128)S(1)} %get-tuple-element.47.cum_ref, f32[512,1280]{1,0:T(8,128)S(1)} %get-tuple-element.41.refs_4_.a_ref, ...), custom_call_target="tpu_custom_call" | custom-call | flops 1000 | bytes 1000 | tf_op jit(solution)/shard_map/pallas_call | solution.py:66
  32.9 0.0 collective-permute-done.6.e_ref
  32.9 0.6 %shard_map.116 = (bf16[512,256]{1,0:T(8,128)(2,1)S(1)}, bf16[392,512]{1,0:T(8,128)(2,1)S(1)}) custom-call(f32[8,128]{1,0:T(8,128)S(1)} %get-tuple-element.46.prev_ref, bf16[512,128]{1,0:T(8,128)(2,1)S(1)} %copy-done, f32[512,128]{1,0:T(8,128)S(1)} %get-tuple-element.47.cum_ref, f32[512,1280]{1,0:T(8,128)S(1)} %get-tuple-element.41.refs_4_.a_ref, ...), custom_call_target="tpu_custom_call" | custom-call | flops 1000 | bytes 1000 | tf_op jit(solution)/shard_map/pallas_call | solution.py:66
  33.6 0.1 collective-permute-start.8
  33.6 0.4 shard_map.117
  34.1 0.6 %collective-permute-start.7 = (bf16[256,512]{1,0:T(8,128)(2,1)S(1)}, bf16[256,512]{1,0:T(8,128)(2,1)S(1)}, u32[]{:S(2)}, u32[]{:S(2)}) collective-permute-start(bf16[256,512]{1,0:T(8,128)(2,1)S(1)} %get-tuple-element.63), channel_id=1, source_target_pairs={{0,1},{1,0},{2,3},{3,2},{4,5},{5,4},{6,7},{7,6},{8,9},{9,8},{10,11... | collective-permute-start | bytes 786440 | tf_op jit(solution)/shard_map/ppermute | solution.py:565
  34.7 0.7 %collective-permute-done.8.got_ref = bf16[392,512]{1,0:T(8,128)(2,1)S(1)} collective-permute-done((bf16[392,512]{1,0:T(8,128)(2,1)S(1)}, bf16[392,512]{1,0:T(8,128)(2,1)S(1)}, u32[]{:S(2)}, u32[]{:S(2)}) %collective-permute-start.8) | collective-permute-done | bytes 401440 | tf_op jit(solution)/shard_map/ppermute | solution.py:565
  35.4 0.1 shard_map.118.refs_2_.factor_ref
  35.5 1.7 %collective-permute-start.14 = (bf16[392,512]{1,0:T(8,128)(2,1)S(1)}, bf16[392,512]{1,0:T(8,128)(2,1)S(1)}, u32[]{:S(2)}, u32[]{:S(2)}) collective-permute-start(bf16[392,512]{1,0:T(8,128)(2,1)S(1)} %shard_map.118.refs_2_.factor_ref), channel_id=1, source_target_pairs={{0,2},{1,3},{2,0},{3,1},{4,6},{5,7},{6,4},{7,5},{8,10},{9,11},{10,... | collective-permute-start | bytes 1204232 | tf_op jit(solution)/shard_map/ppermute | solution.py:565
  37.1 0.0 collective-permute-done.7.refs_1_
  37.1 0.1 shard_map.119.refs_4_
  37.2 1.2 %shard_map.120 = (bf16[160,512]{1,0:T(8,128)(2,1)S(1)}, bf16[160,512]{1,0:T(8,128)(2,1)S(1)}, bf16[160,512]{1,0:T(8,128)(2,1)S(1)}, bf16[160,512]{1,0:T(8,128)(2,1)S(1)}) custom-call(bf16[1280,2560]{1,0:T(8,128)(2,1)S(1)} %bitcast.5, bf16[512,640]{1,0:T(8,128)(2,1)S(1)} %get-tuple-element.53.refs_1_.refs_0_, ...), custom_call_target="tpu_custom_call" | custom-call | flops 1000 | bytes 1000 | tf_op jit(solution)/shard_map/pallas_call | solution.py:66
  38.4 0.1 collective-permute-start.9
  38.5 0.6 %collective-permute-start.13 = (bf16[256,512]{1,0:T(8,128)(2,1)S(1)}, bf16[256,512]{1,0:T(8,128)(2,1)S(1)}, u32[]{:S(2)}, u32[]{:S(2)}) collective-permute-start(bf16[256,512]{1,0:T(8,128)(2,1)S(1)} %shard_map.119.refs_4_), channel_id=1, source_target_pairs={{0,2},{1,3},{2,0},{3,1},{4,6},{5,7},{6,4},{7,5},{8,10},{9,11},{10,... | collective-permute-start | bytes 786440 | tf_op jit(solution)/shard_map/ppermute | solution.py:565
  39.1 0.0 collective-permute-start.10
  39.1 0.5 collective-permute-start.11
  39.7 0.2 collective-permute-done.9.refs_3_
  39.9 0.1 collective-permute-start.12
  40.0 0.5 collective-permute-done.10.refs_4_
  40.5 0.2 collective-permute-done.11.refs_5_
  40.8 0.5 collective-permute-done.12.refs_6_
  41.3 1.2 %shard_map.121.own_ref = f32[640,512]{1,0:T(8,128)S(1)} custom-call(bf16[1280,2560]{1,0:T(8,128)(2,1)S(1)} %bitcast.5, bf16[512,640]{1,0:T(8,128)(2,1)S(1)} %get-tuple-element.53.refs_1_.refs_0_, bf16[512,384]{1,0:T(8,128)(2,1)S(1)} %get-tuple-element.56.refs_2_.refs_1_, bf16[512,256]{1,0:T(8,128)(2,1)S(1)} %get-tuple-element.60.refs_0_.refs_3_.refs_2_, ...), custom_call_target="tpu_custom_call" | custom-call | flops 1000 | bytes 1000 | tf_op jit(solution)/shard_map/pallas_call | solution.py:66
  42.5 5.2 %collective-permute-done.14.far_ref = bf16[392,512]{1,0:T(8,128)(2,1)S(1)} collective-permute-done((bf16[392,512]{1,0:T(8,128)(2,1)S(1)}, bf16[392,512]{1,0:T(8,128)(2,1)S(1)}, u32[]{:S(2)}, u32[]{:S(2)}) %collective-permute-start.14) | collective-permute-done | bytes 401440 | tf_op jit(solution)/shard_map/ppermute | solution.py:565
  47.7 0.8 %shard_map.122 = (bf16[640,512]{1,0:T(8,128)(2,1)}, f32[1,512]{1,0:T(1,128)S(1)}) custom-call(f32[640,512]{1,0:T(8,128)S(1)} %shard_map.121.own_ref, bf16[392,512]{1,0:T(8,128)(2,1)S(1)} %collective-permute-done.14.far_ref, bf16[392,512]{1,0:T(8,128)(2,1)S(1)} %shard_map.118.refs_2_.factor_ref), custom_call_target="tpu_custom_call" | custom-call | flops 1000 | bytes 1000 | tf_op jit(solution)/shard_map/pallas_call | solution.py:542
  48.5 4.0 %collective-permute-done.13.far_ref = bf16[256,512]{1,0:T(8,128)(2,1)S(1)} collective-permute-done((bf16[256,512]{1,0:T(8,128)(2,1)S(1)}, bf16[256,512]{1,0:T(8,128)(2,1)S(1)}, u32[]{:S(2)}, u32[]{:S(2)}) %collective-permute-start.13) | collective-permute-done | bytes 262176 | tf_op jit(solution)/shard_map/ppermute | solution.py:565
  52.5 0.8 %shard_map.123 = bf16[640,512]{1,0:T(8,128)(2,1)} custom-call(f32[640,512]{1,0:T(8,128)S(1)} %shard_map.121.own_ref, bf16[256,512]{1,0:T(8,128)(2,1)S(1)} %collective-permute-done.13.far_ref, f32[1,512]{1,0:T(1,128)S(1)} %get-tuple-element.69.factor_ref, bf16[640,512]{1,0:T(8,128)(2,1)} %get-tuple-element.70.refs_0_), custom_call_target="tpu_custom_call", output_to_operand_aliasing={{}: (3, {})} | custom-call | flops 1000 | bytes 1000 | tf_op jit(solution)/shard_map/pallas_call | solution.py:542
  (19 shorter events, 0.0 us)
Async XLA Ops:
  0.0 8.0 %copy-start = (bf16[512,128]{1,0:T(8,128)(2,1)S(1)}, bf16[512,128]{1,0:T(8,128)(2,1)}, u32[]{:S(2)}) copy-start(bf16[512,128]{1,0:T(8,128)(2,1)} %rd_ref.7) | copy-start | bytes 393220
  0.0 8.0 %copy-start.1 = (bf16[512,1280]{1,0:T(8,128)(2,1)S(1)}, bf16[512,1280]{1,0:T(8,128)(2,1)}, u32[]{:S(2)}) copy-start(bf16[512,1280]{1,0:T(8,128)(2,1)} %x_ref.1) | copy-start | bytes 3932164
  0.0 8.0 %copy-start.2 = (bf16[512,1280]{1,0:T(8,128)(2,1)S(1)}, bf16[512,1280]{1,0:T(8,128)(2,1)}, u32[]{:S(2)}) copy-start(bf16[512,1280]{1,0:T(8,128)(2,1)} %gate_ref.1) | copy-start | bytes 3932164
  0.0 8.0 %copy-start.4 = (bf16[512,128]{1,0:T(8,128)(2,1)S(1)}, bf16[512,128]{1,0:T(8,128)(2,1)}, u32[]{:S(2)}) copy-start(bf16[512,128]{1,0:T(8,128)(2,1)} %wr_ref.1) | copy-start | bytes 393220
  0.0 8.0 %copy-start.5 = (f32[20]{0:T(128)S(1)}, f32[20]{0:T(128)}, u32[]{:S(2)}) copy-start(f32[20]{0:T(128)} %param.19) | copy-start | bytes 244
  3.3 12.6 %collective-permute-start.2 = (bf16[136,640]{1,0:T(8,128)(2,1)}, bf16[136,640]{1,0:T(8,128)(2,1)S(1)}, u32[]{:S(2)}, u32[]{:S(2)}) collective-permute-start(bf16[136,640]{1,0:T(8,128)(2,1)} %get-tuple-element.39), channel_id=1, source_target_pairs={{0,12},{4,8},{8,4},{12,0},{16,28},{20,24},{24,20},{28,16},{1,13},{... | collective-permute-start | bytes 522248 | tf_op jit(solution)/shard_map/ppermute | solution.py:562
  7.4 8.6 %collective-permute-start = (bf16[136,640]{1,0:T(8,128)(2,1)}, bf16[136,640]{1,0:T(8,128)(2,1)S(1)}, u32[]{:S(2)}, u32[]{:S(2)}) collective-permute-start(bf16[136,640]{1,0:T(8,128)(2,1)} %get-tuple-element.39), channel_id=1, source_target_pairs={{0,4},{4,0},{8,12},{12,8},{16,20},{20,16},{24,28},{28,24},{1,5},{5... | collective-permute-start | bytes 522248 | tf_op jit(solution)/shard_map/ppermute | solution.py:562
  7.9 8.1 %collective-permute-start.1 = (bf16[136,640]{1,0:T(8,128)(2,1)}, bf16[136,640]{1,0:T(8,128)(2,1)S(1)}, u32[]{:S(2)}, u32[]{:S(2)}) collective-permute-start(bf16[136,640]{1,0:T(8,128)(2,1)} %get-tuple-element.38.refs_0_), channel_id=1, source_target_pairs={{0,8},{4,12},{8,0},{12,4},{16,24},{20,28},{24,16},{28,20},{1,9},{5... | collective-permute-start | bytes 522248 | tf_op jit(solution)/shard_map/ppermute | solution.py:562
  8.0 0.9 %copy-start.6 = (f32[64,512]{1,0:T(8,128)S(1)}, f32[64,512]{1,0:T(8,128)}, u32[]{:S(2)}) copy-start(f32[64,512]{1,0:T(8,128)} %get-tuple-element.40.stash_ref) | copy-start | bytes 393220
  8.9 7.0 %copy-start.3 = (bf16[136,640]{1,0:T(8,128)(2,1)S(1)}, bf16[136,640]{1,0:T(8,128)(2,1)}, u32[]{:S(2)}) copy-start(bf16[136,640]{1,0:T(8,128)(2,1)} %get-tuple-element.38.refs_0_) | copy-start | bytes 522244
  15.9 13.8 %slice-start = ((s8[6553600]{0:T(1024)(128)(4,1)}), s8[4194304]{0:T(1024)(128)(4,1)S(1)}, s32[]{:S(2)}) async-start(s8[6553600]{0:T(1024)(128)(4,1)} %bitcast.4), calls=%async_computation | async-start | bytes 8388608
  16.0 13.7 %copy-start.7 = (f32[1280]{0:T(1024)S(1)}, f32[1280]{0:T(1024)}, u32[]{:S(2)}) copy-start(f32[1280]{0:T(1024)} %param.20) | copy-start | bytes 15364
  16.0 13.7 %slice-start.1 = ((s8[6553600]{0:T(1024)(128)(4,1)}), s8[2359296]{0:T(1024)(128)(4,1)S(1)}, s32[]{:S(2)}) async-start(s8[6553600]{0:T(1024)(128)(4,1)} %bitcast.4), calls=%async_computation.1 | async-start | bytes 4718592
  16.9 10.0 %collective-permute-start.3 = (bf16[136,384]{1,0:T(8,128)(2,1)S(1)}, bf16[136,384]{1,0:T(8,128)(2,1)S(1)}, u32[]{:S(2)}, u32[]{:S(2)}) collective-permute-start(bf16[136,384]{1,0:T(8,128)(2,1)S(1)} %get-tuple-element.42), channel_id=1, source_target_pairs={{0,16},{4,20},{8,24},{12,28},{16,0},{20,4},{24,8},{28,12},{1,17},{... | collective-permute-start | bytes 313352 | tf_op jit(solution)/shard_map/ppermute | solution.py:562
  19.5 8.2 %collective-permute-start.4 = (bf16[136,256]{1,0:T(8,128)(2,1)S(1)}, bf16[136,256]{1,0:T(8,128)(2,1)S(1)}, u32[]{:S(2)}, u32[]{:S(2)}) collective-permute-start(bf16[136,256]{1,0:T(8,128)(2,1)S(1)} %get-tuple-element.50), channel_id=1, source_target_pairs={{0,16},{4,20},{8,24},{12,28},{16,0},{20,4},{24,8},{28,12},{1,17},{... | collective-permute-start | bytes 208904 | tf_op jit(solution)/shard_map/ppermute | solution.py:562
  27.0 4.7 %collective-permute-start.5 = (bf16[128,384]{1,0:T(8,128)(2,1)S(1)}, bf16[128,384]{1,0:T(8,128)(2,1)S(1)}, u32[]{:S(2)}, u32[]{:S(2)}) collective-permute-start(bf16[128,384]{1,0:T(8,128)(2,1)S(1)} %get-tuple-element.51.refs_4_), channel_id=1, source_target_pairs={{0,4},{4,0},{8,12},{12,8},{16,20},{20,16},{24,28},{28,24},{1,5},{5... | collective-permute-start | bytes 294920 | tf_op jit(solution)/shard_map/ppermute | solution.py:562
  28.3 4.6 %collective-permute-start.6 = (bf16[128,256]{1,0:T(8,128)(2,1)S(1)}, bf16[128,256]{1,0:T(8,128)(2,1)S(1)}, u32[]{:S(2)}, u32[]{:S(2)}) collective-permute-start(bf16[128,256]{1,0:T(8,128)(2,1)S(1)} %get-tuple-element.57), channel_id=1, source_target_pairs={{0,4},{4,0},{8,12},{12,8},{16,20},{20,16},{24,28},{28,24},{1,5},{5... | collective-permute-start | bytes 196616 | tf_op jit(solution)/shard_map/ppermute | solution.py:562
  33.6 1.8 %collective-permute-start.8 = (bf16[392,512]{1,0:T(8,128)(2,1)S(1)}, bf16[392,512]{1,0:T(8,128)(2,1)S(1)}, u32[]{:S(2)}, u32[]{:S(2)}) collective-permute-start(bf16[392,512]{1,0:T(8,128)(2,1)S(1)} %get-tuple-element.61.refs_3_.mine_ref), channel_id=1, source_target_pairs={{0,1},{1,0},{2,3},{3,2},{4,5},{5,4},{6,7},{7,6},{8,9},{9,8},{10,11... | collective-permute-start | bytes 1204232 | tf_op jit(solution)/shard_map/ppermute | solution.py:565
  34.1 3.0 %collective-permute-start.7 = (bf16[256,512]{1,0:T(8,128)(2,1)S(1)}, bf16[256,512]{1,0:T(8,128)(2,1)S(1)}, u32[]{:S(2)}, u32[]{:S(2)}) collective-permute-start(bf16[256,512]{1,0:T(8,128)(2,1)S(1)} %get-tuple-element.63), channel_id=1, source_target_pairs={{0,1},{1,0},{2,3},{3,2},{4,5},{5,4},{6,7},{7,6},{8,9},{9,8},{10,11... | collective-permute-start | bytes 786440 | tf_op jit(solution)/shard_map/ppermute | solution.py:565
  35.5 12.2 %collective-permute-start.14 = (bf16[392,512]{1,0:T(8,128)(2,1)S(1)}, bf16[392,512]{1,0:T(8,128)(2,1)S(1)}, u32[]{:S(2)}, u32[]{:S(2)}) collective-permute-start(bf16[392,512]{1,0:T(8,128)(2,1)S(1)} %shard_map.118.refs_2_.factor_ref), channel_id=1, source_target_pairs={{0,2},{1,3},{2,0},{3,1},{4,6},{5,7},{6,4},{7,5},{8,10},{9,11},{10,... | collective-permute-start | bytes 1204232 | tf_op jit(solution)/shard_map/ppermute | solution.py:565
  38.4 1.5 %collective-permute-start.9 = (bf16[160,512]{1,0:T(8,128)(2,1)S(1)}, bf16[160,512]{1,0:T(8,128)(2,1)S(1)}, u32[]{:S(2)}, u32[]{:S(2)}) collective-permute-start(bf16[160,512]{1,0:T(8,128)(2,1)S(1)} %get-tuple-element.65), channel_id=1, source_target_pairs={{0,1},{1,0},{2,3},{3,2},{4,5},{5,4},{6,7},{7,6},{8,9},{9,8},{10,11... | collective-permute-start | bytes 491528 | tf_op jit(solution)/shard_map/ppermute | solution.py:565
  38.5 14.0 %collective-permute-start.13 = (bf16[256,512]{1,0:T(8,128)(2,1)S(1)}, bf16[256,512]{1,0:T(8,128)(2,1)S(1)}, u32[]{:S(2)}, u32[]{:S(2)}) collective-permute-start(bf16[256,512]{1,0:T(8,128)(2,1)S(1)} %shard_map.119.refs_4_), channel_id=1, source_target_pairs={{0,2},{1,3},{2,0},{3,1},{4,6},{5,7},{6,4},{7,5},{8,10},{9,11},{10,... | collective-permute-start | bytes 786440 | tf_op jit(solution)/shard_map/ppermute | solution.py:565
  39.1 1.4 %collective-permute-start.10 = (bf16[160,512]{1,0:T(8,128)(2,1)S(1)}, bf16[160,512]{1,0:T(8,128)(2,1)S(1)}, u32[]{:S(2)}, u32[]{:S(2)}) collective-permute-start(bf16[160,512]{1,0:T(8,128)(2,1)S(1)} %get-tuple-element.66), channel_id=1, source_target_pairs={{0,1},{1,0},{2,3},{3,2},{4,5},{5,4},{6,7},{7,6},{8,9},{9,8},{10,11... | collective-permute-start | bytes 491528 | tf_op jit(solution)/shard_map/ppermute | solution.py:565
  39.1 1.6 %collective-permute-start.11 = (bf16[160,512]{1,0:T(8,128)(2,1)S(1)}, bf16[160,512]{1,0:T(8,128)(2,1)S(1)}, u32[]{:S(2)}, u32[]{:S(2)}) collective-permute-start(bf16[160,512]{1,0:T(8,128)(2,1)S(1)} %get-tuple-element.67), channel_id=1, source_target_pairs={{0,1},{1,0},{2,3},{3,2},{4,5},{5,4},{6,7},{7,6},{8,9},{9,8},{10,11... | collective-permute-start | bytes 491528 | tf_op jit(solution)/shard_map/ppermute | solution.py:565
  39.9 1.4 %collective-permute-start.12 = (bf16[160,512]{1,0:T(8,128)(2,1)S(1)}, bf16[160,512]{1,0:T(8,128)(2,1)S(1)}, u32[]{:S(2)}, u32[]{:S(2)}) collective-permute-start(bf16[160,512]{1,0:T(8,128)(2,1)S(1)} %get-tuple-element.68), channel_id=1, source_target_pairs={{0,1},{1,0},{2,3},{3,2},{4,5},{5,4},{6,7},{7,6},{8,9},{9,8},{10,11... | collective-permute-start | bytes 491528 | tf_op jit(solution)/shard_map/ppermute | solution.py:565

commit v7 on v6

--- a/solution.py
+++ b/solution.py
@@ -106,7 +106,7 @@
 
 
 def stash_rows():
-    return slice(0, 32), slice(32, 64)
+    return slice(0, 32), slice(32, 64), slice(64, 96), slice(96, 104)
 
 
 def put_rows(rows_ref, rows):
@@ -115,36 +115,63 @@
         rows_ref[at : at + 1] = jnp.broadcast_to(row, (1, lanes))
 
 
+def half_state(half, width, vecs, tails_ref, through_row, last, x_ref, first_lane, out_ref):
+    state = vecs.shape[0]
+    half_w = out_ref.shape[1]
+    per = LANES // width
+    half_h = half_w // width
+    lane = lane_iota(state)
+    mine = jnp.where(half == 1, pltpu.roll(through_row, LANES - half_h, 1), through_row)
+    own, through = [], []
+    for i in range(half_w // LANES):
+        written = []
+        for k in range(per):
+            row = tails_ref[pl.ds(half * half_h + i * per + k, 1), :]
+            written.append((vecs * row).astype(BF16))
+        here = pl.ds(pl.multiple_of(first_lane + i * LANES, LANES), LANES)
+        both = dot(jnp.concatenate(written, axis=0), x_ref[:, here])
+        tile = both[0:state]
+        for k in range(1, per):
+            tile = jnp.where(lane < k * width, tile, both[k * state : (k + 1) * state])
+        own.append(tile)
+        through.append(spread(mine[0:1], i * per, width))
+    group = (jnp.concatenate(own, axis=1), jnp.concatenate(through, axis=1), jnp.broadcast_to(last, (1, half_w)))
+    pack(out_ref, group)
+
+
 def prepare(heads, width, raw, seg, decay_log, bias, x, write):
     toks, state = write.shape
     half_w = x.shape[1] // 2
-    half_h = heads // 2
     blocks = toks // GROUP
     arrays = (raw, seg, decay_log, bias, write, x)
 
     def body(*refs):
-        hbm, (other_ref, keep_ref, stash_ref) = refs[: len(arrays)], refs[len(arrays) : -9]
-        raw_ref, seg_ref, dl_ref, sb_ref, wr_ref, x_ref, rows, pad, sems = refs[-9:]
+        hbm, (other_ref, stash_ref) = refs[: len(arrays)], refs[len(arrays) : -8]
+        raw_ref, seg_ref, dl_ref, sb_ref, wr_ref, x_ref, rows, sems = refs[-8:]
+        half = position()[1]
+        lanes = pl.ds(pl.multiple_of(half * half_w, LANES), half_w)
+        sources = (*hbm[:5], hbm[5].at[:, lanes])
         copies = [
             pltpu.make_async_copy(src, dst, sems.at[k])
-            for k, (src, dst) in enumerate(zip(hbm, (raw_ref, seg_ref, dl_ref, sb_ref, wr_ref, x_ref)))
+            for k, (src, dst) in enumerate(zip(sources, (raw_ref, seg_ref, dl_ref, sb_ref, wr_ref, x_ref)))
         ]
         for copy in copies:
             copy.start()
         rows[...] = jnp.zeros_like(rows)
-        pad[...] = jnp.zeros_like(pad)
         tri = (
             lax.broadcasted_iota(jnp.int32, (GROUP, GROUP), 0)
             <= lax.broadcasted_iota(jnp.int32, (GROUP, GROUP), 1)
         ).astype(BF16)
+        stash_ref[...] = jnp.zeros_like(stash_ref)
+        cum_rows, step_rows, tail_rows, sum_rows = stash_rows()
         for copy in copies[:5]:
             copy.wait()
         vecs = jnp.transpose(wr_ref[...].astype(F32))
         rows[0:1, 0:heads] = dl_ref[...]
         rows[1:2, 0:heads] = sb_ref[...]
-        pad[0:heads] = raw_ref[...].astype(F32)
+        stash_ref[0:heads] = raw_ref[...].astype(F32)
         params = jnp.transpose(rows[...])[0:32]
-        z = pad[0:32] + params[:, 1:2]
+        z = stash_ref[cum_rows] + params[:, 1:2]
         step = jnp.maximum(z, 0.0) + jnp.log1p(jnp.exp(-jnp.abs(z)))
         rate = -jnp.exp(params[:, 0:1]) * step
         cum, full = [], []
@@ -162,52 +189,46 @@
         seg_row = seg_ref[...].astype(F32)
         last = seg_row[:, toks - 1 : toks]
         tail = jnp.exp(base - jnp.concatenate(full, axis=1)) * step
-        cum_rows, step_rows = stash_rows()
         stash_ref[cum_rows] = jnp.concatenate(cum, axis=1)
         stash_ref[SEG_LANE : SEG_LANE + 1] = seg_row
         stash_ref[step_rows] = step
-        tails = jnp.where(seg_row == last, tail, 0.0)
+        stash_ref[tail_rows] = jnp.where(seg_row == last, tail, 0.0)
         rows[...] = jnp.zeros_like(rows)
         rows[0:32] = jnp.broadcast_to(jnp.exp(base), (32, LANES))
-        keep = jnp.transpose(rows[...])[0:1]
-        per = LANES // width
-        odd = lax.rem(lax.axis_index("seq"), 2) == 1
-        lane = lane_iota(state)
+        sums = jnp.transpose(rows[...])[0:8]
+        stash_ref[sum_rows, 0:LANES] = sums
         copies[5].wait()
-        halves = []
-        for j in range(2):
-            own, through = [], []
-            for i in range(half_w // LANES):
-                at = j * half_h + i * per
-                written = [(vecs * tails[at + k : at + k + 1]).astype(BF16) for k in range(per)]
-                both = dot(jnp.concatenate(written, axis=0), x_ref[:, j * half_w + i * LANES : j * half_w + (i + 1) * LANES])
-                tile = both[0:state]
-                for k in range(1, per):
-                    tile = jnp.where(lane < k * width, tile, both[k * state : (k + 1) * state])
-                own.append(tile)
-                through.append(spread(keep, at, width))
-            halves.append((jnp.concatenate(own, axis=1), jnp.concatenate(through, axis=1), last))
-        mine, other = ordered(odd, *halves)
-        pack(keep_ref, mine)
-        pack(other_ref, other)
+        half_state(half, width, vecs, stash_ref.at[tail_rows], sums, last, x_ref, 0, other_ref)
 
     vm = pl.BlockSpec(memory_space=pltpu.VMEM)
-    out_shape = shaped(
-        ((state + EXTRA, half_w), BF16), ((state + EXTRA, half_w), BF16), ((stash_rows()[1].stop, toks), F32),
-    )
+    out_shape = shaped(((state + EXTRA, half_w), BF16), ((stash_rows()[-1].stop, toks), F32))
     return pl.pallas_call(
         body,
         in_specs=[pl.BlockSpec(memory_space=pltpu.HBM)] * len(arrays),
         out_specs=[vm] * len(out_shape),
         out_shape=out_shape,
         scratch_shapes=[
-            *[pltpu.VMEM(a.shape, a.dtype) for a in arrays],
-            pltpu.VMEM((LANES, LANES), F32), pltpu.VMEM((32, toks), F32),
-            pltpu.SemaphoreType.DMA((len(arrays),)),
+            *[pltpu.VMEM(a.shape, a.dtype) for a in arrays[:5]], pltpu.VMEM((toks, half_w), BF16),
+            pltpu.VMEM((LANES, LANES), F32), pltpu.SemaphoreType.DMA((len(arrays),)),
         ],
         compiler_params=pltpu.CompilerParams(vmem_limit_bytes=VMEM_ALL),
         cost_estimate=LONG,
     )(*arrays)
+
+
+def kept_state(width, stash, x, write):
+    toks, state = write.shape
+    half_w = x.shape[1] // 2
+
+    def body(stash_ref, x_ref, wr_ref, keep_ref):
+        half = position()[0]
+        cum_rows, _, tail_rows, sum_rows = stash_rows()
+        vecs = jnp.transpose(wr_ref[...].astype(F32))
+        last = stash_ref[SEG_LANE : SEG_LANE + 1, toks - 1 : toks]
+        sums = stash_ref[sum_rows, 0:LANES]
+        half_state(half, width, vecs, stash_ref.at[tail_rows], sums, last, x_ref, half * half_w, keep_ref)
+
+    return call(body, (stash, x, write), jax.ShapeDtypeStruct((state + EXTRA, half_w), BF16), cost=LONG)
 
 
 def gather_level(upper, entry, other):
@@ -218,115 +239,109 @@
     return state, through * jnp.where(upper, other[1], 1.0), last_id
 
 
-def pair_step(keep, mate, side, cross, after):
-    size, lanes = mate.shape[0] - EXTRA, mate.shape[1]
-
-    def body(
-        keep_ref, mate_ref, side_ref, cross_ref, early_ref, late_ref, entry_ref, first_ref, total_ref, rows_ref
-    ):
+def pair_step(keep, mate, after):
+    size, width = mate.shape[0] - EXTRA, mate.shape[1]
+    pieces = (slice(0, EARLY_LANES), slice(EARLY_LANES, width))
+
+    def body(keep_ref, mate_ref, *refs):
         odd = position()[0] == 1
-        upper = (position()[6] & 2) != 0
         mine, mate = unpack(keep_ref), unpack(mate_ref)
         total = merged(odd, mine, mate)
-        other = merged(odd, unpack(side_ref), unpack(cross_ref))
-        nothing = (0.0, jnp.ones_like(total[1]), jnp.full_like(total[2], -1.0))
-        entry = gather_level(upper, nothing, other)
-        total = merged(upper, total, other)
-        pack_both(early_ref, late_ref, total)
-        entry_ref[...], total_ref[...] = entry[0], total[0]
-        first_ref[...] = jnp.where(odd, mate[0], mine[0])
-        rows = tuple(jnp.where(odd, m, o) for o, m in zip(mine[1:], mate[1:]))
-        put_rows(rows_ref, entry[1:] + rows + total[1:])
+        first = tuple(jnp.where(odd, m, o) for o, m in zip(mine, mate))
+        rows = (jnp.ones_like(total[1]), jnp.full_like(total[2], -1.0)) + first[1:] + total[1:]
+        for k, lanes in enumerate(pieces):
+            send_ref, total_ref, rows_ref, first_ref = refs[4 * k : 4 * k + 4]
+            pack(send_ref, tuple(t[:, lanes] for t in total))
+            total_ref[...], first_ref[...] = total[0][:, lanes], first[0][:, lanes]
+            put_rows(rows_ref, [row[:, lanes] for row in rows])
+
+    out = []
+    for lanes in pieces:
+        wide = lanes.stop - lanes.start
+        out += shaped(((size + EXTRA, wide), BF16), ((size, wide), F32), ((8, wide), F32), ((size, wide), F32))
+    out = call(body, (keep, mate), out, after=after, cost=LONG)
+    return out[:4], out[4:]
+
+
+def level_step(bit, more, got, total, rows, entry=None, after=None):
+    size, lanes = total.shape
+    entries = () if entry is None else (entry,)
+
+    def body(got_ref, total_ref, rows_ref, *refs):
+        send_ref, entry_out, rows_out, *totals = refs[len(entries) :]
+        upper = (position()[6] & bit) != 0
+        other = unpack(got_ref)
+        old = refs[0][...] if entries else jnp.zeros_like(total_ref)
+        new = gather_level(upper, (old, rows_ref[0:1], rows_ref[1:2]), other)
+        held = merged(upper, (total_ref[...], rows_ref[4:5], rows_ref[5:6]), other)
+        pack(send_ref, held)
+        entry_out[...] = new[0]
+        put_rows(rows_out, new[1:] + (rows_ref[2:3], rows_ref[3:4]) + held[1:])
+        if more:
+            totals[0][...] = held[0]
 
     state = ((size, lanes), F32)
     return call(
-        body, (keep, mate, side, cross),
-        lane_parts(mate.shape) + shaped(state, state, state, ((8, lanes), F32)), after=after, cost=LONG,
-    )
-
-
-def pack_both(early_ref, late_ref, total):
-    edge = early_ref.shape[1]
-    pack(early_ref, tuple(t[:, :edge] for t in total))
-    pack(late_ref, tuple(t[:, edge:] for t in total))
-
-
-def lane_parts(shape):
-    rows, lanes = shape
-    return shaped(((rows, EARLY_LANES), BF16), ((rows, lanes - EARLY_LANES), BF16))
-
-
-def level_step(bit, early, late, entry, first, total, rows):
-    size, lanes = entry.shape
-
-    def body(
-        early_ref, late_ref, entry_ref, first_ref, total_ref, rows_ref,
-        early_out, late_out, entry_out, first_out, total_out, rows_out,
-    ):
-        upper = (position()[6] & bit) != 0
-        other = tuple(jnp.concatenate(pair, axis=1) for pair in zip(unpack(early_ref), unpack(late_ref)))
-        new = gather_level(upper, (entry_ref[...], rows_ref[0:1], rows_ref[1:2]), other)
-        held = merged(upper, (total_ref[...], rows_ref[4:5], rows_ref[5:6]), other)
-        pack_both(early_out, late_out, held)
-        entry_out[...], first_out[...], total_out[...] = new[0], first_ref[...], held[0]
-        put_rows(rows_out, new[1:] + (rows_ref[2:3], rows_ref[3:4]) + held[1:])
-
-    state = ((size, lanes), F32)
-    return call(
-        body, (early, late, entry, first, total, rows),
-        lane_parts((early.shape[0], lanes)) + shaped(state, state, state, ((8, lanes), F32)),
-    )
-
-
-def entry_step(bit, lanes, got, entry, first, rows, after=None):
-    size = entry.shape[0]
-    width = lanes.stop - lanes.start
-
-    def body(got_ref, entry_ref, first_ref, rows_ref, other_ref, keep_ref, prev_ref):
+        body, (got, total, rows, *entries),
+        shaped((got.shape, BF16), state, ((8, lanes), F32), *((state,) if more else ())), after=after, cost=LONG,
+    )
+
+
+def entry_step(bit, with_id, got, entry, rows, first, after):
+    def body(got_ref, entry_ref, rows_ref, first_ref, other_ref, keep_ref, *prev_ref):
         upper = (position()[6] & bit) != 0
         even = position()[0] == 0
-        old = (entry_ref[:, lanes], rows_ref[0:1, lanes], rows_ref[1:2, lanes])
-        new = gather_level(upper, old, unpack(got_ref))
-        last_first = rows_ref[3:4, lanes]
-        link = rows_ref[2:3, lanes] * (last_first == new[2]).astype(F32)
-        reached = first_ref[:, lanes] + link * new[0]
+        new = gather_level(upper, (entry_ref[...], rows_ref[0:1], rows_ref[1:2]), unpack(got_ref))
+        last_first = rows_ref[3:4]
+        link = rows_ref[2:3] * (last_first == new[2]).astype(F32)
+        reached = first_ref[...] + link * new[0]
         other_ref[...] = jnp.where(even, reached, new[0]).astype(BF16)
         keep_ref[...] = jnp.where(even, new[0], reached).astype(BF16)
-        prev = jnp.where(even, new[2], last_first)
-        prev_ref[...] = jnp.broadcast_to(prev[:, 0:LANES], (8, LANES))
-
-    block = ((size, width), BF16)
-    return call(body, (got, entry, first, rows), shaped(block, block, ((8, LANES), F32)), after=after)
-
-
-def local_part(heads, width, x, gate, read, write, stash, skip, after):
+        if with_id:
+            prev = jnp.where(even, new[2], last_first)
+            prev_ref[0][...] = jnp.broadcast_to(prev[:, 0:LANES], (8, LANES))
+
+    block = (entry.shape, BF16)
+    prev = (((8, LANES), F32),) if with_id else ()
+    return call(body, (got, entry, rows, first), shaped(block, block, *prev), after=after)
+
+
+def local_part(which, heads, width, x, gate, read, write, stash, skip, after):
     toks = write.shape[0]
-    feats = x.shape[1]
+    half_w = x.shape[1] // 2
+    half_h = heads // 2
     per = LANES // width
     blocks = toks // GROUP
     strip = 64
 
     def body(
         x_ref, gate_ref, rd_ref, wr_ref, stash_ref, skip_ref,
-        a_ref, b_ref, log_cum, scores, mix, pad, tails, rows_ref,
+        a_ref, b_ref, *refs,
     ):
-        cum_ref, step_ref = (stash_ref.at[rows] for rows in stash_rows())
+        *seg_out, log_cum, log_row, scores, mix, pad, tails, rows_ref = refs
+        half = position()[which]
+        second = half == 1
+        cum_ref, step_ref = (stash_ref.at[rows] for rows in stash_rows()[:2])
         lane = lane_iota(GROUP)
         mix[...] = jnp.zeros_like(mix)
         pad[...] = jnp.zeros_like(pad)
         rows_ref[...] = jnp.zeros_like(rows_ref)
         rows_ref[0:1, 0:heads] = skip_ref[...]
-        skips = rows_ref[0:1]
+        skips = jnp.where(second, pltpu.roll(rows_ref[...], LANES - half_h, 1), rows_ref[...])[0:1]
         seg_row = cum_ref[SEG_LANE : SEG_LANE + 1]
-        log_row = cum_ref[...] * LOG2E - jnp.log(step_ref[...]) * LOG2E
+        log_row[...] = cum_ref[...] * LOG2E - jnp.log(step_ref[...]) * LOG2E
         pad[0:32] = cum_ref[...] * LOG2E
         pad[SEG_LANE : SEG_LANE + 1] = seg_row
-        log_cum[...] = jnp.transpose(pad[...])
-        seg_col = log_cum[:, SEG_LANE : SEG_LANE + 1]
+        columns = jnp.transpose(pad[...])
+        seg_col = columns[:, SEG_LANE : SEG_LANE + 1]
+        log_cum[...] = jnp.where(second, pltpu.roll(columns, LANES - half_h, 1), columns)
+        if seg_out:
+            seg_out[0][...] = columns
         tail0 = jnp.exp(cum_ref[:, GROUP - 1 : GROUP] - cum_ref[:, 0:GROUP]) * step_ref[:, 0:GROUP]
         same = seg_row[:, 0:GROUP] == seg_row[:, GROUP - 1 : GROUP]
         pad[0:32, 0:GROUP] = jnp.where(same, tail0, 0.0)
-        tails[...] = jnp.transpose(pad[:, 0:GROUP])
+        columns = jnp.transpose(pad[:, 0:GROUP])
+        tails[...] = jnp.where(second, pltpu.roll(columns, LANES - half_h, 1), columns)
         masked = []
         for b in range(blocks):
             rows = slice(b * GROUP, (b + 1) * GROUP)
@@ -337,21 +352,22 @@
             scores[b] = jnp.where(causal & (seg_col[rows] == seg_row[:, rows]), s, 0.0)
             linked = seg_col[rows] == seg_col[b * GROUP - 1 : b * GROUP] if b else None
             masked.append(jnp.where(linked, rd_ref[rows].astype(F32), 0.0).astype(BF16) if b else None)
-        for i in range(feats // LANES):
+        for i in range(half_w // LANES):
             tile = slice(i * LANES, (i + 1) * LANES)
+            there = pl.ds(pl.multiple_of(half * half_w + i * LANES, LANES), LANES)
             gains = spread(skips, i * per, width)
             carry = None
             start = jnp.ones((1, LANES), F32)
             for b in range(blocks):
                 rows = slice(b * GROUP, (b + 1) * GROUP)
                 slot = (i * blocks + b) % mix.shape[0]
-                xb = x_ref[rows, tile]
+                xb = x_ref[rows, there]
                 logs = []
                 for k in range(per):
                     head = i * per + k
                     cb = jnp.broadcast_to(log_cum[rows, head : head + 1], (GROUP, LANES))
                     logs.append(cb)
-                    ar = log_row[head : head + 1, rows]
+                    ar = log_row[pl.ds(half * half_h + head, 1), rows]
                     for low in range(0, GROUP, strip):
                         for left in range(0, min(low + strip, GROUP), LANES):
                             gap = cb[low : low + strip] - ar[:, left : left + LANES]
@@ -374,7 +390,7 @@
                     s0 = dot(wr_ref[rows], xs, ((0,), (0,)))
                     s0h = s0.astype(BF16)
                     carry = (s0h, (s0 - s0h.astype(F32)).astype(BF16))
-                v = gate_ref[rows, tile].astype(F32)
+                v = gate_ref[rows, there].astype(F32)
                 sg = v / (1.0 + jnp.exp(-v))
                 a_ref[rows, tile] = sg * y
                 b_ref[rows, tile] = sg * (dec * start)
@@ -382,8 +398,9 @@
 
     return call(
         body, (x, gate, read, write, stash, skip),
-        shaped(((toks, feats), F32), ((toks, feats), F32), ((toks, LANES), F32)),
+        shaped(((toks, half_w), F32), ((toks, half_w), F32), *((((toks, LANES), F32),) if which == 0 else ())),
         [
+            pltpu.VMEM((toks, LANES), F32), pltpu.VMEM((32, toks), F32),
             pltpu.VMEM((blocks, GROUP, GROUP), F32), pltpu.VMEM((4, per * GROUP, GROUP), BF16),
             pltpu.VMEM((LANES, toks), F32), pltpu.VMEM((GROUP, LANES), F32), pltpu.VMEM((8, LANES), F32),
         ],
@@ -392,14 +409,14 @@
 
 
 def gated_part(which, lanes, prev_ref, rd_ref, cum_ref, a_ref, b_ref, states, gain_ref):
-    half_w = a_ref.shape[1] // 2
+    half_w = a_ref.shape[1]
     first = pl.multiple_of(position()[which] * half_w + lanes.start, LANES)
     here = pl.ds(first, lanes.stop - lanes.start)
     linked = cum_ref[:, SEG_LANE : SEG_LANE + 1] == prev_ref[0:1, 0:1]
     rm = jnp.where(linked, rd_ref[...].astype(F32), 0.0).astype(BF16)
     carried = [dot(rm, state[...]) for state in states]
     carried = carried[0] if len(carried) == 1 else jnp.concatenate(carried, axis=1)
-    gated = a_ref[:, here] + b_ref[:, here] * carried
+    gated = a_ref[:, lanes] + b_ref[:, lanes] * carried
     sq = gated * gated
     part = sq[:, 0:LANES]
     for i in range(1, sq.shape[1] // LANES):
@@ -564,38 +581,42 @@
     def across(a, bit):
         return lax.ppermute(a, "tp", [(i, i ^ bit) for i in range(n_tp)])
 
-    send_other, send_keep, stash = prepare(
+    other, stash = prepare(
         heads, width, step_raw, segment_ids.reshape(1, toks), decay_log.reshape(1, heads),
         step_bias.reshape(1, heads), head_input, write_vecs,
     )
-    side = swap(send_keep, 2)
-    cross = swap(send_other, 3)
-    mate = swap(send_other, 1)
-    a, b, log_cum = local_part(
-        heads, width, head_input, gate_input, read_vecs, write_vecs, stash,
-        skip_gain.reshape(1, heads), None,
-    )
-    early, late, entry, first, total, rows = pair_step(send_keep, mate, side, cross, a)
-    bit = 4
+    mate = swap(other, 1)
+    keep = kept_state(width, stash, head_input, write_vecs)
+    local = (heads, width, head_input, gate_input, read_vecs, write_vecs, stash, skip_gain.reshape(1, heads))
+    a_keep, b_keep, log_cum = local_part(0, *local, keep)
+    sent, totals, rows, firsts = zip(*pair_step(keep, mate, a_keep))
+    entries = [()] * 2
+    bit = 2
     while 2 * bit < n_seq:
-        early, late, entry, first, total, rows = level_step(
-            bit, swap(early, bit), swap(late, bit), entry, first, total, rows
-        )
+        more = 4 * bit < n_seq
+        got = [swap(piece, bit) for piece in sent]
+        early = level_step(bit, more, got[0], totals[0], rows[0], *entries[0])
+        late = level_step(bit, more, got[1], totals[1], rows[1], *entries[1], after=early[0])
+        sent, entries, rows, *totals = zip(early, late)
+        totals, entries = totals[0] if more else (), [(entry,) for entry in entries]
         bit *= 2
+    a_other, b_other, *_ = local_part(1, *local, sent[1])
     half_w = feats // 2
     quarter = out_weight.shape[1] // 4
-    one, two, half = slice(0, EARLY_LANES), slice(EARLY_LANES, half_w), slice(0, half_w)
+    one, two = slice(0, EARLY_LANES), slice(EARLY_LANES, half_w)
     top, rest, every = slice(0, EARLY_ROWS), slice(EARLY_ROWS, quarter), slice(0, quarter)
-    got_early, got_late = swap(early, bit), swap(late, bit)
-    send_one, keep_one, prev = entry_step(bit, one, got_early, entry, first, rows)
+    send_one, keep_one, prev = entry_step(
+        bit, True, swap(sent[0], bit), *entries[0], rows[0], firsts[0], a_other
+    )
     other_one = swap(send_one, 1)
-    send_two, keep_two, _ = entry_step(bit, two, got_late, entry, first, rows, send_one)
+    send_two, keep_two = entry_step(bit, False, swap(sent[1], bit), *entries[1], rows[1], firsts[1], send_one)
     other_two = swap(send_two, 1)
     gain = norm_gain.reshape(1, feats)
-    shared = (prev, read_vecs, log_cum, a, b)
-    g_keep, squares, partial = gated_sums(0, half, *shared, (keep_one, keep_two), gain, out_weight)
-    g_one, squares, partial = gated_sums(1, one, *shared, (other_one,), gain, out_weight, partial, squares)
-    g_two, near_top = gated_last(two, top, *shared, other_two, gain, out_weight, partial, squares)
+    kept, rest_of = (prev, read_vecs, log_cum, a_keep, b_keep), (prev, read_vecs, log_cum, a_other, b_other)
+    g_near, squares, partial = gated_sums(0, one, *kept, (keep_one,), gain, out_weight)
+    g_keep, squares, partial = gated_sums(0, two, *kept, (keep_two,), gain, out_weight, partial, squares)
+    g_one, squares, partial = gated_sums(1, one, *rest_of, (other_one,), gain, out_weight, partial, squares)
+    g_two, near_top = gated_last(two, top, *rest_of, other_two, gain, out_weight, partial, squares)
     got_top = across(near_top, 1)
     near_rest, far_top, far_rest = project_last(
         two, ((0, rest, BF16), (1, top, F32), (1, rest, F32)), g_two, partial, out_weight, near_top
@@ -605,7 +626,7 @@
     got_far_top = across(to_far_top, 2)
     to_far_rest = add_second(far_rest, got_rest, to_far_top)
     got_far_rest = across(to_far_rest, 2)
-    groups, gs = ((0, half), (1, one), (1, two)), (g_keep, g_one, g_two)
+    groups, gs = ((0, one), (0, two), (1, one), (1, two)), (g_near, g_keep, g_one, g_two)
     y_near = project_whole(2, groups, gs, out_weight, NEAR_PIECES, after=to_far_rest)
     got_own = tuple(across(piece, 1) for piece in y_near)
     (y_own,) = project_whole(3, groups, gs, out_weight, 1, got_own)

time: 53.4 us -> 50.6 us (0.948)
  waiting for transfers between devices: 21.8 us -> 16 us
  starting transfers between devices: 13.4 us -> 15.1 us
  local copies, waits for them, and re-layouts: 0.94 us -> 1.8 us
    ppermute x7, waiting for transfers between devices: 10.4 us -> 4.71 us  [swap(): return lax.ppermute(a, 'seq', [(i, i ^ bit) for i in range(n_seq)])]
    ppermute x7, starting transfers between devices: 9.72 us -> 11.5 us  [swap(): return lax.ppermute(a, 'seq', [(i, i ^ bit) for i in range(n_seq)])]
    unnamed x20, local copies, waits for them, and re-layouts: 0.93 us -> 1.79 us
    pallas_call x12 -> x17, Pallas kernels: 12.1 us -> 12.9 us  [call(): pl.pallas_call(kernel, in_specs=specs, out_specs=jax.tree.map(lambda _: v...]
  transfers between devices with their start and end apart: 15 -> 15, of which waited for: 10 -> 9; matrix products, arithmetic and copies ran while one was open for 0% -> 0% of each run, Pallas kernels for 21% -> 26%
where the time goes in v7:
time: 50.6 us; the launch traced here: 50.4 us
  Pallas kernels  17.3 us (34%)
  waiting for transfers between devices  16 us (32%)
  starting transfers between devices  15.1 us (30%)
  local copies, waits for them, and re-layouts  1.8 us (4%)
    pallas_call x17, Pallas kernels, call(): pl.pallas_call(kernel, in_specs=specs, out_specs=jax.tree.map(lambda _: v...  12.9 us
    ppermute x7, starting transfers between devices, swap(): return lax.ppermute(a, 'seq', [(i, i ^ bit) for i in range(n_seq)])  11.5 us
    ppermute x8, waiting for transfers between devices, across(): return lax.ppermute(a, 'tp', [(i, i ^ bit) for i in range(n_tp)])  11.3 us
    ppermute x7, waiting for transfers between devices, swap(): return lax.ppermute(a, 'seq', [(i, i ^ bit) for i in range(n_seq)])  4.71 us
    ppermute x8, starting transfers between devices, across(): return lax.ppermute(a, 'tp', [(i, i ^ bit) for i in range(n_tp)])  3.66 us
    pallas_call x1, Pallas kernels, prepare(): pl.pallas_call(body, in_specs=[pl.BlockSpec(memory_space=pltpu.HBM)] * le...  2.82 us
    unnamed x20, local copies, waits for them, and re-layouts  1.79 us
    pallas_call x2, Pallas kernels, finish(): pl.pallas_call(body, in_specs=[vm] * 3 + ([] if first else [where]), out_...  1.58 us
  transfers between devices with their start and end apart: 15, of which 9 were waited for; matrix products, arithmetic and copies ran while one was open for 0% of the time, Pallas kernels for 26%

profile of v7, /device:TPU:0, one launch (start us, length us, event | category | flops | bytes accessed | tf_op | source)
XLA Modules:
  0.0 50.4 jit_solution(6758418008429933479)
XLA Ops:
  0.0 2.8 %shard_map.109 = (bf16[136,640]{1,0:T(8,128)(2,1)}, f32[104,512]{1,0:T(8,128)}) custom-call(bf16[20,512]{1,0:T(8,128)(2,1)} %refs_0_.4, s32[1,512]{1,0:T(1,128)} %bitcast.8, f32[1,20]{1,0:T(1,128)} %bitcast.9, f32[1,20]{1,0:T(1,128)} %bitcast.10, bf16[512,128]{1,0:T(8,128)(2,1)} %refs_3_.3, bf16[512,1280]{1,0:T(8,128)(2,1)} %refs_0_.6), custom_call_target="tpu_custom_call" | custom-call | flops 4000000000 | bytes 1000 | tf_op jit(solution)/shard_map/pallas_call | solution.py:205
  2.8 3.0 %collective-permute-start = (bf16[136,640]{1,0:T(8,128)(2,1)}, bf16[136,640]{1,0:T(8,128)(2,1)S(1)}, u32[]{:S(2)}, u32[]{:S(2)}) collective-permute-start(bf16[136,640]{1,0:T(8,128)(2,1)} %get-tuple-element.52), channel_id=1, source_target_pairs={{0,4},{4,0},{8,12},{12,8},{16,20},{20,16},{24,28},{28,24},{1,5},{5... | collective-permute-start | bytes 522248 | tf_op jit(solution)/shard_map/ppermute | solution.py:579
  5.9 0.9 %copy-done.5 = f32[104,512]{1,0:T(8,128)S(1)} copy-done((f32[104,512]{1,0:T(8,128)S(1)}, f32[104,512]{1,0:T(8,128)}, u32[]{:S(2)}) %copy-start.5) | copy-done | bytes 213016
  6.8 0.6 %shard_map.110.refs_6_.refs_0_ = bf16[136,640]{1,0:T(8,128)(2,1)S(1)} custom-call(f32[104,512]{1,0:T(8,128)S(1)} %copy-done.5, bf16[512,1280]{1,0:T(8,128)(2,1)S(1)} %copy-done.1, bf16[512,128]{1,0:T(8,128)(2,1)S(1)} %copy-done.3), custom_call_target="tpu_custom_call" | custom-call | flops 4000000000 | bytes 1000 | tf_op jit(solution)/shard_map/pallas_call | solution.py:66
  7.4 0.3 copy-done
  7.7 0.5 copy-done.2
  8.2 2.5 %shard_map.111 = (f32[512,640]{1,0:T(8,128)S(1)}, f32[512,640]{1,0:T(8,128)S(1)}, f32[512,128]{1,0:T(8,128)S(1)}) custom-call(bf16[512,1280]{1,0:T(8,128)(2,1)S(1)} %copy-done.1, bf16[512,1280]{1,0:T(8,128)(2,1)S(1)} %copy-done.2, bf16[512,128]{1,0:T(8,128)(2,1)S(1)} %copy-done, bf16[512,128]{1,0:T(8,128)(2,1)S(1)} %copy-done.3, f32[104,512]{1,0:T(8,128)S(1)} %copy-done.5, ...), custom_call_target="tpu_custom_call" | custom-call | flops 4000000000 | bytes 1000 | tf_op jit(solution)/shard_map/pallas_call | solution.py:66
  10.7 0.0 collective-permute-done.refs_1_
  10.7 0.1 shard_map.112
  10.8 1.7 %collective-permute-start.1 = (bf16[136,384]{1,0:T(8,128)(2,1)S(1)}, bf16[136,384]{1,0:T(8,128)(2,1)S(1)}, u32[]{:S(2)}, u32[]{:S(2)}) collective-permute-start(bf16[136,384]{1,0:T(8,128)(2,1)S(1)} %get-tuple-element.54), channel_id=1, source_target_pairs={{0,8},{4,12},{8,0},{12,4},{16,24},{20,28},{24,16},{28,20},{1,9},{5... | collective-permute-start | bytes 313352 | tf_op jit(solution)/shard_map/ppermute | solution.py:579
  12.5 0.4 collective-permute-start.3
  12.9 3.3 %collective-permute-done.1.got_ref = bf16[136,384]{1,0:T(8,128)(2,1)S(1)} collective-permute-done((bf16[136,384]{1,0:T(8,128)(2,1)S(1)}, bf16[136,384]{1,0:T(8,128)(2,1)S(1)}, u32[]{:S(2)}, u32[]{:S(2)}) %collective-permute-start.1) | collective-permute-done | bytes 104480 | tf_op jit(solution)/shard_map/ppermute | solution.py:579
  16.2 0.1 shard_map.113
  16.3 2.7 %collective-permute-start.2 = (bf16[136,384]{1,0:T(8,128)(2,1)S(1)}, bf16[136,384]{1,0:T(8,128)(2,1)S(1)}, u32[]{:S(2)}, u32[]{:S(2)}) collective-permute-start(bf16[136,384]{1,0:T(8,128)(2,1)S(1)} %get-tuple-element.57.refs_3_), channel_id=1, source_target_pairs={{0,16},{4,20},{8,24},{12,28},{16,0},{20,4},{24,8},{28,12},{1,17},{... | collective-permute-start | bytes 313352 | tf_op jit(solution)/shard_map/ppermute | solution.py:579
  19.0 0.0 slice-start
  19.0 0.9 %collective-permute-start.4 = (bf16[136,256]{1,0:T(8,128)(2,1)S(1)}, bf16[136,256]{1,0:T(8,128)(2,1)S(1)}, u32[]{:S(2)}, u32[]{:S(2)}) collective-permute-start(bf16[136,256]{1,0:T(8,128)(2,1)S(1)} %get-tuple-element.64.refs_6_), channel_id=1, source_target_pairs={{0,16},{4,20},{8,24},{12,28},{16,0},{20,4},{24,8},{28,12},{1,17},{... | collective-permute-start | bytes 208904 | tf_op jit(solution)/shard_map/ppermute | solution.py:579
  20.0 2.5 %shard_map.115 = (f32[512,640]{1,0:T(8,128)S(1)}, f32[512,640]{1,0:T(8,128)S(1)}) custom-call(bf16[512,1280]{1,0:T(8,128)(2,1)S(1)} %copy-done.1, bf16[512,1280]{1,0:T(8,128)(2,1)S(1)} %copy-done.2, bf16[512,128]{1,0:T(8,128)(2,1)S(1)} %copy-done, bf16[512,128]{1,0:T(8,128)(2,1)S(1)} %copy-done.3, f32[104,512]{1,0:T(8,128)S(1)} %copy-done.6, ...), custom_call_target="tpu_custom_call" | custom-call | flops 4000000000 | bytes 1000 | tf_op jit(solution)/shard_map/pallas_call | solution.py:66
  22.4 0.0 copy-start.7
  22.5 1.4 %collective-permute-done.2.refs_0_ = bf16[136,384]{1,0:T(8,128)(2,1)S(1)} collective-permute-done((bf16[136,384]{1,0:T(8,128)(2,1)S(1)}, bf16[136,384]{1,0:T(8,128)(2,1)S(1)}, u32[]{:S(2)}, u32[]{:S(2)}) %collective-permute-start.2) | collective-permute-done | bytes 104480 | tf_op jit(solution)/shard_map/ppermute | solution.py:579
  23.8 0.1 shard_map.116
  23.9 1.4 %collective-permute-start.5 = (bf16[128,384]{1,0:T(8,128)(2,1)S(1)}, bf16[128,384]{1,0:T(8,128)(2,1)S(1)}, u32[]{:S(2)}, u32[]{:S(2)}) collective-permute-start(bf16[128,384]{1,0:T(8,128)(2,1)S(1)} %get-tuple-element.74.refs_4_), channel_id=1, source_target_pairs={{0,4},{4,0},{8,12},{12,8},{16,20},{20,16},{24,28},{28,24},{1,5},{5... | collective-permute-start | bytes 294920 | tf_op jit(solution)/shard_map/ppermute | solution.py:579
  25.3 0.0 collective-permute-done.4.refs_0_
  25.4 1.4 %collective-permute-start.6 = (bf16[128,256]{1,0:T(8,128)(2,1)S(1)}, bf16[128,256]{1,0:T(8,128)(2,1)S(1)}, u32[]{:S(2)}, u32[]{:S(2)}) collective-permute-start(bf16[128,256]{1,0:T(8,128)(2,1)S(1)} %get-tuple-element.83), channel_id=1, source_target_pairs={{0,4},{4,0},{8,12},{12,8},{16,20},{20,16},{24,28},{28,24},{1,5},{5... | collective-permute-start | bytes 196616 | tf_op jit(solution)/shard_map/ppermute | solution.py:579
  26.8 1.2 %shard_map.117 = (bf16[512,384]{1,0:T(8,128)(2,1)S(1)}, f32[1,512]{1,0:T(1,128)S(1)}, f32[2,640,512]{2,1,0:T(8,128)S(1)}) custom-call(f32[8,128]{1,0:T(8,128)S(1)} %get-tuple-element.66.prev_ref, bf16[512,128]{1,0:T(8,128)(2,1)S(1)} %copy-done, f32[512,128]{1,0:T(8,128)S(1)} %get-tuple-element.67.cum_ref, f32[512,640]{1,0:T(8,128)S(1)} %get-tuple-element.53.refs_2_.a_ref, ...), custom_call_target="tpu_custom_call" | custom-call | flops 1000 | bytes 1000 | tf_op jit(solution)/shard_map/pallas_call | solution.py:66
  28.0 0.9 %shard_map.119 = (bf16[512,256]{1,0:T(8,128)(2,1)S(1)}, f32[1,512]{1,0:T(1,128)S(1)}, f32[2,640,512]{2,1,0:T(8,128)S(1)}) custom-call(f32[8,128]{1,0:T(8,128)S(1)} %get-tuple-element.66.prev_ref, bf16[512,128]{1,0:T(8,128)(2,1)S(1)} %copy-done, f32[512,128]{1,0:T(8,128)S(1)} %get-tuple-element.67.cum_ref, f32[512,640]{1,0:T(8,128)S(1)} %get-tuple-element.53.refs_2_.a_ref, ...), custom_call_target="tpu_custom_call" | custom-call | flops 1000 | bytes 1000 | tf_op jit(solution)/shard_map/pallas_call | solution.py:66
  28.9 1.2 %shard_map.120 = (bf16[512,384]{1,0:T(8,128)(2,1)S(1)}, f32[1,512]{1,0:T(1,128)S(1)}, f32[2,640,512]{2,1,0:T(8,128)S(1)}) custom-call(f32[8,128]{1,0:T(8,128)S(1)} %get-tuple-element.66.prev_ref, bf16[512,128]{1,0:T(8,128)(2,1)S(1)} %copy-done, f32[512,128]{1,0:T(8,128)S(1)} %get-tuple-element.67.cum_ref, f32[512,640]{1,0:T(8,128)S(1)} %get-tuple-element.65.refs_4_.a_ref, ...), custom_call_target="tpu_custom_call" | custom-call | flops 1000 | bytes 1000 | tf_op jit(solution)/shard_map/pallas_call | solution.py:66
  30.1 0.6 %shard_map.121 = (bf16[512,256]{1,0:T(8,128)(2,1)S(1)}, bf16[392,512]{1,0:T(8,128)(2,1)S(1)}) custom-call(f32[8,128]{1,0:T(8,128)S(1)} %get-tuple-element.66.prev_ref, bf16[512,128]{1,0:T(8,128)(2,1)S(1)} %copy-done, f32[512,128]{1,0:T(8,128)S(1)} %get-tuple-element.67.cum_ref, f32[512,640]{1,0:T(8,128)S(1)} %get-tuple-element.65.refs_4_.a_ref, ...), custom_call_target="tpu_custom_call" | custom-call | flops 1000 | bytes 1000 | tf_op jit(solution)/shard_map/pallas_call | solution.py:66
  30.8 0.1 collective-permute-start.8
  30.9 0.5 shard_map.122
  31.3 0.5 %collective-permute-start.7 = (bf16[256,512]{1,0:T(8,128)(2,1)S(1)}, bf16[256,512]{1,0:T(8,128)(2,1)S(1)}, u32[]{:S(2)}, u32[]{:S(2)}) collective-permute-start(bf16[256,512]{1,0:T(8,128)(2,1)S(1)} %get-tuple-element.89), channel_id=1, source_target_pairs={{0,1},{1,0},{2,3},{3,2},{4,5},{5,4},{6,7},{7,6},{8,9},{9,8},{10,11... | collective-permute-start | bytes 786440 | tf_op jit(solution)/shard_map/ppermute | solution.py:582
  31.9 0.7 %collective-permute-done.8.got_ref = bf16[392,512]{1,0:T(8,128)(2,1)S(1)} collective-permute-done((bf16[392,512]{1,0:T(8,128)(2,1)S(1)}, bf16[392,512]{1,0:T(8,128)(2,1)S(1)}, u32[]{:S(2)}, u32[]{:S(2)}) %collective-permute-start.8) | collective-permute-done | bytes 401440 | tf_op jit(solution)/shard_map/ppermute | solution.py:582
  32.6 0.1 shard_map.123.refs_2_.factor_ref
  32.7 1.7 %collective-permute-start.14 = (bf16[392,512]{1,0:T(8,128)(2,1)S(1)}, bf16[392,512]{1,0:T(8,128)(2,1)S(1)}, u32[]{:S(2)}, u32[]{:S(2)}) collective-permute-start(bf16[392,512]{1,0:T(8,128)(2,1)S(1)} %shard_map.123.refs_2_.factor_ref), channel_id=1, source_target_pairs={{0,2},{1,3},{2,0},{3,1},{4,6},{5,7},{6,4},{7,5},{8,10},{9,11},{10,... | collective-permute-start | bytes 1204232 | tf_op jit(solution)/shard_map/ppermute | solution.py:582
  34.3 0.1 shard_map.124.refs_5_
  34.4 1.2 %shard_map.125 = (bf16[160,512]{1,0:T(8,128)(2,1)S(1)}, bf16[160,512]{1,0:T(8,128)(2,1)S(1)}, bf16[160,512]{1,0:T(8,128)(2,1)S(1)}, bf16[160,512]{1,0:T(8,128)(2,1)S(1)}) custom-call(bf16[1280,2560]{1,0:T(8,128)(2,1)S(1)} %bitcast.5, bf16[512,384]{1,0:T(8,128)(2,1)S(1)} %get-tuple-element.70.refs_1_.refs_0_, ...), custom_call_target="tpu_custom_call" | custom-call | flops 1000 | bytes 1000 | tf_op jit(solution)/shard_map/pallas_call | solution.py:66
  35.6 0.1 collective-permute-start.9
  35.7 0.6 %collective-permute-start.13 = (bf16[256,512]{1,0:T(8,128)(2,1)S(1)}, bf16[256,512]{1,0:T(8,128)(2,1)S(1)}, u32[]{:S(2)}, u32[]{:S(2)}) collective-permute-start(bf16[256,512]{1,0:T(8,128)(2,1)S(1)} %shard_map.124.refs_5_), channel_id=1, source_target_pairs={{0,2},{1,3},{2,0},{3,1},{4,6},{5,7},{6,4},{7,5},{8,10},{9,11},{10,... | collective-permute-start | bytes 786440 | tf_op jit(solution)/shard_map/ppermute | solution.py:582
  36.4 0.5 %collective-permute-start.11 = (bf16[160,512]{1,0:T(8,128)(2,1)S(1)}, bf16[160,512]{1,0:T(8,128)(2,1)S(1)}, u32[]{:S(2)}, u32[]{:S(2)}) collective-permute-start(bf16[160,512]{1,0:T(8,128)(2,1)S(1)} %get-tuple-element.93), channel_id=1, source_target_pairs={{0,1},{1,0},{2,3},{3,2},{4,5},{5,4},{6,7},{7,6},{8,9},{9,8},{10,11... | collective-permute-start | bytes 491528 | tf_op jit(solution)/shard_map/ppermute | solution.py:582
  36.9 0.2 collective-permute-done.9.refs_4_
  37.1 0.1 collective-permute-start.12
  37.2 0.5 %collective-permute-done.10.refs_5_ = bf16[160,512]{1,0:T(8,128)(2,1)S(1)} collective-permute-done((bf16[160,512]{1,0:T(8,128)(2,1)S(1)}, bf16[160,512]{1,0:T(8,128)(2,1)S(1)}, u32[]{:S(2)}, u32[]{:S(2)}) %collective-permute-start.10) | collective-permute-done | bytes 163872 | tf_op jit(solution)/shard_map/ppermute | solution.py:582
  37.8 0.2 collective-permute-done.11.refs_6_
  38.0 0.5 collective-permute-done.12.refs_7_
  38.5 1.2 %shard_map.126.own_ref = f32[640,512]{1,0:T(8,128)S(1)} custom-call(bf16[1280,2560]{1,0:T(8,128)(2,1)S(1)} %bitcast.5, bf16[512,384]{1,0:T(8,128)(2,1)S(1)} %get-tuple-element.70.refs_1_.refs_0_, bf16[512,256]{1,0:T(8,128)(2,1)S(1)} %get-tuple-element.78.refs_2_.refs_1_, bf16[512,384]{1,0:T(8,128)(2,1)S(1)} %get-tuple-element.82.refs_3_.refs_2_, ...), custom_call_target="tpu_custom_call" | custom-call | flops 1000 | bytes 1000 | tf_op jit(solution)/shard_map/pallas_call | solution.py:66
  39.7 5.1 %collective-permute-done.14.far_ref = bf16[392,512]{1,0:T(8,128)(2,1)S(1)} collective-permute-done((bf16[392,512]{1,0:T(8,128)(2,1)S(1)}, bf16[392,512]{1,0:T(8,128)(2,1)S(1)}, u32[]{:S(2)}, u32[]{:S(2)}) %collective-permute-start.14) | collective-permute-done | bytes 401440 | tf_op jit(solution)/shard_map/ppermute | solution.py:582
  44.9 0.8 %shard_map.127 = (bf16[640,512]{1,0:T(8,128)(2,1)}, f32[1,512]{1,0:T(1,128)S(1)}) custom-call(f32[640,512]{1,0:T(8,128)S(1)} %shard_map.126.own_ref, bf16[392,512]{1,0:T(8,128)(2,1)S(1)} %collective-permute-done.14.far_ref, bf16[392,512]{1,0:T(8,128)(2,1)S(1)} %shard_map.123.refs_2_.factor_ref), custom_call_target="tpu_custom_call" | custom-call | flops 1000 | bytes 1000 | tf_op jit(solution)/shard_map/pallas_call | solution.py:559
  45.7 4.0 %collective-permute-done.13.far_ref = bf16[256,512]{1,0:T(8,128)(2,1)S(1)} collective-permute-done((bf16[256,512]{1,0:T(8,128)(2,1)S(1)}, bf16[256,512]{1,0:T(8,128)(2,1)S(1)}, u32[]{:S(2)}, u32[]{:S(2)}) %collective-permute-start.13) | collective-permute-done | bytes 262176 | tf_op jit(solution)/shard_map/ppermute | solution.py:582
  49.7 0.8 %shard_map.128 = bf16[640,512]{1,0:T(8,128)(2,1)} custom-call(f32[640,512]{1,0:T(8,128)S(1)} %shard_map.126.own_ref, bf16[256,512]{1,0:T(8,128)(2,1)S(1)} %collective-permute-done.13.far_ref, f32[1,512]{1,0:T(1,128)S(1)} %get-tuple-element.95.factor_ref, bf16[640,512]{1,0:T(8,128)(2,1)} %get-tuple-element.96.refs_0_), custom_call_target="tpu_custom_call", output_to_operand_aliasing={{}: (3, {})} | custom-call | flops 1000 | bytes 1000 | tf_op jit(solution)/shard_map/pallas_call | solution.py:559
  (24 shorter events, 0.1 us)
Async XLA Ops:
  0.0 5.9 %copy-start.1 = (bf16[512,1280]{1,0:T(8,128)(2,1)S(1)}, bf16[512,1280]{1,0:T(8,128)(2,1)}, u32[]{:S(2)}) copy-start(bf16[512,1280]{1,0:T(8,128)(2,1)} %refs_0_.6) | copy-start | bytes 3932164
  0.0 5.9 %copy-start.3 = (bf16[512,128]{1,0:T(8,128)(2,1)S(1)}, bf16[512,128]{1,0:T(8,128)(2,1)}, u32[]{:S(2)}) copy-start(bf16[512,128]{1,0:T(8,128)(2,1)} %refs_3_.3) | copy-start | bytes 393220
  2.8 7.8 %collective-permute-start = (bf16[136,640]{1,0:T(8,128)(2,1)}, bf16[136,640]{1,0:T(8,128)(2,1)S(1)}, u32[]{:S(2)}, u32[]{:S(2)}) collective-permute-start(bf16[136,640]{1,0:T(8,128)(2,1)} %get-tuple-element.52), channel_id=1, source_target_pairs={{0,4},{4,0},{8,12},{12,8},{16,20},{20,16},{24,28},{28,24},{1,5},{5... | collective-permute-start | bytes 522248 | tf_op jit(solution)/shard_map/ppermute | solution.py:579
  5.9 0.9 %copy-start.5 = (f32[104,512]{1,0:T(8,128)S(1)}, f32[104,512]{1,0:T(8,128)}, u32[]{:S(2)}) copy-start(f32[104,512]{1,0:T(8,128)} %get-tuple-element.51.stash_ref.refs_4_) | copy-start | bytes 638980
  6.8 0.9 %copy-start = (bf16[512,128]{1,0:T(8,128)(2,1)S(1)}, bf16[512,128]{1,0:T(8,128)(2,1)}, u32[]{:S(2)}) copy-start(bf16[512,128]{1,0:T(8,128)(2,1)} %rd_ref.7) | copy-start | bytes 393220
  6.8 1.4 %copy-start.2 = (bf16[512,1280]{1,0:T(8,128)(2,1)S(1)}, bf16[512,1280]{1,0:T(8,128)(2,1)}, u32[]{:S(2)}) copy-start(bf16[512,1280]{1,0:T(8,128)(2,1)} %refs_1_.3) | copy-start | bytes 3932164
  6.8 1.4 %copy-start.4 = (f32[20]{0:T(128)S(1)}, f32[20]{0:T(128)}, u32[]{:S(2)}) copy-start(f32[20]{0:T(128)} %param.19) | copy-start | bytes 244
  10.8 5.4 %collective-permute-start.1 = (bf16[136,384]{1,0:T(8,128)(2,1)S(1)}, bf16[136,384]{1,0:T(8,128)(2,1)S(1)}, u32[]{:S(2)}, u32[]{:S(2)}) collective-permute-start(bf16[136,384]{1,0:T(8,128)(2,1)S(1)} %get-tuple-element.54), channel_id=1, source_target_pairs={{0,8},{4,12},{8,0},{12,4},{16,24},{20,28},{24,16},{28,20},{1,9},{5... | collective-permute-start | bytes 313352 | tf_op jit(solution)/shard_map/ppermute | solution.py:579
  12.5 6.4 %collective-permute-start.3 = (bf16[136,256]{1,0:T(8,128)(2,1)S(1)}, bf16[136,256]{1,0:T(8,128)(2,1)S(1)}, u32[]{:S(2)}, u32[]{:S(2)}) collective-permute-start(bf16[136,256]{1,0:T(8,128)(2,1)S(1)} %get-tuple-element.61), channel_id=1, source_target_pairs={{0,8},{4,12},{8,0},{12,4},{16,24},{20,28},{24,16},{28,20},{1,9},{5... | collective-permute-start | bytes 208904 | tf_op jit(solution)/shard_map/ppermute | solution.py:579
  16.3 7.5 %collective-permute-start.2 = (bf16[136,384]{1,0:T(8,128)(2,1)S(1)}, bf16[136,384]{1,0:T(8,128)(2,1)S(1)}, u32[]{:S(2)}, u32[]{:S(2)}) collective-permute-start(bf16[136,384]{1,0:T(8,128)(2,1)S(1)} %get-tuple-element.57.refs_3_), channel_id=1, source_target_pairs={{0,16},{4,20},{8,24},{12,28},{16,0},{20,4},{24,8},{28,12},{1,17},{... | collective-permute-start | bytes 313352 | tf_op jit(solution)/shard_map/ppermute | solution.py:579
  18.9 1.0 %copy-start.6 = (f32[104,512]{1,0:T(8,128)S(1)}, f32[104,512]{1,0:T(8,128)}, u32[]{:S(2)}) copy-start(f32[104,512]{1,0:T(8,128)} %get-tuple-element.51.stash_ref.refs_4_) | copy-start | bytes 638980
  19.0 7.8 %slice-start = ((s8[6553600]{0:T(1024)(128)(4,1)}), s8[4194304]{0:T(1024)(128)(4,1)S(1)}, s32[]{:S(2)}) async-start(s8[6553600]{0:T(1024)(128)(4,1)} %bitcast.4), calls=%async_computation | async-start | bytes 8388608
  19.0 7.8 %slice-start.1 = ((s8[6553600]{0:T(1024)(128)(4,1)}), s8[2359296]{0:T(1024)(128)(4,1)S(1)}, s32[]{:S(2)}) async-start(s8[6553600]{0:T(1024)(128)(4,1)} %bitcast.4), calls=%async_computation.1 | async-start | bytes 4718592
  19.0 6.3 %collective-permute-start.4 = (bf16[136,256]{1,0:T(8,128)(2,1)S(1)}, bf16[136,256]{1,0:T(8,128)(2,1)S(1)}, u32[]{:S(2)}, u32[]{:S(2)}) collective-permute-start(bf16[136,256]{1,0:T(8,128)(2,1)S(1)} %get-tuple-element.64.refs_6_), channel_id=1, source_target_pairs={{0,16},{4,20},{8,24},{12,28},{16,0},{20,4},{24,8},{28,12},{1,17},{... | collective-permute-start | bytes 208904 | tf_op jit(solution)/shard_map/ppermute | solution.py:579
  22.4 4.3 %copy-start.7 = (f32[1280]{0:T(1024)S(1)}, f32[1280]{0:T(1024)}, u32[]{:S(2)}) copy-start(f32[1280]{0:T(1024)} %param.20) | copy-start | bytes 15364
  23.9 5.0 %collective-permute-start.5 = (bf16[128,384]{1,0:T(8,128)(2,1)S(1)}, bf16[128,384]{1,0:T(8,128)(2,1)S(1)}, u32[]{:S(2)}, u32[]{:S(2)}) collective-permute-start(bf16[128,384]{1,0:T(8,128)(2,1)S(1)} %get-tuple-element.74.refs_4_), channel_id=1, source_target_pairs={{0,4},{4,0},{8,12},{12,8},{16,20},{20,16},{24,28},{28,24},{1,5},{5... | collective-permute-start | bytes 294920 | tf_op jit(solution)/shard_map/ppermute | solution.py:579
  25.4 4.8 %collective-permute-start.6 = (bf16[128,256]{1,0:T(8,128)(2,1)S(1)}, bf16[128,256]{1,0:T(8,128)(2,1)S(1)}, u32[]{:S(2)}, u32[]{:S(2)}) collective-permute-start(bf16[128,256]{1,0:T(8,128)(2,1)S(1)} %get-tuple-element.83), channel_id=1, source_target_pairs={{0,4},{4,0},{8,12},{12,8},{16,20},{20,16},{24,28},{28,24},{1,5},{5... | collective-permute-start | bytes 196616 | tf_op jit(solution)/shard_map/ppermute | solution.py:579
  30.8 1.8 %collective-permute-start.8 = (bf16[392,512]{1,0:T(8,128)(2,1)S(1)}, bf16[392,512]{1,0:T(8,128)(2,1)S(1)}, u32[]{:S(2)}, u32[]{:S(2)}) collective-permute-start(bf16[392,512]{1,0:T(8,128)(2,1)S(1)} %get-tuple-element.87.refs_3_.mine_ref), channel_id=1, source_target_pairs={{0,1},{1,0},{2,3},{3,2},{4,5},{5,4},{6,7},{7,6},{8,9},{9,8},{10,11... | collective-permute-start | bytes 1204232 | tf_op jit(solution)/shard_map/ppermute | solution.py:582
  31.3 3.0 %collective-permute-start.7 = (bf16[256,512]{1,0:T(8,128)(2,1)S(1)}, bf16[256,512]{1,0:T(8,128)(2,1)S(1)}, u32[]{:S(2)}, u32[]{:S(2)}) collective-permute-start(bf16[256,512]{1,0:T(8,128)(2,1)S(1)} %get-tuple-element.89), channel_id=1, source_target_pairs={{0,1},{1,0},{2,3},{3,2},{4,5},{5,4},{6,7},{7,6},{8,9},{9,8},{10,11... | collective-permute-start | bytes 786440 | tf_op jit(solution)/shard_map/ppermute | solution.py:582
  32.7 12.2 %collective-permute-start.14 = (bf16[392,512]{1,0:T(8,128)(2,1)S(1)}, bf16[392,512]{1,0:T(8,128)(2,1)S(1)}, u32[]{:S(2)}, u32[]{:S(2)}) collective-permute-start(bf16[392,512]{1,0:T(8,128)(2,1)S(1)} %shard_map.123.refs_2_.factor_ref), channel_id=1, source_target_pairs={{0,2},{1,3},{2,0},{3,1},{4,6},{5,7},{6,4},{7,5},{8,10},{9,11},{10,... | collective-permute-start | bytes 1204232 | tf_op jit(solution)/shard_map/ppermute | solution.py:582
  35.6 1.5 %collective-permute-start.9 = (bf16[160,512]{1,0:T(8,128)(2,1)S(1)}, bf16[160,512]{1,0:T(8,128)(2,1)S(1)}, u32[]{:S(2)}, u32[]{:S(2)}) collective-permute-start(bf16[160,512]{1,0:T(8,128)(2,1)S(1)} %get-tuple-element.91), channel_id=1, source_target_pairs={{0,1},{1,0},{2,3},{3,2},{4,5},{5,4},{6,7},{7,6},{8,9},{9,8},{10,11... | collective-permute-start | bytes 491528 | tf_op jit(solution)/shard_map/ppermute | solution.py:582
  35.7 14.0 %collective-permute-start.13 = (bf16[256,512]{1,0:T(8,128)(2,1)S(1)}, bf16[256,512]{1,0:T(8,128)(2,1)S(1)}, u32[]{:S(2)}, u32[]{:S(2)}) collective-permute-start(bf16[256,512]{1,0:T(8,128)(2,1)S(1)} %shard_map.124.refs_5_), channel_id=1, source_target_pairs={{0,2},{1,3},{2,0},{3,1},{4,6},{5,7},{6,4},{7,5},{8,10},{9,11},{10,... | collective-permute-start | bytes 786440 | tf_op jit(solution)/shard_map/ppermute | solution.py:582
  36.4 1.4 %collective-permute-start.10 = (bf16[160,512]{1,0:T(8,128)(2,1)S(1)}, bf16[160,512]{1,0:T(8,128)(2,1)S(1)}, u32[]{:S(2)}, u32[]{:S(2)}) collective-permute-start(bf16[160,512]{1,0:T(8,128)(2,1)S(1)} %get-tuple-element.92), channel_id=1, source_target_pairs={{0,1},{1,0},{2,3},{3,2},{4,5},{5,4},{6,7},{7,6},{8,9},{9,8},{10,11... | collective-permute-start | bytes 491528 | tf_op jit(solution)/shard_map/ppermute | solution.py:582
  36.4 1.6 %collective-permute-start.11 = (bf16[160,512]{1,0:T(8,128)(2,1)S(1)}, bf16[160,512]{1,0:T(8,128)(2,1)S(1)}, u32[]{:S(2)}, u32[]{:S(2)}) collective-permute-start(bf16[160,512]{1,0:T(8,128)(2,1)S(1)} %get-tuple-element.93), channel_id=1, source_target_pairs={{0,1},{1,0},{2,3},{3,2},{4,5},{5,4},{6,7},{7,6},{8,9},{9,8},{10,11... | collective-permute-start | bytes 491528 | tf_op jit(solution)/shard_map/ppermute | solution.py:582
  37.1 1.4 %collective-permute-start.12 = (bf16[160,512]{1,0:T(8,128)(2,1)S(1)}, bf16[160,512]{1,0:T(8,128)(2,1)S(1)}, u32[]{:S(2)}, u32[]{:S(2)}) collective-permute-start(bf16[160,512]{1,0:T(8,128)(2,1)S(1)} %get-tuple-element.94), channel_id=1, source_target_pairs={{0,1},{1,0},{2,3},{3,2},{4,5},{5,4},{6,7},{7,6},{8,9},{9,8},{10,11... | collective-permute-start | bytes 491528 | tf_op jit(solution)/shard_map/ppermute | solution.py:582

commit v8 on v7

--- a/solution.py
+++ b/solution.py
@@ -115,18 +115,18 @@
         rows_ref[at : at + 1] = jnp.broadcast_to(row, (1, lanes))
 
 
-def half_state(half, width, vecs, tails_ref, through_row, last, x_ref, first_lane, out_ref):
+def some_state(half, half_w, lanes, width, vecs, tails_ref, through_row, last, x_ref, first_lane, out_ref):
     state = vecs.shape[0]
-    half_w = out_ref.shape[1]
     per = LANES // width
     half_h = half_w // width
+    skipped = lanes.start // width
     lane = lane_iota(state)
     mine = jnp.where(half == 1, pltpu.roll(through_row, LANES - half_h, 1), through_row)
     own, through = [], []
-    for i in range(half_w // LANES):
+    for i in range((lanes.stop - lanes.start) // LANES):
         written = []
         for k in range(per):
-            row = tails_ref[pl.ds(half * half_h + i * per + k, 1), :]
+            row = tails_ref[pl.ds(half * half_h + skipped + i * per + k, 1), :]
             written.append((vecs * row).astype(BF16))
         here = pl.ds(pl.multiple_of(first_lane + i * LANES, LANES), LANES)
         both = dot(jnp.concatenate(written, axis=0), x_ref[:, here])
@@ -134,8 +134,9 @@
         for k in range(1, per):
             tile = jnp.where(lane < k * width, tile, both[k * state : (k + 1) * state])
         own.append(tile)
-        through.append(spread(mine[0:1], i * per, width))
-    group = (jnp.concatenate(own, axis=1), jnp.concatenate(through, axis=1), jnp.broadcast_to(last, (1, half_w)))
+        through.append(spread(mine[0:1], skipped + i * per, width))
+    ids = jnp.broadcast_to(last, (1, lanes.stop - lanes.start))
+    group = (jnp.concatenate(own, axis=1), jnp.concatenate(through, axis=1), ids)
     pack(out_ref, group)
 
 
@@ -149,7 +150,7 @@
         hbm, (other_ref, stash_ref) = refs[: len(arrays)], refs[len(arrays) : -8]
         raw_ref, seg_ref, dl_ref, sb_ref, wr_ref, x_ref, rows, sems = refs[-8:]
         half = position()[1]
-        lanes = pl.ds(pl.multiple_of(half * half_w, LANES), half_w)
+        lanes = pl.ds(pl.multiple_of(half * half_w, LANES), EARLY_LANES)
         sources = (*hbm[:5], hbm[5].at[:, lanes])
         copies = [
             pltpu.make_async_copy(src, dst, sems.at[k])
@@ -198,17 +199,18 @@
         sums = jnp.transpose(rows[...])[0:8]
         stash_ref[sum_rows, 0:LANES] = sums
         copies[5].wait()
-        half_state(half, width, vecs, stash_ref.at[tail_rows], sums, last, x_ref, 0, other_ref)
+        piece = slice(0, EARLY_LANES)
+        some_state(half, half_w, piece, width, vecs, stash_ref.at[tail_rows], sums, last, x_ref, 0, other_ref)
 
     vm = pl.BlockSpec(memory_space=pltpu.VMEM)
-    out_shape = shaped(((state + EXTRA, half_w), BF16), ((stash_rows()[-1].stop, toks), F32))
+    out_shape = shaped(((state + EXTRA, EARLY_LANES), BF16), ((stash_rows()[-1].stop, toks), F32))
     return pl.pallas_call(
         body,
         in_specs=[pl.BlockSpec(memory_space=pltpu.HBM)] * len(arrays),
         out_specs=[vm] * len(out_shape),
         out_shape=out_shape,
         scratch_shapes=[
-            *[pltpu.VMEM(a.shape, a.dtype) for a in arrays[:5]], pltpu.VMEM((toks, half_w), BF16),
+            *[pltpu.VMEM(a.shape, a.dtype) for a in arrays[:5]], pltpu.VMEM((toks, EARLY_LANES), BF16),
             pltpu.VMEM((LANES, LANES), F32), pltpu.SemaphoreType.DMA((len(arrays),)),
         ],
         compiler_params=pltpu.CompilerParams(vmem_limit_bytes=VMEM_ALL),
@@ -216,19 +218,25 @@
     )(*arrays)
 
 
-def kept_state(width, stash, x, write):
+def more_states(width, stash, x, write):
     toks, state = write.shape
     half_w = x.shape[1] // 2
-
-    def body(stash_ref, x_ref, wr_ref, keep_ref):
-        half = position()[0]
-        cum_rows, _, tail_rows, sum_rows = stash_rows()
+    one, two = slice(0, EARLY_LANES), slice(EARLY_LANES, half_w)
+    pieces = ((1, two), (0, one), (0, two))
+
+    def body(stash_ref, x_ref, wr_ref, *outs):
+        _, _, tail_rows, sum_rows = stash_rows()
         vecs = jnp.transpose(wr_ref[...].astype(F32))
         last = stash_ref[SEG_LANE : SEG_LANE + 1, toks - 1 : toks]
         sums = stash_ref[sum_rows, 0:LANES]
-        half_state(half, width, vecs, stash_ref.at[tail_rows], sums, last, x_ref, half * half_w, keep_ref)
-
-    return call(body, (stash, x, write), jax.ShapeDtypeStruct((state + EXTRA, half_w), BF16), cost=LONG)
+        tails_ref = stash_ref.at[tail_rows]
+        for (which, lanes), out_ref in zip(pieces, outs):
+            half = position()[which]
+            first = half * half_w + lanes.start
+            some_state(half, half_w, lanes, width, vecs, tails_ref, sums, last, x_ref, first, out_ref)
+
+    out = shaped(*[((state + EXTRA, lanes.stop - lanes.start), BF16) for _, lanes in pieces])
+    return call(body, (stash, x, write), out, cost=LONG)
 
 
 def gather_level(upper, entry, other):
@@ -239,28 +247,22 @@
     return state, through * jnp.where(upper, other[1], 1.0), last_id
 
 
-def pair_step(keep, mate, after):
-    size, width = mate.shape[0] - EXTRA, mate.shape[1]
-    pieces = (slice(0, EARLY_LANES), slice(EARLY_LANES, width))
-
-    def body(keep_ref, mate_ref, *refs):
+def pair_step(keep, mate, after=None):
+    size, lanes = mate.shape[0] - EXTRA, mate.shape[1]
+
+    def body(keep_ref, mate_ref, send_ref, total_ref, rows_ref, first_ref):
         odd = position()[0] == 1
         mine, mate = unpack(keep_ref), unpack(mate_ref)
         total = merged(odd, mine, mate)
         first = tuple(jnp.where(odd, m, o) for o, m in zip(mine, mate))
-        rows = (jnp.ones_like(total[1]), jnp.full_like(total[2], -1.0)) + first[1:] + total[1:]
-        for k, lanes in enumerate(pieces):
-            send_ref, total_ref, rows_ref, first_ref = refs[4 * k : 4 * k + 4]
-            pack(send_ref, tuple(t[:, lanes] for t in total))
-            total_ref[...], first_ref[...] = total[0][:, lanes], first[0][:, lanes]
-            put_rows(rows_ref, [row[:, lanes] for row in rows])
-
-    out = []
-    for lanes in pieces:
-        wide = lanes.stop - lanes.start
-        out += shaped(((size + EXTRA, wide), BF16), ((size, wide), F32), ((8, wide), F32), ((size, wide), F32))
-    out = call(body, (keep, mate), out, after=after, cost=LONG)
-    return out[:4], out[4:]
+        pack(send_ref, total)
+        total_ref[...], first_ref[...] = total[0], first[0]
+        put_rows(rows_ref, (jnp.ones_like(total[1]), jnp.full_like(total[2], -1.0)) + first[1:] + total[1:])
+
+    state = ((size, lanes), F32)
+    return call(
+        body, (keep, mate), shaped((mate.shape, BF16), state, ((8, lanes), F32), state), after=after, cost=LONG
+    )
 
 
 def level_step(bit, more, got, total, rows, entry=None, after=None):
@@ -306,7 +308,62 @@
     return call(body, (got, entry, rows, first), shaped(block, block, *prev), after=after)
 
 
-def local_part(which, heads, width, x, gate, read, write, stash, skip, after):
+def local_setup(heads, width, read, write, stash, skip, after):
+    toks = write.shape[0]
+    half_h = heads // 2
+    blocks = toks // GROUP
+
+    def body(
+        rd_ref, wr_ref, stash_ref, skip_ref,
+        scores, linked_ref, log_cum, log_row, tails, skips, seg_out, pad, rows_ref,
+    ):
+        cum_ref, step_ref = (stash_ref.at[rows] for rows in stash_rows()[:2])
+        second = [position()[which] == 1 for which in range(2)]
+        pad[...] = jnp.zeros_like(pad)
+        rows_ref[...] = jnp.zeros_like(rows_ref)
+        rows_ref[0:1, 0:heads] = skip_ref[...]
+        turned = pltpu.roll(rows_ref[...], LANES - half_h, 1)
+        for which in range(2):
+            skips[which] = jnp.where(second[which], turned, rows_ref[...])
+        seg_row = cum_ref[SEG_LANE : SEG_LANE + 1]
+        log_row[...] = cum_ref[...] * LOG2E - jnp.log(step_ref[...]) * LOG2E
+        pad[0:32] = cum_ref[...] * LOG2E
+        pad[SEG_LANE : SEG_LANE + 1] = seg_row
+        columns = jnp.transpose(pad[...])
+        seg_col = columns[:, SEG_LANE : SEG_LANE + 1]
+        turned = pltpu.roll(columns, LANES - half_h, 1)
+        for which in range(2):
+            log_cum[which] = jnp.where(second[which], turned, columns)
+        seg_out[...] = columns
+        tail0 = jnp.exp(cum_ref[:, GROUP - 1 : GROUP] - cum_ref[:, 0:GROUP]) * step_ref[:, 0:GROUP]
+        same = seg_row[:, 0:GROUP] == seg_row[:, GROUP - 1 : GROUP]
+        pad[0:32, 0:GROUP] = jnp.where(same, tail0, 0.0)
+        columns = jnp.transpose(pad[:, 0:GROUP])
+        turned = pltpu.roll(columns, LANES - half_h, 1)
+        for which in range(2):
+            tails[which] = jnp.where(second[which], turned, columns)
+        causal = lax.broadcasted_iota(jnp.int32, (GROUP, GROUP), 0) >= lax.broadcasted_iota(
+            jnp.int32, (GROUP, GROUP), 1
+        )
+        for b in range(blocks):
+            rows = slice(b * GROUP, (b + 1) * GROUP)
+            s = dot(rd_ref[rows], wr_ref[rows], ((1,), (1,)))
+            scores[b] = jnp.where(causal & (seg_col[rows] == seg_row[:, rows]), s, 0.0)
+        linked = seg_col[GROUP:] == seg_col[GROUP - 1 : GROUP]
+        linked_ref[...] = jnp.where(linked, rd_ref[GROUP:].astype(F32), 0.0).astype(BF16)
+
+    return call(
+        body, (read, write, stash, skip),
+        shaped(
+            ((blocks, GROUP, GROUP), F32), ((toks - GROUP, read.shape[1]), BF16), ((2, toks, LANES), F32),
+            ((32, toks), F32), ((2, GROUP, LANES), F32), ((2, 8, LANES), F32), ((toks, LANES), F32),
+        ),
+        [pltpu.VMEM((LANES, toks), F32), pltpu.VMEM((8, LANES), F32)],
+        cost=LONG, after=after,
+    )
+
+
+def local_part(which, tiles, heads, width, x, gate, write, setup, after):
     toks = write.shape[0]
     half_w = x.shape[1] // 2
     half_h = heads // 2
@@ -315,57 +372,27 @@
     strip = 64
 
     def body(
-        x_ref, gate_ref, rd_ref, wr_ref, stash_ref, skip_ref,
-        a_ref, b_ref, *refs,
+        x_ref, gate_ref, wr_ref, scores, linked_ref, log_cum, log_row, tails, skips, a_ref, b_ref, mix
     ):
-        *seg_out, log_cum, log_row, scores, mix, pad, tails, rows_ref = refs
         half = position()[which]
-        second = half == 1
-        cum_ref, step_ref = (stash_ref.at[rows] for rows in stash_rows()[:2])
         lane = lane_iota(GROUP)
-        mix[...] = jnp.zeros_like(mix)
-        pad[...] = jnp.zeros_like(pad)
-        rows_ref[...] = jnp.zeros_like(rows_ref)
-        rows_ref[0:1, 0:heads] = skip_ref[...]
-        skips = jnp.where(second, pltpu.roll(rows_ref[...], LANES - half_h, 1), rows_ref[...])[0:1]
-        seg_row = cum_ref[SEG_LANE : SEG_LANE + 1]
-        log_row[...] = cum_ref[...] * LOG2E - jnp.log(step_ref[...]) * LOG2E
-        pad[0:32] = cum_ref[...] * LOG2E
-        pad[SEG_LANE : SEG_LANE + 1] = seg_row
-        columns = jnp.transpose(pad[...])
-        seg_col = columns[:, SEG_LANE : SEG_LANE + 1]
-        log_cum[...] = jnp.where(second, pltpu.roll(columns, LANES - half_h, 1), columns)
-        if seg_out:
-            seg_out[0][...] = columns
-        tail0 = jnp.exp(cum_ref[:, GROUP - 1 : GROUP] - cum_ref[:, 0:GROUP]) * step_ref[:, 0:GROUP]
-        same = seg_row[:, 0:GROUP] == seg_row[:, GROUP - 1 : GROUP]
-        pad[0:32, 0:GROUP] = jnp.where(same, tail0, 0.0)
-        columns = jnp.transpose(pad[:, 0:GROUP])
-        tails[...] = jnp.where(second, pltpu.roll(columns, LANES - half_h, 1), columns)
-        masked = []
-        for b in range(blocks):
-            rows = slice(b * GROUP, (b + 1) * GROUP)
-            s = dot(rd_ref[rows], wr_ref[rows], ((1,), (1,)))
-            causal = lax.broadcasted_iota(jnp.int32, (GROUP, GROUP), 0) >= lax.broadcasted_iota(
-                jnp.int32, (GROUP, GROUP), 1
-            )
-            scores[b] = jnp.where(causal & (seg_col[rows] == seg_row[:, rows]), s, 0.0)
-            linked = seg_col[rows] == seg_col[b * GROUP - 1 : b * GROUP] if b else None
-            masked.append(jnp.where(linked, rd_ref[rows].astype(F32), 0.0).astype(BF16) if b else None)
-        for i in range(half_w // LANES):
-            tile = slice(i * LANES, (i + 1) * LANES)
+        for slot in range(mix.shape[0]):
+            for k in range(per):
+                mix[slot, k * GROUP : k * GROUP + LANES, LANES:] = jnp.zeros((LANES, GROUP - LANES), BF16)
+        for n, i in enumerate(tiles):
             there = pl.ds(pl.multiple_of(half * half_w + i * LANES, LANES), LANES)
-            gains = spread(skips, i * per, width)
+            tile = slice(n * LANES, (n + 1) * LANES)
+            gains = spread(skips[which, 0:1], i * per, width)
             carry = None
             start = jnp.ones((1, LANES), F32)
             for b in range(blocks):
                 rows = slice(b * GROUP, (b + 1) * GROUP)
-                slot = (i * blocks + b) % mix.shape[0]
+                slot = (n * blocks + b) % mix.shape[0]
                 xb = x_ref[rows, there]
                 logs = []
                 for k in range(per):
                     head = i * per + k
-                    cb = jnp.broadcast_to(log_cum[rows, head : head + 1], (GROUP, LANES))
+                    cb = jnp.broadcast_to(log_cum[which, rows, head : head + 1], (GROUP, LANES))
                     logs.append(cb)
                     ar = log_row[pl.ds(half * half_h + head, 1), rows]
                     for low in range(0, GROUP, strip):
@@ -384,9 +411,9 @@
                 xf = xb.astype(F32)
                 y = inner + gains * xf
                 if b == 1:
-                    y = y + (dot(masked[b], carry[0]) + dot(masked[b], carry[1])) * dec
+                    y = y + (dot(linked_ref[...], carry[0]) + dot(linked_ref[...], carry[1])) * dec
                 else:
-                    xs = (xf * spread(tails[...], i * per, width)).astype(BF16)
+                    xs = (xf * spread(tails[which], i * per, width)).astype(BF16)
                     s0 = dot(wr_ref[rows], xs, ((0,), (0,)))
                     s0h = s0.astype(BF16)
                     carry = (s0h, (s0 - s0h.astype(F32)).astype(BF16))
@@ -396,27 +423,27 @@
                 b_ref[rows, tile] = sg * (dec * start)
                 start = start * dec[GROUP - 1 : GROUP]
 
+    out = ((toks, len(tiles) * LANES), F32)
     return call(
-        body, (x, gate, read, write, stash, skip),
-        shaped(((toks, half_w), F32), ((toks, half_w), F32), *((((toks, LANES), F32),) if which == 0 else ())),
-        [
-            pltpu.VMEM((toks, LANES), F32), pltpu.VMEM((32, toks), F32),
-            pltpu.VMEM((blocks, GROUP, GROUP), F32), pltpu.VMEM((4, per * GROUP, GROUP), BF16),
-            pltpu.VMEM((LANES, toks), F32), pltpu.VMEM((GROUP, LANES), F32), pltpu.VMEM((8, LANES), F32),
-        ],
-        after=after, cost=LONG,
-    )
-
-
-def gated_part(which, lanes, prev_ref, rd_ref, cum_ref, a_ref, b_ref, states, gain_ref):
-    half_w = a_ref.shape[1]
+        body, (x, gate, write, *setup), shaped(out, out), [pltpu.VMEM((4, per * GROUP, GROUP), BF16)],
+        cost=LONG, after=after,
+    )
+
+
+def side_by_side(refs):
+    values = [ref[...] for ref in refs]
+    return values[0] if len(values) == 1 else jnp.concatenate(values, axis=1)
+
+
+def gated_part(which, lanes, prev_ref, rd_ref, cum_ref, a_refs, b_refs, states, gain_ref):
+    half_w = gain_ref.shape[1] // 2
     first = pl.multiple_of(position()[which] * half_w + lanes.start, LANES)
     here = pl.ds(first, lanes.stop - lanes.start)
     linked = cum_ref[:, SEG_LANE : SEG_LANE + 1] == prev_ref[0:1, 0:1]
     rm = jnp.where(linked, rd_ref[...].astype(F32), 0.0).astype(BF16)
     carried = [dot(rm, state[...]) for state in states]
     carried = carried[0] if len(carried) == 1 else jnp.concatenate(carried, axis=1)
-    gated = a_ref[:, lanes] + b_ref[:, lanes] * carried
+    gated = side_by_side(a_refs) + side_by_side(b_refs) * carried
     sq = gated * gated
     part = sq[:, 0:LANES]
     for i in range(1, sq.shape[1] // LANES):
@@ -447,52 +474,59 @@
     return whole[0:size], whole[size : size + 1] + (whole[size + 1 : size + 2] + whole[size + 2 : size + 3])
 
 
-def gated_sums(which, lanes, prev, read, cum, a, b, states, gain, weight, partial=None, squares=None):
-    toks = a.shape[0]
+def gated_sums(which, lanes, prev, read, seg, a, b, states, gain, weight, partial=None, squares=None):
+    toks = read.shape[0]
     cols = weight.shape[1] // 4
     earlier = () if partial is None else (partial, squares)
-
-    def body(prev_ref, rd_ref, cum_ref, a_ref, b_ref, gain_ref, w_ref, *refs):
-        states = refs[: len(states_in)]
-        old, (g_ref, s_ref, y_ref) = refs[len(states_in) : -3], refs[-3:]
-        g, s = gated_part(which, lanes, prev_ref, rd_ref, cum_ref, a_ref, b_ref, states, gain_ref)
+    ends = [0, len(a), len(a) + len(b), len(a) + len(b) + len(states)]
+
+    def body(prev_ref, rd_ref, seg_ref, gain_ref, w_ref, *refs):
+        a_refs, b_refs, s_refs = (refs[low:high] for low, high in zip(ends, ends[1:]))
+        old, (g_ref, s_ref, y_ref) = refs[ends[-1] : -3], refs[-3:]
+        g, s = gated_part(which, lanes, prev_ref, rd_ref, seg_ref, a_refs, b_refs, s_refs, gain_ref)
         g_ref[...] = g
         s_ref[...] = s + old[1][...] if old else s
-        for quarter in range(2):
-            y = projected(which, lanes, quarter, slice(0, cols), w_ref, g)
-            y_ref[quarter] = y + old[0][quarter] if old else y
-
-    states_in = states
+        y = projected(which, lanes, 0, slice(0, cols), w_ref, g)
+        y_ref[...] = y + old[0][...] if old else y
+
     return call(
-        body, (prev, read, cum, a, b, gain, weight, *states, *earlier),
-        shaped(((toks, lanes.stop - lanes.start), BF16), ((1, toks), F32), ((2, cols, toks), F32)),
-    )
-
-
-def gated_last(lanes, rows, prev, read, cum, a, b, state, gain, weight, partial, squares):
-    toks = a.shape[0]
-
-    def body(prev_ref, rd_ref, cum_ref, a_ref, b_ref, e_ref, gain_ref, w_ref, p_ref, s_ref, g_ref, y_ref):
-        g, s = gated_part(1, lanes, prev_ref, rd_ref, cum_ref, a_ref, b_ref, (e_ref,), gain_ref)
+        body, (prev, read, seg, gain, weight, *a, *b, *states, *earlier),
+        shaped(((toks, lanes.stop - lanes.start), BF16), ((1, toks), F32), ((cols, toks), F32)),
+    )
+
+
+def gated_last(lanes, rows, prev, read, seg, a, b, state, gain, weight, partial, squares):
+    toks = read.shape[0]
+
+    def body(prev_ref, rd_ref, seg_ref, a_ref, b_ref, e_ref, gain_ref, w_ref, p_ref, s_ref, g_ref, y_ref):
+        g, s = gated_part(1, lanes, prev_ref, rd_ref, seg_ref, (a_ref,), (b_ref,), (e_ref,), gain_ref)
         g_ref[...] = g
-        y = p_ref[0, rows] + projected(1, lanes, 0, rows, w_ref, g)
+        y = p_ref[rows] + projected(1, lanes, 0, rows, w_ref, g)
         y_ref[...] = with_squares(y, s_ref[...] + s)
 
     return call(
-        body, (prev, read, cum, a, b, state, gain, weight, partial, squares),
+        body, (prev, read, seg, a, b, state, gain, weight, partial, squares),
         shaped(((toks, lanes.stop - lanes.start), BF16), ((rows.stop - rows.start + EXTRA, toks), BF16)),
     )
 
 
-def project_last(lanes, pieces, g, partial, weight, after):
-    def body(g_ref, p_ref, w_ref, *outs):
-        for (quarter, rows, dtype), y_ref in zip(pieces, outs):
-            y = p_ref[quarter, rows] + projected(1, lanes, quarter, rows, w_ref, g_ref[...])
-            y_ref[...] = y.astype(dtype)
-
-    toks = g.shape[0]
-    out = shaped(*[((rows.stop - rows.start, toks), dtype) for _, rows, dtype in pieces])
-    return call(body, (g, partial, weight), out, after=after)
+def project_next(groups, gs, top, rest, partial, weight, after):
+    toks = gs[0].shape[0]
+
+    def body(p_ref, w_ref, *refs):
+        g_refs, (near_ref, top_ref, rest_ref) = refs[: len(gs)], refs[len(gs) :]
+        which, lanes = groups[-1]
+        near = p_ref[rest] + projected(which, lanes, 0, rest, w_ref, g_refs[-1][...])
+        near_ref[...] = near.astype(BF16)
+        for rows, y_ref in ((top, top_ref), (rest, rest_ref)):
+            y_ref[...] = sum(
+                projected(which, lanes, 1, rows, w_ref, g_ref[...])
+                for (which, lanes), g_ref in zip(groups, g_refs)
+            )
+
+    size = rest.stop - rest.start
+    out = shaped(((size, toks), BF16), ((top.stop, toks), F32), ((size, toks), F32))
+    return call(body, (partial, weight, *gs), out, after=after)
 
 
 def project_whole(quarter, groups, gs, weight, pieces, adds=(), after=None):
@@ -581,52 +615,68 @@
     def across(a, bit):
         return lax.ppermute(a, "tp", [(i, i ^ bit) for i in range(n_tp)])
 
-    other, stash = prepare(
+    other_one, stash = prepare(
         heads, width, step_raw, segment_ids.reshape(1, toks), decay_log.reshape(1, heads),
         step_bias.reshape(1, heads), head_input, write_vecs,
     )
-    mate = swap(other, 1)
-    keep = kept_state(width, stash, head_input, write_vecs)
-    local = (heads, width, head_input, gate_input, read_vecs, write_vecs, stash, skip_gain.reshape(1, heads))
-    a_keep, b_keep, log_cum = local_part(0, *local, keep)
-    sent, totals, rows, firsts = zip(*pair_step(keep, mate, a_keep))
+    mate_one = swap(other_one, 1)
+    other_two, keep_one, keep_two = more_states(width, stash, head_input, write_vecs)
+    mate_two = swap(other_two, 1)
+    *setup, seg = local_setup(
+        heads, width, read_vecs, write_vecs, stash, skip_gain.reshape(1, heads), other_two
+    )
+
+    def local(which, tiles, after):
+        return local_part(which, tiles, heads, width, head_input, gate_input, write_vecs, setup, after)
+
+    tiles = feats // 2 // LANES
+    edge = EARLY_LANES // LANES
+    early = pair_step(keep_one, mate_one, seg)
+    keep_a = local(0, range(0, tiles - edge), early[0])
+    late = pair_step(keep_two, mate_two, keep_a[0])
+    keep_b = local(0, range(tiles - edge, tiles), late[0])
+    sent, totals, rows, firsts = zip(early, late)
     entries = [()] * 2
-    bit = 2
+    bit, before = 2, keep_b[0]
     while 2 * bit < n_seq:
         more = 4 * bit < n_seq
         got = [swap(piece, bit) for piece in sent]
-        early = level_step(bit, more, got[0], totals[0], rows[0], *entries[0])
-        late = level_step(bit, more, got[1], totals[1], rows[1], *entries[1], after=early[0])
+        early = level_step(bit, more, got[0], totals[0], rows[0], *entries[0], after=before)
+        if bit == 2:
+            other_a = local(1, range(0, edge), early[0])
+        late = level_step(bit, more, got[1], totals[1], rows[1], *entries[1], after=other_a[0] if bit == 2 else early[0])
         sent, entries, rows, *totals = zip(early, late)
         totals, entries = totals[0] if more else (), [(entry,) for entry in entries]
-        bit *= 2
-    a_other, b_other, *_ = local_part(1, *local, sent[1])
+        bit, before = bit * 2, None
+    other_b = local(1, range(edge, tiles), sent[1])
     half_w = feats // 2
     quarter = out_weight.shape[1] // 4
     one, two = slice(0, EARLY_LANES), slice(EARLY_LANES, half_w)
     top, rest, every = slice(0, EARLY_ROWS), slice(EARLY_ROWS, quarter), slice(0, quarter)
     send_one, keep_one, prev = entry_step(
-        bit, True, swap(sent[0], bit), *entries[0], rows[0], firsts[0], a_other
+        bit, True, swap(sent[0], bit), *entries[0], rows[0], firsts[0], other_b[0]
     )
     other_one = swap(send_one, 1)
     send_two, keep_two = entry_step(bit, False, swap(sent[1], bit), *entries[1], rows[1], firsts[1], send_one)
     other_two = swap(send_two, 1)
     gain = norm_gain.reshape(1, feats)
-    kept, rest_of = (prev, read_vecs, log_cum, a_keep, b_keep), (prev, read_vecs, log_cum, a_other, b_other)
-    g_near, squares, partial = gated_sums(0, one, *kept, (keep_one,), gain, out_weight)
-    g_keep, squares, partial = gated_sums(0, two, *kept, (keep_two,), gain, out_weight, partial, squares)
-    g_one, squares, partial = gated_sums(1, one, *rest_of, (other_one,), gain, out_weight, partial, squares)
-    g_two, near_top = gated_last(two, top, *rest_of, other_two, gain, out_weight, partial, squares)
+    shared = (prev, read_vecs, seg)
+    whole_half = slice(0, half_w)
+    g_keep, squares, partial = gated_sums(
+        0, whole_half, *shared, (keep_a[0], keep_b[0]), (keep_a[1], keep_b[1]), (keep_one, keep_two), gain, out_weight
+    )
+    g_one, squares, partial = gated_sums(
+        1, one, *shared, other_a[:1], other_a[1:], (other_one,), gain, out_weight, partial, squares
+    )
+    g_two, near_top = gated_last(two, top, *shared, *other_b, other_two, gain, out_weight, partial, squares)
     got_top = across(near_top, 1)
-    near_rest, far_top, far_rest = project_last(
-        two, ((0, rest, BF16), (1, top, F32), (1, rest, F32)), g_two, partial, out_weight, near_top
-    )
+    groups, gs = ((0, whole_half), (1, one), (1, two)), (g_keep, g_one, g_two)
+    near_rest, far_top, far_rest = project_next(groups, gs, top, rest, partial, out_weight, near_top)
     got_rest = across(near_rest, 1)
     to_far_top = add_first(far_top, near_top, got_top)
     got_far_top = across(to_far_top, 2)
     to_far_rest = add_second(far_rest, got_rest, to_far_top)
     got_far_rest = across(to_far_rest, 2)
-    groups, gs = ((0, one), (0, two), (1, one), (1, two)), (g_near, g_keep, g_one, g_two)
     y_near = project_whole(2, groups, gs, out_weight, NEAR_PIECES, after=to_far_rest)
     got_own = tuple(across(piece, 1) for piece in y_near)
     (y_own,) = project_whole(3, groups, gs, out_weight, 1, got_own)

time: 50.6 us -> 49.6 us (0.980)
  starting transfers between devices: 15.1 us -> 17.9 us
  waiting for transfers between devices: 16 us -> 13.3 us
  local copies, waits for them, and re-layouts: 1.8 us -> 1.18 us
    ppermute x7 -> x8, starting transfers between devices: 11.5 us -> 13.8 us  [swap(): return lax.ppermute(a, 'seq', [(i, i ^ bit) for i in range(n_seq)])]
    ppermute x7 -> x8, waiting for transfers between devices: 4.71 us -> 3.26 us  [swap(): return lax.ppermute(a, 'seq', [(i, i ^ bit) for i in range(n_seq)])]
    ppermute x8, waiting for transfers between devices: 11.3 us -> 10.1 us  [across(): return lax.ppermute(a, 'tp', [(i, i ^ bit) for i in range(n_tp)])]
    unnamed x20, local copies, waits for them, and re-layouts: 1.79 us -> 1.17 us
    pallas_call x17 -> x20, Pallas kernels: 12.9 us -> 12.6 us  [call(): pl.pallas_call(kernel, in_specs=specs, out_specs=jax.tree.map(lambda _: v...]
  transfers between devices with their start and end apart: 15 -> 16, of which waited for: 9 -> 8; matrix products, arithmetic and copies ran while one was open for 0% -> 0% of each run, Pallas kernels for 26% -> 26%
where the time goes in v8:
time: 49.6 us; the launch traced here: 49.5 us
  starting transfers between devices  17.9 us (36%)
  Pallas kernels  16.8 us (34%)
  waiting for transfers between devices  13.3 us (27%)
  local copies, waits for them, and re-layouts  1.18 us (2%)
    ppermute x8, starting transfers between devices, swap(): return lax.ppermute(a, 'seq', [(i, i ^ bit) for i in range(n_seq)])  13.8 us
    pallas_call x20, Pallas kernels, call(): pl.pallas_call(kernel, in_specs=specs, out_specs=jax.tree.map(lambda _: v...  12.6 us
    ppermute x8, waiting for transfers between devices, across(): return lax.ppermute(a, 'tp', [(i, i ^ bit) for i in range(n_tp)])  10.1 us
    ppermute x8, starting transfers between devices, across(): return lax.ppermute(a, 'tp', [(i, i ^ bit) for i in range(n_tp)])  4.14 us
    ppermute x8, waiting for transfers between devices, swap(): return lax.ppermute(a, 'seq', [(i, i ^ bit) for i in range(n_seq)])  3.26 us
    pallas_call x1, Pallas kernels, prepare(): pl.pallas_call(body, in_specs=[pl.BlockSpec(memory_space=pltpu.HBM)] * le...  2.65 us
    pallas_call x2, Pallas kernels, finish(): pl.pallas_call(body, in_specs=[vm] * 3 + ([] if first else [where]), out_...  1.57 us
    unnamed x20, local copies, waits for them, and re-layouts  1.17 us
  transfers between devices with their start and end apart: 16, of which 8 were waited for; matrix products, arithmetic and copies ran while one was open for 0% of the time, Pallas kernels for 26%

profile of v8, /device:TPU:0, one launch (start us, length us, event | category | flops | bytes accessed | tf_op | source)
XLA Modules:
  0.0 49.5 jit_solution(7968920783271752708)
XLA Ops:
  0.0 2.7 %shard_map.109 = (bf16[136,384]{1,0:T(8,128)(2,1)}, f32[104,512]{1,0:T(8,128)}) custom-call(bf16[20,512]{1,0:T(8,128)(2,1)} %refs_0_.7, s32[1,512]{1,0:T(1,128)} %bitcast.7, f32[1,20]{1,0:T(1,128)} %bitcast.8, f32[1,20]{1,0:T(1,128)} %bitcast.9, bf16[512,128]{1,0:T(8,128)(2,1)} %refs_2_.7, bf16[512,1280]{1,0:T(8,128)(2,1)} %refs_0_.12), custom_call_target="tpu_custom_call" | custom-call | flops 4000000000 | bytes 1000 | tf_op jit(solution)/shard_map/pallas_call | solution.py:207
  2.7 3.0 %collective-permute-start = (bf16[136,384]{1,0:T(8,128)(2,1)}, bf16[136,384]{1,0:T(8,128)(2,1)S(1)}, u32[]{:S(2)}, u32[]{:S(2)}) collective-permute-start(bf16[136,384]{1,0:T(8,128)(2,1)} %get-tuple-element.63), channel_id=1, source_target_pairs={{0,4},{4,0},{8,12},{12,8},{16,20},{20,16},{24,28},{28,24},{1,5},{5... | collective-permute-start | bytes 313352 | tf_op jit(solution)/shard_map/ppermute | solution.py:613
  5.7 0.9 %copy-done.5 = f32[104,512]{1,0:T(8,128)S(1)} copy-done((f32[104,512]{1,0:T(8,128)S(1)}, f32[104,512]{1,0:T(8,128)}, u32[]{:S(2)}) %copy-start.5) | copy-done | bytes 213016
  6.6 0.7 %shard_map.110 = (bf16[136,256]{1,0:T(8,128)(2,1)S(1)}, bf16[136,384]{1,0:T(8,128)(2,1)S(1)}, bf16[136,256]{1,0:T(8,128)(2,1)S(1)}) custom-call(f32[104,512]{1,0:T(8,128)S(1)} %copy-done.5, bf16[512,1280]{1,0:T(8,128)(2,1)S(1)} %copy-done.1, bf16[512,128]{1,0:T(8,128)(2,1)S(1)} %copy-done.3), custom_call_target="tpu_custom_call" | custom-call | flops 4000000000 | bytes 1000 | tf_op jit(solution)/shard_map/pallas_call | solution.py:66
  7.3 0.1 collective-permute-start.2
  7.4 0.1 copy-done
  7.5 0.1 copy-done.6
  7.6 0.5 %shard_map.111 = (f32[2,256,256]{2,1,0:T(8,128)S(1)}, bf16[256,128]{1,0:T(8,128)(2,1)S(1)}, f32[2,512,128]{2,1,0:T(8,128)S(1)}, f32[32,512]{1,0:T(8,128)S(1)}, f...) custom-call(bf16[512,128]{1,0:T(8,128)(2,1)S(1)} %copy-done, ...), custom_call_target="tpu_custom_call" | custom-call | flops 4000000000 | bytes 1000 | tf_op jit(solution)/shard_map/pallas_call | solution.py:66
  8.2 0.8 %collective-permute-done.refs_1_ = bf16[136,384]{1,0:T(8,128)(2,1)S(1)} collective-permute-done((bf16[136,384]{1,0:T(8,128)(2,1)}, bf16[136,384]{1,0:T(8,128)(2,1)S(1)}, u32[]{:S(2)}, u32[]{:S(2)}) %collective-permute-start) | collective-permute-done | bytes 104480 | tf_op jit(solution)/shard_map/ppermute | solution.py:613
  9.0 0.1 shard_map.112
  9.1 1.8 %collective-permute-start.1 = (bf16[136,384]{1,0:T(8,128)(2,1)S(1)}, bf16[136,384]{1,0:T(8,128)(2,1)S(1)}, u32[]{:S(2)}, u32[]{:S(2)}) collective-permute-start(bf16[136,384]{1,0:T(8,128)(2,1)S(1)} %get-tuple-element.66.refs_9_), channel_id=1, source_target_pairs={{0,8},{4,12},{8,0},{12,4},{16,24},{20,28},{24,16},{28,20},{1,9},{5... | collective-permute-start | bytes 313352 | tf_op jit(solution)/shard_map/ppermute | solution.py:613
  10.8 0.9 %shard_map.113 = (f32[512,256]{1,0:T(8,128)S(1)}, f32[512,256]{1,0:T(8,128)S(1)}) custom-call(bf16[512,1280]{1,0:T(8,128)(2,1)S(1)} %copy-done.1, bf16[512,1280]{1,0:T(8,128)(2,1)S(1)} %copy-done.2, bf16[512,128]{1,0:T(8,128)(2,1)S(1)} %copy-done.3, f32[2,256,256]{2,1,0:T(8,128)S(1)} %get-tuple-element.69.refs_3_, ...), custom_call_target="tpu_custom_call" | custom-call | flops 4000000000 | bytes 1000 | tf_op jit(solution)/shard_map/pallas_call | solution.py:66
  11.7 0.1 shard_map.114
  11.8 1.6 %collective-permute-start.4 = (bf16[136,256]{1,0:T(8,128)(2,1)S(1)}, bf16[136,256]{1,0:T(8,128)(2,1)S(1)}, u32[]{:S(2)}, u32[]{:S(2)}) collective-permute-start(bf16[136,256]{1,0:T(8,128)(2,1)S(1)} %get-tuple-element.77.refs_9_), channel_id=1, source_target_pairs={{0,8},{4,12},{8,0},{12,4},{16,24},{20,28},{24,16},{28,20},{1,9},{5... | collective-permute-start | bytes 208904 | tf_op jit(solution)/shard_map/ppermute | solution.py:613
  13.4 1.3 %shard_map.115 = (f32[512,384]{1,0:T(8,128)S(1)}, f32[512,384]{1,0:T(8,128)S(1)}) custom-call(bf16[512,1280]{1,0:T(8,128)(2,1)S(1)} %copy-done.1, bf16[512,1280]{1,0:T(8,128)(2,1)S(1)} %copy-done.2, bf16[512,128]{1,0:T(8,128)(2,1)S(1)} %copy-done.3, f32[2,256,256]{2,1,0:T(8,128)S(1)} %get-tuple-element.69.refs_3_, ...), custom_call_target="tpu_custom_call" | custom-call | flops 4000000000 | bytes 1000 | tf_op jit(solution)/shard_map/pallas_call | solution.py:66
  14.7 0.1 shard_map.116
  14.8 2.7 %collective-permute-start.3 = (bf16[136,384]{1,0:T(8,128)(2,1)S(1)}, bf16[136,384]{1,0:T(8,128)(2,1)S(1)}, u32[]{:S(2)}, u32[]{:S(2)}) collective-permute-start(bf16[136,384]{1,0:T(8,128)(2,1)S(1)} %get-tuple-element.79.refs_9_), channel_id=1, source_target_pairs={{0,16},{4,20},{8,24},{12,28},{16,0},{20,4},{24,8},{28,12},{1,17},{... | collective-permute-start | bytes 313352 | tf_op jit(solution)/shard_map/ppermute | solution.py:613
  17.5 1.3 %shard_map.117 = (f32[512,384]{1,0:T(8,128)S(1)}, f32[512,384]{1,0:T(8,128)S(1)}) custom-call(bf16[512,1280]{1,0:T(8,128)(2,1)S(1)} %copy-done.1, bf16[512,1280]{1,0:T(8,128)(2,1)S(1)} %copy-done.2, bf16[512,128]{1,0:T(8,128)(2,1)S(1)} %copy-done.3, f32[2,256,256]{2,1,0:T(8,128)S(1)} %get-tuple-element.69.refs_3_, ...), custom_call_target="tpu_custom_call" | custom-call | flops 4000000000 | bytes 1000 | tf_op jit(solution)/shard_map/pallas_call | solution.py:66
  18.9 0.0 slice-start
  18.9 0.4 collective-permute-start.5
  19.3 0.9 %shard_map.119 = (f32[512,256]{1,0:T(8,128)S(1)}, f32[512,256]{1,0:T(8,128)S(1)}) custom-call(bf16[512,1280]{1,0:T(8,128)(2,1)S(1)} %copy-done.1, bf16[512,1280]{1,0:T(8,128)(2,1)S(1)} %copy-done.2, bf16[512,128]{1,0:T(8,128)(2,1)S(1)} %copy-done.3, f32[2,256,256]{2,1,0:T(8,128)S(1)} %get-tuple-element.69.refs_3_, ...), custom_call_target="tpu_custom_call" | custom-call | flops 4000000000 | bytes 1000 | tf_op jit(solution)/shard_map/pallas_call | solution.py:66
  20.2 0.0 copy-start.7
  20.2 2.3 %collective-permute-done.3.refs_0_ = bf16[136,384]{1,0:T(8,128)(2,1)S(1)} collective-permute-done((bf16[136,384]{1,0:T(8,128)(2,1)S(1)}, bf16[136,384]{1,0:T(8,128)(2,1)S(1)}, u32[]{:S(2)}, u32[]{:S(2)}) %collective-permute-start.3) | collective-permute-done | bytes 104480 | tf_op jit(solution)/shard_map/ppermute | solution.py:613
  22.5 0.1 shard_map.120
  22.6 2.1 %collective-permute-start.6 = (bf16[128,384]{1,0:T(8,128)(2,1)S(1)}, bf16[128,384]{1,0:T(8,128)(2,1)S(1)}, u32[]{:S(2)}, u32[]{:S(2)}) collective-permute-start(bf16[128,384]{1,0:T(8,128)(2,1)S(1)} %get-tuple-element.95.refs_4_), channel_id=1, source_target_pairs={{0,4},{4,0},{8,12},{12,8},{16,20},{20,16},{24,28},{28,24},{1,5},{5... | collective-permute-start | bytes 294920 | tf_op jit(solution)/shard_map/ppermute | solution.py:613
  24.8 2.1 %collective-permute-start.7 = (bf16[128,256]{1,0:T(8,128)(2,1)S(1)}, bf16[128,256]{1,0:T(8,128)(2,1)S(1)}, u32[]{:S(2)}, u32[]{:S(2)}) collective-permute-start(bf16[128,256]{1,0:T(8,128)(2,1)S(1)} %get-tuple-element.103), channel_id=1, source_target_pairs={{0,4},{4,0},{8,12},{12,8},{16,20},{20,16},{24,28},{28,24},{1,5},{5... | collective-permute-start | bytes 196616 | tf_op jit(solution)/shard_map/ppermute | solution.py:613
  26.9 1.1 %shard_map.122 = (bf16[512,640]{1,0:T(8,128)(2,1)S(1)}, f32[1,512]{1,0:T(1,128)S(1)}, f32[640,512]{1,0:T(8,128)S(1)}) custom-call(f32[8,128]{1,0:T(8,128)S(1)} %get-tuple-element.88.prev_ref, bf16[512,128]{1,0:T(8,128)(2,1)S(1)} %copy-done, f32[512,128]{1,0:T(8,128)S(1)} %get-tuple-element.65.refs_2_.seg_ref, f32[1,1280]{1,0:T(1,128)S(1)} %reshape.19.gain_ref, ...), custom_call_target="tpu_custom_call" | custom-call | flops 1000 | bytes 1000 | tf_op jit(solution)/shard_map/pallas_call | solution.py:66
  28.1 0.9 %shard_map.123 = (bf16[512,384]{1,0:T(8,128)(2,1)S(1)}, f32[1,512]{1,0:T(1,128)S(1)}, f32[640,512]{1,0:T(8,128)S(1)}) custom-call(f32[8,128]{1,0:T(8,128)S(1)} %get-tuple-element.88.prev_ref, bf16[512,128]{1,0:T(8,128)(2,1)S(1)} %copy-done, f32[512,128]{1,0:T(8,128)S(1)} %get-tuple-element.65.refs_2_.seg_ref, f32[1,1280]{1,0:T(1,128)S(1)} %reshape.19.gain_ref, ...), custom_call_target="tpu_custom_call" | custom-call | flops 1000 | bytes 1000 | tf_op jit(solution)/shard_map/pallas_call | solution.py:66
  29.0 0.2 collective-permute-done.7.e_ref
  29.1 0.6 %shard_map.124 = (bf16[512,256]{1,0:T(8,128)(2,1)S(1)}, bf16[392,512]{1,0:T(8,128)(2,1)S(1)}) custom-call(f32[8,128]{1,0:T(8,128)S(1)} %get-tuple-element.88.prev_ref, bf16[512,128]{1,0:T(8,128)(2,1)S(1)} %copy-done, f32[512,128]{1,0:T(8,128)S(1)} %get-tuple-element.65.refs_2_.seg_ref, f32[512,256]{1,0:T(8,128)S(1)} %get-tuple-element.87.refs_4_.a_ref, ...), custom_call_target="tpu_custom_call" | custom-call | flops 1000 | bytes 1000 | tf_op jit(solution)/shard_map/pallas_call | solution.py:66
  29.8 0.1 collective-permute-start.9
  29.9 1.3 %shard_map.125 = (bf16[256,512]{1,0:T(8,128)(2,1)S(1)}, f32[384,512]{1,0:T(8,128)S(1)}, f32[256,512]{1,0:T(8,128)S(1)}) custom-call(f32[640,512]{1,0:T(8,128)S(1)} %get-tuple-element.104.p_ref.refs_0_, bf16[1280,2560]{1,0:T(8,128)(2,1)S(1)} %bitcast.5, bf16[512,640]{1,0:T(8,128)(2,1)S(1)} %get-tuple-element.97.refs_2_.refs_1_.refs_0_, ...), custom_call_target="tpu_custom_call" | custom-call | flops 1000 | bytes 1000 | tf_op jit(solution)/shard_map/pallas_call | solution.py:66
  31.1 0.6 %collective-permute-start.8 = (bf16[256,512]{1,0:T(8,128)(2,1)S(1)}, bf16[256,512]{1,0:T(8,128)(2,1)S(1)}, u32[]{:S(2)}, u32[]{:S(2)}) collective-permute-start(bf16[256,512]{1,0:T(8,128)(2,1)S(1)} %get-tuple-element.109), channel_id=1, source_target_pairs={{0,1},{1,0},{2,3},{3,2},{4,5},{5,4},{6,7},{7,6},{8,9},{9,8},{10,11... | collective-permute-start | bytes 786440 | tf_op jit(solution)/shard_map/ppermute | solution.py:616
  31.7 0.1 shard_map.126.refs_2_.factor_ref
  31.8 1.6 %collective-permute-start.15 = (bf16[392,512]{1,0:T(8,128)(2,1)S(1)}, bf16[392,512]{1,0:T(8,128)(2,1)S(1)}, u32[]{:S(2)}, u32[]{:S(2)}) collective-permute-start(bf16[392,512]{1,0:T(8,128)(2,1)S(1)} %shard_map.126.refs_2_.factor_ref), channel_id=1, source_target_pairs={{0,2},{1,3},{2,0},{3,1},{4,6},{5,7},{6,4},{7,5},{8,10},{9,11},{10,... | collective-permute-start | bytes 1204232 | tf_op jit(solution)/shard_map/ppermute | solution.py:616
  33.4 1.2 %shard_map.128 = (bf16[160,512]{1,0:T(8,128)(2,1)S(1)}, bf16[160,512]{1,0:T(8,128)(2,1)S(1)}, bf16[160,512]{1,0:T(8,128)(2,1)S(1)}, bf16[160,512]{1,0:T(8,128)(2,1)S(1)}) custom-call(bf16[1280,2560]{1,0:T(8,128)(2,1)S(1)} %bitcast.5, bf16[512,640]{1,0:T(8,128)(2,1)S(1)} %get-tuple-element.97.refs_2_.refs_1_.refs_0_, ...), custom_call_target="tpu_custom_call" | custom-call | flops 1000 | bytes 1000 | tf_op jit(solution)/shard_map/pallas_call | solution.py:66
  34.6 0.1 collective-permute-start.10
  34.7 1.4 %collective-permute-start.14 = (bf16[256,512]{1,0:T(8,128)(2,1)S(1)}, bf16[256,512]{1,0:T(8,128)(2,1)S(1)}, u32[]{:S(2)}, u32[]{:S(2)}) collective-permute-start(bf16[256,512]{1,0:T(8,128)(2,1)S(1)} %shard_map.127.refs_4_), channel_id=1, source_target_pairs={{0,2},{1,3},{2,0},{3,1},{4,6},{5,7},{6,4},{7,5},{8,10},{9,11},{10,... | collective-permute-start | bytes 786440 | tf_op jit(solution)/shard_map/ppermute | solution.py:616
  36.1 0.5 %collective-permute-start.12 = (bf16[160,512]{1,0:T(8,128)(2,1)S(1)}, bf16[160,512]{1,0:T(8,128)(2,1)S(1)}, u32[]{:S(2)}, u32[]{:S(2)}) collective-permute-start(bf16[160,512]{1,0:T(8,128)(2,1)S(1)} %get-tuple-element.113), channel_id=1, source_target_pairs={{0,1},{1,0},{2,3},{3,2},{4,5},{5,4},{6,7},{7,6},{8,9},{9,8},{10,11... | collective-permute-start | bytes 491528 | tf_op jit(solution)/shard_map/ppermute | solution.py:616
  36.6 0.0 collective-permute-start.13
  36.6 0.9 %collective-permute-done.11.refs_4_ = bf16[160,512]{1,0:T(8,128)(2,1)S(1)} collective-permute-done((bf16[160,512]{1,0:T(8,128)(2,1)S(1)}, bf16[160,512]{1,0:T(8,128)(2,1)S(1)}, u32[]{:S(2)}, u32[]{:S(2)}) %collective-permute-start.11) | collective-permute-done | bytes 163872 | tf_op jit(solution)/shard_map/ppermute | solution.py:616
  37.5 0.2 collective-permute-done.12.refs_5_
  37.7 0.3 collective-permute-done.13.refs_6_
  38.0 1.2 %shard_map.129.own_ref = f32[640,512]{1,0:T(8,128)S(1)} custom-call(bf16[1280,2560]{1,0:T(8,128)(2,1)S(1)} %bitcast.5, bf16[512,640]{1,0:T(8,128)(2,1)S(1)} %get-tuple-element.97.refs_2_.refs_1_.refs_0_, bf16[512,384]{1,0:T(8,128)(2,1)S(1)} %get-tuple-element.101.refs_3_.refs_2_.refs_1_, bf16[512,256]{1,0:T(8,128)(2,1)S(1)} %get-tuple-element.106.refs_4_.refs_3_.refs_2_, ...), custom_call_target="tpu_custom_call" | custom-call | flops 1000 | bytes 1000 | tf_op jit(solution)/shard_map/pallas_call | solution.py:66
  39.2 4.8 %collective-permute-done.15.far_ref = bf16[392,512]{1,0:T(8,128)(2,1)S(1)} collective-permute-done((bf16[392,512]{1,0:T(8,128)(2,1)S(1)}, bf16[392,512]{1,0:T(8,128)(2,1)S(1)}, u32[]{:S(2)}, u32[]{:S(2)}) %collective-permute-start.15) | collective-permute-done | bytes 401440 | tf_op jit(solution)/shard_map/ppermute | solution.py:616
  44.0 0.8 %shard_map.130 = (bf16[640,512]{1,0:T(8,128)(2,1)}, f32[1,512]{1,0:T(1,128)S(1)}) custom-call(f32[640,512]{1,0:T(8,128)S(1)} %shard_map.129.own_ref, bf16[392,512]{1,0:T(8,128)(2,1)S(1)} %collective-permute-done.15.far_ref, bf16[392,512]{1,0:T(8,128)(2,1)S(1)} %shard_map.126.refs_2_.factor_ref), custom_call_target="tpu_custom_call" | custom-call | flops 1000 | bytes 1000 | tf_op jit(solution)/shard_map/pallas_call | solution.py:593
  44.9 3.9 %collective-permute-done.14.far_ref = bf16[256,512]{1,0:T(8,128)(2,1)S(1)} collective-permute-done((bf16[256,512]{1,0:T(8,128)(2,1)S(1)}, bf16[256,512]{1,0:T(8,128)(2,1)S(1)}, u32[]{:S(2)}, u32[]{:S(2)}) %collective-permute-start.14) | collective-permute-done | bytes 262176 | tf_op jit(solution)/shard_map/ppermute | solution.py:616
  48.7 0.7 %shard_map.131 = bf16[640,512]{1,0:T(8,128)(2,1)} custom-call(f32[640,512]{1,0:T(8,128)S(1)} %shard_map.129.own_ref, bf16[256,512]{1,0:T(8,128)(2,1)S(1)} %collective-permute-done.14.far_ref, f32[1,512]{1,0:T(1,128)S(1)} %get-tuple-element.115.factor_ref, bf16[640,512]{1,0:T(8,128)(2,1)} %get-tuple-element.116.refs_0_), custom_call_target="tpu_custom_call", output_to_operand_aliasing={{}: (3, {})} | custom-call | flops 1000 | bytes 1000 | tf_op jit(solution)/shard_map/pallas_call | solution.py:593
  (29 shorter events, 0.2 us)
Async XLA Ops:
  0.0 5.7 %copy-start.1 = (bf16[512,1280]{1,0:T(8,128)(2,1)S(1)}, bf16[512,1280]{1,0:T(8,128)(2,1)}, u32[]{:S(2)}) copy-start(bf16[512,1280]{1,0:T(8,128)(2,1)} %refs_0_.12) | copy-start | bytes 3932164
  0.0 5.7 %copy-start.3 = (bf16[512,128]{1,0:T(8,128)(2,1)S(1)}, bf16[512,128]{1,0:T(8,128)(2,1)}, u32[]{:S(2)}) copy-start(bf16[512,128]{1,0:T(8,128)(2,1)} %refs_2_.7) | copy-start | bytes 393220
  2.7 6.3 %collective-permute-start = (bf16[136,384]{1,0:T(8,128)(2,1)}, bf16[136,384]{1,0:T(8,128)(2,1)S(1)}, u32[]{:S(2)}, u32[]{:S(2)}) collective-permute-start(bf16[136,384]{1,0:T(8,128)(2,1)} %get-tuple-element.63), channel_id=1, source_target_pairs={{0,4},{4,0},{8,12},{12,8},{16,20},{20,16},{24,28},{28,24},{1,5},{5... | collective-permute-start | bytes 313352 | tf_op jit(solution)/shard_map/ppermute | solution.py:613
  5.7 0.9 %copy-start.5 = (f32[104,512]{1,0:T(8,128)S(1)}, f32[104,512]{1,0:T(8,128)}, u32[]{:S(2)}) copy-start(f32[104,512]{1,0:T(8,128)} %get-tuple-element.61.stash_ref.refs_2_) | copy-start | bytes 638980
  6.6 0.9 %copy-start = (bf16[512,128]{1,0:T(8,128)(2,1)S(1)}, bf16[512,128]{1,0:T(8,128)(2,1)}, u32[]{:S(2)}) copy-start(bf16[512,128]{1,0:T(8,128)(2,1)} %rd_ref.5) | copy-start | bytes 393220
  6.6 0.9 %copy-start.4 = (f32[20]{0:T(128)S(1)}, f32[20]{0:T(128)}, u32[]{:S(2)}) copy-start(f32[20]{0:T(128)} %param.19) | copy-start | bytes 244
  6.6 1.0 %copy-start.6 = (f32[104,512]{1,0:T(8,128)S(1)}, f32[104,512]{1,0:T(8,128)}, u32[]{:S(2)}) copy-start(f32[104,512]{1,0:T(8,128)} %get-tuple-element.61.stash_ref.refs_2_) | copy-start | bytes 638980
  7.3 4.4 %collective-permute-start.2 = (bf16[136,256]{1,0:T(8,128)(2,1)S(1)}, bf16[136,256]{1,0:T(8,128)(2,1)S(1)}, u32[]{:S(2)}, u32[]{:S(2)}) collective-permute-start(bf16[136,256]{1,0:T(8,128)(2,1)S(1)} %get-tuple-element.64.refs_4_), channel_id=1, source_target_pairs={{0,4},{4,0},{8,12},{12,8},{16,20},{20,16},{24,28},{28,24},{1,5},{5... | collective-permute-start | bytes 208904 | tf_op jit(solution)/shard_map/ppermute | solution.py:613
  9.0 1.8 %copy-start.2 = (bf16[512,1280]{1,0:T(8,128)(2,1)S(1)}, bf16[512,1280]{1,0:T(8,128)(2,1)}, u32[]{:S(2)}) copy-start(bf16[512,1280]{1,0:T(8,128)(2,1)} %refs_1_.10) | copy-start | bytes 3932164
  9.1 5.7 %collective-permute-start.1 = (bf16[136,384]{1,0:T(8,128)(2,1)S(1)}, bf16[136,384]{1,0:T(8,128)(2,1)S(1)}, u32[]{:S(2)}, u32[]{:S(2)}) collective-permute-start(bf16[136,384]{1,0:T(8,128)(2,1)S(1)} %get-tuple-element.66.refs_9_), channel_id=1, source_target_pairs={{0,8},{4,12},{8,0},{12,4},{16,24},{20,28},{24,16},{28,20},{1,9},{5... | collective-permute-start | bytes 313352 | tf_op jit(solution)/shard_map/ppermute | solution.py:613
  11.8 7.0 %collective-permute-start.4 = (bf16[136,256]{1,0:T(8,128)(2,1)S(1)}, bf16[136,256]{1,0:T(8,128)(2,1)S(1)}, u32[]{:S(2)}, u32[]{:S(2)}) collective-permute-start(bf16[136,256]{1,0:T(8,128)(2,1)S(1)} %get-tuple-element.77.refs_9_), channel_id=1, source_target_pairs={{0,8},{4,12},{8,0},{12,4},{16,24},{20,28},{24,16},{28,20},{1,9},{5... | collective-permute-start | bytes 208904 | tf_op jit(solution)/shard_map/ppermute | solution.py:613
  14.8 7.7 %collective-permute-start.3 = (bf16[136,384]{1,0:T(8,128)(2,1)S(1)}, bf16[136,384]{1,0:T(8,128)(2,1)S(1)}, u32[]{:S(2)}, u32[]{:S(2)}) collective-permute-start(bf16[136,384]{1,0:T(8,128)(2,1)S(1)} %get-tuple-element.79.refs_9_), channel_id=1, source_target_pairs={{0,16},{4,20},{8,24},{12,28},{16,0},{20,4},{24,8},{28,12},{1,17},{... | collective-permute-start | bytes 313352 | tf_op jit(solution)/shard_map/ppermute | solution.py:613
  18.9 8.0 %slice-start = ((s8[6553600]{0:T(1024)(128)(4,1)}), s8[4194304]{0:T(1024)(128)(4,1)S(1)}, s32[]{:S(2)}) async-start(s8[6553600]{0:T(1024)(128)(4,1)} %bitcast.4), calls=%async_computation | async-start | bytes 8388608
  18.9 8.0 %slice-start.1 = ((s8[6553600]{0:T(1024)(128)(4,1)}), s8[2359296]{0:T(1024)(128)(4,1)S(1)}, s32[]{:S(2)}) async-start(s8[6553600]{0:T(1024)(128)(4,1)} %bitcast.4), calls=%async_computation.1 | async-start | bytes 4718592
  18.9 5.8 %collective-permute-start.5 = (bf16[136,256]{1,0:T(8,128)(2,1)S(1)}, bf16[136,256]{1,0:T(8,128)(2,1)S(1)}, u32[]{:S(2)}, u32[]{:S(2)}) collective-permute-start(bf16[136,256]{1,0:T(8,128)(2,1)S(1)} %get-tuple-element.86.refs_9_), channel_id=1, source_target_pairs={{0,16},{4,20},{8,24},{12,28},{16,0},{20,4},{24,8},{28,12},{1,17},{... | collective-permute-start | bytes 208904 | tf_op jit(solution)/shard_map/ppermute | solution.py:613
  20.2 6.7 %copy-start.7 = (f32[1280]{0:T(1024)S(1)}, f32[1280]{0:T(1024)}, u32[]{:S(2)}) copy-start(f32[1280]{0:T(1024)} %param.20) | copy-start | bytes 15364
  22.6 5.4 %collective-permute-start.6 = (bf16[128,384]{1,0:T(8,128)(2,1)S(1)}, bf16[128,384]{1,0:T(8,128)(2,1)S(1)}, u32[]{:S(2)}, u32[]{:S(2)}) collective-permute-start(bf16[128,384]{1,0:T(8,128)(2,1)S(1)} %get-tuple-element.95.refs_4_), channel_id=1, source_target_pairs={{0,4},{4,0},{8,12},{12,8},{16,20},{20,16},{24,28},{28,24},{1,5},{5... | collective-permute-start | bytes 294920 | tf_op jit(solution)/shard_map/ppermute | solution.py:613
  24.8 4.4 %collective-permute-start.7 = (bf16[128,256]{1,0:T(8,128)(2,1)S(1)}, bf16[128,256]{1,0:T(8,128)(2,1)S(1)}, u32[]{:S(2)}, u32[]{:S(2)}) collective-permute-start(bf16[128,256]{1,0:T(8,128)(2,1)S(1)} %get-tuple-element.103), channel_id=1, source_target_pairs={{0,4},{4,0},{8,12},{12,8},{16,20},{20,16},{24,28},{28,24},{1,5},{5... | collective-permute-start | bytes 196616 | tf_op jit(solution)/shard_map/ppermute | solution.py:613
  29.8 1.9 %collective-permute-start.9 = (bf16[392,512]{1,0:T(8,128)(2,1)S(1)}, bf16[392,512]{1,0:T(8,128)(2,1)S(1)}, u32[]{:S(2)}, u32[]{:S(2)}) collective-permute-start(bf16[392,512]{1,0:T(8,128)(2,1)S(1)} %get-tuple-element.107.refs_5_.mine_ref), channel_id=1, source_target_pairs={{0,1},{1,0},{2,3},{3,2},{4,5},{5,4},{6,7},{7,6},{8,9},{9,8},{10,11... | collective-permute-start | bytes 1204232 | tf_op jit(solution)/shard_map/ppermute | solution.py:616
  31.1 2.2 %collective-permute-start.8 = (bf16[256,512]{1,0:T(8,128)(2,1)S(1)}, bf16[256,512]{1,0:T(8,128)(2,1)S(1)}, u32[]{:S(2)}, u32[]{:S(2)}) collective-permute-start(bf16[256,512]{1,0:T(8,128)(2,1)S(1)} %get-tuple-element.109), channel_id=1, source_target_pairs={{0,1},{1,0},{2,3},{3,2},{4,5},{5,4},{6,7},{7,6},{8,9},{9,8},{10,11... | collective-permute-start | bytes 786440 | tf_op jit(solution)/shard_map/ppermute | solution.py:616
  31.8 12.2 %collective-permute-start.15 = (bf16[392,512]{1,0:T(8,128)(2,1)S(1)}, bf16[392,512]{1,0:T(8,128)(2,1)S(1)}, u32[]{:S(2)}, u32[]{:S(2)}) collective-permute-start(bf16[392,512]{1,0:T(8,128)(2,1)S(1)} %shard_map.126.refs_2_.factor_ref), channel_id=1, source_target_pairs={{0,2},{1,3},{2,0},{3,1},{4,6},{5,7},{6,4},{7,5},{8,10},{9,11},{10,... | collective-permute-start | bytes 1204232 | tf_op jit(solution)/shard_map/ppermute | solution.py:616
  34.6 2.0 %collective-permute-start.10 = (bf16[160,512]{1,0:T(8,128)(2,1)S(1)}, bf16[160,512]{1,0:T(8,128)(2,1)S(1)}, u32[]{:S(2)}, u32[]{:S(2)}) collective-permute-start(bf16[160,512]{1,0:T(8,128)(2,1)S(1)} %get-tuple-element.111), channel_id=1, source_target_pairs={{0,1},{1,0},{2,3},{3,2},{4,5},{5,4},{6,7},{7,6},{8,9},{9,8},{10,11... | collective-permute-start | bytes 491528 | tf_op jit(solution)/shard_map/ppermute | solution.py:616
  34.7 14.0 %collective-permute-start.14 = (bf16[256,512]{1,0:T(8,128)(2,1)S(1)}, bf16[256,512]{1,0:T(8,128)(2,1)S(1)}, u32[]{:S(2)}, u32[]{:S(2)}) collective-permute-start(bf16[256,512]{1,0:T(8,128)(2,1)S(1)} %shard_map.127.refs_4_), channel_id=1, source_target_pairs={{0,2},{1,3},{2,0},{3,1},{4,6},{5,7},{6,4},{7,5},{8,10},{9,11},{10,... | collective-permute-start | bytes 786440 | tf_op jit(solution)/shard_map/ppermute | solution.py:616
  36.1 1.4 %collective-permute-start.11 = (bf16[160,512]{1,0:T(8,128)(2,1)S(1)}, bf16[160,512]{1,0:T(8,128)(2,1)S(1)}, u32[]{:S(2)}, u32[]{:S(2)}) collective-permute-start(bf16[160,512]{1,0:T(8,128)(2,1)S(1)} %get-tuple-element.112), channel_id=1, source_target_pairs={{0,1},{1,0},{2,3},{3,2},{4,5},{5,4},{6,7},{7,6},{8,9},{9,8},{10,11... | collective-permute-start | bytes 491528 | tf_op jit(solution)/shard_map/ppermute | solution.py:616
  36.1 1.6 %collective-permute-start.12 = (bf16[160,512]{1,0:T(8,128)(2,1)S(1)}, bf16[160,512]{1,0:T(8,128)(2,1)S(1)}, u32[]{:S(2)}, u32[]{:S(2)}) collective-permute-start(bf16[160,512]{1,0:T(8,128)(2,1)S(1)} %get-tuple-element.113), channel_id=1, source_target_pairs={{0,1},{1,0},{2,3},{3,2},{4,5},{5,4},{6,7},{7,6},{8,9},{9,8},{10,11... | collective-permute-start | bytes 491528 | tf_op jit(solution)/shard_map/ppermute | solution.py:616
  36.6 1.4 %collective-permute-start.13 = (bf16[160,512]{1,0:T(8,128)(2,1)S(1)}, bf16[160,512]{1,0:T(8,128)(2,1)S(1)}, u32[]{:S(2)}, u32[]{:S(2)}) collective-permute-start(bf16[160,512]{1,0:T(8,128)(2,1)S(1)} %get-tuple-element.114), channel_id=1, source_target_pairs={{0,1},{1,0},{2,3},{3,2},{4,5},{5,4},{6,7},{7,6},{8,9},{9,8},{10,11... | collective-permute-start | bytes 491528 | tf_op jit(solution)/shard_map/ppermute | solution.py:616

commit v9 on v8

--- a/solution.py
+++ b/solution.py
@@ -97,12 +97,6 @@
     link = later * (one[2] == two[2]).astype(F32)
     state = jnp.where(swapped, 1.0, link) * one[0] + jnp.where(swapped, link, 1.0) * two[0]
     return state, one[1] * two[1], jnp.where(swapped, one[2], two[2])
-
-
-def ordered(swapped, one, two):
-    firsts = tuple(jnp.where(swapped, t, o) for o, t in zip(one, two))
-    seconds = tuple(jnp.where(swapped, o, t) for o, t in zip(one, two))
-    return firsts, seconds
 
 
 def stash_rows():
@@ -236,7 +230,7 @@
             some_state(half, half_w, lanes, width, vecs, tails_ref, sums, last, x_ref, first, out_ref)
 
     out = shaped(*[((state + EXTRA, lanes.stop - lanes.start), BF16) for _, lanes in pieces])
-    return call(body, (stash, x, write), out, cost=LONG)
+    return call(body, (stash, x, write), out)
 
 
 def gather_level(upper, entry, other):

time: 49.6 us -> 49.6 us (level)
    unnamed x20 -> x18, local copies, waits for them, and re-layouts: 1.17 us -> 0.97 us
where the time goes in v9:
time: 49.6 us; the launch traced here: 49.5 us
  starting transfers between devices  17.9 us (36%)
  Pallas kernels  16.8 us (34%)
  waiting for transfers between devices  13.5 us (27%)
  local copies, waits for them, and re-layouts  0.98 us (2%)
    ppermute x8, starting transfers between devices, swap(): return lax.ppermute(a, 'seq', [(i, i ^ bit) for i in range(n_seq)])  13.8 us
    pallas_call x20, Pallas kernels, call(): pl.pallas_call(kernel, in_specs=specs, out_specs=jax.tree.map(lambda _: v...  12.6 us
    ppermute x8, waiting for transfers between devices, across(): return lax.ppermute(a, 'tp', [(i, i ^ bit) for i in range(n_tp)])  10.1 us
    ppermute x8, starting transfers between devices, across(): return lax.ppermute(a, 'tp', [(i, i ^ bit) for i in range(n_tp)])  4.13 us
    ppermute x8, waiting for transfers between devices, swap(): return lax.ppermute(a, 'seq', [(i, i ^ bit) for i in range(n_seq)])  3.45 us
    pallas_call x1, Pallas kernels, prepare(): pl.pallas_call(body, in_specs=[pl.BlockSpec(memory_space=pltpu.HBM)] * le...  2.66 us
    pallas_call x2, Pallas kernels, finish(): pl.pallas_call(body, in_specs=[vm] * 3 + ([] if first else [where]), out_...  1.57 us
  transfers between devices with their start and end apart: 16, of which 8 were waited for; matrix products, arithmetic and copies ran while one was open for 0% of the time, Pallas kernels for 26%

profile of v9, /device:TPU:0, one launch (start us, length us, event | category | flops | bytes accessed | tf_op | source)
XLA Modules:
  0.0 49.5 jit_solution(14388654459100878401)
XLA Ops:
  0.0 2.7 %shard_map.109 = (bf16[136,384]{1,0:T(8,128)(2,1)}, f32[104,512]{1,0:T(8,128)}) custom-call(bf16[20,512]{1,0:T(8,128)(2,1)} %refs_0_.7, s32[1,512]{1,0:T(1,128)} %bitcast.7, f32[1,20]{1,0:T(1,128)} %bitcast.8, f32[1,20]{1,0:T(1,128)} %bitcast.9, bf16[512,128]{1,0:T(8,128)(2,1)} %refs_2_.7, bf16[512,1280]{1,0:T(8,128)(2,1)} %refs_0_.12), custom_call_target="tpu_custom_call" | custom-call | flops 4000000000 | bytes 1000 | tf_op jit(solution)/shard_map/pallas_call | solution.py:201
  2.7 0.0 copy-start.1
  2.7 3.0 %collective-permute-start = (bf16[136,384]{1,0:T(8,128)(2,1)}, bf16[136,384]{1,0:T(8,128)(2,1)S(1)}, u32[]{:S(2)}, u32[]{:S(2)}) collective-permute-start(bf16[136,384]{1,0:T(8,128)(2,1)} %get-tuple-element.63), channel_id=1, source_target_pairs={{0,4},{4,0},{8,12},{12,8},{16,20},{20,16},{24,28},{28,24},{1,5},{5... | collective-permute-start | bytes 313352 | tf_op jit(solution)/shard_map/ppermute | solution.py:607
  5.7 0.9 %copy-done.2 = f32[104,512]{1,0:T(8,128)S(1)} copy-done((f32[104,512]{1,0:T(8,128)S(1)}, f32[104,512]{1,0:T(8,128)}, u32[]{:S(2)}) %copy-start.2) | copy-done | bytes 213016
  6.7 0.7 %shard_map.110 = (bf16[136,256]{1,0:T(8,128)(2,1)S(1)}, bf16[136,384]{1,0:T(8,128)(2,1)S(1)}, bf16[136,256]{1,0:T(8,128)(2,1)S(1)}) custom-call(f32[104,512]{1,0:T(8,128)S(1)} %copy-done.2, bf16[512,1280]{1,0:T(8,128)(2,1)S(1)} %copy-done, bf16[512,128]{1,0:T(8,128)(2,1)S(1)} %copy-done.3), custom_call_target="tpu_custom_call" | custom-call | flops 1000 | bytes 1000 | tf_op jit(solution)/shard_map/pallas_call | solution.py:66
  7.4 0.1 collective-permute-start.2
  7.5 0.6 %shard_map.111 = (f32[2,256,256]{2,1,0:T(8,128)S(1)}, bf16[256,128]{1,0:T(8,128)(2,1)S(1)}, f32[2,512,128]{2,1,0:T(8,128)S(1)}, f32[32,512]{1,0:T(8,128)S(1)}, f...) custom-call(bf16[512,128]{1,0:T(8,128)(2,1)S(1)} %copy-done.1, ...), custom_call_target="tpu_custom_call" | custom-call | flops 4000000000 | bytes 1000 | tf_op jit(solution)/shard_map/pallas_call | solution.py:66
  8.0 1.0 %collective-permute-done.refs_1_ = bf16[136,384]{1,0:T(8,128)(2,1)S(1)} collective-permute-done((bf16[136,384]{1,0:T(8,128)(2,1)}, bf16[136,384]{1,0:T(8,128)(2,1)S(1)}, u32[]{:S(2)}, u32[]{:S(2)}) %collective-permute-start) | collective-permute-done | bytes 104480 | tf_op jit(solution)/shard_map/ppermute | solution.py:607
  9.0 0.1 shard_map.112
  9.1 1.8 %collective-permute-start.1 = (bf16[136,384]{1,0:T(8,128)(2,1)S(1)}, bf16[136,384]{1,0:T(8,128)(2,1)S(1)}, u32[]{:S(2)}, u32[]{:S(2)}) collective-permute-start(bf16[136,384]{1,0:T(8,128)(2,1)S(1)} %get-tuple-element.66.refs_9_), channel_id=1, source_target_pairs={{0,8},{4,12},{8,0},{12,4},{16,24},{20,28},{24,16},{28,20},{1,9},{5... | collective-permute-start | bytes 313352 | tf_op jit(solution)/shard_map/ppermute | solution.py:607
  10.8 0.9 %shard_map.113 = (f32[512,256]{1,0:T(8,128)S(1)}, f32[512,256]{1,0:T(8,128)S(1)}) custom-call(bf16[512,1280]{1,0:T(8,128)(2,1)S(1)} %copy-done, bf16[512,1280]{1,0:T(8,128)(2,1)S(1)} %copy-done.4, bf16[512,128]{1,0:T(8,128)(2,1)S(1)} %copy-done.3, f32[2,256,256]{2,1,0:T(8,128)S(1)} %get-tuple-element.69.refs_3_, ...), custom_call_target="tpu_custom_call" | custom-call | flops 4000000000 | bytes 1000 | tf_op jit(solution)/shard_map/pallas_call | solution.py:66
  11.8 0.1 shard_map.114
  11.8 1.6 %collective-permute-start.4 = (bf16[136,256]{1,0:T(8,128)(2,1)S(1)}, bf16[136,256]{1,0:T(8,128)(2,1)S(1)}, u32[]{:S(2)}, u32[]{:S(2)}) collective-permute-start(bf16[136,256]{1,0:T(8,128)(2,1)S(1)} %get-tuple-element.77.refs_9_), channel_id=1, source_target_pairs={{0,8},{4,12},{8,0},{12,4},{16,24},{20,28},{24,16},{28,20},{1,9},{5... | collective-permute-start | bytes 208904 | tf_op jit(solution)/shard_map/ppermute | solution.py:607
  13.4 1.3 %shard_map.115 = (f32[512,384]{1,0:T(8,128)S(1)}, f32[512,384]{1,0:T(8,128)S(1)}) custom-call(bf16[512,1280]{1,0:T(8,128)(2,1)S(1)} %copy-done, bf16[512,1280]{1,0:T(8,128)(2,1)S(1)} %copy-done.4, bf16[512,128]{1,0:T(8,128)(2,1)S(1)} %copy-done.3, f32[2,256,256]{2,1,0:T(8,128)S(1)} %get-tuple-element.69.refs_3_, ...), custom_call_target="tpu_custom_call" | custom-call | flops 4000000000 | bytes 1000 | tf_op jit(solution)/shard_map/pallas_call | solution.py:66
  14.8 0.1 shard_map.116
  14.8 2.7 %collective-permute-start.3 = (bf16[136,384]{1,0:T(8,128)(2,1)S(1)}, bf16[136,384]{1,0:T(8,128)(2,1)S(1)}, u32[]{:S(2)}, u32[]{:S(2)}) collective-permute-start(bf16[136,384]{1,0:T(8,128)(2,1)S(1)} %get-tuple-element.79.refs_9_), channel_id=1, source_target_pairs={{0,16},{4,20},{8,24},{12,28},{16,0},{20,4},{24,8},{28,12},{1,17},{... | collective-permute-start | bytes 313352 | tf_op jit(solution)/shard_map/ppermute | solution.py:607
  17.5 1.3 %shard_map.117 = (f32[512,384]{1,0:T(8,128)S(1)}, f32[512,384]{1,0:T(8,128)S(1)}) custom-call(bf16[512,1280]{1,0:T(8,128)(2,1)S(1)} %copy-done, bf16[512,1280]{1,0:T(8,128)(2,1)S(1)} %copy-done.4, bf16[512,128]{1,0:T(8,128)(2,1)S(1)} %copy-done.3, f32[2,256,256]{2,1,0:T(8,128)S(1)} %get-tuple-element.69.refs_3_, ...), custom_call_target="tpu_custom_call" | custom-call | flops 4000000000 | bytes 1000 | tf_op jit(solution)/shard_map/pallas_call | solution.py:66
  18.8 0.1 shard_map.118
  18.9 0.0 slice-start
  18.9 0.4 collective-permute-start.5
  19.3 0.9 %shard_map.119 = (f32[512,256]{1,0:T(8,128)S(1)}, f32[512,256]{1,0:T(8,128)S(1)}) custom-call(bf16[512,1280]{1,0:T(8,128)(2,1)S(1)} %copy-done, bf16[512,1280]{1,0:T(8,128)(2,1)S(1)} %copy-done.4, bf16[512,128]{1,0:T(8,128)(2,1)S(1)} %copy-done.3, f32[2,256,256]{2,1,0:T(8,128)S(1)} %get-tuple-element.69.refs_3_, ...), custom_call_target="tpu_custom_call" | custom-call | flops 4000000000 | bytes 1000 | tf_op jit(solution)/shard_map/pallas_call | solution.py:66
  20.2 0.0 copy-start.6
  20.3 2.3 %collective-permute-done.3.refs_0_ = bf16[136,384]{1,0:T(8,128)(2,1)S(1)} collective-permute-done((bf16[136,384]{1,0:T(8,128)(2,1)S(1)}, bf16[136,384]{1,0:T(8,128)(2,1)S(1)}, u32[]{:S(2)}, u32[]{:S(2)}) %collective-permute-start.3) | collective-permute-done | bytes 104480 | tf_op jit(solution)/shard_map/ppermute | solution.py:607
  22.5 0.1 shard_map.120
  22.6 2.2 %collective-permute-start.6 = (bf16[128,384]{1,0:T(8,128)(2,1)S(1)}, bf16[128,384]{1,0:T(8,128)(2,1)S(1)}, u32[]{:S(2)}, u32[]{:S(2)}) collective-permute-start(bf16[128,384]{1,0:T(8,128)(2,1)S(1)} %get-tuple-element.95.refs_4_), channel_id=1, source_target_pairs={{0,4},{4,0},{8,12},{12,8},{16,20},{20,16},{24,28},{28,24},{1,5},{5... | collective-permute-start | bytes 294920 | tf_op jit(solution)/shard_map/ppermute | solution.py:607
  24.8 2.1 %collective-permute-start.7 = (bf16[128,256]{1,0:T(8,128)(2,1)S(1)}, bf16[128,256]{1,0:T(8,128)(2,1)S(1)}, u32[]{:S(2)}, u32[]{:S(2)}) collective-permute-start(bf16[128,256]{1,0:T(8,128)(2,1)S(1)} %get-tuple-element.103), channel_id=1, source_target_pairs={{0,4},{4,0},{8,12},{12,8},{16,20},{20,16},{24,28},{28,24},{1,5},{5... | collective-permute-start | bytes 196616 | tf_op jit(solution)/shard_map/ppermute | solution.py:607
  26.9 1.1 %shard_map.122 = (bf16[512,640]{1,0:T(8,128)(2,1)S(1)}, f32[1,512]{1,0:T(1,128)S(1)}, f32[640,512]{1,0:T(8,128)S(1)}) custom-call(f32[8,128]{1,0:T(8,128)S(1)} %get-tuple-element.88.prev_ref, bf16[512,128]{1,0:T(8,128)(2,1)S(1)} %copy-done.1, f32[512,128]{1,0:T(8,128)S(1)} %get-tuple-element.65.refs_2_.seg_ref, f32[1,1280]{1,0:T(1,128)S(1)} %reshape.19.gain_ref, ...), custom_call_target="tpu_custom_call" | custom-call | flops 1000 | bytes 1000 | tf_op jit(solution)/shard_map/pallas_call | solution.py:66
  28.1 0.9 %shard_map.123 = (bf16[512,384]{1,0:T(8,128)(2,1)S(1)}, f32[1,512]{1,0:T(1,128)S(1)}, f32[640,512]{1,0:T(8,128)S(1)}) custom-call(f32[8,128]{1,0:T(8,128)S(1)} %get-tuple-element.88.prev_ref, bf16[512,128]{1,0:T(8,128)(2,1)S(1)} %copy-done.1, f32[512,128]{1,0:T(8,128)S(1)} %get-tuple-element.65.refs_2_.seg_ref, f32[1,1280]{1,0:T(1,128)S(1)} %reshape.19.gain_ref, ...), custom_call_target="tpu_custom_call" | custom-call | flops 1000 | bytes 1000 | tf_op jit(solution)/shard_map/pallas_call | solution.py:66
  29.0 0.2 collective-permute-done.7.e_ref
  29.2 0.6 %shard_map.124 = (bf16[512,256]{1,0:T(8,128)(2,1)S(1)}, bf16[392,512]{1,0:T(8,128)(2,1)S(1)}) custom-call(f32[8,128]{1,0:T(8,128)S(1)} %get-tuple-element.88.prev_ref, bf16[512,128]{1,0:T(8,128)(2,1)S(1)} %copy-done.1, f32[512,128]{1,0:T(8,128)S(1)} %get-tuple-element.65.refs_2_.seg_ref, f32[512,256]{1,0:T(8,128)S(1)} %get-tuple-element.87.refs_4_.a_ref, ...), custom_call_target="tpu_custom_call" | custom-call | flops 1000 | bytes 1000 | tf_op jit(solution)/shard_map/pallas_call | solution.py:66
  29.8 0.1 collective-permute-start.9
  29.9 1.3 %shard_map.125 = (bf16[256,512]{1,0:T(8,128)(2,1)S(1)}, f32[384,512]{1,0:T(8,128)S(1)}, f32[256,512]{1,0:T(8,128)S(1)}) custom-call(f32[640,512]{1,0:T(8,128)S(1)} %get-tuple-element.104.p_ref.refs_0_, bf16[1280,2560]{1,0:T(8,128)(2,1)S(1)} %bitcast.5, bf16[512,640]{1,0:T(8,128)(2,1)S(1)} %get-tuple-element.97.refs_2_.refs_1_.refs_0_, ...), custom_call_target="tpu_custom_call" | custom-call | flops 1000 | bytes 1000 | tf_op jit(solution)/shard_map/pallas_call | solution.py:66
  31.2 0.6 %collective-permute-start.8 = (bf16[256,512]{1,0:T(8,128)(2,1)S(1)}, bf16[256,512]{1,0:T(8,128)(2,1)S(1)}, u32[]{:S(2)}, u32[]{:S(2)}) collective-permute-start(bf16[256,512]{1,0:T(8,128)(2,1)S(1)} %get-tuple-element.109), channel_id=1, source_target_pairs={{0,1},{1,0},{2,3},{3,2},{4,5},{5,4},{6,7},{7,6},{8,9},{9,8},{10,11... | collective-permute-start | bytes 786440 | tf_op jit(solution)/shard_map/ppermute | solution.py:610
  31.7 0.1 shard_map.126.refs_2_.factor_ref
  31.8 1.6 %collective-permute-start.15 = (bf16[392,512]{1,0:T(8,128)(2,1)S(1)}, bf16[392,512]{1,0:T(8,128)(2,1)S(1)}, u32[]{:S(2)}, u32[]{:S(2)}) collective-permute-start(bf16[392,512]{1,0:T(8,128)(2,1)S(1)} %shard_map.126.refs_2_.factor_ref), channel_id=1, source_target_pairs={{0,2},{1,3},{2,0},{3,1},{4,6},{5,7},{6,4},{7,5},{8,10},{9,11},{10,... | collective-permute-start | bytes 1204232 | tf_op jit(solution)/shard_map/ppermute | solution.py:610
  33.4 1.2 %shard_map.128 = (bf16[160,512]{1,0:T(8,128)(2,1)S(1)}, bf16[160,512]{1,0:T(8,128)(2,1)S(1)}, bf16[160,512]{1,0:T(8,128)(2,1)S(1)}, bf16[160,512]{1,0:T(8,128)(2,1)S(1)}) custom-call(bf16[1280,2560]{1,0:T(8,128)(2,1)S(1)} %bitcast.5, bf16[512,640]{1,0:T(8,128)(2,1)S(1)} %get-tuple-element.97.refs_2_.refs_1_.refs_0_, ...), custom_call_target="tpu_custom_call" | custom-call | flops 1000 | bytes 1000 | tf_op jit(solution)/shard_map/pallas_call | solution.py:66
  34.7 0.1 collective-permute-start.10
  34.7 1.4 %collective-permute-start.14 = (bf16[256,512]{1,0:T(8,128)(2,1)S(1)}, bf16[256,512]{1,0:T(8,128)(2,1)S(1)}, u32[]{:S(2)}, u32[]{:S(2)}) collective-permute-start(bf16[256,512]{1,0:T(8,128)(2,1)S(1)} %shard_map.127.refs_4_), channel_id=1, source_target_pairs={{0,2},{1,3},{2,0},{3,1},{4,6},{5,7},{6,4},{7,5},{8,10},{9,11},{10,... | collective-permute-start | bytes 786440 | tf_op jit(solution)/shard_map/ppermute | solution.py:610
  36.1 0.5 %collective-permute-start.12 = (bf16[160,512]{1,0:T(8,128)(2,1)S(1)}, bf16[160,512]{1,0:T(8,128)(2,1)S(1)}, u32[]{:S(2)}, u32[]{:S(2)}) collective-permute-start(bf16[160,512]{1,0:T(8,128)(2,1)S(1)} %get-tuple-element.113), channel_id=1, source_target_pairs={{0,1},{1,0},{2,3},{3,2},{4,5},{5,4},{6,7},{7,6},{8,9},{9,8},{10,11... | collective-permute-start | bytes 491528 | tf_op jit(solution)/shard_map/ppermute | solution.py:610
  36.6 0.0 collective-permute-start.13
  36.6 0.9 %collective-permute-done.11.refs_4_ = bf16[160,512]{1,0:T(8,128)(2,1)S(1)} collective-permute-done((bf16[160,512]{1,0:T(8,128)(2,1)S(1)}, bf16[160,512]{1,0:T(8,128)(2,1)S(1)}, u32[]{:S(2)}, u32[]{:S(2)}) %collective-permute-start.11) | collective-permute-done | bytes 163872 | tf_op jit(solution)/shard_map/ppermute | solution.py:610
  37.5 0.2 collective-permute-done.12.refs_5_
  37.7 0.3 collective-permute-done.13.refs_6_
  38.0 1.2 %shard_map.129.own_ref = f32[640,512]{1,0:T(8,128)S(1)} custom-call(bf16[1280,2560]{1,0:T(8,128)(2,1)S(1)} %bitcast.5, bf16[512,640]{1,0:T(8,128)(2,1)S(1)} %get-tuple-element.97.refs_2_.refs_1_.refs_0_, bf16[512,384]{1,0:T(8,128)(2,1)S(1)} %get-tuple-element.101.refs_3_.refs_2_.refs_1_, bf16[512,256]{1,0:T(8,128)(2,1)S(1)} %get-tuple-element.106.refs_4_.refs_3_.refs_2_, ...), custom_call_target="tpu_custom_call" | custom-call | flops 1000 | bytes 1000 | tf_op jit(solution)/shard_map/pallas_call | solution.py:66
  39.2 4.8 %collective-permute-done.15.far_ref = bf16[392,512]{1,0:T(8,128)(2,1)S(1)} collective-permute-done((bf16[392,512]{1,0:T(8,128)(2,1)S(1)}, bf16[392,512]{1,0:T(8,128)(2,1)S(1)}, u32[]{:S(2)}, u32[]{:S(2)}) %collective-permute-start.15) | collective-permute-done | bytes 401440 | tf_op jit(solution)/shard_map/ppermute | solution.py:610
  44.0 0.8 %shard_map.130 = (bf16[640,512]{1,0:T(8,128)(2,1)}, f32[1,512]{1,0:T(1,128)S(1)}) custom-call(f32[640,512]{1,0:T(8,128)S(1)} %shard_map.129.own_ref, bf16[392,512]{1,0:T(8,128)(2,1)S(1)} %collective-permute-done.15.far_ref, bf16[392,512]{1,0:T(8,128)(2,1)S(1)} %shard_map.126.refs_2_.factor_ref), custom_call_target="tpu_custom_call" | custom-call | flops 1000 | bytes 1000 | tf_op jit(solution)/shard_map/pallas_call | solution.py:587
  44.9 3.9 %collective-permute-done.14.far_ref = bf16[256,512]{1,0:T(8,128)(2,1)S(1)} collective-permute-done((bf16[256,512]{1,0:T(8,128)(2,1)S(1)}, bf16[256,512]{1,0:T(8,128)(2,1)S(1)}, u32[]{:S(2)}, u32[]{:S(2)}) %collective-permute-start.14) | collective-permute-done | bytes 262176 | tf_op jit(solution)/shard_map/ppermute | solution.py:610
  48.7 0.7 %shard_map.131 = bf16[640,512]{1,0:T(8,128)(2,1)} custom-call(f32[640,512]{1,0:T(8,128)S(1)} %shard_map.129.own_ref, bf16[256,512]{1,0:T(8,128)(2,1)S(1)} %collective-permute-done.14.far_ref, f32[1,512]{1,0:T(1,128)S(1)} %get-tuple-element.115.factor_ref, bf16[640,512]{1,0:T(8,128)(2,1)} %get-tuple-element.116.refs_0_), custom_call_target="tpu_custom_call", output_to_operand_aliasing={{}: (3, {})} | custom-call | flops 1000 | bytes 1000 | tf_op jit(solution)/shard_map/pallas_call | solution.py:587
  (27 shorter events, 0.1 us)
Async XLA Ops:
  0.0 5.7 %copy-start = (bf16[512,1280]{1,0:T(8,128)(2,1)S(1)}, bf16[512,1280]{1,0:T(8,128)(2,1)}, u32[]{:S(2)}) copy-start(bf16[512,1280]{1,0:T(8,128)(2,1)} %refs_0_.12) | copy-start | bytes 3932164
  0.0 5.7 %copy-start.3 = (bf16[512,128]{1,0:T(8,128)(2,1)S(1)}, bf16[512,128]{1,0:T(8,128)(2,1)}, u32[]{:S(2)}) copy-start(bf16[512,128]{1,0:T(8,128)(2,1)} %refs_2_.7) | copy-start | bytes 393220
  0.0 7.5 %copy-start.5 = (f32[20]{0:T(128)S(1)}, f32[20]{0:T(128)}, u32[]{:S(2)}) copy-start(f32[20]{0:T(128)} %param.19) | copy-start | bytes 244
  2.7 4.8 %copy-start.1 = (bf16[512,128]{1,0:T(8,128)(2,1)S(1)}, bf16[512,128]{1,0:T(8,128)(2,1)}, u32[]{:S(2)}) copy-start(bf16[512,128]{1,0:T(8,128)(2,1)} %rd_ref.5) | copy-start | bytes 393220
  2.7 6.3 %collective-permute-start = (bf16[136,384]{1,0:T(8,128)(2,1)}, bf16[136,384]{1,0:T(8,128)(2,1)S(1)}, u32[]{:S(2)}, u32[]{:S(2)}) collective-permute-start(bf16[136,384]{1,0:T(8,128)(2,1)} %get-tuple-element.63), channel_id=1, source_target_pairs={{0,4},{4,0},{8,12},{12,8},{16,20},{20,16},{24,28},{28,24},{1,5},{5... | collective-permute-start | bytes 313352 | tf_op jit(solution)/shard_map/ppermute | solution.py:607
  5.7 0.9 %copy-start.2 = (f32[104,512]{1,0:T(8,128)S(1)}, f32[104,512]{1,0:T(8,128)}, u32[]{:S(2)}) copy-start(f32[104,512]{1,0:T(8,128)} %get-tuple-element.61.stash_ref.refs_2_) | copy-start | bytes 638980
  7.4 4.4 %collective-permute-start.2 = (bf16[136,256]{1,0:T(8,128)(2,1)S(1)}, bf16[136,256]{1,0:T(8,128)(2,1)S(1)}, u32[]{:S(2)}, u32[]{:S(2)}) collective-permute-start(bf16[136,256]{1,0:T(8,128)(2,1)S(1)} %get-tuple-element.64.refs_4_), channel_id=1, source_target_pairs={{0,4},{4,0},{8,12},{12,8},{16,20},{20,16},{24,28},{28,24},{1,5},{5... | collective-permute-start | bytes 208904 | tf_op jit(solution)/shard_map/ppermute | solution.py:607
  9.0 1.8 %copy-start.4 = (bf16[512,1280]{1,0:T(8,128)(2,1)S(1)}, bf16[512,1280]{1,0:T(8,128)(2,1)}, u32[]{:S(2)}) copy-start(bf16[512,1280]{1,0:T(8,128)(2,1)} %refs_1_.10) | copy-start | bytes 3932164
  9.1 5.7 %collective-permute-start.1 = (bf16[136,384]{1,0:T(8,128)(2,1)S(1)}, bf16[136,384]{1,0:T(8,128)(2,1)S(1)}, u32[]{:S(2)}, u32[]{:S(2)}) collective-permute-start(bf16[136,384]{1,0:T(8,128)(2,1)S(1)} %get-tuple-element.66.refs_9_), channel_id=1, source_target_pairs={{0,8},{4,12},{8,0},{12,4},{16,24},{20,28},{24,16},{28,20},{1,9},{5... | collective-permute-start | bytes 313352 | tf_op jit(solution)/shard_map/ppermute | solution.py:607
  11.8 7.0 %collective-permute-start.4 = (bf16[136,256]{1,0:T(8,128)(2,1)S(1)}, bf16[136,256]{1,0:T(8,128)(2,1)S(1)}, u32[]{:S(2)}, u32[]{:S(2)}) collective-permute-start(bf16[136,256]{1,0:T(8,128)(2,1)S(1)} %get-tuple-element.77.refs_9_), channel_id=1, source_target_pairs={{0,8},{4,12},{8,0},{12,4},{16,24},{20,28},{24,16},{28,20},{1,9},{5... | collective-permute-start | bytes 208904 | tf_op jit(solution)/shard_map/ppermute | solution.py:607
  14.8 7.7 %collective-permute-start.3 = (bf16[136,384]{1,0:T(8,128)(2,1)S(1)}, bf16[136,384]{1,0:T(8,128)(2,1)S(1)}, u32[]{:S(2)}, u32[]{:S(2)}) collective-permute-start(bf16[136,384]{1,0:T(8,128)(2,1)S(1)} %get-tuple-element.79.refs_9_), channel_id=1, source_target_pairs={{0,16},{4,20},{8,24},{12,28},{16,0},{20,4},{24,8},{28,12},{1,17},{... | collective-permute-start | bytes 313352 | tf_op jit(solution)/shard_map/ppermute | solution.py:607
  18.9 8.0 %slice-start = ((s8[6553600]{0:T(1024)(128)(4,1)}), s8[4194304]{0:T(1024)(128)(4,1)S(1)}, s32[]{:S(2)}) async-start(s8[6553600]{0:T(1024)(128)(4,1)} %bitcast.4), calls=%async_computation | async-start | bytes 8388608
  18.9 8.0 %slice-start.1 = ((s8[6553600]{0:T(1024)(128)(4,1)}), s8[2359296]{0:T(1024)(128)(4,1)S(1)}, s32[]{:S(2)}) async-start(s8[6553600]{0:T(1024)(128)(4,1)} %bitcast.4), calls=%async_computation.1 | async-start | bytes 4718592
  18.9 5.9 %collective-permute-start.5 = (bf16[136,256]{1,0:T(8,128)(2,1)S(1)}, bf16[136,256]{1,0:T(8,128)(2,1)S(1)}, u32[]{:S(2)}, u32[]{:S(2)}) collective-permute-start(bf16[136,256]{1,0:T(8,128)(2,1)S(1)} %get-tuple-element.86.refs_9_), channel_id=1, source_target_pairs={{0,16},{4,20},{8,24},{12,28},{16,0},{20,4},{24,8},{28,12},{1,17},{... | collective-permute-start | bytes 208904 | tf_op jit(solution)/shard_map/ppermute | solution.py:607
  20.2 6.7 %copy-start.6 = (f32[1280]{0:T(1024)S(1)}, f32[1280]{0:T(1024)}, u32[]{:S(2)}) copy-start(f32[1280]{0:T(1024)} %param.20) | copy-start | bytes 15364
  22.6 5.4 %collective-permute-start.6 = (bf16[128,384]{1,0:T(8,128)(2,1)S(1)}, bf16[128,384]{1,0:T(8,128)(2,1)S(1)}, u32[]{:S(2)}, u32[]{:S(2)}) collective-permute-start(bf16[128,384]{1,0:T(8,128)(2,1)S(1)} %get-tuple-element.95.refs_4_), channel_id=1, source_target_pairs={{0,4},{4,0},{8,12},{12,8},{16,20},{20,16},{24,28},{28,24},{1,5},{5... | collective-permute-start | bytes 294920 | tf_op jit(solution)/shard_map/ppermute | solution.py:607
  24.8 4.3 %collective-permute-start.7 = (bf16[128,256]{1,0:T(8,128)(2,1)S(1)}, bf16[128,256]{1,0:T(8,128)(2,1)S(1)}, u32[]{:S(2)}, u32[]{:S(2)}) collective-permute-start(bf16[128,256]{1,0:T(8,128)(2,1)S(1)} %get-tuple-element.103), channel_id=1, source_target_pairs={{0,4},{4,0},{8,12},{12,8},{16,20},{20,16},{24,28},{28,24},{1,5},{5... | collective-permute-start | bytes 196616 | tf_op jit(solution)/shard_map/ppermute | solution.py:607
  29.8 1.9 %collective-permute-start.9 = (bf16[392,512]{1,0:T(8,128)(2,1)S(1)}, bf16[392,512]{1,0:T(8,128)(2,1)S(1)}, u32[]{:S(2)}, u32[]{:S(2)}) collective-permute-start(bf16[392,512]{1,0:T(8,128)(2,1)S(1)} %get-tuple-element.107.refs_5_.mine_ref), channel_id=1, source_target_pairs={{0,1},{1,0},{2,3},{3,2},{4,5},{5,4},{6,7},{7,6},{8,9},{9,8},{10,11... | collective-permute-start | bytes 1204232 | tf_op jit(solution)/shard_map/ppermute | solution.py:610
  31.2 2.2 %collective-permute-start.8 = (bf16[256,512]{1,0:T(8,128)(2,1)S(1)}, bf16[256,512]{1,0:T(8,128)(2,1)S(1)}, u32[]{:S(2)}, u32[]{:S(2)}) collective-permute-start(bf16[256,512]{1,0:T(8,128)(2,1)S(1)} %get-tuple-element.109), channel_id=1, source_target_pairs={{0,1},{1,0},{2,3},{3,2},{4,5},{5,4},{6,7},{7,6},{8,9},{9,8},{10,11... | collective-permute-start | bytes 786440 | tf_op jit(solution)/shard_map/ppermute | solution.py:610
  31.8 12.2 %collective-permute-start.15 = (bf16[392,512]{1,0:T(8,128)(2,1)S(1)}, bf16[392,512]{1,0:T(8,128)(2,1)S(1)}, u32[]{:S(2)}, u32[]{:S(2)}) collective-permute-start(bf16[392,512]{1,0:T(8,128)(2,1)S(1)} %shard_map.126.refs_2_.factor_ref), channel_id=1, source_target_pairs={{0,2},{1,3},{2,0},{3,1},{4,6},{5,7},{6,4},{7,5},{8,10},{9,11},{10,... | collective-permute-start | bytes 1204232 | tf_op jit(solution)/shard_map/ppermute | solution.py:610
  34.7 2.0 %collective-permute-start.10 = (bf16[160,512]{1,0:T(8,128)(2,1)S(1)}, bf16[160,512]{1,0:T(8,128)(2,1)S(1)}, u32[]{:S(2)}, u32[]{:S(2)}) collective-permute-start(bf16[160,512]{1,0:T(8,128)(2,1)S(1)} %get-tuple-element.111), channel_id=1, source_target_pairs={{0,1},{1,0},{2,3},{3,2},{4,5},{5,4},{6,7},{7,6},{8,9},{9,8},{10,11... | collective-permute-start | bytes 491528 | tf_op jit(solution)/shard_map/ppermute | solution.py:610
  34.7 14.0 %collective-permute-start.14 = (bf16[256,512]{1,0:T(8,128)(2,1)S(1)}, bf16[256,512]{1,0:T(8,128)(2,1)S(1)}, u32[]{:S(2)}, u32[]{:S(2)}) collective-permute-start(bf16[256,512]{1,0:T(8,128)(2,1)S(1)} %shard_map.127.refs_4_), channel_id=1, source_target_pairs={{0,2},{1,3},{2,0},{3,1},{4,6},{5,7},{6,4},{7,5},{8,10},{9,11},{10,... | collective-permute-start | bytes 786440 | tf_op jit(solution)/shard_map/ppermute | solution.py:610
  36.1 1.4 %collective-permute-start.11 = (bf16[160,512]{1,0:T(8,128)(2,1)S(1)}, bf16[160,512]{1,0:T(8,128)(2,1)S(1)}, u32[]{:S(2)}, u32[]{:S(2)}) collective-permute-start(bf16[160,512]{1,0:T(8,128)(2,1)S(1)} %get-tuple-element.112), channel_id=1, source_target_pairs={{0,1},{1,0},{2,3},{3,2},{4,5},{5,4},{6,7},{7,6},{8,9},{9,8},{10,11... | collective-permute-start | bytes 491528 | tf_op jit(solution)/shard_map/ppermute | solution.py:610
  36.1 1.6 %collective-permute-start.12 = (bf16[160,512]{1,0:T(8,128)(2,1)S(1)}, bf16[160,512]{1,0:T(8,128)(2,1)S(1)}, u32[]{:S(2)}, u32[]{:S(2)}) collective-permute-start(bf16[160,512]{1,0:T(8,128)(2,1)S(1)} %get-tuple-element.113), channel_id=1, source_target_pairs={{0,1},{1,0},{2,3},{3,2},{4,5},{5,4},{6,7},{7,6},{8,9},{9,8},{10,11... | collective-permute-start | bytes 491528 | tf_op jit(solution)/shard_map/ppermute | solution.py:610
  36.6 1.4 %collective-permute-start.13 = (bf16[160,512]{1,0:T(8,128)(2,1)S(1)}, bf16[160,512]{1,0:T(8,128)(2,1)S(1)}, u32[]{:S(2)}, u32[]{:S(2)}) collective-permute-start(bf16[160,512]{1,0:T(8,128)(2,1)S(1)} %get-tuple-element.114), channel_id=1, source_target_pairs={{0,1},{1,0},{2,3},{3,2},{4,5},{5,4},{6,7},{7,6},{8,9},{9,8},{10,11... | collective-permute-start | bytes 491528 | tf_op jit(solution)/shard_map/ppermute | solution.py:610

commit v10 on v9

--- a/solution.py
+++ b/solution.py
@@ -159,9 +159,8 @@
         ).astype(BF16)
         stash_ref[...] = jnp.zeros_like(stash_ref)
         cum_rows, step_rows, tail_rows, sum_rows = stash_rows()
-        for copy in copies[:5]:
+        for copy in copies[:4]:
             copy.wait()
-        vecs = jnp.transpose(wr_ref[...].astype(F32))
         rows[0:1, 0:heads] = dl_ref[...]
         rows[1:2, 0:heads] = sb_ref[...]
         stash_ref[0:heads] = raw_ref[...].astype(F32)
@@ -192,7 +191,9 @@
         rows[0:32] = jnp.broadcast_to(jnp.exp(base), (32, LANES))
         sums = jnp.transpose(rows[...])[0:8]
         stash_ref[sum_rows, 0:LANES] = sums
-        copies[5].wait()
+        for copy in copies[4:]:
+            copy.wait()
+        vecs = jnp.transpose(wr_ref[...].astype(F32))
         piece = slice(0, EARLY_LANES)
         some_state(half, half_w, piece, width, vecs, stash_ref.at[tail_rows], sums, last, x_ref, 0, other_ref)
 
@@ -429,12 +430,10 @@
     return values[0] if len(values) == 1 else jnp.concatenate(values, axis=1)
 
 
-def gated_part(which, lanes, prev_ref, rd_ref, cum_ref, a_refs, b_refs, states, gain_ref):
+def gated_part(which, lanes, rm, a_refs, b_refs, states, gain_ref):
     half_w = gain_ref.shape[1] // 2
     first = pl.multiple_of(position()[which] * half_w + lanes.start, LANES)
     here = pl.ds(first, lanes.stop - lanes.start)
-    linked = cum_ref[:, SEG_LANE : SEG_LANE + 1] == prev_ref[0:1, 0:1]
-    rm = jnp.where(linked, rd_ref[...].astype(F32), 0.0).astype(BF16)
     carried = [dot(rm, state[...]) for state in states]
     carried = carried[0] if len(carried) == 1 else jnp.concatenate(carried, axis=1)
     gated = side_by_side(a_refs) + side_by_side(b_refs) * carried
@@ -468,38 +467,49 @@
     return whole[0:size], whole[size : size + 1] + (whole[size + 1 : size + 2] + whole[size + 2 : size + 3])
 
 
-def gated_sums(which, lanes, prev, read, seg, a, b, states, gain, weight, partial=None, squares=None):
-    toks = read.shape[0]
+def gated_sums(which, lanes, reads, a, b, states, gain, weight, partial=None, squares=None):
+    toks = reads[0].shape[0]
+    masks = len(reads) > 1
     cols = weight.shape[1] // 4
     earlier = () if partial is None else (partial, squares)
     ends = [0, len(a), len(a) + len(b), len(a) + len(b) + len(states)]
 
-    def body(prev_ref, rd_ref, seg_ref, gain_ref, w_ref, *refs):
+    def body(gain_ref, w_ref, rd_ref, *refs):
+        if masks:
+            prev_ref, seg_ref, *refs, rm_ref = refs
+            linked = seg_ref[:, SEG_LANE : SEG_LANE + 1] == prev_ref[0:1, 0:1]
+            rm = jnp.where(linked, rd_ref[...].astype(F32), 0.0).astype(BF16)
+            rm_ref[...] = rm
+        else:
+            rm = rd_ref[...]
         a_refs, b_refs, s_refs = (refs[low:high] for low, high in zip(ends, ends[1:]))
         old, (g_ref, s_ref, y_ref) = refs[ends[-1] : -3], refs[-3:]
-        g, s = gated_part(which, lanes, prev_ref, rd_ref, seg_ref, a_refs, b_refs, s_refs, gain_ref)
+        g, s = gated_part(which, lanes, rm, a_refs, b_refs, s_refs, gain_ref)
         g_ref[...] = g
         s_ref[...] = s + old[1][...] if old else s
         y = projected(which, lanes, 0, slice(0, cols), w_ref, g)
         y_ref[...] = y + old[0][...] if old else y
 
     return call(
-        body, (prev, read, seg, gain, weight, *a, *b, *states, *earlier),
-        shaped(((toks, lanes.stop - lanes.start), BF16), ((1, toks), F32), ((cols, toks), F32)),
-    )
-
-
-def gated_last(lanes, rows, prev, read, seg, a, b, state, gain, weight, partial, squares):
+        body, (gain, weight, *reads, *a, *b, *states, *earlier),
+        shaped(
+            ((toks, lanes.stop - lanes.start), BF16), ((1, toks), F32), ((cols, toks), F32),
+            *([(reads[0].shape, BF16)] if masks else []),
+        ),
+    )
+
+
+def gated_last(lanes, rows, read, a, b, state, gain, weight, partial, squares):
     toks = read.shape[0]
 
-    def body(prev_ref, rd_ref, seg_ref, a_ref, b_ref, e_ref, gain_ref, w_ref, p_ref, s_ref, g_ref, y_ref):
-        g, s = gated_part(1, lanes, prev_ref, rd_ref, seg_ref, (a_ref,), (b_ref,), (e_ref,), gain_ref)
+    def body(rd_ref, a_ref, b_ref, e_ref, gain_ref, w_ref, p_ref, s_ref, g_ref, y_ref):
+        g, s = gated_part(1, lanes, rd_ref[...], (a_ref,), (b_ref,), (e_ref,), gain_ref)
         g_ref[...] = g
         y = p_ref[rows] + projected(1, lanes, 0, rows, w_ref, g)
         y_ref[...] = with_squares(y, s_ref[...] + s)
 
     return call(
-        body, (prev, read, seg, a, b, state, gain, weight, partial, squares),
+        body, (read, a, b, state, gain, weight, partial, squares),
         shaped(((toks, lanes.stop - lanes.start), BF16), ((rows.stop - rows.start + EXTRA, toks), BF16)),
     )
 
@@ -654,15 +664,14 @@
     send_two, keep_two = entry_step(bit, False, swap(sent[1], bit), *entries[1], rows[1], firsts[1], send_one)
     other_two = swap(send_two, 1)
     gain = norm_gain.reshape(1, feats)
-    shared = (prev, read_vecs, seg)
     whole_half = slice(0, half_w)
-    g_keep, squares, partial = gated_sums(
-        0, whole_half, *shared, (keep_a[0], keep_b[0]), (keep_a[1], keep_b[1]), (keep_one, keep_two), gain, out_weight
+    g_keep, squares, partial, linked = gated_sums(
+        0, whole_half, (read_vecs, prev, seg), (keep_a[0], keep_b[0]), (keep_a[1], keep_b[1]), (keep_one, keep_two), gain, out_weight
     )
     g_one, squares, partial = gated_sums(
-        1, one, *shared, other_a[:1], other_a[1:], (other_one,), gain, out_weight, partial, squares
-    )
-    g_two, near_top = gated_last(two, top, *shared, *other_b, other_two, gain, out_weight, partial, squares)
+        1, one, (linked,), other_a[:1], other_a[1:], (other_one,), gain, out_weight, partial, squares
+    )
+    g_two, near_top = gated_last(two, top, linked, *other_b, other_two, gain, out_weight, partial, squares)
     got_top = across(near_top, 1)
     groups, gs = ((0, whole_half), (1, one), (1, two)), (g_keep, g_one, g_two)
     near_rest, far_top, far_rest = project_next(groups, gs, top, rest, partial, out_weight, near_top)

time: 49.6 us -> 49.4 us (level)
  no operation moved by 1% of the time
where the time goes in v10:
time: 49.4 us; the launch traced here: 49.2 us
  starting transfers between devices  17.9 us (36%)
  Pallas kernels  16.6 us (34%)
  waiting for transfers between devices  13.6 us (28%)
  local copies, waits for them, and re-layouts  0.98 us (2%)
    ppermute x8, starting transfers between devices, swap(): return lax.ppermute(a, 'seq', [(i, i ^ bit) for i in range(n_seq)])  13.8 us
    pallas_call x20, Pallas kernels, call(): pl.pallas_call(kernel, in_specs=specs, out_specs=jax.tree.map(lambda _: v...  12.5 us
    ppermute x8, waiting for transfers between devices, across(): return lax.ppermute(a, 'tp', [(i, i ^ bit) for i in range(n_tp)])  10 us
    ppermute x8, starting transfers between devices, across(): return lax.ppermute(a, 'tp', [(i, i ^ bit) for i in range(n_tp)])  4.12 us
    ppermute x8, waiting for transfers between devices, swap(): return lax.ppermute(a, 'seq', [(i, i ^ bit) for i in range(n_seq)])  3.51 us
    pallas_call x1, Pallas kernels, prepare(): pl.pallas_call(body, in_specs=[pl.BlockSpec(memory_space=pltpu.HBM)] * le...  2.5 us
    pallas_call x2, Pallas kernels, finish(): pl.pallas_call(body, in_specs=[vm] * 3 + ([] if first else [where]), out_...  1.58 us
  transfers between devices with their start and end apart: 16, of which 8 were waited for; matrix products, arithmetic and copies ran while one was open for 0% of the time, Pallas kernels for 26%

profile of v10, /device:TPU:0, one launch (start us, length us, event | category | flops | bytes accessed | tf_op | source)
XLA Modules:
  0.0 49.2 jit_solution(5877285253905512961)
XLA Ops:
  0.0 2.5 %shard_map.109 = (bf16[136,384]{1,0:T(8,128)(2,1)}, f32[104,512]{1,0:T(8,128)}) custom-call(bf16[20,512]{1,0:T(8,128)(2,1)} %refs_0_.7, s32[1,512]{1,0:T(1,128)} %bitcast.7, f32[1,20]{1,0:T(1,128)} %bitcast.8, f32[1,20]{1,0:T(1,128)} %bitcast.9, bf16[512,128]{1,0:T(8,128)(2,1)} %refs_2_.7, bf16[512,1280]{1,0:T(8,128)(2,1)} %refs_0_.12), custom_call_target="tpu_custom_call" | custom-call | flops 4000000000 | bytes 1000 | tf_op jit(solution)/shard_map/pallas_call | solution.py:202
  2.5 0.0 copy-start.5
  2.5 3.0 %collective-permute-start = (bf16[136,384]{1,0:T(8,128)(2,1)}, bf16[136,384]{1,0:T(8,128)(2,1)S(1)}, u32[]{:S(2)}, u32[]{:S(2)}) collective-permute-start(bf16[136,384]{1,0:T(8,128)(2,1)} %get-tuple-element.64), channel_id=1, source_target_pairs={{0,4},{4,0},{8,12},{12,8},{16,20},{20,16},{24,28},{28,24},{1,5},{5... | collective-permute-start | bytes 313352 | tf_op jit(solution)/shard_map/ppermute | solution.py:617
  5.6 0.9 %copy-done.1 = f32[104,512]{1,0:T(8,128)S(1)} copy-done((f32[104,512]{1,0:T(8,128)S(1)}, f32[104,512]{1,0:T(8,128)}, u32[]{:S(2)}) %copy-start.1) | copy-done | bytes 213016
  6.5 0.7 %shard_map.110 = (bf16[136,256]{1,0:T(8,128)(2,1)S(1)}, bf16[136,384]{1,0:T(8,128)(2,1)S(1)}, bf16[136,256]{1,0:T(8,128)(2,1)S(1)}) custom-call(f32[104,512]{1,0:T(8,128)S(1)} %copy-done.1, bf16[512,1280]{1,0:T(8,128)(2,1)S(1)} %copy-done, bf16[512,128]{1,0:T(8,128)(2,1)S(1)} %copy-done.3), custom_call_target="tpu_custom_call" | custom-call | flops 1000 | bytes 1000 | tf_op jit(solution)/shard_map/pallas_call | solution.py:66
  7.2 0.1 collective-permute-start.2
  7.3 0.6 %shard_map.111 = (f32[2,256,256]{2,1,0:T(8,128)S(1)}, bf16[256,128]{1,0:T(8,128)(2,1)S(1)}, f32[2,512,128]{2,1,0:T(8,128)S(1)}, f32[32,512]{1,0:T(8,128)S(1)}, f...) custom-call(bf16[512,128]{1,0:T(8,128)(2,1)S(1)} %copy-done.2, ...), custom_call_target="tpu_custom_call" | custom-call | flops 4000000000 | bytes 1000 | tf_op jit(solution)/shard_map/pallas_call | solution.py:66
  7.9 1.0 %collective-permute-done.refs_1_ = bf16[136,384]{1,0:T(8,128)(2,1)S(1)} collective-permute-done((bf16[136,384]{1,0:T(8,128)(2,1)}, bf16[136,384]{1,0:T(8,128)(2,1)S(1)}, u32[]{:S(2)}, u32[]{:S(2)}) %collective-permute-start) | collective-permute-done | bytes 104480 | tf_op jit(solution)/shard_map/ppermute | solution.py:617
  8.8 0.1 shard_map.112
  8.9 1.8 %collective-permute-start.1 = (bf16[136,384]{1,0:T(8,128)(2,1)S(1)}, bf16[136,384]{1,0:T(8,128)(2,1)S(1)}, u32[]{:S(2)}, u32[]{:S(2)}) collective-permute-start(bf16[136,384]{1,0:T(8,128)(2,1)S(1)} %get-tuple-element.67.refs_9_), channel_id=1, source_target_pairs={{0,8},{4,12},{8,0},{12,4},{16,24},{20,28},{24,16},{28,20},{1,9},{5... | collective-permute-start | bytes 313352 | tf_op jit(solution)/shard_map/ppermute | solution.py:617
  10.7 0.9 %shard_map.113 = (f32[512,256]{1,0:T(8,128)S(1)}, f32[512,256]{1,0:T(8,128)S(1)}) custom-call(bf16[512,1280]{1,0:T(8,128)(2,1)S(1)} %copy-done, bf16[512,1280]{1,0:T(8,128)(2,1)S(1)} %copy-done.4, bf16[512,128]{1,0:T(8,128)(2,1)S(1)} %copy-done.3, f32[2,256,256]{2,1,0:T(8,128)S(1)} %get-tuple-element.70.refs_3_, ...), custom_call_target="tpu_custom_call" | custom-call | flops 4000000000 | bytes 1000 | tf_op jit(solution)/shard_map/pallas_call | solution.py:66
  11.6 0.1 shard_map.114
  11.7 1.6 %collective-permute-start.4 = (bf16[136,256]{1,0:T(8,128)(2,1)S(1)}, bf16[136,256]{1,0:T(8,128)(2,1)S(1)}, u32[]{:S(2)}, u32[]{:S(2)}) collective-permute-start(bf16[136,256]{1,0:T(8,128)(2,1)S(1)} %get-tuple-element.78.refs_9_), channel_id=1, source_target_pairs={{0,8},{4,12},{8,0},{12,4},{16,24},{20,28},{24,16},{28,20},{1,9},{5... | collective-permute-start | bytes 208904 | tf_op jit(solution)/shard_map/ppermute | solution.py:617
  13.3 1.3 %shard_map.115 = (f32[512,384]{1,0:T(8,128)S(1)}, f32[512,384]{1,0:T(8,128)S(1)}) custom-call(bf16[512,1280]{1,0:T(8,128)(2,1)S(1)} %copy-done, bf16[512,1280]{1,0:T(8,128)(2,1)S(1)} %copy-done.4, bf16[512,128]{1,0:T(8,128)(2,1)S(1)} %copy-done.3, f32[2,256,256]{2,1,0:T(8,128)S(1)} %get-tuple-element.70.refs_3_, ...), custom_call_target="tpu_custom_call" | custom-call | flops 4000000000 | bytes 1000 | tf_op jit(solution)/shard_map/pallas_call | solution.py:66
  14.6 0.1 shard_map.116
  14.7 2.7 %collective-permute-start.3 = (bf16[136,384]{1,0:T(8,128)(2,1)S(1)}, bf16[136,384]{1,0:T(8,128)(2,1)S(1)}, u32[]{:S(2)}, u32[]{:S(2)}) collective-permute-start(bf16[136,384]{1,0:T(8,128)(2,1)S(1)} %get-tuple-element.80.refs_9_), channel_id=1, source_target_pairs={{0,16},{4,20},{8,24},{12,28},{16,0},{20,4},{24,8},{28,12},{1,17},{... | collective-permute-start | bytes 313352 | tf_op jit(solution)/shard_map/ppermute | solution.py:617
  17.3 1.3 %shard_map.117 = (f32[512,384]{1,0:T(8,128)S(1)}, f32[512,384]{1,0:T(8,128)S(1)}) custom-call(bf16[512,1280]{1,0:T(8,128)(2,1)S(1)} %copy-done, bf16[512,1280]{1,0:T(8,128)(2,1)S(1)} %copy-done.4, bf16[512,128]{1,0:T(8,128)(2,1)S(1)} %copy-done.3, f32[2,256,256]{2,1,0:T(8,128)S(1)} %get-tuple-element.70.refs_3_, ...), custom_call_target="tpu_custom_call" | custom-call | flops 4000000000 | bytes 1000 | tf_op jit(solution)/shard_map/pallas_call | solution.py:66
  18.7 0.0 slice-start
  18.8 0.4 collective-permute-start.5
  19.2 0.9 %shard_map.119 = (f32[512,256]{1,0:T(8,128)S(1)}, f32[512,256]{1,0:T(8,128)S(1)}) custom-call(bf16[512,1280]{1,0:T(8,128)(2,1)S(1)} %copy-done, bf16[512,1280]{1,0:T(8,128)(2,1)S(1)} %copy-done.4, bf16[512,128]{1,0:T(8,128)(2,1)S(1)} %copy-done.3, f32[2,256,256]{2,1,0:T(8,128)S(1)} %get-tuple-element.70.refs_3_, ...), custom_call_target="tpu_custom_call" | custom-call | flops 4000000000 | bytes 1000 | tf_op jit(solution)/shard_map/pallas_call | solution.py:66
  20.1 0.0 copy-start.6
  20.1 2.3 %collective-permute-done.3.refs_0_ = bf16[136,384]{1,0:T(8,128)(2,1)S(1)} collective-permute-done((bf16[136,384]{1,0:T(8,128)(2,1)S(1)}, bf16[136,384]{1,0:T(8,128)(2,1)S(1)}, u32[]{:S(2)}, u32[]{:S(2)}) %collective-permute-start.3) | collective-permute-done | bytes 104480 | tf_op jit(solution)/shard_map/ppermute | solution.py:617
  22.4 0.1 shard_map.120
  22.5 2.1 %collective-permute-start.6 = (bf16[128,384]{1,0:T(8,128)(2,1)S(1)}, bf16[128,384]{1,0:T(8,128)(2,1)S(1)}, u32[]{:S(2)}, u32[]{:S(2)}) collective-permute-start(bf16[128,384]{1,0:T(8,128)(2,1)S(1)} %get-tuple-element.96.refs_4_), channel_id=1, source_target_pairs={{0,4},{4,0},{8,12},{12,8},{16,20},{20,16},{24,28},{28,24},{1,5},{5... | collective-permute-start | bytes 294920 | tf_op jit(solution)/shard_map/ppermute | solution.py:617
  24.6 0.1 shard_map.121
  24.7 2.1 %collective-permute-start.7 = (bf16[128,256]{1,0:T(8,128)(2,1)S(1)}, bf16[128,256]{1,0:T(8,128)(2,1)S(1)}, u32[]{:S(2)}, u32[]{:S(2)}) collective-permute-start(bf16[128,256]{1,0:T(8,128)(2,1)S(1)} %get-tuple-element.105), channel_id=1, source_target_pairs={{0,4},{4,0},{8,12},{12,8},{16,20},{20,16},{24,28},{28,24},{1,5},{5... | collective-permute-start | bytes 196616 | tf_op jit(solution)/shard_map/ppermute | solution.py:617
  26.8 1.1 %shard_map.122 = (bf16[512,640]{1,0:T(8,128)(2,1)S(1)}, f32[1,512]{1,0:T(1,128)S(1)}, f32[640,512]{1,0:T(8,128)S(1)}, bf16[512,128]{1,0:T(8,128)(2,1)S(1)}) custom-call(f32[1,1280]{1,0:T(1,128)S(1)} %reshape.15.gain_ref, bf16[1280,2560]{1,0:T(8,128)(2,1)S(1)} %bitcast.5, bf16[512,128]{1,0:T(8,128)(2,1)S(1)} %copy-done.2, ...), custom_call_target="tpu_custom_call" | custom-call | flops 1000 | bytes 1000 | tf_op jit(solution)/shard_map/pallas_call | solution.py:66
  27.9 0.8 %shard_map.123 = (bf16[512,384]{1,0:T(8,128)(2,1)S(1)}, f32[1,512]{1,0:T(1,128)S(1)}, f32[640,512]{1,0:T(8,128)S(1)}) custom-call(f32[1,1280]{1,0:T(1,128)S(1)} %reshape.15.gain_ref, bf16[1280,2560]{1,0:T(8,128)(2,1)S(1)} %bitcast.5, bf16[512,128]{1,0:T(8,128)(2,1)S(1)} %get-tuple-element.99.rd_ref, f32[512,384]{1,0:T(8,128)S(1)} %get-tuple-element.86.refs_3_.refs_0_, ...), custom_call_target="tpu_custom_call" | custom-call | flops 1000 | bytes 1000 | tf_op jit(solution)/shard_map/pallas_call | solution.py:66
  28.8 0.2 collective-permute-done.7.e_ref
  29.0 0.5 %shard_map.124 = (bf16[512,256]{1,0:T(8,128)(2,1)S(1)}, bf16[392,512]{1,0:T(8,128)(2,1)S(1)}) custom-call(bf16[512,128]{1,0:T(8,128)(2,1)S(1)} %get-tuple-element.99.rd_ref, f32[512,256]{1,0:T(8,128)S(1)} %get-tuple-element.88.refs_4_.a_ref, f32[512,256]{1,0:T(8,128)S(1)} %get-tuple-element.104.b_ref, bf16[128,256]{1,0:T(8,128)(2,1)S(1)} %collective-permute-done.7.e_ref, ...), custom_call_target="tpu_custom_call" | custom-call | flops 1000 | bytes 1000 | tf_op jit(solution)/shard_map/pallas_call | solution.py:66
  29.5 0.1 collective-permute-start.9
  29.6 1.3 %shard_map.125 = (bf16[256,512]{1,0:T(8,128)(2,1)S(1)}, f32[384,512]{1,0:T(8,128)S(1)}, f32[256,512]{1,0:T(8,128)S(1)}) custom-call(f32[640,512]{1,0:T(8,128)S(1)} %get-tuple-element.106.p_ref.refs_0_, bf16[1280,2560]{1,0:T(8,128)(2,1)S(1)} %bitcast.5, bf16[512,640]{1,0:T(8,128)(2,1)S(1)} %get-tuple-element.98.refs_2_.refs_1_.refs_0_, ...), custom_call_target="tpu_custom_call" | custom-call | flops 1000 | bytes 1000 | tf_op jit(solution)/shard_map/pallas_call | solution.py:66
  30.9 0.6 %collective-permute-start.8 = (bf16[256,512]{1,0:T(8,128)(2,1)S(1)}, bf16[256,512]{1,0:T(8,128)(2,1)S(1)}, u32[]{:S(2)}, u32[]{:S(2)}) collective-permute-start(bf16[256,512]{1,0:T(8,128)(2,1)S(1)} %get-tuple-element.111), channel_id=1, source_target_pairs={{0,1},{1,0},{2,3},{3,2},{4,5},{5,4},{6,7},{7,6},{8,9},{9,8},{10,11... | collective-permute-start | bytes 786440 | tf_op jit(solution)/shard_map/ppermute | solution.py:620
  31.5 0.1 shard_map.126.refs_2_.factor_ref
  31.6 1.6 %collective-permute-start.15 = (bf16[392,512]{1,0:T(8,128)(2,1)S(1)}, bf16[392,512]{1,0:T(8,128)(2,1)S(1)}, u32[]{:S(2)}, u32[]{:S(2)}) collective-permute-start(bf16[392,512]{1,0:T(8,128)(2,1)S(1)} %shard_map.126.refs_2_.factor_ref), channel_id=1, source_target_pairs={{0,2},{1,3},{2,0},{3,1},{4,6},{5,7},{6,4},{7,5},{8,10},{9,11},{10,... | collective-permute-start | bytes 1204232 | tf_op jit(solution)/shard_map/ppermute | solution.py:620
  33.1 0.1 shard_map.127.refs_4_
  33.2 1.2 %shard_map.128 = (bf16[160,512]{1,0:T(8,128)(2,1)S(1)}, bf16[160,512]{1,0:T(8,128)(2,1)S(1)}, bf16[160,512]{1,0:T(8,128)(2,1)S(1)}, bf16[160,512]{1,0:T(8,128)(2,1)S(1)}) custom-call(bf16[1280,2560]{1,0:T(8,128)(2,1)S(1)} %bitcast.5, bf16[512,640]{1,0:T(8,128)(2,1)S(1)} %get-tuple-element.98.refs_2_.refs_1_.refs_0_, ...), custom_call_target="tpu_custom_call" | custom-call | flops 1000 | bytes 1000 | tf_op jit(solution)/shard_map/pallas_call | solution.py:66
  34.4 0.1 collective-permute-start.10
  34.5 1.3 %collective-permute-start.14 = (bf16[256,512]{1,0:T(8,128)(2,1)S(1)}, bf16[256,512]{1,0:T(8,128)(2,1)S(1)}, u32[]{:S(2)}, u32[]{:S(2)}) collective-permute-start(bf16[256,512]{1,0:T(8,128)(2,1)S(1)} %shard_map.127.refs_4_), channel_id=1, source_target_pairs={{0,2},{1,3},{2,0},{3,1},{4,6},{5,7},{6,4},{7,5},{8,10},{9,11},{10,... | collective-permute-start | bytes 786440 | tf_op jit(solution)/shard_map/ppermute | solution.py:620
  35.9 0.5 %collective-permute-start.12 = (bf16[160,512]{1,0:T(8,128)(2,1)S(1)}, bf16[160,512]{1,0:T(8,128)(2,1)S(1)}, u32[]{:S(2)}, u32[]{:S(2)}) collective-permute-start(bf16[160,512]{1,0:T(8,128)(2,1)S(1)} %get-tuple-element.115), channel_id=1, source_target_pairs={{0,1},{1,0},{2,3},{3,2},{4,5},{5,4},{6,7},{7,6},{8,9},{9,8},{10,11... | collective-permute-start | bytes 491528 | tf_op jit(solution)/shard_map/ppermute | solution.py:620
  36.4 0.9 %collective-permute-done.11.refs_4_ = bf16[160,512]{1,0:T(8,128)(2,1)S(1)} collective-permute-done((bf16[160,512]{1,0:T(8,128)(2,1)S(1)}, bf16[160,512]{1,0:T(8,128)(2,1)S(1)}, u32[]{:S(2)}, u32[]{:S(2)}) %collective-permute-start.11) | collective-permute-done | bytes 163872 | tf_op jit(solution)/shard_map/ppermute | solution.py:620
  37.2 0.2 collective-permute-done.12.refs_5_
  37.5 0.3 collective-permute-done.13.refs_6_
  37.8 1.2 %shard_map.129.own_ref = f32[640,512]{1,0:T(8,128)S(1)} custom-call(bf16[1280,2560]{1,0:T(8,128)(2,1)S(1)} %bitcast.5, bf16[512,640]{1,0:T(8,128)(2,1)S(1)} %get-tuple-element.98.refs_2_.refs_1_.refs_0_, bf16[512,384]{1,0:T(8,128)(2,1)S(1)} %get-tuple-element.103.refs_3_.refs_2_.refs_1_, bf16[512,256]{1,0:T(8,128)(2,1)S(1)} %get-tuple-element.108.refs_4_.refs_3_.refs_2_, ...), custom_call_target="tpu_custom_call" | custom-call | flops 1000 | bytes 1000 | tf_op jit(solution)/shard_map/pallas_call | solution.py:66
  39.0 4.8 %collective-permute-done.15.far_ref = bf16[392,512]{1,0:T(8,128)(2,1)S(1)} collective-permute-done((bf16[392,512]{1,0:T(8,128)(2,1)S(1)}, bf16[392,512]{1,0:T(8,128)(2,1)S(1)}, u32[]{:S(2)}, u32[]{:S(2)}) %collective-permute-start.15) | collective-permute-done | bytes 401440 | tf_op jit(solution)/shard_map/ppermute | solution.py:620
  43.8 0.8 %shard_map.130 = (bf16[640,512]{1,0:T(8,128)(2,1)}, f32[1,512]{1,0:T(1,128)S(1)}) custom-call(f32[640,512]{1,0:T(8,128)S(1)} %shard_map.129.own_ref, bf16[392,512]{1,0:T(8,128)(2,1)S(1)} %collective-permute-done.15.far_ref, bf16[392,512]{1,0:T(8,128)(2,1)S(1)} %shard_map.126.refs_2_.factor_ref), custom_call_target="tpu_custom_call" | custom-call | flops 1000 | bytes 1000 | tf_op jit(solution)/shard_map/pallas_call | solution.py:597
  44.6 3.9 %collective-permute-done.14.far_ref = bf16[256,512]{1,0:T(8,128)(2,1)S(1)} collective-permute-done((bf16[256,512]{1,0:T(8,128)(2,1)S(1)}, bf16[256,512]{1,0:T(8,128)(2,1)S(1)}, u32[]{:S(2)}, u32[]{:S(2)}) %collective-permute-start.14) | collective-permute-done | bytes 262176 | tf_op jit(solution)/shard_map/ppermute | solution.py:620
  48.5 0.8 %shard_map.131 = bf16[640,512]{1,0:T(8,128)(2,1)} custom-call(f32[640,512]{1,0:T(8,128)S(1)} %shard_map.129.own_ref, bf16[256,512]{1,0:T(8,128)(2,1)S(1)} %collective-permute-done.14.far_ref, f32[1,512]{1,0:T(1,128)S(1)} %get-tuple-element.117.factor_ref, bf16[640,512]{1,0:T(8,128)(2,1)} %get-tuple-element.118.refs_0_), custom_call_target="tpu_custom_call", output_to_operand_aliasing={{}: (3, {})} | custom-call | flops 1000 | bytes 1000 | tf_op jit(solution)/shard_map/pallas_call | solution.py:597
  (27 shorter events, 0.1 us)
Async XLA Ops:
  0.0 5.6 %copy-start = (bf16[512,1280]{1,0:T(8,128)(2,1)S(1)}, bf16[512,1280]{1,0:T(8,128)(2,1)}, u32[]{:S(2)}) copy-start(bf16[512,1280]{1,0:T(8,128)(2,1)} %refs_0_.12) | copy-start | bytes 3932164
  0.0 5.6 %copy-start.3 = (bf16[512,128]{1,0:T(8,128)(2,1)S(1)}, bf16[512,128]{1,0:T(8,128)(2,1)}, u32[]{:S(2)}) copy-start(bf16[512,128]{1,0:T(8,128)(2,1)} %refs_2_.7) | copy-start | bytes 393220
  0.0 7.3 %copy-start.2 = (bf16[512,128]{1,0:T(8,128)(2,1)S(1)}, bf16[512,128]{1,0:T(8,128)(2,1)}, u32[]{:S(2)}) copy-start(bf16[512,128]{1,0:T(8,128)(2,1)} %rd_ref.1) | copy-start | bytes 393220
  2.5 4.8 %copy-start.5 = (f32[20]{0:T(128)S(1)}, f32[20]{0:T(128)}, u32[]{:S(2)}) copy-start(f32[20]{0:T(128)} %param.19) | copy-start | bytes 244
  2.5 6.3 %collective-permute-start = (bf16[136,384]{1,0:T(8,128)(2,1)}, bf16[136,384]{1,0:T(8,128)(2,1)S(1)}, u32[]{:S(2)}, u32[]{:S(2)}) collective-permute-start(bf16[136,384]{1,0:T(8,128)(2,1)} %get-tuple-element.64), channel_id=1, source_target_pairs={{0,4},{4,0},{8,12},{12,8},{16,20},{20,16},{24,28},{28,24},{1,5},{5... | collective-permute-start | bytes 313352 | tf_op jit(solution)/shard_map/ppermute | solution.py:617
  5.6 0.9 %copy-start.1 = (f32[104,512]{1,0:T(8,128)S(1)}, f32[104,512]{1,0:T(8,128)}, u32[]{:S(2)}) copy-start(f32[104,512]{1,0:T(8,128)} %get-tuple-element.62.stash_ref.refs_2_) | copy-start | bytes 638980
  7.2 4.4 %collective-permute-start.2 = (bf16[136,256]{1,0:T(8,128)(2,1)S(1)}, bf16[136,256]{1,0:T(8,128)(2,1)S(1)}, u32[]{:S(2)}, u32[]{:S(2)}) collective-permute-start(bf16[136,256]{1,0:T(8,128)(2,1)S(1)} %get-tuple-element.65.refs_4_), channel_id=1, source_target_pairs={{0,4},{4,0},{8,12},{12,8},{16,20},{20,16},{24,28},{28,24},{1,5},{5... | collective-permute-start | bytes 208904 | tf_op jit(solution)/shard_map/ppermute | solution.py:617
  8.8 1.8 %copy-start.4 = (bf16[512,1280]{1,0:T(8,128)(2,1)S(1)}, bf16[512,1280]{1,0:T(8,128)(2,1)}, u32[]{:S(2)}) copy-start(bf16[512,1280]{1,0:T(8,128)(2,1)} %refs_1_.10) | copy-start | bytes 3932164
  8.9 5.7 %collective-permute-start.1 = (bf16[136,384]{1,0:T(8,128)(2,1)S(1)}, bf16[136,384]{1,0:T(8,128)(2,1)S(1)}, u32[]{:S(2)}, u32[]{:S(2)}) collective-permute-start(bf16[136,384]{1,0:T(8,128)(2,1)S(1)} %get-tuple-element.67.refs_9_), channel_id=1, source_target_pairs={{0,8},{4,12},{8,0},{12,4},{16,24},{20,28},{24,16},{28,20},{1,9},{5... | collective-permute-start | bytes 313352 | tf_op jit(solution)/shard_map/ppermute | solution.py:617
  11.7 7.0 %collective-permute-start.4 = (bf16[136,256]{1,0:T(8,128)(2,1)S(1)}, bf16[136,256]{1,0:T(8,128)(2,1)S(1)}, u32[]{:S(2)}, u32[]{:S(2)}) collective-permute-start(bf16[136,256]{1,0:T(8,128)(2,1)S(1)} %get-tuple-element.78.refs_9_), channel_id=1, source_target_pairs={{0,8},{4,12},{8,0},{12,4},{16,24},{20,28},{24,16},{28,20},{1,9},{5... | collective-permute-start | bytes 208904 | tf_op jit(solution)/shard_map/ppermute | solution.py:617
  14.7 7.7 %collective-permute-start.3 = (bf16[136,384]{1,0:T(8,128)(2,1)S(1)}, bf16[136,384]{1,0:T(8,128)(2,1)S(1)}, u32[]{:S(2)}, u32[]{:S(2)}) collective-permute-start(bf16[136,384]{1,0:T(8,128)(2,1)S(1)} %get-tuple-element.80.refs_9_), channel_id=1, source_target_pairs={{0,16},{4,20},{8,24},{12,28},{16,0},{20,4},{24,8},{28,12},{1,17},{... | collective-permute-start | bytes 313352 | tf_op jit(solution)/shard_map/ppermute | solution.py:617
  18.7 8.0 %slice-start = ((s8[6553600]{0:T(1024)(128)(4,1)}), s8[4194304]{0:T(1024)(128)(4,1)S(1)}, s32[]{:S(2)}) async-start(s8[6553600]{0:T(1024)(128)(4,1)} %bitcast.4), calls=%async_computation | async-start | bytes 8388608
  18.7 8.0 %slice-start.1 = ((s8[6553600]{0:T(1024)(128)(4,1)}), s8[2359296]{0:T(1024)(128)(4,1)S(1)}, s32[]{:S(2)}) async-start(s8[6553600]{0:T(1024)(128)(4,1)} %bitcast.4), calls=%async_computation.1 | async-start | bytes 4718592
  18.8 5.9 %collective-permute-start.5 = (bf16[136,256]{1,0:T(8,128)(2,1)S(1)}, bf16[136,256]{1,0:T(8,128)(2,1)S(1)}, u32[]{:S(2)}, u32[]{:S(2)}) collective-permute-start(bf16[136,256]{1,0:T(8,128)(2,1)S(1)} %get-tuple-element.87.refs_9_), channel_id=1, source_target_pairs={{0,16},{4,20},{8,24},{12,28},{16,0},{20,4},{24,8},{28,12},{1,17},{... | collective-permute-start | bytes 208904 | tf_op jit(solution)/shard_map/ppermute | solution.py:617
  20.1 6.7 %copy-start.6 = (f32[1280]{0:T(1024)S(1)}, f32[1280]{0:T(1024)}, u32[]{:S(2)}) copy-start(f32[1280]{0:T(1024)} %param.20) | copy-start | bytes 15364
  22.5 5.5 %collective-permute-start.6 = (bf16[128,384]{1,0:T(8,128)(2,1)S(1)}, bf16[128,384]{1,0:T(8,128)(2,1)S(1)}, u32[]{:S(2)}, u32[]{:S(2)}) collective-permute-start(bf16[128,384]{1,0:T(8,128)(2,1)S(1)} %get-tuple-element.96.refs_4_), channel_id=1, source_target_pairs={{0,4},{4,0},{8,12},{12,8},{16,20},{20,16},{24,28},{28,24},{1,5},{5... | collective-permute-start | bytes 294920 | tf_op jit(solution)/shard_map/ppermute | solution.py:617
  24.7 4.3 %collective-permute-start.7 = (bf16[128,256]{1,0:T(8,128)(2,1)S(1)}, bf16[128,256]{1,0:T(8,128)(2,1)S(1)}, u32[]{:S(2)}, u32[]{:S(2)}) collective-permute-start(bf16[128,256]{1,0:T(8,128)(2,1)S(1)} %get-tuple-element.105), channel_id=1, source_target_pairs={{0,4},{4,0},{8,12},{12,8},{16,20},{20,16},{24,28},{28,24},{1,5},{5... | collective-permute-start | bytes 196616 | tf_op jit(solution)/shard_map/ppermute | solution.py:617
  29.5 1.9 %collective-permute-start.9 = (bf16[392,512]{1,0:T(8,128)(2,1)S(1)}, bf16[392,512]{1,0:T(8,128)(2,1)S(1)}, u32[]{:S(2)}, u32[]{:S(2)}) collective-permute-start(bf16[392,512]{1,0:T(8,128)(2,1)S(1)} %get-tuple-element.109.refs_5_.mine_ref), channel_id=1, source_target_pairs={{0,1},{1,0},{2,3},{3,2},{4,5},{5,4},{6,7},{7,6},{8,9},{9,8},{10,11... | collective-permute-start | bytes 1204232 | tf_op jit(solution)/shard_map/ppermute | solution.py:620
  30.9 2.3 %collective-permute-start.8 = (bf16[256,512]{1,0:T(8,128)(2,1)S(1)}, bf16[256,512]{1,0:T(8,128)(2,1)S(1)}, u32[]{:S(2)}, u32[]{:S(2)}) collective-permute-start(bf16[256,512]{1,0:T(8,128)(2,1)S(1)} %get-tuple-element.111), channel_id=1, source_target_pairs={{0,1},{1,0},{2,3},{3,2},{4,5},{5,4},{6,7},{7,6},{8,9},{9,8},{10,11... | collective-permute-start | bytes 786440 | tf_op jit(solution)/shard_map/ppermute | solution.py:620
  31.6 12.2 %collective-permute-start.15 = (bf16[392,512]{1,0:T(8,128)(2,1)S(1)}, bf16[392,512]{1,0:T(8,128)(2,1)S(1)}, u32[]{:S(2)}, u32[]{:S(2)}) collective-permute-start(bf16[392,512]{1,0:T(8,128)(2,1)S(1)} %shard_map.126.refs_2_.factor_ref), channel_id=1, source_target_pairs={{0,2},{1,3},{2,0},{3,1},{4,6},{5,7},{6,4},{7,5},{8,10},{9,11},{10,... | collective-permute-start | bytes 1204232 | tf_op jit(solution)/shard_map/ppermute | solution.py:620
  34.4 1.9 %collective-permute-start.10 = (bf16[160,512]{1,0:T(8,128)(2,1)S(1)}, bf16[160,512]{1,0:T(8,128)(2,1)S(1)}, u32[]{:S(2)}, u32[]{:S(2)}) collective-permute-start(bf16[160,512]{1,0:T(8,128)(2,1)S(1)} %get-tuple-element.113), channel_id=1, source_target_pairs={{0,1},{1,0},{2,3},{3,2},{4,5},{5,4},{6,7},{7,6},{8,9},{9,8},{10,11... | collective-permute-start | bytes 491528 | tf_op jit(solution)/shard_map/ppermute | solution.py:620
  34.5 13.9 %collective-permute-start.14 = (bf16[256,512]{1,0:T(8,128)(2,1)S(1)}, bf16[256,512]{1,0:T(8,128)(2,1)S(1)}, u32[]{:S(2)}, u32[]{:S(2)}) collective-permute-start(bf16[256,512]{1,0:T(8,128)(2,1)S(1)} %shard_map.127.refs_4_), channel_id=1, source_target_pairs={{0,2},{1,3},{2,0},{3,1},{4,6},{5,7},{6,4},{7,5},{8,10},{9,11},{10,... | collective-permute-start | bytes 786440 | tf_op jit(solution)/shard_map/ppermute | solution.py:620
  35.9 1.4 %collective-permute-start.11 = (bf16[160,512]{1,0:T(8,128)(2,1)S(1)}, bf16[160,512]{1,0:T(8,128)(2,1)S(1)}, u32[]{:S(2)}, u32[]{:S(2)}) collective-permute-start(bf16[160,512]{1,0:T(8,128)(2,1)S(1)} %get-tuple-element.114), channel_id=1, source_target_pairs={{0,1},{1,0},{2,3},{3,2},{4,5},{5,4},{6,7},{7,6},{8,9},{9,8},{10,11... | collective-permute-start | bytes 491528 | tf_op jit(solution)/shard_map/ppermute | solution.py:620
  35.9 1.6 %collective-permute-start.12 = (bf16[160,512]{1,0:T(8,128)(2,1)S(1)}, bf16[160,512]{1,0:T(8,128)(2,1)S(1)}, u32[]{:S(2)}, u32[]{:S(2)}) collective-permute-start(bf16[160,512]{1,0:T(8,128)(2,1)S(1)} %get-tuple-element.115), channel_id=1, source_target_pairs={{0,1},{1,0},{2,3},{3,2},{4,5},{5,4},{6,7},{7,6},{8,9},{9,8},{10,11... | collective-permute-start | bytes 491528 | tf_op jit(solution)/shard_map/ppermute | solution.py:620
  36.4 1.4 %collective-permute-start.13 = (bf16[160,512]{1,0:T(8,128)(2,1)S(1)}, bf16[160,512]{1,0:T(8,128)(2,1)S(1)}, u32[]{:S(2)}, u32[]{:S(2)}) collective-permute-start(bf16[160,512]{1,0:T(8,128)(2,1)S(1)} %get-tuple-element.116), channel_id=1, source_target_pairs={{0,1},{1,0},{2,3},{3,2},{4,5},{5,4},{6,7},{7,6},{8,9},{9,8},{10,11... | collective-permute-start | bytes 491528 | tf_op jit(solution)/shard_map/ppermute | solution.py:620

commit v11 on v10

--- a/solution.py
+++ b/solution.py
@@ -518,18 +518,16 @@
     toks = gs[0].shape[0]
 
     def body(p_ref, w_ref, *refs):
-        g_refs, (near_ref, top_ref, rest_ref) = refs[: len(gs)], refs[len(gs) :]
+        g_refs, (near_ref, top_ref) = refs[: len(gs)], refs[len(gs) :]
         which, lanes = groups[-1]
         near = p_ref[rest] + projected(which, lanes, 0, rest, w_ref, g_refs[-1][...])
         near_ref[...] = near.astype(BF16)
-        for rows, y_ref in ((top, top_ref), (rest, rest_ref)):
-            y_ref[...] = sum(
-                projected(which, lanes, 1, rows, w_ref, g_ref[...])
-                for (which, lanes), g_ref in zip(groups, g_refs)
-            )
+        top_ref[...] = sum(
+            projected(which, lanes, 1, top, w_ref, g_ref[...]) for (which, lanes), g_ref in zip(groups, g_refs)
+        )
 
     size = rest.stop - rest.start
-    out = shaped(((size, toks), BF16), ((top.stop, toks), F32), ((size, toks), F32))
+    out = shaped(((size, toks), BF16), ((top.stop, toks), F32))
     return call(body, (partial, weight, *gs), out, after=after)
 
 
@@ -562,11 +560,15 @@
     return call(body, (y_far, to_near, got_near), jax.ShapeDtypeStruct(got_near.shape, BF16))
 
 
-def add_second(y_far, got_near, after):
-    def body(y_ref, got_ref, out_ref):
-        out_ref[...] = (y_ref[...] + got_ref[...].astype(F32)).astype(BF16)
-
-    return call(body, (y_far, got_near), jax.ShapeDtypeStruct(got_near.shape, BF16), after=after)
+def add_second(groups, gs, rows, weight, got_near, after):
+    def body(w_ref, got_ref, *refs):
+        y = sum(
+            projected(which, lanes, 1, rows, w_ref, g_ref[...]) for (which, lanes), g_ref in zip(groups, refs)
+        )
+        refs[-1][...] = (y + got_ref[...].astype(F32)).astype(BF16)
+
+    out = jax.ShapeDtypeStruct(got_near.shape, BF16)
+    return call(body, (weight, got_near, *gs), out, after=after)
 
 
 def finish(rows, y_own, inputs, out=None, features=None):
@@ -674,11 +676,11 @@
     g_two, near_top = gated_last(two, top, linked, *other_b, other_two, gain, out_weight, partial, squares)
     got_top = across(near_top, 1)
     groups, gs = ((0, whole_half), (1, one), (1, two)), (g_keep, g_one, g_two)
-    near_rest, far_top, far_rest = project_next(groups, gs, top, rest, partial, out_weight, near_top)
+    near_rest, far_top = project_next(groups, gs, top, rest, partial, out_weight, near_top)
     got_rest = across(near_rest, 1)
     to_far_top = add_first(far_top, near_top, got_top)
     got_far_top = across(to_far_top, 2)
-    to_far_rest = add_second(far_rest, got_rest, to_far_top)
+    to_far_rest = add_second(groups, gs, rest, out_weight, got_rest, to_far_top)
     got_far_rest = across(to_far_rest, 2)
     y_near = project_whole(2, groups, gs, out_weight, NEAR_PIECES, after=to_far_rest)
     got_own = tuple(across(piece, 1) for piece in y_near)

time: 49.4 us -> 49.3 us (level)
  transfers between devices with their start and end apart: 16 -> 16, of which waited for: 8 -> 9; matrix products, arithmetic and copies ran while one was open for 0% -> 0% of each run, Pallas kernels for 26% -> 26%
where the time goes in v11:
time: 49.3 us; the launch traced here: 49.2 us
  starting transfers between devices  17.7 us (36%)
  Pallas kernels  16.6 us (34%)
  waiting for transfers between devices  13.6 us (28%)
  local copies, waits for them, and re-layouts  0.98 us (2%)
    ppermute x8, starting transfers between devices, swap(): return lax.ppermute(a, 'seq', [(i, i ^ bit) for i in range(n_seq)])  13.8 us
    pallas_call x20, Pallas kernels, call(): pl.pallas_call(kernel, in_specs=specs, out_specs=jax.tree.map(lambda _: v...  12.6 us
    ppermute x8, waiting for transfers between devices, across(): return lax.ppermute(a, 'tp', [(i, i ^ bit) for i in range(n_tp)])  10.1 us
    ppermute x8, starting transfers between devices, across(): return lax.ppermute(a, 'tp', [(i, i ^ bit) for i in range(n_tp)])  3.9 us
    ppermute x8, waiting for transfers between devices, swap(): return lax.ppermute(a, 'seq', [(i, i ^ bit) for i in range(n_seq)])  3.52 us
    pallas_call x1, Pallas kernels, prepare(): pl.pallas_call(body, in_specs=[pl.BlockSpec(memory_space=pltpu.HBM)] * le...  2.5 us
    pallas_call x2, Pallas kernels, finish(): pl.pallas_call(body, in_specs=[vm] * 3 + ([] if first else [where]), out_...  1.57 us
  transfers between devices with their start and end apart: 16, of which 9 were waited for; matrix products, arithmetic and copies ran while one was open for 0% of the time, Pallas kernels for 26%

profile of v11, /device:TPU:0, one launch (start us, length us, event | category | flops | bytes accessed | tf_op | source)
XLA Modules:
  0.0 49.2 jit_solution(15526768641166058778)
XLA Ops:
  0.0 2.5 %shard_map.109 = (bf16[136,384]{1,0:T(8,128)(2,1)}, f32[104,512]{1,0:T(8,128)}) custom-call(bf16[20,512]{1,0:T(8,128)(2,1)} %refs_0_.8, s32[1,512]{1,0:T(1,128)} %bitcast.7, f32[1,20]{1,0:T(1,128)} %bitcast.8, f32[1,20]{1,0:T(1,128)} %bitcast.9, bf16[512,128]{1,0:T(8,128)(2,1)} %refs_2_.7, bf16[512,1280]{1,0:T(8,128)(2,1)} %refs_0_.13), custom_call_target="tpu_custom_call" | custom-call | flops 4000000000 | bytes 1000 | tf_op jit(solution)/shard_map/pallas_call | solution.py:202
  2.5 0.0 copy-start.5
  2.5 3.0 %collective-permute-start = (bf16[136,384]{1,0:T(8,128)(2,1)}, bf16[136,384]{1,0:T(8,128)(2,1)S(1)}, u32[]{:S(2)}, u32[]{:S(2)}) collective-permute-start(bf16[136,384]{1,0:T(8,128)(2,1)} %get-tuple-element.63), channel_id=1, source_target_pairs={{0,4},{4,0},{8,12},{12,8},{16,20},{20,16},{24,28},{28,24},{1,5},{5... | collective-permute-start | bytes 313352 | tf_op jit(solution)/shard_map/ppermute | solution.py:619
  5.6 0.9 %copy-done.1 = f32[104,512]{1,0:T(8,128)S(1)} copy-done((f32[104,512]{1,0:T(8,128)S(1)}, f32[104,512]{1,0:T(8,128)}, u32[]{:S(2)}) %copy-start.1) | copy-done | bytes 213016
  6.5 0.7 %shard_map.110 = (bf16[136,256]{1,0:T(8,128)(2,1)S(1)}, bf16[136,384]{1,0:T(8,128)(2,1)S(1)}, bf16[136,256]{1,0:T(8,128)(2,1)S(1)}) custom-call(f32[104,512]{1,0:T(8,128)S(1)} %copy-done.1, bf16[512,1280]{1,0:T(8,128)(2,1)S(1)} %copy-done, bf16[512,128]{1,0:T(8,128)(2,1)S(1)} %copy-done.3), custom_call_target="tpu_custom_call" | custom-call | flops 1000 | bytes 1000 | tf_op jit(solution)/shard_map/pallas_call | solution.py:66
  7.2 0.1 collective-permute-start.2
  7.3 0.6 %shard_map.111 = (f32[2,256,256]{2,1,0:T(8,128)S(1)}, bf16[256,128]{1,0:T(8,128)(2,1)S(1)}, f32[2,512,128]{2,1,0:T(8,128)S(1)}, f32[32,512]{1,0:T(8,128)S(1)}, f...) custom-call(bf16[512,128]{1,0:T(8,128)(2,1)S(1)} %copy-done.2, ...), custom_call_target="tpu_custom_call" | custom-call | flops 4000000000 | bytes 1000 | tf_op jit(solution)/shard_map/pallas_call | solution.py:66
  7.9 1.0 %collective-permute-done.refs_1_ = bf16[136,384]{1,0:T(8,128)(2,1)S(1)} collective-permute-done((bf16[136,384]{1,0:T(8,128)(2,1)}, bf16[136,384]{1,0:T(8,128)(2,1)S(1)}, u32[]{:S(2)}, u32[]{:S(2)}) %collective-permute-start) | collective-permute-done | bytes 104480 | tf_op jit(solution)/shard_map/ppermute | solution.py:619
  8.8 0.1 shard_map.112
  8.9 1.8 %collective-permute-start.1 = (bf16[136,384]{1,0:T(8,128)(2,1)S(1)}, bf16[136,384]{1,0:T(8,128)(2,1)S(1)}, u32[]{:S(2)}, u32[]{:S(2)}) collective-permute-start(bf16[136,384]{1,0:T(8,128)(2,1)S(1)} %get-tuple-element.66.refs_9_), channel_id=1, source_target_pairs={{0,8},{4,12},{8,0},{12,4},{16,24},{20,28},{24,16},{28,20},{1,9},{5... | collective-permute-start | bytes 313352 | tf_op jit(solution)/shard_map/ppermute | solution.py:619
  10.7 0.9 %shard_map.113 = (f32[512,256]{1,0:T(8,128)S(1)}, f32[512,256]{1,0:T(8,128)S(1)}) custom-call(bf16[512,1280]{1,0:T(8,128)(2,1)S(1)} %copy-done, bf16[512,1280]{1,0:T(8,128)(2,1)S(1)} %copy-done.4, bf16[512,128]{1,0:T(8,128)(2,1)S(1)} %copy-done.3, f32[2,256,256]{2,1,0:T(8,128)S(1)} %get-tuple-element.69.refs_3_, ...), custom_call_target="tpu_custom_call" | custom-call | flops 4000000000 | bytes 1000 | tf_op jit(solution)/shard_map/pallas_call | solution.py:66
  11.6 0.1 shard_map.114
  11.7 1.6 %collective-permute-start.4 = (bf16[136,256]{1,0:T(8,128)(2,1)S(1)}, bf16[136,256]{1,0:T(8,128)(2,1)S(1)}, u32[]{:S(2)}, u32[]{:S(2)}) collective-permute-start(bf16[136,256]{1,0:T(8,128)(2,1)S(1)} %get-tuple-element.77.refs_9_), channel_id=1, source_target_pairs={{0,8},{4,12},{8,0},{12,4},{16,24},{20,28},{24,16},{28,20},{1,9},{5... | collective-permute-start | bytes 208904 | tf_op jit(solution)/shard_map/ppermute | solution.py:619
  13.3 1.3 %shard_map.115 = (f32[512,384]{1,0:T(8,128)S(1)}, f32[512,384]{1,0:T(8,128)S(1)}) custom-call(bf16[512,1280]{1,0:T(8,128)(2,1)S(1)} %copy-done, bf16[512,1280]{1,0:T(8,128)(2,1)S(1)} %copy-done.4, bf16[512,128]{1,0:T(8,128)(2,1)S(1)} %copy-done.3, f32[2,256,256]{2,1,0:T(8,128)S(1)} %get-tuple-element.69.refs_3_, ...), custom_call_target="tpu_custom_call" | custom-call | flops 4000000000 | bytes 1000 | tf_op jit(solution)/shard_map/pallas_call | solution.py:66
  14.6 0.1 shard_map.116
  14.7 2.7 %collective-permute-start.3 = (bf16[136,384]{1,0:T(8,128)(2,1)S(1)}, bf16[136,384]{1,0:T(8,128)(2,1)S(1)}, u32[]{:S(2)}, u32[]{:S(2)}) collective-permute-start(bf16[136,384]{1,0:T(8,128)(2,1)S(1)} %get-tuple-element.79.refs_9_), channel_id=1, source_target_pairs={{0,16},{4,20},{8,24},{12,28},{16,0},{20,4},{24,8},{28,12},{1,17},{... | collective-permute-start | bytes 313352 | tf_op jit(solution)/shard_map/ppermute | solution.py:619
  17.3 1.3 %shard_map.117 = (f32[512,384]{1,0:T(8,128)S(1)}, f32[512,384]{1,0:T(8,128)S(1)}) custom-call(bf16[512,1280]{1,0:T(8,128)(2,1)S(1)} %copy-done, bf16[512,1280]{1,0:T(8,128)(2,1)S(1)} %copy-done.4, bf16[512,128]{1,0:T(8,128)(2,1)S(1)} %copy-done.3, f32[2,256,256]{2,1,0:T(8,128)S(1)} %get-tuple-element.69.refs_3_, ...), custom_call_target="tpu_custom_call" | custom-call | flops 4000000000 | bytes 1000 | tf_op jit(solution)/shard_map/pallas_call | solution.py:66
  18.7 0.1 shard_map.118
  18.7 0.0 slice-start
  18.7 0.4 collective-permute-start.5
  19.1 0.9 %shard_map.119 = (f32[512,256]{1,0:T(8,128)S(1)}, f32[512,256]{1,0:T(8,128)S(1)}) custom-call(bf16[512,1280]{1,0:T(8,128)(2,1)S(1)} %copy-done, bf16[512,1280]{1,0:T(8,128)(2,1)S(1)} %copy-done.4, bf16[512,128]{1,0:T(8,128)(2,1)S(1)} %copy-done.3, f32[2,256,256]{2,1,0:T(8,128)S(1)} %get-tuple-element.69.refs_3_, ...), custom_call_target="tpu_custom_call" | custom-call | flops 4000000000 | bytes 1000 | tf_op jit(solution)/shard_map/pallas_call | solution.py:66
  20.1 2.3 %collective-permute-done.3.refs_0_ = bf16[136,384]{1,0:T(8,128)(2,1)S(1)} collective-permute-done((bf16[136,384]{1,0:T(8,128)(2,1)S(1)}, bf16[136,384]{1,0:T(8,128)(2,1)S(1)}, u32[]{:S(2)}, u32[]{:S(2)}) %collective-permute-start.3) | collective-permute-done | bytes 104480 | tf_op jit(solution)/shard_map/ppermute | solution.py:619
  22.4 0.1 shard_map.120
  22.5 2.1 %collective-permute-start.6 = (bf16[128,384]{1,0:T(8,128)(2,1)S(1)}, bf16[128,384]{1,0:T(8,128)(2,1)S(1)}, u32[]{:S(2)}, u32[]{:S(2)}) collective-permute-start(bf16[128,384]{1,0:T(8,128)(2,1)S(1)} %get-tuple-element.95.refs_4_), channel_id=1, source_target_pairs={{0,4},{4,0},{8,12},{12,8},{16,20},{20,16},{24,28},{28,24},{1,5},{5... | collective-permute-start | bytes 294920 | tf_op jit(solution)/shard_map/ppermute | solution.py:619
  24.7 2.1 %collective-permute-start.7 = (bf16[128,256]{1,0:T(8,128)(2,1)S(1)}, bf16[128,256]{1,0:T(8,128)(2,1)S(1)}, u32[]{:S(2)}, u32[]{:S(2)}) collective-permute-start(bf16[128,256]{1,0:T(8,128)(2,1)S(1)} %get-tuple-element.104), channel_id=1, source_target_pairs={{0,4},{4,0},{8,12},{12,8},{16,20},{20,16},{24,28},{28,24},{1,5},{5... | collective-permute-start | bytes 196616 | tf_op jit(solution)/shard_map/ppermute | solution.py:619
  26.8 1.1 %shard_map.122 = (bf16[512,640]{1,0:T(8,128)(2,1)S(1)}, f32[1,512]{1,0:T(1,128)S(1)}, f32[640,512]{1,0:T(8,128)S(1)}, bf16[512,128]{1,0:T(8,128)(2,1)S(1)}) custom-call(f32[1,1280]{1,0:T(1,128)S(1)} %reshape.15.gain_ref, bf16[1280,2560]{1,0:T(8,128)(2,1)S(1)} %bitcast.5, bf16[512,128]{1,0:T(8,128)(2,1)S(1)} %copy-done.2, ...), custom_call_target="tpu_custom_call" | custom-call | flops 1000 | bytes 1000 | tf_op jit(solution)/shard_map/pallas_call | solution.py:66
  27.9 0.8 %shard_map.123 = (bf16[512,384]{1,0:T(8,128)(2,1)S(1)}, f32[1,512]{1,0:T(1,128)S(1)}, f32[640,512]{1,0:T(8,128)S(1)}) custom-call(f32[1,1280]{1,0:T(1,128)S(1)} %reshape.15.gain_ref, bf16[1280,2560]{1,0:T(8,128)(2,1)S(1)} %bitcast.5, bf16[512,128]{1,0:T(8,128)(2,1)S(1)} %get-tuple-element.98.rd_ref, f32[512,384]{1,0:T(8,128)S(1)} %get-tuple-element.85.refs_3_.refs_0_, ...), custom_call_target="tpu_custom_call" | custom-call | flops 1000 | bytes 1000 | tf_op jit(solution)/shard_map/pallas_call | solution.py:66
  28.8 0.2 collective-permute-done.7.e_ref
  29.0 0.5 %shard_map.124 = (bf16[512,256]{1,0:T(8,128)(2,1)S(1)}, bf16[392,512]{1,0:T(8,128)(2,1)S(1)}) custom-call(bf16[512,128]{1,0:T(8,128)(2,1)S(1)} %get-tuple-element.98.rd_ref, f32[512,256]{1,0:T(8,128)S(1)} %get-tuple-element.87.refs_4_.a_ref, f32[512,256]{1,0:T(8,128)S(1)} %get-tuple-element.103.b_ref, bf16[128,256]{1,0:T(8,128)(2,1)S(1)} %collective-permute-done.7.e_ref, ...), custom_call_target="tpu_custom_call" | custom-call | flops 1000 | bytes 1000 | tf_op jit(solution)/shard_map/pallas_call | solution.py:66
  29.5 0.1 collective-permute-start.9
  29.6 0.9 %shard_map.125 = (bf16[256,512]{1,0:T(8,128)(2,1)S(1)}, f32[384,512]{1,0:T(8,128)S(1)}) custom-call(f32[640,512]{1,0:T(8,128)S(1)} %get-tuple-element.105.p_ref.refs_0_, bf16[1280,2560]{1,0:T(8,128)(2,1)S(1)} %bitcast.5, bf16[512,640]{1,0:T(8,128)(2,1)S(1)} %get-tuple-element.97.refs_2_.refs_1_.refs_0_, ...), custom_call_target="tpu_custom_call" | custom-call | flops 1000 | bytes 1000 | tf_op jit(solution)/shard_map/pallas_call | solution.py:66
  30.5 0.6 %collective-permute-start.8 = (bf16[256,512]{1,0:T(8,128)(2,1)S(1)}, bf16[256,512]{1,0:T(8,128)(2,1)S(1)}, u32[]{:S(2)}, u32[]{:S(2)}) collective-permute-start(bf16[256,512]{1,0:T(8,128)(2,1)S(1)} %get-tuple-element.109), channel_id=1, source_target_pairs={{0,1},{1,0},{2,3},{3,2},{4,5},{5,4},{6,7},{7,6},{8,9},{9,8},{10,11... | collective-permute-start | bytes 786440 | tf_op jit(solution)/shard_map/ppermute | solution.py:622
  31.0 0.3 collective-permute-done.9.got_ref
  31.3 0.1 shard_map.126.refs_5_.factor_ref
  31.4 1.6 %collective-permute-start.15 = (bf16[392,512]{1,0:T(8,128)(2,1)S(1)}, bf16[392,512]{1,0:T(8,128)(2,1)S(1)}, u32[]{:S(2)}, u32[]{:S(2)}) collective-permute-start(bf16[392,512]{1,0:T(8,128)(2,1)S(1)} %shard_map.126.refs_5_.factor_ref), channel_id=1, source_target_pairs={{0,2},{1,3},{2,0},{3,1},{4,6},{5,7},{6,4},{7,5},{8,10},{9,11},{10,... | collective-permute-start | bytes 1204232 | tf_op jit(solution)/shard_map/ppermute | solution.py:622
  33.0 0.6 %shard_map.127.refs_4_ = bf16[256,512]{1,0:T(8,128)(2,1)S(1)} custom-call(bf16[1280,2560]{1,0:T(8,128)(2,1)S(1)} %bitcast.5, bf16[256,512]{1,0:T(8,128)(2,1)S(1)} %collective-permute-done.8.refs_1_, bf16[512,640]{1,0:T(8,128)(2,1)S(1)} %get-tuple-element.97.refs_2_.refs_1_.refs_0_, bf16[512,384]{1,0:T(8,128)(2,1)S(1)} %get-tuple-element.102.refs_3_.refs_2_.refs_1_, ...), custom_call_target="tpu_custom_call" | custom-call | flops 1000 | bytes 1000 | tf_op jit(solution)/shard_map/pallas_call | solution.py:66
  33.6 1.2 %shard_map.128 = (bf16[160,512]{1,0:T(8,128)(2,1)S(1)}, bf16[160,512]{1,0:T(8,128)(2,1)S(1)}, bf16[160,512]{1,0:T(8,128)(2,1)S(1)}, bf16[160,512]{1,0:T(8,128)(2,1)S(1)}) custom-call(bf16[1280,2560]{1,0:T(8,128)(2,1)S(1)} %bitcast.5, bf16[512,640]{1,0:T(8,128)(2,1)S(1)} %get-tuple-element.97.refs_2_.refs_1_.refs_0_, ...), custom_call_target="tpu_custom_call" | custom-call | flops 1000 | bytes 1000 | tf_op jit(solution)/shard_map/pallas_call | solution.py:66
  34.8 0.1 collective-permute-start.10
  34.9 1.1 %collective-permute-start.14 = (bf16[256,512]{1,0:T(8,128)(2,1)S(1)}, bf16[256,512]{1,0:T(8,128)(2,1)S(1)}, u32[]{:S(2)}, u32[]{:S(2)}) collective-permute-start(bf16[256,512]{1,0:T(8,128)(2,1)S(1)} %shard_map.127.refs_4_), channel_id=1, source_target_pairs={{0,2},{1,3},{2,0},{3,1},{4,6},{5,7},{6,4},{7,5},{8,10},{9,11},{10,... | collective-permute-start | bytes 786440 | tf_op jit(solution)/shard_map/ppermute | solution.py:622
  36.0 0.5 %collective-permute-start.12 = (bf16[160,512]{1,0:T(8,128)(2,1)S(1)}, bf16[160,512]{1,0:T(8,128)(2,1)S(1)}, u32[]{:S(2)}, u32[]{:S(2)}) collective-permute-start(bf16[160,512]{1,0:T(8,128)(2,1)S(1)} %get-tuple-element.113), channel_id=1, source_target_pairs={{0,1},{1,0},{2,3},{3,2},{4,5},{5,4},{6,7},{7,6},{8,9},{9,8},{10,11... | collective-permute-start | bytes 491528 | tf_op jit(solution)/shard_map/ppermute | solution.py:622
  36.5 0.9 %collective-permute-done.11.refs_4_ = bf16[160,512]{1,0:T(8,128)(2,1)S(1)} collective-permute-done((bf16[160,512]{1,0:T(8,128)(2,1)S(1)}, bf16[160,512]{1,0:T(8,128)(2,1)S(1)}, u32[]{:S(2)}, u32[]{:S(2)}) %collective-permute-start.11) | collective-permute-done | bytes 163872 | tf_op jit(solution)/shard_map/ppermute | solution.py:622
  37.4 0.2 collective-permute-done.12.refs_5_
  37.6 0.3 collective-permute-done.13.refs_6_
  37.9 1.2 %shard_map.129.own_ref = f32[640,512]{1,0:T(8,128)S(1)} custom-call(bf16[1280,2560]{1,0:T(8,128)(2,1)S(1)} %bitcast.5, bf16[512,640]{1,0:T(8,128)(2,1)S(1)} %get-tuple-element.97.refs_2_.refs_1_.refs_0_, bf16[512,384]{1,0:T(8,128)(2,1)S(1)} %get-tuple-element.102.refs_3_.refs_2_.refs_1_, bf16[512,256]{1,0:T(8,128)(2,1)S(1)} %get-tuple-element.107.refs_4_.refs_3_.refs_2_, ...), custom_call_target="tpu_custom_call" | custom-call | flops 1000 | bytes 1000 | tf_op jit(solution)/shard_map/pallas_call | solution.py:66
  39.1 4.5 %collective-permute-done.15.far_ref = bf16[392,512]{1,0:T(8,128)(2,1)S(1)} collective-permute-done((bf16[392,512]{1,0:T(8,128)(2,1)S(1)}, bf16[392,512]{1,0:T(8,128)(2,1)S(1)}, u32[]{:S(2)}, u32[]{:S(2)}) %collective-permute-start.15) | collective-permute-done | bytes 401440 | tf_op jit(solution)/shard_map/ppermute | solution.py:622
  43.6 0.8 %shard_map.130 = (bf16[640,512]{1,0:T(8,128)(2,1)}, f32[1,512]{1,0:T(1,128)S(1)}) custom-call(f32[640,512]{1,0:T(8,128)S(1)} %shard_map.129.own_ref, bf16[392,512]{1,0:T(8,128)(2,1)S(1)} %collective-permute-done.15.far_ref, bf16[392,512]{1,0:T(8,128)(2,1)S(1)} %shard_map.126.refs_5_.factor_ref), custom_call_target="tpu_custom_call" | custom-call | flops 1000 | bytes 1000 | tf_op jit(solution)/shard_map/pallas_call | solution.py:599
  44.4 4.0 %collective-permute-done.14.far_ref = bf16[256,512]{1,0:T(8,128)(2,1)S(1)} collective-permute-done((bf16[256,512]{1,0:T(8,128)(2,1)S(1)}, bf16[256,512]{1,0:T(8,128)(2,1)S(1)}, u32[]{:S(2)}, u32[]{:S(2)}) %collective-permute-start.14) | collective-permute-done | bytes 262176 | tf_op jit(solution)/shard_map/ppermute | solution.py:622
  48.4 0.8 %shard_map.131 = bf16[640,512]{1,0:T(8,128)(2,1)} custom-call(f32[640,512]{1,0:T(8,128)S(1)} %shard_map.129.own_ref, bf16[256,512]{1,0:T(8,128)(2,1)S(1)} %collective-permute-done.14.far_ref, f32[1,512]{1,0:T(1,128)S(1)} %get-tuple-element.115.factor_ref, bf16[640,512]{1,0:T(8,128)(2,1)} %get-tuple-element.116.refs_0_), custom_call_target="tpu_custom_call", output_to_operand_aliasing={{}: (3, {})} | custom-call | flops 1000 | bytes 1000 | tf_op jit(solution)/shard_map/pallas_call | solution.py:599
  (27 shorter events, 0.1 us)
Async XLA Ops:
  0.0 5.6 %copy-start = (bf16[512,1280]{1,0:T(8,128)(2,1)S(1)}, bf16[512,1280]{1,0:T(8,128)(2,1)}, u32[]{:S(2)}) copy-start(bf16[512,1280]{1,0:T(8,128)(2,1)} %refs_0_.13) | copy-start | bytes 3932164
  0.0 5.6 %copy-start.3 = (bf16[512,128]{1,0:T(8,128)(2,1)S(1)}, bf16[512,128]{1,0:T(8,128)(2,1)}, u32[]{:S(2)}) copy-start(bf16[512,128]{1,0:T(8,128)(2,1)} %refs_2_.7) | copy-start | bytes 393220
  0.0 7.3 %copy-start.2 = (bf16[512,128]{1,0:T(8,128)(2,1)S(1)}, bf16[512,128]{1,0:T(8,128)(2,1)}, u32[]{:S(2)}) copy-start(bf16[512,128]{1,0:T(8,128)(2,1)} %rd_ref.1) | copy-start | bytes 393220
  2.5 4.8 %copy-start.5 = (f32[20]{0:T(128)S(1)}, f32[20]{0:T(128)}, u32[]{:S(2)}) copy-start(f32[20]{0:T(128)} %param.19) | copy-start | bytes 244
  2.5 6.3 %collective-permute-start = (bf16[136,384]{1,0:T(8,128)(2,1)}, bf16[136,384]{1,0:T(8,128)(2,1)S(1)}, u32[]{:S(2)}, u32[]{:S(2)}) collective-permute-start(bf16[136,384]{1,0:T(8,128)(2,1)} %get-tuple-element.63), channel_id=1, source_target_pairs={{0,4},{4,0},{8,12},{12,8},{16,20},{20,16},{24,28},{28,24},{1,5},{5... | collective-permute-start | bytes 313352 | tf_op jit(solution)/shard_map/ppermute | solution.py:619
  5.6 0.9 %copy-start.1 = (f32[104,512]{1,0:T(8,128)S(1)}, f32[104,512]{1,0:T(8,128)}, u32[]{:S(2)}) copy-start(f32[104,512]{1,0:T(8,128)} %get-tuple-element.61.stash_ref.refs_2_) | copy-start | bytes 638980
  7.2 4.4 %collective-permute-start.2 = (bf16[136,256]{1,0:T(8,128)(2,1)S(1)}, bf16[136,256]{1,0:T(8,128)(2,1)S(1)}, u32[]{:S(2)}, u32[]{:S(2)}) collective-permute-start(bf16[136,256]{1,0:T(8,128)(2,1)S(1)} %get-tuple-element.64.refs_4_), channel_id=1, source_target_pairs={{0,4},{4,0},{8,12},{12,8},{16,20},{20,16},{24,28},{28,24},{1,5},{5... | collective-permute-start | bytes 208904 | tf_op jit(solution)/shard_map/ppermute | solution.py:619
  8.8 1.8 %copy-start.4 = (bf16[512,1280]{1,0:T(8,128)(2,1)S(1)}, bf16[512,1280]{1,0:T(8,128)(2,1)}, u32[]{:S(2)}) copy-start(bf16[512,1280]{1,0:T(8,128)(2,1)} %refs_1_.10) | copy-start | bytes 3932164
  8.9 5.7 %collective-permute-start.1 = (bf16[136,384]{1,0:T(8,128)(2,1)S(1)}, bf16[136,384]{1,0:T(8,128)(2,1)S(1)}, u32[]{:S(2)}, u32[]{:S(2)}) collective-permute-start(bf16[136,384]{1,0:T(8,128)(2,1)S(1)} %get-tuple-element.66.refs_9_), channel_id=1, source_target_pairs={{0,8},{4,12},{8,0},{12,4},{16,24},{20,28},{24,16},{28,20},{1,9},{5... | collective-permute-start | bytes 313352 | tf_op jit(solution)/shard_map/ppermute | solution.py:619
  11.7 7.0 %collective-permute-start.4 = (bf16[136,256]{1,0:T(8,128)(2,1)S(1)}, bf16[136,256]{1,0:T(8,128)(2,1)S(1)}, u32[]{:S(2)}, u32[]{:S(2)}) collective-permute-start(bf16[136,256]{1,0:T(8,128)(2,1)S(1)} %get-tuple-element.77.refs_9_), channel_id=1, source_target_pairs={{0,8},{4,12},{8,0},{12,4},{16,24},{20,28},{24,16},{28,20},{1,9},{5... | collective-permute-start | bytes 208904 | tf_op jit(solution)/shard_map/ppermute | solution.py:619
  14.7 7.7 %collective-permute-start.3 = (bf16[136,384]{1,0:T(8,128)(2,1)S(1)}, bf16[136,384]{1,0:T(8,128)(2,1)S(1)}, u32[]{:S(2)}, u32[]{:S(2)}) collective-permute-start(bf16[136,384]{1,0:T(8,128)(2,1)S(1)} %get-tuple-element.79.refs_9_), channel_id=1, source_target_pairs={{0,16},{4,20},{8,24},{12,28},{16,0},{20,4},{24,8},{28,12},{1,17},{... | collective-permute-start | bytes 313352 | tf_op jit(solution)/shard_map/ppermute | solution.py:619
  18.7 8.0 %slice-start = ((s8[6553600]{0:T(1024)(128)(4,1)}), s8[4194304]{0:T(1024)(128)(4,1)S(1)}, s32[]{:S(2)}) async-start(s8[6553600]{0:T(1024)(128)(4,1)} %bitcast.4), calls=%async_computation | async-start | bytes 8388608
  18.7 8.0 %slice-start.1 = ((s8[6553600]{0:T(1024)(128)(4,1)}), s8[2359296]{0:T(1024)(128)(4,1)S(1)}, s32[]{:S(2)}) async-start(s8[6553600]{0:T(1024)(128)(4,1)} %bitcast.4), calls=%async_computation.1 | async-start | bytes 4718592
  18.7 5.9 %collective-permute-start.5 = (bf16[136,256]{1,0:T(8,128)(2,1)S(1)}, bf16[136,256]{1,0:T(8,128)(2,1)S(1)}, u32[]{:S(2)}, u32[]{:S(2)}) collective-permute-start(bf16[136,256]{1,0:T(8,128)(2,1)S(1)} %get-tuple-element.86.refs_9_), channel_id=1, source_target_pairs={{0,16},{4,20},{8,24},{12,28},{16,0},{20,4},{24,8},{28,12},{1,17},{... | collective-permute-start | bytes 208904 | tf_op jit(solution)/shard_map/ppermute | solution.py:619
  20.1 6.7 %copy-start.6 = (f32[1280]{0:T(1024)S(1)}, f32[1280]{0:T(1024)}, u32[]{:S(2)}) copy-start(f32[1280]{0:T(1024)} %param.20) | copy-start | bytes 15364
  22.5 5.5 %collective-permute-start.6 = (bf16[128,384]{1,0:T(8,128)(2,1)S(1)}, bf16[128,384]{1,0:T(8,128)(2,1)S(1)}, u32[]{:S(2)}, u32[]{:S(2)}) collective-permute-start(bf16[128,384]{1,0:T(8,128)(2,1)S(1)} %get-tuple-element.95.refs_4_), channel_id=1, source_target_pairs={{0,4},{4,0},{8,12},{12,8},{16,20},{20,16},{24,28},{28,24},{1,5},{5... | collective-permute-start | bytes 294920 | tf_op jit(solution)/shard_map/ppermute | solution.py:619
  24.7 4.3 %collective-permute-start.7 = (bf16[128,256]{1,0:T(8,128)(2,1)S(1)}, bf16[128,256]{1,0:T(8,128)(2,1)S(1)}, u32[]{:S(2)}, u32[]{:S(2)}) collective-permute-start(bf16[128,256]{1,0:T(8,128)(2,1)S(1)} %get-tuple-element.104), channel_id=1, source_target_pairs={{0,4},{4,0},{8,12},{12,8},{16,20},{20,16},{24,28},{28,24},{1,5},{5... | collective-permute-start | bytes 196616 | tf_op jit(solution)/shard_map/ppermute | solution.py:619
  29.5 1.8 %collective-permute-start.9 = (bf16[392,512]{1,0:T(8,128)(2,1)S(1)}, bf16[392,512]{1,0:T(8,128)(2,1)S(1)}, u32[]{:S(2)}, u32[]{:S(2)}) collective-permute-start(bf16[392,512]{1,0:T(8,128)(2,1)S(1)} %get-tuple-element.108.refs_5_.mine_ref), channel_id=1, source_target_pairs={{0,1},{1,0},{2,3},{3,2},{4,5},{5,4},{6,7},{7,6},{8,9},{9,8},{10,11... | collective-permute-start | bytes 1204232 | tf_op jit(solution)/shard_map/ppermute | solution.py:622
  30.5 2.5 %collective-permute-start.8 = (bf16[256,512]{1,0:T(8,128)(2,1)S(1)}, bf16[256,512]{1,0:T(8,128)(2,1)S(1)}, u32[]{:S(2)}, u32[]{:S(2)}) collective-permute-start(bf16[256,512]{1,0:T(8,128)(2,1)S(1)} %get-tuple-element.109), channel_id=1, source_target_pairs={{0,1},{1,0},{2,3},{3,2},{4,5},{5,4},{6,7},{7,6},{8,9},{9,8},{10,11... | collective-permute-start | bytes 786440 | tf_op jit(solution)/shard_map/ppermute | solution.py:622
  31.4 12.2 %collective-permute-start.15 = (bf16[392,512]{1,0:T(8,128)(2,1)S(1)}, bf16[392,512]{1,0:T(8,128)(2,1)S(1)}, u32[]{:S(2)}, u32[]{:S(2)}) collective-permute-start(bf16[392,512]{1,0:T(8,128)(2,1)S(1)} %shard_map.126.refs_5_.factor_ref), channel_id=1, source_target_pairs={{0,2},{1,3},{2,0},{3,1},{4,6},{5,7},{6,4},{7,5},{8,10},{9,11},{10,... | collective-permute-start | bytes 1204232 | tf_op jit(solution)/shard_map/ppermute | solution.py:622
  34.8 1.7 %collective-permute-start.10 = (bf16[160,512]{1,0:T(8,128)(2,1)S(1)}, bf16[160,512]{1,0:T(8,128)(2,1)S(1)}, u32[]{:S(2)}, u32[]{:S(2)}) collective-permute-start(bf16[160,512]{1,0:T(8,128)(2,1)S(1)} %get-tuple-element.111), channel_id=1, source_target_pairs={{0,1},{1,0},{2,3},{3,2},{4,5},{5,4},{6,7},{7,6},{8,9},{9,8},{10,11... | collective-permute-start | bytes 491528 | tf_op jit(solution)/shard_map/ppermute | solution.py:622
  34.9 13.5 %collective-permute-start.14 = (bf16[256,512]{1,0:T(8,128)(2,1)S(1)}, bf16[256,512]{1,0:T(8,128)(2,1)S(1)}, u32[]{:S(2)}, u32[]{:S(2)}) collective-permute-start(bf16[256,512]{1,0:T(8,128)(2,1)S(1)} %shard_map.127.refs_4_), channel_id=1, source_target_pairs={{0,2},{1,3},{2,0},{3,1},{4,6},{5,7},{6,4},{7,5},{8,10},{9,11},{10,... | collective-permute-start | bytes 786440 | tf_op jit(solution)/shard_map/ppermute | solution.py:622
  36.0 1.4 %collective-permute-start.11 = (bf16[160,512]{1,0:T(8,128)(2,1)S(1)}, bf16[160,512]{1,0:T(8,128)(2,1)S(1)}, u32[]{:S(2)}, u32[]{:S(2)}) collective-permute-start(bf16[160,512]{1,0:T(8,128)(2,1)S(1)} %get-tuple-element.112), channel_id=1, source_target_pairs={{0,1},{1,0},{2,3},{3,2},{4,5},{5,4},{6,7},{7,6},{8,9},{9,8},{10,11... | collective-permute-start | bytes 491528 | tf_op jit(solution)/shard_map/ppermute | solution.py:622
  36.0 1.6 %collective-permute-start.12 = (bf16[160,512]{1,0:T(8,128)(2,1)S(1)}, bf16[160,512]{1,0:T(8,128)(2,1)S(1)}, u32[]{:S(2)}, u32[]{:S(2)}) collective-permute-start(bf16[160,512]{1,0:T(8,128)(2,1)S(1)} %get-tuple-element.113), channel_id=1, source_target_pairs={{0,1},{1,0},{2,3},{3,2},{4,5},{5,4},{6,7},{7,6},{8,9},{9,8},{10,11... | collective-permute-start | bytes 491528 | tf_op jit(solution)/shard_map/ppermute | solution.py:622
  36.5 1.4 %collective-permute-start.13 = (bf16[160,512]{1,0:T(8,128)(2,1)S(1)}, bf16[160,512]{1,0:T(8,128)(2,1)S(1)}, u32[]{:S(2)}, u32[]{:S(2)}) collective-permute-start(bf16[160,512]{1,0:T(8,128)(2,1)S(1)} %get-tuple-element.114), channel_id=1, source_target_pairs={{0,1},{1,0},{2,3},{3,2},{4,5},{5,4},{6,7},{7,6},{8,9},{9,8},{10,11... | collective-permute-start | bytes 491528 | tf_op jit(solution)/shard_map/ppermute | solution.py:622
